TPU v7x, 512 devices: a whole 4x8x8 slice. The times are simulated.
512 devices in a mesh: batch: 128 (over y, x, z_hi), rep: 4 (over z_lo, core).
Axes of the slice: x: 4, y: 8, z: 8 (z_hi: 4, z_lo: 2; z = z_hi * 2 + z_lo), core: 2. Of those that a mesh axis runs over, the one named last changes fastest.
Arguments:
- img_feat: bfloat16 [16384, 1152], P('batch'), may hold values from -48 to 48
- head_weight: bfloat16 [1152, 1152], replicated, may hold values from -1 to 3
- text_embed: bfloat16 [16384, 1152], P(('batch', 'rep')), may hold values from -48 to 48
- log_temp: float32 [1], replicated, may hold values from 3.5 to 4.7
- logit_bias: float32 [1], replicated, may hold values from -14 to -6
Outputs:
- loss: float32 [1], replicated
- feat_grad: bfloat16 [16384, 1152], P('batch')
- head_grad: bfloat16 [1152, 1152], P(None, 'rep')
All inputs are finite; a program needn't handle non-finite values.
Results may differ from a plain program's by a relative error of at most 0.0058.
Values may be sent and summed in bfloat16 or wider, within the bound.
No kernel may reach another device: no remote copies, remote signals or barrier semaphores. Data moves between devices by JAX's collectives and lax.ppermute only.
A program may use at most 64 MiB of HBM per device.

v0:
```python
import jax
import jax.numpy as jnp
from jax import lax
from jax.sharding import PartitionSpec as P

EPS = 1e-06


def normalize(values):
    inverse = lax.rsqrt(jnp.sum(values * values, axis=-1, keepdims=True) + EPS)
    return (values * inverse, inverse)


def back_norm(direction, unit, inverse):
    return (direction - unit * jnp.sum(unit * direction, axis=-1, keepdims=True)) * inverse


def local(img_feat, head_weight, text_embed, log_temp, logit_bias):
    rows = img_feat.shape[0]
    width = head_weight.shape[1]
    quarter = text_embed.shape[0]
    rep_at = lax.axis_index("rep")
    scale = jnp.exp(log_temp[0])
    shift = logit_bias[0]
    image_head = jnp.dot(img_feat, head_weight, preferred_element_type=jnp.float32)
    image_unit, image_inv = normalize(image_head)
    image_low = image_unit.astype(jnp.bfloat16)
    own_index = lax.axis_index("batch") * rows + jnp.arange(rows, dtype=jnp.int32)[:, None]
    text_unit, text_inv = normalize(text_embed.astype(jnp.float32))
    text_low = text_unit.astype(jnp.bfloat16)
    piece_low = lax.all_gather(text_low, "batch", axis=0, tiled=True)
    position = jnp.arange(piece_low.shape[0], dtype=jnp.int32)
    columns = (position // quarter * rows + rep_at * quarter + position % quarter)[None, :]
    logits = (
        scale
        * lax.dot_general(
            image_low, piece_low, (((1,), (1,)), ((), ())), preferred_element_type=jnp.float32
        )
        + shift
    )
    label = jnp.where(own_index == columns, 1.0, -1.0).astype(jnp.float32)
    partial_loss = jnp.sum(-jax.nn.log_sigmoid(label * logits))
    slope = (-label * jax.nn.sigmoid(-label * logits)).astype(jnp.bfloat16)
    image_dir = scale * jnp.dot(slope, piece_low, preferred_element_type=jnp.float32)
    image_dir, total = (image_dir, partial_loss)
    cols = width // lax.axis_size("rep")
    image_dir, rep_total = lax.psum((image_dir, total), "rep")
    image_back = back_norm(image_dir, image_unit, image_inv).astype(jnp.bfloat16)
    back_cols = lax.dynamic_slice_in_dim(image_back, rep_at * cols, cols, 1)
    feat_grad = lax.dot_general(
        image_back, head_weight, (((1,), (1,)), ((), ())), preferred_element_type=jnp.float32
    ).astype(jnp.bfloat16)
    partial_head = lax.dot_general(
        img_feat, back_cols, (((0,), (0,)), ((), ())), preferred_element_type=jnp.float32
    )
    head_part, whole_total = lax.psum((partial_head, rep_total), "batch")
    group_rows = rows * lax.axis_size("batch")
    loss = (whole_total / (group_rows * group_rows)).reshape(1)
    return (loss, feat_grad, head_part.astype(jnp.bfloat16))


def solution(mesh):
    in_specs = (P("batch", None), P(), P(("batch", "rep"), None), P(), P())
    out_specs = (P(), P("batch", None), P(None, "rep"))
    return jax.shard_map(local, mesh=mesh, in_specs=in_specs, out_specs=out_specs, check_vma=False)
```

profile of v0, /device:TPU:64, one launch (start us, length us, event | category | flops | bytes accessed | tf_op | source)
XLA Modules:
  0.0 1011.0 jit_solution(7837025172830174020)
XLA Ops:
  7.2 0.0 copy-start
  7.2 0.0 all-gather.2.cloned.1.call-start
  7.2 1.2 fusion.16
  8.4 1.6 fusion.17
  10.0 0.0 all-gather.2.cloned.1.call-update
  10.0 0.0 all-reduce.4.cloned.1.call-start
  11.4 0.0 copy-done
  11.5 1.6 multiply_reduce_fusion.1
  13.1 165.4 %all-gather.2.cloned.1.call-done = bf16[4096,1152]{1,0:T(8,128)(2,1)} async-done(((bf16[32,1152]{1,0:T(8,128)(2,1)}), bf16[4096,1152]{1,0:T(8,128)(2,1)}) %all-gather.2.cloned.1.call-update) | async-done | bytes 9437200 | tf_op jit(solution)/shard_map/all_gather | solution.py:31
  178.5 0.0 copy-start.2
  178.5 8.2 fusion.8
  186.8 0.0 copy-done.2
  186.8 2.7 convolution_multiply_fusion.1
  189.4 0.0 copy-start.1
  189.4 0.0 all-reduce.4.cloned.1.call-update
  189.4 6.3 psum.28
  195.8 38.1 %all-reduce.4.cloned.1.call-done = f32[128,1152]{1,0:T(8,128)} async-done(((f32[128,1152]{1,0:T(8,128)}), f32[128,1152]{1,0:T(8,128)}) %all-reduce.4.cloned.1.call-update) | async-done | bytes 589840 | tf_op jit(solution)/shard_map/psum | solution.py:47
  233.8 1.3 multiply_reduce_fusion
  235.1 1.2 multiply_convert_fusion
  236.3 0.0 copy-done.1
  236.3 1.5 convolution_bitcast_fusion
  237.9 1.6 convolution_convert_fusion
  239.5 762.9 %all-reduce.5 = (f32[]{:T(128)}, bf16[1152,288]{0,1:T(8,128)(2,1)}) all-reduce(f32[]{:T(128)} %psum.28, f32[1152,288]{0,1:T(8,128)} %convolution_bitcast_fusion), channel_id=1, replica_groups=mesh['batch'=128,'rep'=4] {'batch'}, use_global_device_ids=true, to_apply=%region_4.5 | all-reduce | flops 331777 | bytes 1990664 | tf_op jit(solution)/shard_map/psum | solution.py:56
  (4 shorter events, 0.0 us)
Async XLA Ops:
  7.2 4.3 copy-start
  7.2 171.3 %all-gather.2.cloned.1.call-start = ((), (), s32[]{:S(2)}) async-start(), calls=%async_computation | async-start | bytes 9510912 | tf_op jit(solution)/shard_map/all_gather | solution.py:31
  10.0 223.8 %all-reduce.4.cloned.1.call-start = ((), (), s32[]{:S(2)}) async-start(), calls=%async_computation.1 | async-start | bytes 1179648 | tf_op jit(solution)/shard_map/psum | solution.py:47
  178.5 8.2 copy-start.2
  189.4 46.9 %copy-start.1 = (bf16[128,1152]{1,0:T(8,128)(2,1)S(1)}, bf16[128,1152]{1,0:T(8,128)(2,1)}, u32[]{:S(2)}) copy-start(bf16[128,1152]{1,0:T(8,128)(2,1)} %param.5) | copy-start | bytes 884740
Sparse Core Ops, SparseCore 0:
  13.0 165.4 all-gather.1
  189.6 44.2 all-reduce.3
where the time goes:
time: 1010 us
  blocking collectives  769 us (76%)
  waiting for transfers between devices  203 us (20%)
  between operations  17.2 us (2%)
  matrix products  15.7 us (2%)
    psum x1, blocking collectives, local(): head_part, whole_total = lax.psum((partial_head, rep_total), 'batch')  763 us
    all_gather x1, waiting for transfers between devices, local(): piece_low = lax.all_gather(text_low, 'batch', axis=0, tiled=True)  165 us
    psum x1, waiting for transfers between devices, local(): image_dir, rep_total = lax.psum((image_dir, total), 'rep')  38.1 us
  transfers between devices with their start and end apart: 2, of which 2 were waited for; matrix products, arithmetic and copies ran while one was open for 0% of the time, Pallas kernels for 0%

commit v1 on v0

v1 whole, which is shorter than its diff:
```python
import jax
import jax.numpy as jnp
from jax import lax
from jax.sharding import Mesh
from jax.sharding import PartitionSpec as P

EPS = 1e-06
BF16 = jnp.bfloat16
F32 = jnp.float32


def normalize(values):
    inverse = lax.rsqrt(jnp.sum(values * values, axis=-1, keepdims=True) + EPS)
    return (values * inverse, inverse)


def back_norm(direction, unit, inverse):
    return (direction - unit * jnp.sum(unit * direction, axis=-1, keepdims=True)) * inverse


def spread(block, axes):
    n = lax.axis_size(axes)
    copies = jnp.broadcast_to(block[None], (n,) + block.shape).reshape((n * block.shape[0],) + block.shape[1:])
    return lax.all_to_all(copies, axes, 0, 0, tiled=True)


def split3(value):
    hi = value.astype(BF16)
    rest = value - hi.astype(F32)
    mid = rest.astype(BF16)
    low = (rest - mid.astype(F32)).astype(BF16)
    return (hi, mid, low)


def local(img_feat, head_weight, text_embed, log_temp, logit_bias):
    rows, width = img_feat.shape
    quarter = text_embed.shape[0]
    ny, nx, nzh, nzl, nc = (lax.axis_size(a) for a in ("y", "x", "zh", "zl", "c"))
    nrep = nzl * nc
    y_at, x_at, zh_at, zl_at, c_at = (lax.axis_index(a) for a in ("y", "x", "zh", "zl", "c"))
    rep_at = zl_at * nc + c_at
    scale = jnp.exp(log_temp[0])
    shift = logit_bias[0]

    text_unit, _ = normalize(text_embed.astype(F32))
    text_low = text_unit.astype(BF16)

    image_head = jnp.dot(img_feat, head_weight, preferred_element_type=F32)
    image_unit, image_inv = normalize(image_head)
    image_low = image_unit.astype(BF16)
    images = lax.all_gather(image_low, "zh", axis=0)
    images = images.reshape(nzh, nzl, nc, quarter, width).transpose(2, 0, 1, 3, 4)
    images = images.reshape(nzh * rows, width)

    texts = spread(text_low, "y")
    texts = spread(texts, "x")

    logits = (
        scale * lax.dot_general(images, texts, (((1,), (1,)), ((), ())), preferred_element_type=F32)
        + shift
    )
    row = jnp.arange(nzh * rows, dtype=jnp.int32)[:, None]
    col = jnp.arange(nx * ny * quarter, dtype=jnp.int32)[None, :]
    own_row = c_at * (nzh * nzl * quarter) + (zh_at * nzl + zl_at) * quarter
    own_col = (x_at * ny + y_at) * quarter
    own = (row - own_row == col - own_col) & (row >= own_row) & (row < own_row + quarter)
    label = jnp.where(own, 1.0, -1.0).astype(F32)
    partial_loss = jnp.sum(-jax.nn.log_sigmoid(label * logits))
    slope = (-label * jax.nn.sigmoid(-label * logits)).astype(BF16)
    partial_dir = scale * jnp.dot(slope, texts, preferred_element_type=F32)

    half = nzh * nzl * quarter
    mine = lax.dynamic_slice_in_dim(partial_dir, c_at * half, half, 0)
    other = lax.dynamic_slice_in_dim(partial_dir, (1 - c_at) * half, half, 0).astype(BF16)
    other = lax.ppermute(other, "c", [(0, 1), (1, 0)])
    both = (mine + other.astype(F32)).astype(BF16)
    parts = lax.all_to_all(both, ("zh", "zl"), 0, 0, tiled=True)
    image_dir = jnp.sum(parts.reshape(nzh * nzl, quarter, width).astype(F32), axis=0)

    own_unit = lax.dynamic_slice_in_dim(image_unit, rep_at * quarter, quarter, 0)
    own_inv = lax.dynamic_slice_in_dim(image_inv, rep_at * quarter, quarter, 0)
    own_back = back_norm(image_dir, own_unit, own_inv).astype(BF16)
    loss_terms = jnp.concatenate([jnp.full((1, 1), t, BF16) for t in split3(partial_loss)], axis=1)
    sent = jnp.concatenate([own_back, jnp.pad(loss_terms, ((0, 15), (0, width - 3)))], axis=0)
    gathered = spread(sent, ("zl", "c")).reshape(nrep, quarter + 16, width)
    image_back = gathered[:, :quarter].reshape(rows, width)
    rep_loss = jnp.sum(gathered[:, quarter, :3].astype(F32))

    feat_grad = lax.dot_general(
        image_back, head_weight, (((1,), (1,)), ((), ())), preferred_element_type=F32
    ).astype(BF16)
    cols = width // nrep
    back_cols = lax.dynamic_slice_in_dim(image_back, rep_at * cols, cols, 1)
    head_t = lax.dot_general(
        back_cols, img_feat, (((0,), (0,)), ((), ())), preferred_element_type=F32
    ).astype(BF16)
    lanes = 128
    tiles = width // lanes
    flat = head_t.reshape(cols, tiles, lanes).transpose(1, 0, 2).reshape(tiles * cols, lanes)
    plane = nx * ny
    piece = -(-(tiles * cols + 16) // (plane * 16)) * 16
    tail = jnp.concatenate([jnp.full((1, 1), t, BF16) for t in split3(rep_loss)], axis=1)
    tail = jnp.pad(tail, ((0, plane * piece - tiles * cols - 1), (0, lanes - 3)))
    flat = jnp.concatenate([flat, tail], axis=0)
    parts = lax.all_to_all(flat, ("y", "x"), 0, 0, tiled=True)
    part = jnp.sum(parts.reshape(plane, piece, lanes).astype(F32), axis=0)
    part = jnp.sum(spread(part, "zh").reshape(nzh, piece, lanes), axis=0)
    at_loss = tiles * cols
    whole = lax.axis_index(("y", "x"))
    holds = whole == at_loss // piece
    line = at_loss % piece
    total = jnp.where(holds, jnp.sum(part[line, :3]), 0.0)
    terms = jnp.concatenate([jnp.full((1, 1), t, BF16) for t in split3(total)], axis=1)
    terms = jnp.pad(terms, ((0, 0), (0, lanes - 3)))
    low = part.astype(BF16)
    low = jnp.concatenate([low[:line], jnp.where(holds, terms, low[line : line + 1]), low[line + 1 :]], axis=0)
    full = spread(low, ("y", "x"))
    head_grad = full[:at_loss].reshape(tiles, cols, lanes).transpose(0, 2, 1).reshape(width, cols)
    group = rows * ny * nx * nzh
    loss = (jnp.sum(full[at_loss, :3].astype(F32)) / (group * group)).reshape(1)
    return (loss, feat_grad, head_grad)


def solution(mesh):
    devices = mesh.devices.reshape(8, 4, 4, 2, 2)
    fine = Mesh(devices, ("y", "x", "zh", "zl", "c"))
    batch, rep = (("y", "x", "zh"), ("zl", "c"))
    in_specs = (P(batch, None), P(), P(batch + rep, None), P(), P())
    out_specs = (P(), P(batch, None), P(None, rep))
    return jax.shard_map(local, mesh=fine, in_specs=in_specs, out_specs=out_specs, check_vma=False)
```

time: 1010 us -> 226 us (0.22)
  the two profiles are of different devices: /device:TPU:64 before, /device:TPU:2 now
where the time goes in v1:
time: 226 us; the launch traced here: 225 us
  waiting for transfers between devices  95.4 us (42%)
  starting transfers between devices  36.7 us (16%)
  blocking collectives  26.7 us (12%)
  between operations  20.6 us (9%)
  local copies, waits for them, and re-layouts  17.7 us (8%)
  matrix products  14.3 us (6%)
  other arithmetic  13 us (6%)
    all_to_all x5, waiting for transfers between devices, spread(): return lax.all_to_all(copies, axes, 0, 0, tiled=True)  54.2 us
    all_to_all x1, blocking collectives, local(): parts = lax.all_to_all(flat, ('y', 'x'), 0, 0, tiled=True)  26.7 us
    all_to_all x5, starting transfers between devices, spread(): return lax.all_to_all(copies, axes, 0, 0, tiled=True)  24.3 us
    all_gather x1, waiting for transfers between devices, local(): images = lax.all_gather(image_low, 'zh', axis=0)  21.9 us
    all_to_all x1, waiting for transfers between devices, local(): parts = lax.all_to_all(both, ('zh', 'zl'), 0, 0, tiled=True)  17.1 us
    all_to_all x1, starting transfers between devices, local(): parts = lax.all_to_all(both, ('zh', 'zl'), 0, 0, tiled=True)  10.5 us
    dot_general x1, matrix products, local(): lax.dot_general(images, texts, (((1,), (1,)), ((), ())), preferred_elemen...  5.71 us
    broadcast_in_dim x5, local copies, waits for them, and re-layouts, spread(): jnp.broadcast_to(block[None], (n,) + block.shape)  4.87 us
  transfers between devices with their start and end apart: 8, of which 8 were waited for; matrix products, arithmetic and copies ran while one was open for 4% of the time, Pallas kernels for 0%

profile of v1, /device:TPU:2, one launch (start us, length us, event | category | flops | bytes accessed | tf_op | source)
XLA Modules:
  0.0 224.5 jit_solution(7548129037297165929)
XLA Ops:
  7.2 1.2 fusion.22
  8.4 1.0 fusion.23
  9.3 0.9 broadcast_in_dim.74
  10.2 7.1 %all-to-all-start = ((bf16[8,32,1152]{2,1,0:T(8,128)(2,1)}), bf16[8,32,1152]{2,1,0:T(8,128)(2,1)S(1)}, u32[]{:S(2)}, u32[]{:S(2)}) async-start(bf16[8,32,1152]{2,1,0:T(8,128)(2,1)} %broadcast_in_dim.74), calls=%async_computation | async-start | bytes 1179648 | tf_op jit(solution)/shard_map/all_to_all | solution.py:24
  17.3 0.7 multiply_reduce_fusion
  18.0 1.0 fusion.43
  19.1 17.1 %all-to-all-done = bf16[8,32,1152]{2,1,0:T(8,128)(2,1)S(1)} async-done(((bf16[8,32,1152]{2,1,0:T(8,128)(2,1)}), bf16[8,32,1152]{2,1,0:T(8,128)(2,1)S(1)}, u32[]{:S(2)}, u32[]{:S(2)}) %all-to-all-start) | async-done | bytes 589856 | tf_op jit(solution)/shard_map/all_to_all | solution.py:24
  36.2 1.6 broadcast_in_dim.76
  37.7 5.0 %all-to-all-start.1 = ((bf16[4,256,1152]{2,1,0:T(8,128)(2,1)}), bf16[4,256,1152]{2,1,0:T(8,128)(2,1)}, u32[]{:S(2)}, u32[]{:S(2)}) async-start(bf16[4,256,1152]{2,1,0:T(8,128)(2,1)} %broadcast_in_dim.76), calls=%async_computation.1 | async-start | bytes 4718592 | tf_op jit(solution)/shard_map/all_to_all | solution.py:24
  44.1 21.9 %all-gather.3.cloned.1.call-done = bf16[512,1152]{1,0:T(8,128)(2,1)} async-done(((bf16[128,1152]{1,0:T(8,128)(2,1)}), bf16[512,1152]{1,0:T(8,128)(2,1)}) %all-gather.3.cloned.1.call-update) | async-done | bytes 1179664 | tf_op jit(solution)/shard_map/all_gather | solution.py:51
  66.0 2.4 %copy.32 = bf16[4,2,2,32,1152]{4,3,1,0,2:T(8,128)(2,1)} copy(bf16[4,2,2,32,1152]{4,3,2,1,0:T(8,128)(2,1)} %bitcast.49) | data formatting | bytes 2359296 | tf_op jit(solution)/shard_map/reshape | solution.py:52
  68.4 2.4 %all-to-all-done.1 = bf16[4,256,1152]{2,1,0:T(8,128)(2,1)} async-done(((bf16[4,256,1152]{2,1,0:T(8,128)(2,1)}), bf16[4,256,1152]{2,1,0:T(8,128)(2,1)}, u32[]{:S(2)}, u32[]{:S(2)}) %all-to-all-start.1) | async-done | bytes 2359328 | tf_op jit(solution)/shard_map/all_to_all | solution.py:24
  70.8 5.7 %fusion.7 = (f32[]{:T(128)}, f32[512,1024]{1,0:T(8,128)S(1)}) fusion(f32[]{:T(128)} %bitcast.39, f32[]{:T(128)} %bitcast, s32[1024]{0:T(1024)S(1)} %iota_subtract_fusion, s32[512]{0:T(512)S(1)} %iota_subtract_fusion.1, pred[512]{0:T(512)(128)(4,1)S(1)} %get-tuple-element.24, pred[512]{0:T(512)(128)(4,1)S(1)} %get-tuple-element.25, ...), kind=kOutput, calls=%fused_computation.13 | convolution fusion | flops 1215823872 | bytes 5643276 | tf_op jit(solution)/shard_map/dot_general | solution.py:59
  76.6 4.1 %convolution_multiply_fusion = f32[512,1152]{1,0:T(8,128)S(1)} fusion(bf16[1024,1152]{1,0:T(8,128)(2,1)} %bitcast.5, f32[]{:T(128)} %bitcast, f32[512,1024]{1,0:T(8,128)S(1)} %get-tuple-element.23, f32[]{:T(128)} %bitcast.38, s32[1024]{0:T(1024)S(1)} %iota_subtract_fusion, s32[512]{0:T(512)S(1)} %iota_subtract_fusion.1, ...), kind=kOutput, calls=%fused_computation.1 | convolution fusion | flops 1215365120 | bytes 6822920 | tf_op jit(solution)/shard_map/dot_general | solution.py:70
  80.7 1.4 copy-done.3
  82.1 0.9 dynamic-slice_convert_fusion
  82.9 1.9 collective-permute-start
  84.9 2.2 collective-permute-done
  87.0 2.2 add_convert_fusion
  89.2 10.5 %all-to-all-start.2 = ((bf16[8,32,1152]{2,1,0:T(8,128)(2,1)}), bf16[8,32,1152]{2,1,0:T(8,128)(2,1)S(1)}, u32[]{:S(2)}, u32[]{:S(2)}) async-start(bf16[8,32,1152]{2,1,0:T(8,128)(2,1)} %bitcast.7), calls=%async_computation.2 | async-start | bytes 1179648 | tf_op jit(solution)/shard_map/all_to_all | solution.py:77
  101.1 0.7 fusion.38
  101.8 17.1 %all-to-all-done.2 = bf16[8,32,1152]{2,1,0:T(8,128)(2,1)S(1)} async-done(((bf16[8,32,1152]{2,1,0:T(8,128)(2,1)}), bf16[8,32,1152]{2,1,0:T(8,128)(2,1)S(1)}, u32[]{:S(2)}, u32[]{:S(2)}) %all-to-all-start.2) | async-done | bytes 589856 | tf_op jit(solution)/shard_map/all_to_all | solution.py:77
  119.0 1.1 multiply_reduce_fusion.1
  120.0 1.0 multiply_convert_fusion
  121.0 0.8 pad_maximum_fusion.1
  121.8 0.8 broadcast_in_dim.80
  122.6 3.5 %all-to-all-start.3 = ((bf16[4,48,1152]{2,1,0:T(8,128)(2,1)}), bf16[4,48,1152]{2,1,0:T(8,128)(2,1)S(1)}, u32[]{:S(2)}, u32[]{:S(2)}) async-start(bf16[4,48,1152]{2,1,0:T(8,128)(2,1)} %broadcast_in_dim.80), calls=%async_computation.3 | async-start | bytes 884736 | tf_op jit(solution)/shard_map/all_to_all | solution.py:24
  126.1 7.9 %all-to-all-done.3 = bf16[4,48,1152]{2,1,0:T(8,128)(2,1)S(1)} async-done(((bf16[4,48,1152]{2,1,0:T(8,128)(2,1)}), bf16[4,48,1152]{2,1,0:T(8,128)(2,1)S(1)}, u32[]{:S(2)}, u32[]{:S(2)}) %all-to-all-start.3) | async-done | bytes 442400 | tf_op jit(solution)/shard_map/all_to_all | solution.py:24
  134.1 0.7 copy-done.4
  134.9 1.3 convolution_convert_fusion
  136.2 1.5 copy.33
  137.7 1.2 copy.34
  138.8 0.7 slice.30
  139.7 0.6 convert_reduce_fusion.2
  141.7 1.1 pad_maximum_fusion
  142.8 26.7 %all_to_all.54 = bf16[32,96,128]{2,1,0:T(8,128)(2,1)S(1)} all-to-all(bf16[32,96,128]{2,1,0:T(8,128)(2,1)S(1)} %bitcast.42), channel_id=1, replica_groups=mesh['y'=8,'x'=4,'zh'=4,'zl'=2,'c'=2] {'y','x'}, dimensions={0} | all-to-all | bytes 1572864 | tf_op jit(solution)/shard_map/all_to_all | solution.py:105
  169.6 0.7 broadcast_in_dim.84
  170.3 3.4 %all-to-all-start.5 = ((f32[4,96,128]{2,1,0:T(8,128)}), f32[4,96,128]{2,1,0:T(8,128)S(1)}, u32[]{:S(2)}, u32[]{:S(2)}) async-start(f32[4,96,128]{2,1,0:T(8,128)} %broadcast_in_dim.84), calls=%async_computation.5 | async-start | bytes 393216 | tf_op jit(solution)/shard_map/all_to_all | solution.py:24
  173.7 9.2 %all-to-all-done.5 = f32[4,96,128]{2,1,0:T(8,128)S(1)} async-done(((f32[4,96,128]{2,1,0:T(8,128)}), f32[4,96,128]{2,1,0:T(8,128)S(1)}, u32[]{:S(2)}, u32[]{:S(2)}) %all-to-all-start.5) | async-done | bytes 196640 | tf_op jit(solution)/shard_map/all_to_all | solution.py:24
  182.9 0.6 slice_reduce_fusion
  184.3 1.0 broadcast_in_dim.88
  185.3 5.4 %all-to-all-start.6 = ((bf16[32,96,128]{2,1,0:T(8,128)(2,1)}), bf16[32,96,128]{2,1,0:T(8,128)(2,1)S(1)}, u32[]{:S(2)}, u32[]{:S(2)}) async-start(bf16[32,96,128]{2,1,0:T(8,128)(2,1)} %broadcast_in_dim.88), calls=%async_computation.6 | async-start | bytes 1572864 | tf_op jit(solution)/shard_map/all_to_all | solution.py:24
  190.7 2.6 %convolution_convert_fusion.1 = bf16[128,1152]{1,0:T(8,128)(2,1)} fusion(bf16[128,1152]{1,0:T(8,128)(2,1)} %bitcast.48, bf16[1152,1152]{1,0:T(8,128)(2,1)S(1)} %copy-done), kind=kOutput, calls=%fused_computation.7 | convolution fusion | flops 339886080 | bytes 3244032 | tf_op jit(solution)/shard_map/dot_general | solution.py:89
  193.3 17.6 %all-to-all-done.6 = bf16[32,96,128]{2,1,0:T(8,128)(2,1)S(1)} async-done(((bf16[32,96,128]{2,1,0:T(8,128)(2,1)}), bf16[32,96,128]{2,1,0:T(8,128)(2,1)S(1)}, u32[]{:S(2)}, u32[]{:S(2)}) %all-to-all-start.6) | async-done | bytes 786464 | tf_op jit(solution)/shard_map/all_to_all | solution.py:24
  210.9 0.9 slice.35
  212.0 1.5 copy.36
  213.5 1.1 copy.37
  214.6 1.3 fusion.40
  (28 shorter events, 1.0 us)
Async XLA Ops:
  7.2 10.2 %copy-start = (bf16[1152,1152]{1,0:T(8,128)(2,1)S(1)}, bf16[1152,1152]{1,0:T(8,128)(2,1)}, u32[]{:S(2)}) copy-start(bf16[1152,1152]{1,0:T(8,128)(2,1)} %param.6) | copy-start | bytes 7962628
  7.2 10.2 %copy-start.5 = (bf16[128,1152]{1,0:T(8,128)(2,1)S(1)}, bf16[128,1152]{1,0:T(8,128)(2,1)}, u32[]{:S(2)}) copy-start(bf16[128,1152]{1,0:T(8,128)(2,1)} %param.5) | copy-start | bytes 884740
  10.2 26.0 %all-to-all-start = ((bf16[8,32,1152]{2,1,0:T(8,128)(2,1)}), bf16[8,32,1152]{2,1,0:T(8,128)(2,1)S(1)}, u32[]{:S(2)}, u32[]{:S(2)}) async-start(bf16[8,32,1152]{2,1,0:T(8,128)(2,1)} %broadcast_in_dim.74), calls=%async_computation | async-start | bytes 1179648 | tf_op jit(solution)/shard_map/all_to_all | solution.py:24
  17.3 48.7 %all-gather.3.cloned.1.call-start = ((), (), s32[]{:S(2)}) async-start(), calls=%async_computation.7 | async-start | bytes 1474560 | tf_op jit(solution)/shard_map/all_gather | solution.py:51
  37.7 33.1 %all-to-all-start.1 = ((bf16[4,256,1152]{2,1,0:T(8,128)(2,1)}), bf16[4,256,1152]{2,1,0:T(8,128)(2,1)}, u32[]{:S(2)}, u32[]{:S(2)}) async-start(bf16[4,256,1152]{2,1,0:T(8,128)(2,1)} %broadcast_in_dim.76), calls=%async_computation.1 | async-start | bytes 4718592 | tf_op jit(solution)/shard_map/all_to_all | solution.py:24
  80.6 1.4 copy-start.3
  82.9 4.1 %collective-permute-start = (bf16[256,1152]{1,0:T(8,128)(2,1)}, bf16[256,1152]{1,0:T(8,128)(2,1)S(1)}, u32[]{:S(2)}, u32[]{:S(2)}) collective-permute-start(bf16[256,1152]{1,0:T(8,128)(2,1)} %dynamic-slice_convert_fusion), channel_id=1, source_target_pairs={{0,1},{1,0},{2,3},{3,2},{4,5},{5,4},{6,7},{7,6},{8,9},{9,8},{10,11... | collective-permute-start | bytes 1769480 | tf_op jit(solution)/shard_map/ppermute | solution.py:75
  89.2 29.7 %all-to-all-start.2 = ((bf16[8,32,1152]{2,1,0:T(8,128)(2,1)}), bf16[8,32,1152]{2,1,0:T(8,128)(2,1)S(1)}, u32[]{:S(2)}, u32[]{:S(2)}) async-start(bf16[8,32,1152]{2,1,0:T(8,128)(2,1)} %bitcast.7), calls=%async_computation.2 | async-start | bytes 1179648 | tf_op jit(solution)/shard_map/all_to_all | solution.py:77
  122.6 11.4 %all-to-all-start.3 = ((bf16[4,48,1152]{2,1,0:T(8,128)(2,1)}), bf16[4,48,1152]{2,1,0:T(8,128)(2,1)S(1)}, u32[]{:S(2)}, u32[]{:S(2)}) async-start(bf16[4,48,1152]{2,1,0:T(8,128)(2,1)} %broadcast_in_dim.80), calls=%async_computation.3 | async-start | bytes 884736 | tf_op jit(solution)/shard_map/all_to_all | solution.py:24
  134.0 0.8 copy-start.4
  134.1 0.8 copy-start.2
  170.3 12.6 %all-to-all-start.5 = ((f32[4,96,128]{2,1,0:T(8,128)}), f32[4,96,128]{2,1,0:T(8,128)S(1)}, u32[]{:S(2)}, u32[]{:S(2)}) async-start(f32[4,96,128]{2,1,0:T(8,128)} %broadcast_in_dim.84), calls=%async_computation.5 | async-start | bytes 393216 | tf_op jit(solution)/shard_map/all_to_all | solution.py:24
  185.3 25.6 %all-to-all-start.6 = ((bf16[32,96,128]{2,1,0:T(8,128)(2,1)}), bf16[32,96,128]{2,1,0:T(8,128)(2,1)S(1)}, u32[]{:S(2)}, u32[]{:S(2)}) async-start(bf16[32,96,128]{2,1,0:T(8,128)(2,1)} %broadcast_in_dim.88), calls=%async_computation.6 | async-start | bytes 1572864 | tf_op jit(solution)/shard_map/all_to_all | solution.py:24
  210.9 1.1 copy-start.1
Sparse Core Ops, SparseCore 0:
  20.8 45.1 all-gather.2

commit v2 on v0

v2 whole, which is shorter than its diff:
```python
import functools

import jax
import jax.numpy as jnp
from jax import lax
from jax.experimental import pallas as pl
from jax.experimental.pallas import tpu as pltpu
from jax.sharding import Mesh
from jax.sharding import PartitionSpec as P

EPS = 1e-06
BF16 = jnp.bfloat16
F32 = jnp.float32
LANES = 128
EXTRA = 16
VMEM = pl.BlockSpec(memory_space=pltpu.VMEM)
SMEM = pl.BlockSpec(memory_space=pltpu.SMEM)


def call(body, outs, *args, smem=0, flops=0, **kwargs):
    many = isinstance(outs, (tuple, list))
    specs = [SMEM] * smem + [VMEM] * (len(args) - smem)
    size = sum(a.size * a.dtype.itemsize for a in args)
    return pl.pallas_call(
        body,
        out_shape=outs,
        in_specs=specs,
        out_specs=[VMEM] * len(outs) if many else VMEM,
        cost_estimate=pl.CostEstimate(flops=flops, bytes_accessed=size, transcendentals=0),
        compiler_params=pltpu.CompilerParams(vmem_limit_bytes=40 * 2**20),
        **kwargs,
    )(*args)


def shape(dims, dtype):
    return jax.ShapeDtypeStruct(dims, dtype)


def split3(value):
    hi = value.astype(BF16)
    rest = value - hi.astype(F32)
    mid = rest.astype(BF16)
    low = (rest - mid.astype(F32)).astype(BF16)
    return [hi, mid, low]


def to_all(copies, axes):
    return lax.all_to_all(copies, axes, 0, 0, tiled=True)


def text_kernel(text_ref, out_ref):
    values = text_ref[...].astype(F32)
    inverse = lax.rsqrt(jnp.sum(values * values, axis=-1, keepdims=True) + EPS)
    low = (values * inverse).astype(BF16)
    n = text_ref.shape[0]
    for k in range(out_ref.shape[0] // n):
        out_ref[k * n : (k + 1) * n] = low


def repeat_kernel(x_ref, out_ref):
    out_ref[...] = x_ref[...]


def repeat(x, n):
    rows, width = x.shape
    return pl.pallas_call(
        repeat_kernel,
        grid=(n,),
        out_shape=shape((n * rows, width), x.dtype),
        in_specs=[pl.BlockSpec((rows, width), lambda k: (0, 0))],
        out_specs=pl.BlockSpec((rows, width), lambda k: (k, 0)),
    )(x)


def image_kernel(at_ref, wt_ref, feats_ref, unit_ref, low_ref, inv_ref, own_unit_ref, cols_ref):
    head = lax.dot_general(
        wt_ref[...], feats_ref[...], (((1,), (1,)), ((), ())), preferred_element_type=F32
    )
    inv = lax.rsqrt(jnp.sum(head * head, axis=0, keepdims=True) + EPS)
    unit = head * inv
    unit_ref[...] = unit
    low_ref[...] = unit.astype(BF16)
    inv_ref[...] = inv
    cols = cols_ref.shape[0]
    start = pl.multiple_of(at_ref[0] * cols, 16)
    cols_ref[...] = unit_ref[pl.ds(start, cols), :]
    rows = own_unit_ref.shape[1]
    lane = pl.multiple_of(at_ref[1] * rows, rows)
    own_unit_ref[...] = unit_ref[pl.ds(start, cols), pl.ds(lane, rows)]


def pair_kernel(at_ref, par_ref, texts_ref, low_ref, unit_ref, keep_ref, send_ref, acc_ref, loss_ref):
    step = pl.program_id(0)
    chunk = texts_ref.shape[0]
    images = low_ref.shape[1]
    scale = par_ref[0]
    shift = par_ref[1]

    @pl.when(step == 0)
    def _():
        acc_ref[...] = jnp.zeros_like(acc_ref)
        loss_ref[...] = jnp.zeros_like(loss_ref)

    texts = texts_ref[...]
    z = scale * jnp.dot(texts, low_ref[...], preferred_element_type=F32) + shift
    col = lax.broadcasted_iota(jnp.int32, (chunk, images), 0) + (step * chunk - at_ref[2])
    row = lax.broadcasted_iota(jnp.int32, (chunk, images), 1) - at_ref[3]
    own = (row == col) & (col >= 0) & (col < at_ref[4])
    v = jnp.where(own, -z, z)
    e = jnp.exp(-jnp.abs(v))
    one = 1.0 + e
    series = e * (1.0 - e * (0.5 - e * (1.0 / 3.0 - e * (0.25 - e * 0.2))))
    log1p = jnp.where(e < 0.03, series, jnp.log(one))
    soft = jnp.maximum(v, 0.0) + log1p
    s = jnp.where(v >= 0.0, 1.0, e) / one
    slope = jnp.where(own, -s, s).astype(BF16)
    loss_ref[...] += jnp.sum(soft, axis=0, keepdims=True)
    acc_ref[...] += lax.dot_general(
        texts, slope, (((0,), (0,)), ((), ())), preferred_element_type=F32
    )

    @pl.when(step == pl.num_programs(0) - 1)
    def _():
        cols = (keep_ref.shape[0] - EXTRA) // 2
        c = at_ref[5]
        loss = loss_ref[...]
        dots = scale * jnp.sum(unit_ref[...] * acc_ref[...], axis=0, keepdims=True)
        for k in range(2):
            mine = pl.multiple_of((2 * k + c) * cols, 16)
            other = pl.multiple_of((2 * k + 1 - c) * cols, 16)
            keep_ref[k * cols : (k + 1) * cols] = scale * acc_ref[pl.ds(mine, cols), :]
            send_ref[k * cols : (k + 1) * cols] = (scale * acc_ref[pl.ds(other, cols), :]).astype(BF16)
        pack(keep_ref, send_ref, 2 * cols, dots, loss)


def pack(keep_ref, send_ref, at, dots, loss):
    zeros = jnp.zeros((EXTRA - 2, dots.shape[1]), F32)
    keep_ref[at : at + EXTRA] = jnp.concatenate([dots, loss, zeros], axis=0)
    terms = [t.astype(F32) for t in split3(dots) + split3(loss)]
    zeros = jnp.zeros((EXTRA - 6, dots.shape[1]), F32)
    send_ref[at : at + EXTRA] = jnp.concatenate(terms + [zeros], axis=0).astype(BF16)


def unpack(keep_ref, got_ref, at):
    kept = keep_ref[at : at + EXTRA]
    got = got_ref[at : at + EXTRA].astype(F32)
    dots = kept[0:1] + (got[0:1] + got[1:2] + got[2:3])
    loss = kept[1:2] + (got[3:4] + got[4:5] + got[5:6])
    return dots, loss


def middle_kernel(at_ref, keep_ref, got_ref, keep2_ref, send2_ref):
    cols = keep2_ref.shape[0] - EXTRA
    dots, loss = unpack(keep_ref, got_ref, 2 * cols)
    zl = at_ref[6]
    mine = pl.multiple_of(zl * cols, 16)
    other = pl.multiple_of((1 - zl) * cols, 16)
    keep2_ref[:cols] = keep_ref[pl.ds(mine, cols), :] + got_ref[pl.ds(mine, cols), :].astype(F32)
    send2_ref[:cols] = (
        keep_ref[pl.ds(other, cols), :] + got_ref[pl.ds(other, cols), :].astype(F32)
    ).astype(BF16)
    pack(keep2_ref, send2_ref, cols, dots, loss)


def head_kernel(keep_ref, got_ref, unit_ref, inv_ref, feats_ref, flat_ref, dirs_ref):
    cols = keep_ref.shape[0] - EXTRA
    dots, loss = unpack(keep_ref, got_ref, cols)
    total = keep_ref[:cols] + got_ref[:cols].astype(F32)
    back = ((total - unit_ref[...] * dots) * inv_ref[...]).astype(BF16)
    head = jnp.dot(back, feats_ref[...], preferred_element_type=F32).astype(BF16)
    tiles = feats_ref.shape[1] // LANES
    for k in range(tiles):
        flat_ref[k * cols : (k + 1) * cols] = head[:, k * LANES : (k + 1) * LANES]
    blocks = dirs_ref.shape[0]
    part = loss[:, :LANES]
    for k in range(1, blocks):
        part = part + loss[:, k * LANES : (k + 1) * LANES]
    terms = [t.astype(F32) for t in split3(part)]
    tail = jnp.concatenate(terms + [jnp.zeros((EXTRA - 3, LANES), F32)], axis=0)
    at = tiles * cols
    flat_ref[at : at + EXTRA] = tail.astype(BF16)
    flat_ref[at + EXTRA :] = jnp.zeros((flat_ref.shape[0] - at - EXTRA, LANES), BF16)
    low = total.astype(BF16)
    terms = [t.astype(F32) for t in split3(dots)]
    rows = jnp.concatenate(terms + [jnp.zeros((EXTRA - 3, dots.shape[1]), F32)], axis=0).astype(BF16)
    for k in range(blocks):
        dirs_ref[k, :cols] = low[:, k * LANES : (k + 1) * LANES]
        dirs_ref[k, cols:] = rows[:, k * LANES : (k + 1) * LANES]


def back_kernel(at_ref, parts_ref, unit_ref, inv_ref, out_ref):
    cols, rows = unit_ref.shape
    parts = parts_ref[...].astype(F32)
    total = parts[0]
    for k in range(1, parts.shape[0]):
        total = total + parts[k]
    dots = total[cols : cols + 1] + total[cols + 1 : cols + 2] + total[cols + 2 : cols + 3]
    inv = inv_ref[:, pl.ds(pl.multiple_of(at_ref[1] * rows, rows), rows)]
    back = ((total[:cols] - unit_ref[...] * dots) * inv).astype(BF16)
    for k in range(out_ref.shape[0]):
        out_ref[k] = back


def sum_kernel(parts_ref, out_ref):
    total = jnp.sum(parts_ref[...].astype(F32), axis=0)
    for k in range(out_ref.shape[0]):
        out_ref[k] = total


def last_sum_kernel(at_ref, parts_ref, out_ref):
    total = jnp.sum(parts_ref[...], axis=0)
    low = total.astype(BF16)
    first = total[:EXTRA]
    terms = [t.astype(F32) for t in split3(first[0:1] + first[1:2] + first[2:3])]
    row = jnp.concatenate(terms + [jnp.zeros((EXTRA - 3, LANES), F32)], axis=0).astype(BF16)
    first = jnp.where(at_ref[7] > 0, row.astype(F32), first).astype(BF16)
    for k in range(out_ref.shape[0]):
        out_ref[k, :EXTRA] = first
        out_ref[k, EXTRA:] = low[EXTRA:]


def final_kernel(pairs, full_ref, head_ref, loss_ref):
    width, cols = head_ref.shape
    tiles = width // LANES
    for k in range(tiles):
        head_ref[k * LANES : (k + 1) * LANES] = full_ref[k * cols : (k + 1) * cols].astype(F32).T.astype(BF16)
    at = tiles * cols
    total = jnp.sum(full_ref[at : at + EXTRA].astype(F32), axis=0, keepdims=True)
    loss_ref[...] = jnp.sum(total, axis=1, keepdims=True) / pairs


def local(img_feat, head_weight, text_embed, log_temp, logit_bias):
    rows, width = img_feat.shape
    quarter = text_embed.shape[0]
    ny, nx, nzh, nzl, nc = (lax.axis_size(a) for a in ("y", "x", "zh", "zl", "c"))
    nrep = nzl * nc
    plane = nx * ny
    cols = width // nrep
    images = nzh * rows
    texts_n = plane * quarter
    tiles = width // LANES
    y_at, x_at, zh_at, zl_at, c_at = (lax.axis_index(a) for a in ("y", "x", "zh", "zl", "c"))
    rep_at = zl_at * nc + c_at
    at_loss = tiles * cols
    piece = -(-(at_loss + EXTRA) // (plane * 16)) * 16
    assert at_loss % piece == 0
    at = jnp.stack(
        [
            rep_at,
            zh_at,
            (x_at * ny + y_at) * quarter,
            zh_at * rows + rep_at * quarter,
            quarter + 0 * rep_at,
            c_at,
            zl_at,
            (y_at * nx + x_at == at_loss // piece).astype(jnp.int32),
        ]
    ).astype(jnp.int32)
    par = jnp.stack([jnp.exp(log_temp[0]), logit_bias[0]])

    feats = lax.all_gather(img_feat, "zh", axis=0, tiled=True)
    texts = call(text_kernel, shape((ny * quarter, width), BF16), text_embed)
    texts = to_all(texts, "y")
    texts = to_all(repeat(texts, nx), "x")

    unit, low, inv, own_unit, col_unit = call(
        image_kernel,
        [
            shape((width, images), F32),
            shape((width, images), BF16),
            shape((1, images), F32),
            shape((cols, rows), F32),
            shape((cols, images), F32),
        ],
        at,
        head_weight.T,
        feats,
        smem=1,
        flops=2 * width * width * images,
    )

    steps = 4
    chunk = texts_n // steps
    keep, send = pl.pallas_call(
        pair_kernel,
        grid=(steps,),
        out_shape=[shape((2 * cols + EXTRA, images), F32), shape((2 * cols + EXTRA, images), BF16)],
        in_specs=[
            SMEM,
            SMEM,
            pl.BlockSpec((chunk, width), lambda k: (k, 0)),
            pl.BlockSpec((width, images), lambda k: (0, 0)),
            pl.BlockSpec((width, images), lambda k: (0, 0)),
        ],
        out_specs=[
            pl.BlockSpec((2 * cols + EXTRA, images), lambda k: (0, 0)),
            pl.BlockSpec((2 * cols + EXTRA, images), lambda k: (0, 0)),
        ],
        scratch_shapes=[pltpu.VMEM((width, images), F32), pltpu.VMEM((1, images), F32)],
        cost_estimate=pl.CostEstimate(
            flops=4 * width * images * texts_n, bytes_accessed=8 * 2**20, transcendentals=3 * images * texts_n
        ),
        compiler_params=pltpu.CompilerParams(vmem_limit_bytes=48 * 2**20),
    )(at, par, texts, low, unit)
    got = lax.ppermute(send, "c", [(0, 1), (1, 0)])
    keep2, send2 = call(
        middle_kernel,
        [shape((cols + EXTRA, images), F32), shape((cols + EXTRA, images), BF16)],
        at,
        keep,
        got,
        smem=1,
    )
    got2 = lax.ppermute(send2, "zl", [(0, 1), (1, 0)])
    flat, dirs = call(
        head_kernel,
        [shape((plane * piece, LANES), BF16), shape((nzh, cols + EXTRA, rows), BF16)],
        keep2,
        got2,
        col_unit,
        inv,
        feats,
        flops=2 * cols * images * width,
    )

    parts = to_all(flat, ("y", "x")).reshape(plane, piece, LANES)
    part = call(sum_kernel, shape((nzh, piece, LANES), F32), parts)
    part = to_all(part, "zh")
    low_part = call(last_sum_kernel, shape((plane, piece, LANES), BF16), at, part, smem=1)
    full = to_all(low_part.reshape(plane * piece, LANES), ("y", "x"))
    group = rows * plane * nzh
    head_grad, loss = call(
        functools.partial(final_kernel, float(group) * float(group)),
        [shape((width, cols), BF16), shape((1, 1), F32)],
        full,
    )

    dirs = to_all(dirs, "zh")
    back = call(back_kernel, shape((nrep, cols, rows), BF16), at, dirs, own_unit, inv, smem=1)
    back = to_all(back, ("zl", "c")).reshape(width, rows)
    feat_grad = lax.dot_general(
        back, head_weight, (((0,), (1,)), ((), ())), preferred_element_type=F32
    ).astype(BF16)
    return (loss.reshape(1), feat_grad, head_grad)


def solution(mesh):
    devices = mesh.devices.reshape(8, 4, 4, 2, 2)
    fine = Mesh(devices, ("y", "x", "zh", "zl", "c"))
    batch, rep = (("y", "x", "zh"), ("zl", "c"))
    in_specs = (P(batch, None), P(), P(batch + rep, None), P(), P())
    out_specs = (P(), P(batch, None), P(None, rep))
    return jax.shard_map(local, mesh=fine, in_specs=in_specs, out_specs=out_specs, check_vma=False)
```

time: 1010 us -> 207 us (0.20)
  the two profiles are of different devices: /device:TPU:64 before, /device:TPU:2 now
where the time goes in v2:
time: 207 us; the launch traced here: 206 us
  waiting for transfers between devices  86 us (42%)
  starting transfers between devices  38.8 us (19%)
  blocking collectives  29.7 us (14%)
  Pallas kernels  21.3 us (10%)
  between operations  15.5 us (7%)
  local copies, waits for them, and re-layouts  12.1 us (6%)
  matrix products  2.61 us (1%)
    all_to_all x6, waiting for transfers between devices, to_all(): return lax.all_to_all(copies, axes, 0, 0, tiled=True)  60.9 us
    all_to_all x6, starting transfers between devices, to_all(): return lax.all_to_all(copies, axes, 0, 0, tiled=True)  32.2 us
    all_to_all x1, blocking collectives, to_all(): return lax.all_to_all(copies, axes, 0, 0, tiled=True)  29.7 us
    all_gather x1, waiting for transfers between devices, local(): feats = lax.all_gather(img_feat, 'zh', axis=0, tiled=True)  14.8 us
    unnamed x18, local copies, waits for them, and re-layouts  12 us
    pallas_call x8, Pallas kernels, call(): pl.pallas_call(body, out_shape=outs, in_specs=specs, out_specs=[VMEM] * l...  9.63 us
    pallas_call x1, Pallas kernels, local(): pl.pallas_call(pair_kernel, grid=(steps,), out_shape=[shape((2 * cols + E...  8.64 us
    ppermute x1, waiting for transfers between devices, local(): got2 = lax.ppermute(send2, 'zl', [(0, 1), (1, 0)])  7.64 us
  transfers between devices with their start and end apart: 9, of which 9 were waited for; matrix products, arithmetic and copies ran while one was open for 3% of the time, Pallas kernels for 5%

profile of v2, /device:TPU:2, one launch (start us, length us, event | category | flops | bytes accessed | tf_op | source)
XLA Modules:
  0.0 206.1 jit_solution(8264561275516925652)
XLA Ops:
  7.2 0.0 copy-start.2
  7.2 0.9 copy-done.2
  8.0 1.0 shard_map.76
  9.0 7.1 %all-to-all-start = ((bf16[8,32,1152]{2,1,0:T(8,128)(2,1)}), bf16[8,32,1152]{2,1,0:T(8,128)(2,1)S(1)}, u32[]{:S(2)}, u32[]{:S(2)}) async-start(bf16[8,32,1152]{2,1,0:T(8,128)(2,1)} %bitcast.7), calls=%async_computation | async-start | bytes 1179648 | tf_op jit(solution)/shard_map/all_to_all | solution.py:48
  16.1 0.0 all-gather.2.cloned.1.call-start
  16.1 0.7 all-gather.2.cloned.1.call-update
  16.8 18.2 %all-to-all-done = bf16[8,32,1152]{2,1,0:T(8,128)(2,1)S(1)} async-done(((bf16[8,32,1152]{2,1,0:T(8,128)(2,1)}), bf16[8,32,1152]{2,1,0:T(8,128)(2,1)S(1)}, u32[]{:S(2)}, u32[]{:S(2)}) %all-to-all-start) | async-done | bytes 589856 | tf_op jit(solution)/shard_map/all_to_all | solution.py:48
  35.0 0.0 copy-start.7
  35.0 0.8 copy-done.7
  35.8 3.0 %shard_map.77 = bf16[1024,1152]{1,0:T(8,128)(2,1)} custom-call(bf16[256,1152]{1,0:T(8,128)(2,1)} %bitcast.22), custom_call_target="tpu_custom_call" | custom-call | tf_op jit(solution)/shard_map/pallas_call | solution.py:66
  38.8 5.0 %all-to-all-start.1 = ((bf16[4,256,1152]{2,1,0:T(8,128)(2,1)}), bf16[4,256,1152]{2,1,0:T(8,128)(2,1)}, u32[]{:S(2)}, u32[]{:S(2)}) async-start(bf16[4,256,1152]{2,1,0:T(8,128)(2,1)} %bitcast.21), calls=%async_computation.1 | async-start | bytes 4718592 | tf_op jit(solution)/shard_map/all_to_all | solution.py:48
  43.8 4.1 %copy.8 = bf16[1152,1152]{0,1:T(8,128)(2,1)S(1)} copy(bf16[1152,1152]{1,0:T(8,128)(2,1)} %param.6) | data formatting | bytes 5308416 | tf_op args[1]
  49.3 0.1 stack.39.at_ref
  49.4 0.1 pad_maximum_fusion.par_ref
  49.4 14.8 %all-gather.2.cloned.1.call-done.feats_ref = bf16[512,1152]{1,0:T(8,128)(2,1)} async-done(((bf16[128,1152]{1,0:T(8,128)(2,1)}), bf16[512,1152]{1,0:T(8,128)(2,1)}) %all-gather.2.cloned.1.call-update) | async-done | bytes 1179664 | tf_op jit(solution)/shard_map/all_gather | solution.py:261
  64.2 0.0 copy-start
  64.2 1.3 copy-done
  65.5 2.9 %shard_map.78 = (f32[1152,512]{1,0:T(8,128)S(1)}, bf16[1152,512]{1,0:T(8,128)(2,1)S(1)}, f32[1,512]{1,0:T(1,128)S(1)}, f32[288,128]{1,0:T(8,128)S(1)}, f32[288,512]{1,0:T(8,128)S(1)}) custom-call(s32[8]{0:T(128)S(1)} %stack.39.at_ref, bf16[1152,1152]{1,0:T(8,128)(2,1)S(1)} %bitcast.19, bf16[512,1152]{1,0:T(8,128)(2,1)S(1)} %copy-done), custom_call_target="tpu_custom_call" | custom-call | flops 1358954496 | bytes 3833888 | tf_op jit(solution)/shard_map/pallas_call | solution.py:24
  68.4 0.0 copy-start.3
  68.4 1.4 copy-done.3
  69.8 1.1 copy-done.4
  70.9 1.0 all-to-all-done.1
  71.9 1.3 copy-done.5
  73.2 8.6 %shard_map.79 = (f32[592,512]{1,0:T(8,128)S(1)}, bf16[592,512]{1,0:T(8,128)(2,1)S(1)}) custom-call(s32[8]{0:T(128)S(1)} %stack.39.at_ref, f32[2]{0:T(128)S(1)} %pad_maximum_fusion.par_ref, bf16[1024,1152]{1,0:T(8,128)(2,1)} %bitcast.10.texts_ref, bf16[1152,512]{1,0:T(8,128)(2,1)S(1)} %copy-done.5, f32[1152,512]{1,0:T(8,128)} %copy-done.3), custom_call_target="tpu_custom_call" | custom-call | flops 2415919104 | bytes 8388608 | tf_op jit(solution)/shard_map/pallas_call | solution.py:284
  81.8 0.0 copy-start.1
  81.8 2.1 collective-permute-start
  83.9 2.0 collective-permute-done.got_ref
  85.9 0.7 shard_map.80
  86.6 4.5 %collective-permute-start.1 = (bf16[304,512]{1,0:T(8,128)(2,1)S(1)}, bf16[304,512]{1,0:T(8,128)(2,1)S(1)}, u32[]{:S(2)}, u32[]{:S(2)}) collective-permute-start(bf16[304,512]{1,0:T(8,128)(2,1)S(1)} %get-tuple-element.21), channel_id=1, source_target_pairs={{0,2},{2,0},{1,3},{3,1},{4,6},{6,4},{5,7},{7,5},{8,10},{10,8},{9,1... | collective-permute-start | bytes 933896 | tf_op jit(solution)/shard_map/ppermute | solution.py:314
  91.1 7.6 %collective-permute-done.1.got_ref = bf16[304,512]{1,0:T(8,128)(2,1)S(1)} collective-permute-done((bf16[304,512]{1,0:T(8,128)(2,1)S(1)}, bf16[304,512]{1,0:T(8,128)(2,1)S(1)}, u32[]{:S(2)}, u32[]{:S(2)}) %collective-permute-start.1) | collective-permute-done | bytes 311328 | tf_op jit(solution)/shard_map/ppermute | solution.py:314
  98.7 0.0 copy-done.1
  98.7 0.9 shard_map.81
  99.6 29.7 %all_to_all.54.parts_ref = bf16[32,96,128]{2,1,0:T(8,128)(2,1)S(1)} all-to-all(bf16[32,96,128]{2,1,0:T(8,128)(2,1)S(1)} %bitcast.20), channel_id=1, replica_groups=mesh['y'=8,'x'=4,'zh'=4,'zl'=2,'c'=2] {'y','x'}, dimensions={0} | all-to-all | bytes 1572864 | tf_op jit(solution)/shard_map/all_to_all | solution.py:48
  129.4 6.3 %all-to-all-start.5 = ((bf16[4,304,128]{2,1,0:T(8,128)(2,1)}), bf16[4,304,128]{2,1,0:T(8,128)(2,1)S(1)}, u32[]{:S(2)}, u32[]{:S(2)}) async-start(bf16[4,304,128]{2,1,0:T(8,128)(2,1)} %get-tuple-element.26), calls=%async_computation.5 | async-start | bytes 622592 | tf_op jit(solution)/shard_map/all_to_all | solution.py:48
  135.6 0.8 shard_map.82
  136.4 9.8 %all-to-all-done.5.parts_ref = bf16[4,304,128]{2,1,0:T(8,128)(2,1)S(1)} async-done(((bf16[4,304,128]{2,1,0:T(8,128)(2,1)}), bf16[4,304,128]{2,1,0:T(8,128)(2,1)S(1)}, u32[]{:S(2)}, u32[]{:S(2)}) %all-to-all-start.5) | async-done | bytes 311328 | tf_op jit(solution)/shard_map/all_to_all | solution.py:48
  146.2 3.4 %all-to-all-start.3 = ((f32[4,96,128]{2,1,0:T(8,128)}), f32[4,96,128]{2,1,0:T(8,128)S(1)}, u32[]{:S(2)}, u32[]{:S(2)}) async-start(f32[4,96,128]{2,1,0:T(8,128)} %shard_map.82), calls=%async_computation.3 | async-start | bytes 393216 | tf_op jit(solution)/shard_map/all_to_all | solution.py:48
  149.6 1.3 shard_map.85
  150.9 7.4 %all-to-all-done.3.parts_ref = f32[4,96,128]{2,1,0:T(8,128)S(1)} async-done(((f32[4,96,128]{2,1,0:T(8,128)}), f32[4,96,128]{2,1,0:T(8,128)S(1)}, u32[]{:S(2)}, u32[]{:S(2)}) %all-to-all-start.3) | async-done | bytes 196640 | tf_op jit(solution)/shard_map/all_to_all | solution.py:48
  158.3 4.1 %all-to-all-start.6 = ((bf16[4,288,128]{2,1,0:T(8,128)(2,1)}), bf16[4,288,128]{2,1,0:T(8,128)(2,1)}, u32[]{:S(2)}, u32[]{:S(2)}) async-start(bf16[4,288,128]{2,1,0:T(8,128)(2,1)} %shard_map.85), calls=%async_computation.6 | async-start | bytes 589824 | tf_op jit(solution)/shard_map/all_to_all | solution.py:48
  162.4 1.5 shard_map.83
  163.9 5.0 %all-to-all-done.6 = bf16[4,288,128]{2,1,0:T(8,128)(2,1)} async-done(((bf16[4,288,128]{2,1,0:T(8,128)(2,1)}), bf16[4,288,128]{2,1,0:T(8,128)(2,1)}, u32[]{:S(2)}, u32[]{:S(2)}) %all-to-all-start.6) | async-done | bytes 294944 | tf_op jit(solution)/shard_map/all_to_all | solution.py:48
  168.8 6.4 %all-to-all-start.4 = ((bf16[32,96,128]{2,1,0:T(8,128)(2,1)}), bf16[32,96,128]{2,1,0:T(8,128)(2,1)S(1)}, u32[]{:S(2)}, u32[]{:S(2)}) async-start(bf16[32,96,128]{2,1,0:T(8,128)(2,1)} %shard_map.83), calls=%async_computation.4 | async-start | bytes 1572864 | tf_op jit(solution)/shard_map/all_to_all | solution.py:48
  175.3 0.0 copy-done.6
  175.3 2.6 %convolution_convert_fusion = bf16[128,1152]{1,0:T(8,128)(2,1)} fusion(bf16[1152,128]{1,0:T(8,128)(2,1)} %bitcast.15, bf16[1152,1152]{1,0:T(8,128)(2,1)S(1)} %copy-done.6), kind=kOutput, calls=%fused_computation | convolution fusion | flops 339886080 | bytes 3244032 | tf_op jit(solution)/shard_map/dot_general | solution.py:341
  177.9 19.6 %all-to-all-done.4 = bf16[32,96,128]{2,1,0:T(8,128)(2,1)S(1)} async-done(((bf16[32,96,128]{2,1,0:T(8,128)(2,1)}), bf16[32,96,128]{2,1,0:T(8,128)(2,1)S(1)}, u32[]{:S(2)}, u32[]{:S(2)}) %all-to-all-start.4) | async-done | bytes 786464 | tf_op jit(solution)/shard_map/all_to_all | solution.py:48
  197.5 0.6 shard_map.84
  198.1 1.1 copy.9
  (3 shorter events, 0.0 us)
Async XLA Ops:
  7.2 0.9 copy-start.2
  9.0 26.0 %all-to-all-start = ((bf16[8,32,1152]{2,1,0:T(8,128)(2,1)}), bf16[8,32,1152]{2,1,0:T(8,128)(2,1)S(1)}, u32[]{:S(2)}, u32[]{:S(2)}) async-start(bf16[8,32,1152]{2,1,0:T(8,128)(2,1)} %bitcast.7), calls=%async_computation | async-start | bytes 1179648 | tf_op jit(solution)/shard_map/all_to_all | solution.py:48
  16.1 48.1 %all-gather.2.cloned.1.call-start = ((), (), s32[]{:S(2)}) async-start(), calls=%async_computation.7 | async-start | bytes 1474560 | tf_op jit(solution)/shard_map/all_gather | solution.py:261
  35.0 0.8 copy-start.7
  38.8 33.1 %all-to-all-start.1 = ((bf16[4,256,1152]{2,1,0:T(8,128)(2,1)}), bf16[4,256,1152]{2,1,0:T(8,128)(2,1)}, u32[]{:S(2)}, u32[]{:S(2)}) async-start(bf16[4,256,1152]{2,1,0:T(8,128)(2,1)} %bitcast.21), calls=%async_computation.1 | async-start | bytes 4718592 | tf_op jit(solution)/shard_map/all_to_all | solution.py:48
  64.2 1.3 copy-start
  68.4 1.4 copy-start.3
  69.8 1.1 copy-start.4
  71.9 1.3 copy-start.5
  81.8 16.9 %copy-start.1 = (bf16[512,1152]{1,0:T(8,128)(2,1)S(1)}, bf16[512,1152]{1,0:T(8,128)(2,1)}, u32[]{:S(2)}) copy-start(bf16[512,1152]{1,0:T(8,128)(2,1)} %all-gather.2.cloned.1.call-done.feats_ref) | copy-start | bytes 3538948
  81.8 4.1 %collective-permute-start = (bf16[592,512]{1,0:T(8,128)(2,1)S(1)}, bf16[592,512]{1,0:T(8,128)(2,1)S(1)}, u32[]{:S(2)}, u32[]{:S(2)}) collective-permute-start(bf16[592,512]{1,0:T(8,128)(2,1)S(1)} %get-tuple-element.19), channel_id=1, source_target_pairs={{0,1},{1,0},{2,3},{3,2},{4,5},{5,4},{6,7},{7,6},{8,9},{9,8},{10,11... | collective-permute-start | bytes 1818632 | tf_op jit(solution)/shard_map/ppermute | solution.py:305
  86.6 12.1 %collective-permute-start.1 = (bf16[304,512]{1,0:T(8,128)(2,1)S(1)}, bf16[304,512]{1,0:T(8,128)(2,1)S(1)}, u32[]{:S(2)}, u32[]{:S(2)}) collective-permute-start(bf16[304,512]{1,0:T(8,128)(2,1)S(1)} %get-tuple-element.21), channel_id=1, source_target_pairs={{0,2},{2,0},{1,3},{3,1},{4,6},{6,4},{5,7},{7,5},{8,10},{10,8},{9,1... | collective-permute-start | bytes 933896 | tf_op jit(solution)/shard_map/ppermute | solution.py:314
  129.4 16.9 %all-to-all-start.5 = ((bf16[4,304,128]{2,1,0:T(8,128)(2,1)}), bf16[4,304,128]{2,1,0:T(8,128)(2,1)S(1)}, u32[]{:S(2)}, u32[]{:S(2)}) async-start(bf16[4,304,128]{2,1,0:T(8,128)(2,1)} %get-tuple-element.26), calls=%async_computation.5 | async-start | bytes 622592 | tf_op jit(solution)/shard_map/all_to_all | solution.py:48
  136.4 38.8 %copy-start.6 = (bf16[1152,1152]{1,0:T(8,128)(2,1)S(1)}, bf16[1152,1152]{1,0:T(8,128)(2,1)}, u32[]{:S(2)}) copy-start(bf16[1152,1152]{1,0:T(8,128)(2,1)} %param.6) | copy-start | bytes 7962628
  146.2 12.1 %all-to-all-start.3 = ((f32[4,96,128]{2,1,0:T(8,128)}), f32[4,96,128]{2,1,0:T(8,128)S(1)}, u32[]{:S(2)}, u32[]{:S(2)}) async-start(f32[4,96,128]{2,1,0:T(8,128)} %shard_map.82), calls=%async_computation.3 | async-start | bytes 393216 | tf_op jit(solution)/shard_map/all_to_all | solution.py:48
  158.3 10.6 %all-to-all-start.6 = ((bf16[4,288,128]{2,1,0:T(8,128)(2,1)}), bf16[4,288,128]{2,1,0:T(8,128)(2,1)}, u32[]{:S(2)}, u32[]{:S(2)}) async-start(bf16[4,288,128]{2,1,0:T(8,128)(2,1)} %shard_map.85), calls=%async_computation.6 | async-start | bytes 589824 | tf_op jit(solution)/shard_map/all_to_all | solution.py:48
  168.8 28.7 %all-to-all-start.4 = ((bf16[32,96,128]{2,1,0:T(8,128)(2,1)}), bf16[32,96,128]{2,1,0:T(8,128)(2,1)S(1)}, u32[]{:S(2)}, u32[]{:S(2)}) async-start(bf16[32,96,128]{2,1,0:T(8,128)(2,1)} %shard_map.83), calls=%async_computation.4 | async-start | bytes 1572864 | tf_op jit(solution)/shard_map/all_to_all | solution.py:48
Sparse Core Ops, SparseCore 0:
  19.0 45.1 all-gather.1

commit v3 on v2

v3 whole, which is shorter than its diff:
```python
import functools

import jax
import jax.numpy as jnp
from jax import lax
from jax.experimental import pallas as pl
from jax.experimental.pallas import tpu as pltpu
from jax.sharding import Mesh
from jax.sharding import PartitionSpec as P

EPS = 1e-06
BF16 = jnp.bfloat16
F32 = jnp.float32
LANES = 128
EXTRA = 16
VMEM = pl.BlockSpec(memory_space=pltpu.VMEM)
SMEM = pl.BlockSpec(memory_space=pltpu.SMEM)


def call(body, outs, *args, smem=0, flops=0, **kwargs):
    many = isinstance(outs, (tuple, list))
    specs = [SMEM] * smem + [VMEM] * (len(args) - smem)
    size = sum(a.size * a.dtype.itemsize for a in args)
    return pl.pallas_call(
        body,
        out_shape=outs,
        in_specs=specs,
        out_specs=[VMEM] * len(outs) if many else VMEM,
        cost_estimate=pl.CostEstimate(flops=flops, bytes_accessed=size, transcendentals=0),
        compiler_params=pltpu.CompilerParams(vmem_limit_bytes=40 * 2**20),
        **kwargs,
    )(*args)


def shape(dims, dtype):
    return jax.ShapeDtypeStruct(dims, dtype)


def split3(value):
    hi = value.astype(BF16)
    rest = value - hi.astype(F32)
    mid = rest.astype(BF16)
    low = (rest - mid.astype(F32)).astype(BF16)
    return [hi, mid, low]


def to_all(copies, axes):
    return lax.all_to_all(copies, axes, 0, 0, tiled=True)


def text_kernel(text_ref, out_ref):
    values = text_ref[...].astype(F32)
    inverse = lax.rsqrt(jnp.sum(values * values, axis=-1, keepdims=True) + EPS)
    low = (values * inverse).astype(BF16)
    n = text_ref.shape[0]
    for k in range(out_ref.shape[0] // n):
        out_ref[k * n : (k + 1) * n] = low


def image_kernel(at_ref, wt_ref, *refs):
    feat_refs = refs[:-6]
    unit_ref, low_ref, inv_ref, own_unit_ref, cols_ref, feats_ref = refs[-6:]
    n = len(feat_refs)
    rows = feat_refs[0].shape[0]
    for k in range(n):
        feats_ref[k * rows : (k + 1) * rows] = feat_refs[k][...]
    head = lax.dot_general(
        wt_ref[...], feats_ref[...], (((1,), (1,)), ((), ())), preferred_element_type=F32
    )
    inv = lax.rsqrt(jnp.sum(head * head, axis=0, keepdims=True) + EPS)
    unit = head * inv
    unit_ref[...] = unit
    low_ref[...] = unit.astype(BF16)
    inv_ref[...] = inv
    cols = cols_ref.shape[0]
    start = pl.multiple_of(at_ref[0] * cols, 16)
    cols_ref[...] = unit_ref[pl.ds(start, cols), :]
    own_unit_ref[...] = unit_ref[pl.ds(start, cols), :rows]


def pairs(par_ref, texts, low_ref, own=None):
    z = par_ref[0] * jnp.dot(texts, low_ref[...], preferred_element_type=F32) + par_ref[1]
    v = z if own is None else jnp.where(own, -z, z)
    e = jnp.exp(-jnp.abs(v))
    one = 1.0 + e
    series = e * (1.0 - e * (0.5 - e * (1.0 / 3.0 - e * (0.25 - e * 0.2))))
    log1p = jnp.where(e < 0.03, series, jnp.log(one))
    soft = jnp.maximum(v, 0.0) + log1p
    s = jnp.where(v >= 0.0, 1.0, e) / one
    slope = (s if own is None else jnp.where(own, -s, s)).astype(BF16)
    return slope, jnp.sum(soft, axis=0, keepdims=True)


def turn(texts, slope):
    return lax.dot_general(texts, slope, (((0,), (0,)), ((), ())), preferred_element_type=F32)


def first_kernel(at_ref, par_ref, own_ref, left_ref, right_ref, low_ref, acc_ref, loss_ref):
    size = (own_ref.shape[0], low_ref.shape[1])
    col = lax.broadcasted_iota(jnp.int32, size, 0) - at_ref[2]
    row = lax.broadcasted_iota(jnp.int32, size, 1) - at_ref[3]
    own = (row == col) & (col >= 0) & (col < at_ref[4])
    slope, loss = pairs(par_ref, own_ref[...], low_ref, own)
    acc_ref[...] = turn(own_ref[...], slope)
    for ref in (left_ref, right_ref):
        slope, more = pairs(par_ref, ref[...], low_ref)
        acc_ref[...] += turn(ref[...], slope)
        loss = loss + more
    loss_ref[...] = loss


def second_kernel(at_ref, par_ref, a_ref, b_ref, low_ref, unit_ref, acc_ref, loss_ref, keep_ref, send_ref, sum_ref):
    scale = par_ref[0]
    texts = jnp.concatenate([a_ref[...], b_ref[...]], axis=0)
    slope, loss = pairs(par_ref, texts, low_ref)
    loss = loss_ref[...] + loss
    total = scale * (acc_ref[...] + turn(texts, slope))
    sum_ref[...] = total
    dots = jnp.sum(unit_ref[...] * total, axis=0, keepdims=True)
    cols = (keep_ref.shape[0] - EXTRA) // 2
    c = at_ref[5]
    for k in range(2):
        mine = pl.multiple_of((2 * k + c) * cols, 16)
        other = pl.multiple_of((2 * k + 1 - c) * cols, 16)
        keep_ref[k * cols : (k + 1) * cols] = sum_ref[pl.ds(mine, cols), :]
        send_ref[k * cols : (k + 1) * cols] = sum_ref[pl.ds(other, cols), :].astype(BF16)
    pack(keep_ref, send_ref, 2 * cols, dots, loss)


def pack(keep_ref, send_ref, at, dots, loss):
    zeros = jnp.zeros((EXTRA - 2, dots.shape[1]), F32)
    keep_ref[at : at + EXTRA] = jnp.concatenate([dots, loss, zeros], axis=0)
    terms = [t.astype(F32) for t in split3(dots) + split3(loss)]
    zeros = jnp.zeros((EXTRA - 6, dots.shape[1]), F32)
    send_ref[at : at + EXTRA] = jnp.concatenate(terms + [zeros], axis=0).astype(BF16)


def unpack(keep_ref, got_ref, at):
    kept = keep_ref[at : at + EXTRA]
    got = got_ref[at : at + EXTRA].astype(F32)
    dots = kept[0:1] + (got[0:1] + got[1:2] + got[2:3])
    loss = kept[1:2] + (got[3:4] + got[4:5] + got[5:6])
    return dots, loss


def middle_kernel(at_ref, keep_ref, got_ref, keep2_ref, send2_ref):
    cols = keep2_ref.shape[0] - EXTRA
    dots, loss = unpack(keep_ref, got_ref, 2 * cols)
    zl = at_ref[6]
    mine = pl.multiple_of(zl * cols, 16)
    other = pl.multiple_of((1 - zl) * cols, 16)
    keep2_ref[:cols] = keep_ref[pl.ds(mine, cols), :] + got_ref[pl.ds(mine, cols), :].astype(F32)
    send2_ref[:cols] = (
        keep_ref[pl.ds(other, cols), :] + got_ref[pl.ds(other, cols), :].astype(F32)
    ).astype(BF16)
    pack(keep2_ref, send2_ref, cols, dots, loss)


def head_kernel(keep_ref, got_ref, unit_ref, inv_ref, feats_ref, flat_ref, *dir_refs):
    cols = keep_ref.shape[0] - EXTRA
    dots, loss = unpack(keep_ref, got_ref, cols)
    total = keep_ref[:cols] + got_ref[:cols].astype(F32)
    back = ((total - unit_ref[...] * dots) * inv_ref[...]).astype(BF16)
    head = jnp.dot(back, feats_ref[...], preferred_element_type=F32).astype(BF16)
    tiles = feats_ref.shape[1] // LANES
    for k in range(tiles):
        flat_ref[k * cols : (k + 1) * cols] = head[:, k * LANES : (k + 1) * LANES]
    part = loss[:, :LANES]
    for k in range(1, loss.shape[1] // LANES):
        part = part + loss[:, k * LANES : (k + 1) * LANES]
    terms = [t.astype(F32) for t in split3(part)]
    tail = jnp.concatenate(terms + [jnp.zeros((EXTRA - 3, LANES), F32)], axis=0)
    at = tiles * cols
    flat_ref[at : at + EXTRA] = tail.astype(BF16)
    flat_ref[at + EXTRA :] = jnp.zeros((flat_ref.shape[0] - at - EXTRA, LANES), BF16)
    low = total.astype(BF16)
    terms = [t.astype(F32) for t in split3(dots)]
    lines = jnp.concatenate(terms + [jnp.zeros((EXTRA - 3, dots.shape[1]), F32)], axis=0).astype(BF16)
    rows = dir_refs[0].shape[1]
    for k, ref in enumerate(dir_refs):
        ref[:cols] = low[:, k * rows : (k + 1) * rows]
        ref[cols:] = lines[:, k * rows : (k + 1) * rows]


def back_kernel(unit_ref, inv_ref, *refs):
    out_ref = refs[-1]
    cols, rows = unit_ref.shape
    total = refs[0][...].astype(F32)
    for ref in refs[1:-1]:
        total = total + ref[...].astype(F32)
    dots = total[cols : cols + 1] + total[cols + 1 : cols + 2] + total[cols + 2 : cols + 3]
    out_ref[...] = ((total[:cols] - unit_ref[...] * dots) * inv_ref[:, :rows]).astype(BF16)


def sum_kernel(parts_ref, after_ref, out_ref):
    total = jnp.sum(parts_ref[...].astype(F32), axis=0)
    for k in range(out_ref.shape[0]):
        out_ref[k] = total


def feat_kernel(at_ref, weight_ref, *refs):
    out_ref, back_ref = refs[-2:]
    cols = refs[0].shape[0]
    for d, ref in enumerate(refs[:-2]):
        back_ref[pl.ds(pl.multiple_of(at_ref[8 + d] * cols, 16), cols), :] = ref[...]
    out_ref[...] = lax.dot_general(
        back_ref[...], weight_ref[...], (((0,), (1,)), ((), ())), preferred_element_type=F32
    ).astype(BF16)


def last_sum_kernel(at_ref, parts_ref, out_ref):
    total = jnp.sum(parts_ref[...], axis=0)
    low = total.astype(BF16)
    first = total[:EXTRA]
    terms = [t.astype(F32) for t in split3(first[0:1] + first[1:2] + first[2:3])]
    row = jnp.concatenate(terms + [jnp.zeros((EXTRA - 3, LANES), F32)], axis=0).astype(BF16)
    first = jnp.where(at_ref[7] > 0, row.astype(F32), first).astype(BF16)
    for k in range(out_ref.shape[0]):
        out_ref[k, :EXTRA] = first
        out_ref[k, EXTRA:] = low[EXTRA:]


def final_kernel(pairs, full_ref, head_ref, loss_ref):
    width, cols = head_ref.shape
    tiles = width // LANES
    for k in range(tiles):
        head_ref[k * LANES : (k + 1) * LANES] = full_ref[k * cols : (k + 1) * cols].astype(F32).T.astype(BF16)
    at = tiles * cols
    total = jnp.sum(full_ref[at : at + EXTRA].astype(F32), axis=0, keepdims=True)
    loss_ref[...] = jnp.sum(total, axis=1, keepdims=True) / pairs


def shift_by(x, axis, step):
    n = lax.axis_size(axis)
    return lax.ppermute(x, axis, [(k, (k + step) % n) for k in range(n)])


def local(img_feat, head_weight, text_embed, log_temp, logit_bias):
    rows, width = img_feat.shape
    quarter = text_embed.shape[0]
    ny, nx, nzh, nzl, nc = (lax.axis_size(a) for a in ("y", "x", "zh", "zl", "c"))
    nrep = nzl * nc
    plane = nx * ny
    cols = width // nrep
    images = nzh * rows
    tiles = width // LANES
    y_at, x_at, zl_at, c_at = (lax.axis_index(a) for a in ("y", "x", "zl", "c"))
    rep_at = zl_at * nc + c_at
    at_loss = tiles * cols
    piece = -(-(at_loss + EXTRA) // (plane * 16)) * 16
    assert at_loss % piece == 0
    at = jnp.stack(
        [
            rep_at,
            0 * rep_at,
            y_at * quarter,
            rep_at * quarter,
            quarter + 0 * rep_at,
            c_at,
            zl_at,
            (y_at * nx + x_at == at_loss // piece).astype(jnp.int32),
        ]
        + [rep_at ^ d for d in range(nrep)]
    ).astype(jnp.int32)
    par = jnp.stack([jnp.exp(log_temp[0]), logit_bias[0]])

    copies = call(text_kernel, shape((ny * quarter, width), BF16), text_embed)
    feats = [img_feat] + [shift_by(img_feat, "zh", s) for s in range(1, nzh)]
    own = to_all(copies, "y")
    left = shift_by(own, "x", 1)
    right = shift_by(own, "x", -1)
    half = own.shape[0] // 2
    far_a = shift_by(left[:half], "x", 1)
    far_b = shift_by(right[half:], "x", -1)

    unit, low, inv, own_unit, col_unit, feats = call(
        image_kernel,
        [
            shape((width, images), F32),
            shape((width, images), BF16),
            shape((1, images), F32),
            shape((cols, rows), F32),
            shape((cols, images), F32),
            shape((images, width), BF16),
        ],
        at,
        head_weight.T,
        *feats,
        smem=1,
        flops=2 * width * width * images,
    )
    acc, loss_row = call(
        first_kernel,
        [shape((width, images), F32), shape((1, images), F32)],
        at,
        par,
        own,
        left,
        right,
        low,
        smem=2,
        flops=4 * width * images * 3 * own.shape[0],
    )
    keep, send = call(
        second_kernel,
        [shape((2 * cols + EXTRA, images), F32), shape((2 * cols + EXTRA, images), BF16)],
        at,
        par,
        far_a,
        far_b,
        low,
        unit,
        acc,
        loss_row,
        smem=2,
        flops=4 * width * images * own.shape[0],
        scratch_shapes=[pltpu.VMEM((width, images), F32)],
    )
    got = lax.ppermute(send, "c", [(0, 1), (1, 0)])
    keep2, send2 = call(
        middle_kernel,
        [shape((cols + EXTRA, images), F32), shape((cols + EXTRA, images), BF16)],
        at,
        keep,
        got,
        smem=1,
    )
    got2 = lax.ppermute(send2, "zl", [(0, 1), (1, 0)])
    flat, *dirs = call(
        head_kernel,
        [shape((plane * piece, LANES), BF16)] + [shape((cols + EXTRA, rows), BF16)] * nzh,
        keep2,
        got2,
        col_unit,
        inv,
        feats,
        flops=2 * cols * images * width,
    )

    dirs = [dirs[0]] + [shift_by(dirs[s], "zh", -s) for s in range(1, nzh)]
    back = call(back_kernel, shape((cols, rows), BF16), own_unit, inv, *dirs)

    parts = to_all(flat, ("y", "x")).reshape(plane, piece, LANES)
    part = pl.pallas_call(
        sum_kernel,
        out_shape=shape((nzh, piece, LANES), F32),
        in_specs=[VMEM, pl.BlockSpec(memory_space=pl.ANY)],
        out_specs=VMEM,
    )(parts, back)
    part = to_all(part, "zh")
    low_part = call(last_sum_kernel, shape((plane, piece, LANES), BF16), at, part, smem=1)
    full = to_all(low_part.reshape(plane * piece, LANES), ("y", "x"))
    group = rows * plane * nzh
    head_grad, loss = call(
        functools.partial(final_kernel, float(group) * float(group)),
        [shape((width, cols), BF16), shape((1, 1), F32)],
        full,
    )

    backs = [back]
    for d in range(1, nrep):
        backs.append(lax.ppermute(back, ("zl", "c"), [(k, k ^ d) for k in range(nrep)]))
    feat_grad = call(
        feat_kernel,
        shape((rows, width), BF16),
        at,
        head_weight,
        *backs,
        smem=1,
        flops=2 * rows * width * width,
        scratch_shapes=[pltpu.VMEM((width, rows), BF16)],
    )
    return (loss.reshape(1), feat_grad, head_grad)


def solution(mesh):
    devices = mesh.devices.reshape(8, 4, 4, 2, 2)
    fine = Mesh(devices, ("y", "x", "zh", "zl", "c"))
    batch, rep = (("y", "x", "zh"), ("zl", "c"))
    in_specs = (P(batch, None), P(), P(batch + rep, None), P(), P())
    out_specs = (P(), P(batch, None), P(None, rep))
    return jax.shard_map(local, mesh=fine, in_specs=in_specs, out_specs=out_specs, check_vma=False)
```

time: 207 us -> 176 us (0.85)
  waiting for transfers between devices: 86 us -> 35.6 us
  starting transfers between devices: 38.8 us -> 68 us
  between operations: 15.5 us -> 2.27 us
  blocking collectives: 29.7 us -> 40.1 us
  Pallas kernels: 21.3 us -> 18.6 us
  matrix products: 2.61 us -> 0 us
    ppermute x0 -> x13, starting transfers between devices: none -> 52 us  [the longest x10 44.4 us: shift_by(): return lax.ppermute(x, axis, [(k, (k + step) % n) for k in range(n)])]
    all_to_all x6 -> x2, waiting for transfers between devices: 60.9 us -> 9.63 us  [to_all(): return lax.all_to_all(copies, axes, 0, 0, tiled=True)]
    all_to_all x6 -> x2, starting transfers between devices: 32.2 us -> 12.1 us  [to_all(): return lax.all_to_all(copies, axes, 0, 0, tiled=True)]
    all_gather x1 -> x0, waiting for transfers between devices: 14.8 us -> none  [local(): feats = lax.all_gather(img_feat, 'zh', axis=0, tiled=True)]
    ppermute x0 -> x13, waiting for transfers between devices: none -> 14.7 us  [the longest x10 11.7 us: shift_by(): return lax.ppermute(x, axis, [(k, (k + step) % n) for k in range(n)])]
    all_to_all x1 -> x2, blocking collectives: 29.7 us -> 40.1 us  [to_all(): return lax.all_to_all(copies, axes, 0, 0, tiled=True)]
    pallas_call x2 -> x1, Pallas kernels: 11.6 us -> 1.96 us  [local(): pl.pallas_call(sum_kernel, out_shape=shape((nzh, piece, LANES), F32), in_...]
    pallas_call x8 -> x10, Pallas kernels: 9.63 us -> 16.6 us  [call(): pl.pallas_call(body, out_shape=outs, in_specs=specs, out_specs=[VMEM] * l...]
  transfers between devices with their start and end apart: 9 -> 17, of which waited for: 9 -> 10; matrix products, arithmetic and copies ran while one was open for 3% -> 4% of each run, Pallas kernels for 5% -> 6%
where the time goes in v3:
time: 176 us; the launch traced here: 175 us
  starting transfers between devices  68 us (39%)
  blocking collectives  40.1 us (23%)
  waiting for transfers between devices  35.6 us (20%)
  Pallas kernels  18.6 us (11%)
  local copies, waits for them, and re-layouts  10.7 us (6%)
  between operations  2.27 us (1%)
    ppermute x10, starting transfers between devices, shift_by(): return lax.ppermute(x, axis, [(k, (k + step) % n) for k in range(n)])  44.4 us
    all_to_all x2, blocking collectives, to_all(): return lax.all_to_all(copies, axes, 0, 0, tiled=True)  40.1 us
    pallas_call x10, Pallas kernels, call(): pl.pallas_call(body, out_shape=outs, in_specs=specs, out_specs=[VMEM] * l...  16.6 us
    all_to_all x2, starting transfers between devices, to_all(): return lax.all_to_all(copies, axes, 0, 0, tiled=True)  12.1 us
    ppermute x10, waiting for transfers between devices, shift_by(): return lax.ppermute(x, axis, [(k, (k + step) % n) for k in range(n)])  11.7 us
    all_to_all x2, waiting for transfers between devices, to_all(): return lax.all_to_all(copies, axes, 0, 0, tiled=True)  9.63 us
    ppermute x1, waiting for transfers between devices, local(): got2 = lax.ppermute(send2, 'zl', [(0, 1), (1, 0)])  9.37 us
    unnamed x14, local copies, waits for them, and re-layouts  8.62 us
  transfers between devices with their start and end apart: 17, of which 10 were waited for; matrix products, arithmetic and copies ran while one was open for 4% of the time, Pallas kernels for 6%

profile of v3, /device:TPU:2, one launch (start us, length us, event | category | flops | bytes accessed | tf_op | source)
XLA Modules:
  0.0 175.3 jit_solution(15247054550035170953)
XLA Ops:
  0.6 0.9 copy-done.4
  1.5 0.1 shard_map.76
  1.7 25.8 %all_to_all.33 = bf16[8,32,1152]{2,1,0:T(8,128)(2,1)S(1)} all-to-all(bf16[8,32,1152]{2,1,0:T(8,128)(2,1)S(1)} %bitcast.17), channel_id=1, replica_groups=mesh['y'=8,'x'=4,'zh'=4,'zl'=2,'c'=2] {'y'}, dimensions={0} | all-to-all | bytes 1179648 | tf_op jit(solution)/shard_map/all_to_all | solution.py:48
  27.5 3.4 %collective-permute-start = (bf16[256,1152]{1,0:T(8,128)(2,1)S(1)}, bf16[256,1152]{1,0:T(8,128)(2,1)}, u32[]{:S(2)}, u32[]{:S(2)}) collective-permute-start(bf16[256,1152]{1,0:T(8,128)(2,1)S(1)} %bitcast.18), channel_id=1, source_target_pairs={{0,16},{16,32},{32,48},{48,0},{1,17},{17,33},{33,49},{49,1},{2,18}... | collective-permute-start | bytes 1769480 | tf_op jit(solution)/shard_map/ppermute | solution.py:235
  30.9 2.4 %collective-permute-start.2 = (bf16[256,1152]{1,0:T(8,128)(2,1)S(1)}, bf16[256,1152]{1,0:T(8,128)(2,1)}, u32[]{:S(2)}, u32[]{:S(2)}) collective-permute-start(bf16[256,1152]{1,0:T(8,128)(2,1)S(1)} %bitcast.19), channel_id=1, source_target_pairs={{0,48},{16,0},{32,16},{48,32},{1,49},{17,1},{33,17},{49,33},{2,50}... | collective-permute-start | bytes 1769480 | tf_op jit(solution)/shard_map/ppermute | solution.py:235
  33.3 6.1 %collective-permute-start.4 = (bf16[128,1152]{1,0:T(8,128)(2,1)}, bf16[128,1152]{1,0:T(8,128)(2,1)}, u32[]{:S(2)}, u32[]{:S(2)}) collective-permute-start(bf16[128,1152]{1,0:T(8,128)(2,1)} %refs_0_.1), channel_id=1, source_target_pairs={{0,4},{4,8},{8,12},{12,0},{1,5},{5,9},{9,13},{13,1},{2,6},{6,10},{... | collective-permute-start | bytes 884744 | tf_op jit(solution)/shard_map/ppermute | solution.py:235
  39.4 9.1 %collective-permute-start.5 = (bf16[128,1152]{1,0:T(8,128)(2,1)}, bf16[128,1152]{1,0:T(8,128)(2,1)}, u32[]{:S(2)}, u32[]{:S(2)}) collective-permute-start(bf16[128,1152]{1,0:T(8,128)(2,1)} %refs_0_.1), channel_id=1, source_target_pairs={{0,8},{4,12},{8,0},{12,4},{1,9},{5,13},{9,1},{13,5},{2,10},{6,14},... | collective-permute-start | bytes 884744 | tf_op jit(solution)/shard_map/ppermute | solution.py:235
  48.5 3.7 %collective-permute-start.6 = (bf16[128,1152]{1,0:T(8,128)(2,1)}, bf16[128,1152]{1,0:T(8,128)(2,1)}, u32[]{:S(2)}, u32[]{:S(2)}) collective-permute-start(bf16[128,1152]{1,0:T(8,128)(2,1)} %refs_0_.1), channel_id=1, source_target_pairs={{0,12},{4,0},{8,4},{12,8},{1,13},{5,1},{9,5},{13,9},{2,14},{6,2},{... | collective-permute-start | bytes 884744 | tf_op jit(solution)/shard_map/ppermute | solution.py:235
  52.2 4.1 %copy.8 = bf16[1152,1152]{0,1:T(8,128)(2,1)S(1)} copy(bf16[1152,1152]{1,0:T(8,128)(2,1)} %weight_ref.1) | data formatting | bytes 5308416 | tf_op args[1]
  57.7 0.1 stack.48.at_ref
  57.8 1.0 slice.8
  58.8 3.4 %collective-permute-start.1 = (bf16[128,1152]{1,0:T(8,128)(2,1)S(1)}, bf16[128,1152]{1,0:T(8,128)(2,1)S(1)}, u32[]{:S(2)}, u32[]{:S(2)}) collective-permute-start(bf16[128,1152]{1,0:T(8,128)(2,1)S(1)} %slice.8), channel_id=1, source_target_pairs={{0,16},{16,32},{32,48},{48,0},{1,17},{17,33},{33,49},{49,1},{2,18}... | collective-permute-start | bytes 884744 | tf_op jit(solution)/shard_map/ppermute | solution.py:235
  62.3 1.0 slice.9
  63.2 2.4 %collective-permute-start.3 = (bf16[128,1152]{1,0:T(8,128)(2,1)S(1)}, bf16[128,1152]{1,0:T(8,128)(2,1)S(1)}, u32[]{:S(2)}, u32[]{:S(2)}) collective-permute-start(bf16[128,1152]{1,0:T(8,128)(2,1)S(1)} %slice.9), channel_id=1, source_target_pairs={{0,48},{16,0},{32,16},{48,32},{1,49},{17,1},{33,17},{49,33},{2,50}... | collective-permute-start | bytes 884744 | tf_op jit(solution)/shard_map/ppermute | solution.py:235
  65.7 0.8 collective-permute-done.5.refs_2_
  66.5 6.7 %collective-permute-done.6.refs_3_ = bf16[128,1152]{1,0:T(8,128)(2,1)} collective-permute-done((bf16[128,1152]{1,0:T(8,128)(2,1)}, bf16[128,1152]{1,0:T(8,128)(2,1)}, u32[]{:S(2)}, u32[]{:S(2)}) %collective-permute-start.6) | collective-permute-done | bytes 294944 | tf_op jit(solution)/shard_map/ppermute | solution.py:235
  73.2 1.0 copy-done.5
  74.2 3.5 %shard_map.77 = (f32[1152,512]{1,0:T(8,128)S(1)}, bf16[1152,512]{1,0:T(8,128)(2,1)S(1)}, f32[1,512]{1,0:T(1,128)S(1)}, f32[288,128]{1,0:T(8,128)S(1)}, f32[288,5...) custom-call(s32[12]{0:T(128)S(1)} %stack.48.at_ref, bf16[1152,1152]{1,0:T(8,128)(2,1)S(1)} %bitcast.16, ...), custom_call_target="tpu_custom_call" | custom-call | flops 1358954496 | bytes 3833904 | tf_op jit(solution)/shard_map/pallas_call | solution.py:24
  77.7 5.2 %shard_map.78 = (f32[1152,512]{1,0:T(8,128)S(1)}, f32[1,512]{1,0:T(1,128)S(1)}) custom-call(s32[12]{0:T(128)S(1)} %stack.48.at_ref, f32[2]{0:T(128)S(1)} %pad_maximum_fusion.par_ref, bf16[256,1152]{1,0:T(8,128)(2,1)S(1)} %bitcast.20, bf16[256,1152]{1,0:T(8,128)(2,1)} %collective-permute-done.left_ref, bf16[256,1152]{1,0:T(8,128)(2,1)} %collective-permute-done.2.right_ref, ...), custom_call_target="tpu_custom_call" | custom-call | flops 1811939328 | bytes 2949176 | tf_op jit(solution)/shard_map/pallas_call | solution.py:24
  82.9 2.1 %shard_map.79 = (f32[592,512]{1,0:T(8,128)S(1)}, bf16[592,512]{1,0:T(8,128)(2,1)S(1)}) custom-call(s32[12]{0:T(128)S(1)} %stack.48.at_ref, f32[2]{0:T(128)S(1)} %pad_maximum_fusion.par_ref, bf16[128,1152]{1,0:T(8,128)(2,1)S(1)} %collective-permute-done.1.a_ref, bf16[128,1152]{1,0:T(8,128)(2,1)S(1)} %collective-permute-done.3.b_ref, ...), custom_call_target="tpu_custom_call" | custom-call | flops 603979776 | bytes 6490168 | tf_op jit(solution)/shard_map/pallas_call | solution.py:24
  85.0 1.9 %collective-permute-start.7 = (bf16[592,512]{1,0:T(8,128)(2,1)S(1)}, bf16[592,512]{1,0:T(8,128)(2,1)S(1)}, u32[]{:S(2)}, u32[]{:S(2)}) collective-permute-start(bf16[592,512]{1,0:T(8,128)(2,1)S(1)} %get-tuple-element.27), channel_id=1, source_target_pairs={{0,1},{1,0},{2,3},{3,2},{4,5},{5,4},{6,7},{7,6},{8,9},{9,8},{10,11... | collective-permute-start | bytes 1818632 | tf_op jit(solution)/shard_map/ppermute | solution.py:319
  86.9 2.0 %collective-permute-done.7.got_ref = bf16[592,512]{1,0:T(8,128)(2,1)S(1)} collective-permute-done((bf16[592,512]{1,0:T(8,128)(2,1)S(1)}, bf16[592,512]{1,0:T(8,128)(2,1)S(1)}, u32[]{:S(2)}, u32[]{:S(2)}) %collective-permute-start.7) | collective-permute-done | bytes 606240 | tf_op jit(solution)/shard_map/ppermute | solution.py:319
  88.9 0.7 shard_map.80
  89.6 1.9 %collective-permute-start.8 = (bf16[304,512]{1,0:T(8,128)(2,1)S(1)}, bf16[304,512]{1,0:T(8,128)(2,1)S(1)}, u32[]{:S(2)}, u32[]{:S(2)}) collective-permute-start(bf16[304,512]{1,0:T(8,128)(2,1)S(1)} %get-tuple-element.29), channel_id=1, source_target_pairs={{0,2},{2,0},{1,3},{3,1},{4,6},{6,4},{5,7},{7,5},{8,10},{10,8},{9,1... | collective-permute-start | bytes 933896 | tf_op jit(solution)/shard_map/ppermute | solution.py:328
  91.6 9.4 %collective-permute-done.8.got_ref = bf16[304,512]{1,0:T(8,128)(2,1)S(1)} collective-permute-done((bf16[304,512]{1,0:T(8,128)(2,1)S(1)}, bf16[304,512]{1,0:T(8,128)(2,1)S(1)}, u32[]{:S(2)}, u32[]{:S(2)}) %collective-permute-start.8) | collective-permute-done | bytes 311328 | tf_op jit(solution)/shard_map/ppermute | solution.py:328
  100.9 1.5 shard_map.81
  102.5 6.4 %all-to-all-start.1 = ((bf16[32,96,128]{2,1,0:T(8,128)(2,1)}), bf16[32,96,128]{2,1,0:T(8,128)(2,1)}, u32[]{:S(2)}, u32[]{:S(2)}) async-start(bf16[32,96,128]{2,1,0:T(8,128)(2,1)} %bitcast.12), calls=%async_computation.1 | async-start | bytes 1572864 | tf_op jit(solution)/shard_map/all_to_all | solution.py:48
  108.9 5.9 %collective-permute-start.10 = (bf16[304,128]{1,0:T(8,128)(2,1)S(1)}, bf16[304,128]{1,0:T(8,128)(2,1)S(1)}, u32[]{:S(2)}, u32[]{:S(2)}) collective-permute-start(bf16[304,128]{1,0:T(8,128)(2,1)S(1)} %get-tuple-element.37), channel_id=1, source_target_pairs={{0,8},{4,12},{8,0},{12,4},{1,9},{5,13},{9,1},{13,5},{2,10},{6,14},... | collective-permute-start | bytes 233480 | tf_op jit(solution)/shard_map/ppermute | solution.py:235
  114.9 4.1 %collective-permute-start.11 = (bf16[304,128]{1,0:T(8,128)(2,1)S(1)}, bf16[304,128]{1,0:T(8,128)(2,1)S(1)}, u32[]{:S(2)}, u32[]{:S(2)}) collective-permute-start(bf16[304,128]{1,0:T(8,128)(2,1)S(1)} %get-tuple-element.38), channel_id=1, source_target_pairs={{0,4},{4,8},{8,12},{12,0},{1,5},{5,9},{9,13},{13,1},{2,6},{6,10},{... | collective-permute-start | bytes 233480 | tf_op jit(solution)/shard_map/ppermute | solution.py:235
  119.0 3.8 %collective-permute-start.9 = (bf16[304,128]{1,0:T(8,128)(2,1)S(1)}, bf16[304,128]{1,0:T(8,128)(2,1)S(1)}, u32[]{:S(2)}, u32[]{:S(2)}) collective-permute-start(bf16[304,128]{1,0:T(8,128)(2,1)S(1)} %get-tuple-element.36), channel_id=1, source_target_pairs={{0,12},{4,0},{8,4},{12,8},{1,13},{5,1},{9,5},{13,9},{2,14},{6,2},{... | collective-permute-start | bytes 233480 | tf_op jit(solution)/shard_map/ppermute | solution.py:235
  122.8 0.7 collective-permute-done.11.refs_3_
  123.6 3.5 %collective-permute-done.9.refs_1_ = bf16[304,128]{1,0:T(8,128)(2,1)S(1)} collective-permute-done((bf16[304,128]{1,0:T(8,128)(2,1)S(1)}, bf16[304,128]{1,0:T(8,128)(2,1)S(1)}, u32[]{:S(2)}, u32[]{:S(2)}) %collective-permute-start.9) | collective-permute-done | bytes 77856 | tf_op jit(solution)/shard_map/ppermute | solution.py:235
  127.1 0.6 copy-done.2
  127.7 3.1 %all-to-all-done.1.parts_ref = bf16[32,96,128]{2,1,0:T(8,128)(2,1)} async-done(((bf16[32,96,128]{2,1,0:T(8,128)(2,1)}), bf16[32,96,128]{2,1,0:T(8,128)(2,1)}, u32[]{:S(2)}, u32[]{:S(2)}) %all-to-all-start.1) | async-done | bytes 786464 | tf_op jit(solution)/shard_map/all_to_all | solution.py:48
  130.9 2.0 %shard_map.83 = f32[4,96,128]{2,1,0:T(8,128)} custom-call(bf16[32,96,128]{2,1,0:T(8,128)(2,1)} %all-to-all-done.1.parts_ref, bf16[288,128]{1,0:T(8,128)(2,1)} %copy-done.2), custom_call_target="tpu_custom_call" | custom-call | tf_op jit(solution)/shard_map/pallas_call | solution.py:344
  132.8 14.3 %all_to_all.34.parts_ref = f32[4,96,128]{2,1,0:T(8,128)S(1)} all-to-all(f32[4,96,128]{2,1,0:T(8,128)} %shard_map.83), channel_id=1, replica_groups=mesh['y'=8,'x'=4,'zh'=4,'zl'=2,'c'=2] {'zh'}, dimensions={0} | all-to-all | bytes 393216 | tf_op jit(solution)/shard_map/all_to_all | solution.py:48
  147.1 0.6 shard_map.84
  147.7 0.9 copy-done.1
  148.6 5.7 %all-to-all-start.3 = ((bf16[32,96,128]{2,1,0:T(8,128)(2,1)}), bf16[32,96,128]{2,1,0:T(8,128)(2,1)S(1)}, u32[]{:S(2)}, u32[]{:S(2)}) async-start(bf16[32,96,128]{2,1,0:T(8,128)(2,1)} %copy-done.1), calls=%async_computation.3 | async-start | bytes 1572864 | tf_op jit(solution)/shard_map/all_to_all | solution.py:48
  154.4 1.9 %collective-permute-start.12 = (bf16[288,128]{1,0:T(8,128)(2,1)S(1)}, bf16[288,128]{1,0:T(8,128)(2,1)S(1)}, u32[]{:S(2)}, u32[]{:S(2)}) collective-permute-start(bf16[288,128]{1,0:T(8,128)(2,1)S(1)} %copy-done.3), channel_id=1, source_target_pairs={{0,1},{1,0},{2,3},{3,2},{4,5},{5,4},{6,7},{7,6},{8,9},{9,8},{10,11... | collective-permute-start | bytes 221192 | tf_op jit(solution)/shard_map/ppermute | solution.py:362
  156.3 2.5 %collective-permute-start.13 = (bf16[288,128]{1,0:T(8,128)(2,1)S(1)}, bf16[288,128]{1,0:T(8,128)(2,1)S(1)}, u32[]{:S(2)}, u32[]{:S(2)}) collective-permute-start(bf16[288,128]{1,0:T(8,128)(2,1)S(1)} %copy-done.3), channel_id=1, source_target_pairs={{0,2},{1,3},{2,0},{3,1},{4,6},{5,7},{6,4},{7,5},{8,10},{9,11},{10,... | collective-permute-start | bytes 221192 | tf_op jit(solution)/shard_map/ppermute | solution.py:362
  158.8 3.2 %collective-permute-start.14 = (bf16[288,128]{1,0:T(8,128)(2,1)S(1)}, bf16[288,128]{1,0:T(8,128)(2,1)S(1)}, u32[]{:S(2)}, u32[]{:S(2)}) collective-permute-start(bf16[288,128]{1,0:T(8,128)(2,1)S(1)} %copy-done.3), channel_id=1, source_target_pairs={{0,3},{1,2},{2,1},{3,0},{4,7},{5,6},{6,5},{7,4},{8,11},{9,10},{10,... | collective-permute-start | bytes 221192 | tf_op jit(solution)/shard_map/ppermute | solution.py:362
  162.0 0.9 collective-permute-done.13.refs_2_
  162.9 2.1 %collective-permute-done.14.refs_3_ = bf16[288,128]{1,0:T(8,128)(2,1)S(1)} collective-permute-done((bf16[288,128]{1,0:T(8,128)(2,1)S(1)}, bf16[288,128]{1,0:T(8,128)(2,1)S(1)}, u32[]{:S(2)}, u32[]{:S(2)}) %collective-permute-start.14) | collective-permute-done | bytes 73760 | tf_op jit(solution)/shard_map/ppermute | solution.py:362
  164.9 2.2 %shard_map.86 = bf16[128,1152]{1,0:T(8,128)(2,1)} custom-call(s32[12]{0:T(128)S(1)} %stack.48.at_ref, bf16[1152,1152]{1,0:T(8,128)(2,1)S(1)} %copy-done, bf16[288,128]{1,0:T(8,128)(2,1)S(1)} %copy-done.3, bf16[288,128]{1,0:T(8,128)(2,1)S(1)} %collective-permute-done.12.refs_1_, bf16[288,128]{1,0:T(8,128)(2,1)S(1)} %collective-permute-done.13.refs_2_, ...), custom_call_target="tpu_custom_call" | custom-call | flops 339738624 | bytes 2949168 | tf_op jit(solution)/shard_map/pallas_call | solution.py:24
  167.1 6.5 %all-to-all-done.3 = bf16[32,96,128]{2,1,0:T(8,128)(2,1)S(1)} async-done(((bf16[32,96,128]{2,1,0:T(8,128)(2,1)}), bf16[32,96,128]{2,1,0:T(8,128)(2,1)S(1)}, u32[]{:S(2)}, u32[]{:S(2)}) %all-to-all-start.3) | async-done | bytes 786464 | tf_op jit(solution)/shard_map/all_to_all | solution.py:48
  173.6 0.6 shard_map.85
  174.2 1.1 copy.9
  (17 shorter events, 0.2 us)
Async XLA Ops:
  0.6 0.9 copy-start.4
  27.5 30.4 %collective-permute-start = (bf16[256,1152]{1,0:T(8,128)(2,1)S(1)}, bf16[256,1152]{1,0:T(8,128)(2,1)}, u32[]{:S(2)}, u32[]{:S(2)}) collective-permute-start(bf16[256,1152]{1,0:T(8,128)(2,1)S(1)} %bitcast.18), channel_id=1, source_target_pairs={{0,16},{16,32},{32,48},{48,0},{1,17},{17,33},{33,49},{49,1},{2,18}... | collective-permute-start | bytes 1769480 | tf_op jit(solution)/shard_map/ppermute | solution.py:235
  30.9 31.4 %collective-permute-start.2 = (bf16[256,1152]{1,0:T(8,128)(2,1)S(1)}, bf16[256,1152]{1,0:T(8,128)(2,1)}, u32[]{:S(2)}, u32[]{:S(2)}) collective-permute-start(bf16[256,1152]{1,0:T(8,128)(2,1)S(1)} %bitcast.19), channel_id=1, source_target_pairs={{0,48},{16,0},{32,16},{48,32},{1,49},{17,1},{33,17},{49,33},{2,50}... | collective-permute-start | bytes 1769480 | tf_op jit(solution)/shard_map/ppermute | solution.py:235
  33.3 32.4 %collective-permute-start.4 = (bf16[128,1152]{1,0:T(8,128)(2,1)}, bf16[128,1152]{1,0:T(8,128)(2,1)}, u32[]{:S(2)}, u32[]{:S(2)}) collective-permute-start(bf16[128,1152]{1,0:T(8,128)(2,1)} %refs_0_.1), channel_id=1, source_target_pairs={{0,4},{4,8},{8,12},{12,0},{1,5},{5,9},{9,13},{13,1},{2,6},{6,10},{... | collective-permute-start | bytes 884744 | tf_op jit(solution)/shard_map/ppermute | solution.py:235
  39.4 27.1 %collective-permute-start.5 = (bf16[128,1152]{1,0:T(8,128)(2,1)}, bf16[128,1152]{1,0:T(8,128)(2,1)}, u32[]{:S(2)}, u32[]{:S(2)}) collective-permute-start(bf16[128,1152]{1,0:T(8,128)(2,1)} %refs_0_.1), channel_id=1, source_target_pairs={{0,8},{4,12},{8,0},{12,4},{1,9},{5,13},{9,1},{13,5},{2,10},{6,14},... | collective-permute-start | bytes 884744 | tf_op jit(solution)/shard_map/ppermute | solution.py:235
  48.5 24.7 %collective-permute-start.6 = (bf16[128,1152]{1,0:T(8,128)(2,1)}, bf16[128,1152]{1,0:T(8,128)(2,1)}, u32[]{:S(2)}, u32[]{:S(2)}) collective-permute-start(bf16[128,1152]{1,0:T(8,128)(2,1)} %refs_0_.1), channel_id=1, source_target_pairs={{0,12},{4,0},{8,4},{12,8},{1,13},{5,1},{9,5},{13,9},{2,14},{6,2},{... | collective-permute-start | bytes 884744 | tf_op jit(solution)/shard_map/ppermute | solution.py:235
  58.8 24.0 %collective-permute-start.1 = (bf16[128,1152]{1,0:T(8,128)(2,1)S(1)}, bf16[128,1152]{1,0:T(8,128)(2,1)S(1)}, u32[]{:S(2)}, u32[]{:S(2)}) collective-permute-start(bf16[128,1152]{1,0:T(8,128)(2,1)S(1)} %slice.8), channel_id=1, source_target_pairs={{0,16},{16,32},{32,48},{48,0},{1,17},{17,33},{33,49},{49,1},{2,18}... | collective-permute-start | bytes 884744 | tf_op jit(solution)/shard_map/ppermute | solution.py:235
  63.2 19.6 %collective-permute-start.3 = (bf16[128,1152]{1,0:T(8,128)(2,1)S(1)}, bf16[128,1152]{1,0:T(8,128)(2,1)S(1)}, u32[]{:S(2)}, u32[]{:S(2)}) collective-permute-start(bf16[128,1152]{1,0:T(8,128)(2,1)S(1)} %slice.9), channel_id=1, source_target_pairs={{0,48},{16,0},{32,16},{48,32},{1,49},{17,1},{33,17},{49,33},{2,50}... | collective-permute-start | bytes 884744 | tf_op jit(solution)/shard_map/ppermute | solution.py:235
  73.2 1.0 copy-start.5
  85.0 3.9 %collective-permute-start.7 = (bf16[592,512]{1,0:T(8,128)(2,1)S(1)}, bf16[592,512]{1,0:T(8,128)(2,1)S(1)}, u32[]{:S(2)}, u32[]{:S(2)}) collective-permute-start(bf16[592,512]{1,0:T(8,128)(2,1)S(1)} %get-tuple-element.27), channel_id=1, source_target_pairs={{0,1},{1,0},{2,3},{3,2},{4,5},{5,4},{6,7},{7,6},{8,9},{9,8},{10,11... | collective-permute-start | bytes 1818632 | tf_op jit(solution)/shard_map/ppermute | solution.py:319
  89.6 11.3 %collective-permute-start.8 = (bf16[304,512]{1,0:T(8,128)(2,1)S(1)}, bf16[304,512]{1,0:T(8,128)(2,1)S(1)}, u32[]{:S(2)}, u32[]{:S(2)}) collective-permute-start(bf16[304,512]{1,0:T(8,128)(2,1)S(1)} %get-tuple-element.29), channel_id=1, source_target_pairs={{0,2},{2,0},{1,3},{3,1},{4,6},{6,4},{5,7},{7,5},{8,10},{10,8},{9,1... | collective-permute-start | bytes 933896 | tf_op jit(solution)/shard_map/ppermute | solution.py:328
  102.5 28.4 %all-to-all-start.1 = ((bf16[32,96,128]{2,1,0:T(8,128)(2,1)}), bf16[32,96,128]{2,1,0:T(8,128)(2,1)}, u32[]{:S(2)}, u32[]{:S(2)}) async-start(bf16[32,96,128]{2,1,0:T(8,128)(2,1)} %bitcast.12), calls=%async_computation.1 | async-start | bytes 1572864 | tf_op jit(solution)/shard_map/all_to_all | solution.py:48
  108.9 56.0 %copy-start = (bf16[1152,1152]{1,0:T(8,128)(2,1)S(1)}, bf16[1152,1152]{1,0:T(8,128)(2,1)}, u32[]{:S(2)}) copy-start(bf16[1152,1152]{1,0:T(8,128)(2,1)} %weight_ref.1) | copy-start | bytes 7962628
  108.9 13.9 %collective-permute-start.10 = (bf16[304,128]{1,0:T(8,128)(2,1)S(1)}, bf16[304,128]{1,0:T(8,128)(2,1)S(1)}, u32[]{:S(2)}, u32[]{:S(2)}) collective-permute-start(bf16[304,128]{1,0:T(8,128)(2,1)S(1)} %get-tuple-element.37), channel_id=1, source_target_pairs={{0,8},{4,12},{8,0},{12,4},{1,9},{5,13},{9,1},{13,5},{2,10},{6,14},... | collective-permute-start | bytes 233480 | tf_op jit(solution)/shard_map/ppermute | solution.py:235
  114.9 8.7 %collective-permute-start.11 = (bf16[304,128]{1,0:T(8,128)(2,1)S(1)}, bf16[304,128]{1,0:T(8,128)(2,1)S(1)}, u32[]{:S(2)}, u32[]{:S(2)}) collective-permute-start(bf16[304,128]{1,0:T(8,128)(2,1)S(1)} %get-tuple-element.38), channel_id=1, source_target_pairs={{0,4},{4,8},{8,12},{12,0},{1,5},{5,9},{9,13},{13,1},{2,6},{6,10},{... | collective-permute-start | bytes 233480 | tf_op jit(solution)/shard_map/ppermute | solution.py:235
  119.0 8.0 %collective-permute-start.9 = (bf16[304,128]{1,0:T(8,128)(2,1)S(1)}, bf16[304,128]{1,0:T(8,128)(2,1)S(1)}, u32[]{:S(2)}, u32[]{:S(2)}) collective-permute-start(bf16[304,128]{1,0:T(8,128)(2,1)S(1)} %get-tuple-element.36), channel_id=1, source_target_pairs={{0,12},{4,0},{8,4},{12,8},{1,13},{5,1},{9,5},{13,9},{2,14},{6,2},{... | collective-permute-start | bytes 233480 | tf_op jit(solution)/shard_map/ppermute | solution.py:235
  127.1 0.6 copy-start.2
  130.9 23.5 %copy-start.3 = (bf16[288,128]{1,0:T(8,128)(2,1)S(1)}, bf16[288,128]{1,0:T(8,128)(2,1)}, u32[]{:S(2)}) copy-start(bf16[288,128]{1,0:T(8,128)(2,1)} %copy-done.2) | copy-start | bytes 221188
  147.7 0.9 copy-start.1
  148.6 25.0 %all-to-all-start.3 = ((bf16[32,96,128]{2,1,0:T(8,128)(2,1)}), bf16[32,96,128]{2,1,0:T(8,128)(2,1)S(1)}, u32[]{:S(2)}, u32[]{:S(2)}) async-start(bf16[32,96,128]{2,1,0:T(8,128)(2,1)} %copy-done.1), calls=%async_computation.3 | async-start | bytes 1572864 | tf_op jit(solution)/shard_map/all_to_all | solution.py:48
  154.4 7.6 %collective-permute-start.12 = (bf16[288,128]{1,0:T(8,128)(2,1)S(1)}, bf16[288,128]{1,0:T(8,128)(2,1)S(1)}, u32[]{:S(2)}, u32[]{:S(2)}) collective-permute-start(bf16[288,128]{1,0:T(8,128)(2,1)S(1)} %copy-done.3), channel_id=1, source_target_pairs={{0,1},{1,0},{2,3},{3,2},{4,5},{5,4},{6,7},{7,6},{8,9},{9,8},{10,11... | collective-permute-start | bytes 221192 | tf_op jit(solution)/shard_map/ppermute | solution.py:362
  156.3 6.6 %collective-permute-start.13 = (bf16[288,128]{1,0:T(8,128)(2,1)S(1)}, bf16[288,128]{1,0:T(8,128)(2,1)S(1)}, u32[]{:S(2)}, u32[]{:S(2)}) collective-permute-start(bf16[288,128]{1,0:T(8,128)(2,1)S(1)} %copy-done.3), channel_id=1, source_target_pairs={{0,2},{1,3},{2,0},{3,1},{4,6},{5,7},{6,4},{7,5},{8,10},{9,11},{10,... | collective-permute-start | bytes 221192 | tf_op jit(solution)/shard_map/ppermute | solution.py:362
  158.8 6.1 %collective-permute-start.14 = (bf16[288,128]{1,0:T(8,128)(2,1)S(1)}, bf16[288,128]{1,0:T(8,128)(2,1)S(1)}, u32[]{:S(2)}, u32[]{:S(2)}) collective-permute-start(bf16[288,128]{1,0:T(8,128)(2,1)S(1)} %copy-done.3), channel_id=1, source_target_pairs={{0,3},{1,2},{2,1},{3,0},{4,7},{5,6},{6,5},{7,4},{8,11},{9,10},{10,... | collective-permute-start | bytes 221192 | tf_op jit(solution)/shard_map/ppermute | solution.py:362

commit v4 on v3

--- a/solution.py
+++ b/solution.py
@@ -57,13 +57,17 @@
         out_ref[k * n : (k + 1) * n] = low
 
 
-def image_kernel(at_ref, wt_ref, *refs):
-    feat_refs = refs[:-6]
-    unit_ref, low_ref, inv_ref, own_unit_ref, cols_ref, feats_ref = refs[-6:]
-    n = len(feat_refs)
-    rows = feat_refs[0].shape[0]
-    for k in range(n):
-        feats_ref[k * rows : (k + 1) * rows] = feat_refs[k][...]
+def image_kernel(at_ref, wt_ref, own_ref, fetched_ref, swapped_ref, *refs):
+    unit_ref, low_ref, inv_ref, own_unit_ref, cols_ref, feats_ref = refs
+    rows = own_ref.shape[0]
+    part = rows // 2
+    c = at_ref[5]
+    feats_ref[:rows] = own_ref[...]
+    for k in range(fetched_ref.shape[0] // part):
+        base = (k + 1) * rows
+        block = pl.ds(k * part, part)
+        feats_ref[pl.ds(pl.multiple_of(base + c * part, 16), part), :] = fetched_ref[block, :]
+        feats_ref[pl.ds(pl.multiple_of(base + (1 - c) * part, 16), part), :] = swapped_ref[block, :]
     head = lax.dot_general(
         wt_ref[...], feats_ref[...], (((1,), (1,)), ((), ())), preferred_element_type=F32
     )
@@ -265,14 +269,14 @@
     par = jnp.stack([jnp.exp(log_temp[0]), logit_bias[0]])
 
     copies = call(text_kernel, shape((ny * quarter, width), BF16), text_embed)
-    feats = [img_feat] + [shift_by(img_feat, "zh", s) for s in range(1, nzh)]
+    part = rows // nc
+    half_rows = lax.dynamic_slice_in_dim(img_feat, c_at * part, part, 0)
+    fetched = jnp.concatenate([shift_by(half_rows, "zh", s) for s in range(1, nzh)], axis=0)
     own = to_all(copies, "y")
+    own, fetched = lax.optimization_barrier((own, fetched))
+    swapped = lax.ppermute(fetched, "c", [(0, 1), (1, 0)])
     left = shift_by(own, "x", 1)
     right = shift_by(own, "x", -1)
-    half = own.shape[0] // 2
-    far_a = shift_by(left[:half], "x", 1)
-    far_b = shift_by(right[half:], "x", -1)
-
     unit, low, inv, own_unit, col_unit, feats = call(
         image_kernel,
         [
@@ -285,10 +289,16 @@
         ],
         at,
         head_weight.T,
-        *feats,
+        img_feat,
+        fetched,
+        swapped,
         smem=1,
         flops=2 * width * width * images,
     )
+    left, right, low = lax.optimization_barrier((left, right, low))
+    half = own.shape[0] // 2
+    far_a = shift_by(left[:half], "x", 1)
+    far_b = shift_by(right[half:], "x", -1)
     acc, loss_row = call(
         first_kernel,
         [shape((width, images), F32), shape((1, images), F32)],

time: 176 us -> 174 us (0.989)
  blocking collectives: 40.1 us -> 14.3 us
  starting transfers between devices: 68 us -> 81.5 us
  waiting for transfers between devices: 35.6 us -> 41.2 us
  local copies, waits for them, and re-layouts: 10.7 us -> 13.7 us
    all_to_all x2 -> x1, blocking collectives: 40.1 us -> 14.3 us  [to_all(): return lax.all_to_all(copies, axes, 0, 0, tiled=True)]
    all_to_all x2 -> x3, starting transfers between devices: 12.1 us -> 25.1 us  [to_all(): return lax.all_to_all(copies, axes, 0, 0, tiled=True)]
    ppermute x10, waiting for transfers between devices: 11.7 us -> 17.3 us  [shift_by(): return lax.ppermute(x, axis, [(k, (k + step) % n) for k in range(n)])]
    unnamed x14 -> x18, local copies, waits for them, and re-layouts: 8.62 us -> 10.7 us
    ppermute x0 -> x1, starting transfers between devices: none -> 1.92 us  [local(): swapped = lax.ppermute(fetched, 'c', [(0, 1), (1, 0)])]
    all_to_all x2 -> x3, waiting for transfers between devices: 9.63 us -> 8.68 us  [to_all(): return lax.all_to_all(copies, axes, 0, 0, tiled=True)]
  transfers between devices with their start and end apart: 17 -> 19, of which waited for: 10 -> 11; matrix products, arithmetic and copies ran while one was open for 4% -> 4% of each run, Pallas kernels for 6% -> 6%
where the time goes in v4:
time: 174 us; the launch traced here: 173 us
  starting transfers between devices  81.5 us (47%)
  waiting for transfers between devices  41.2 us (24%)
  Pallas kernels  19.2 us (11%)
  blocking collectives  14.3 us (8%)
  local copies, waits for them, and re-layouts  13.7 us (8%)
  between operations  2.29 us (1%)
    ppermute x10, starting transfers between devices, shift_by(): return lax.ppermute(x, axis, [(k, (k + step) % n) for k in range(n)])  43 us
    all_to_all x3, starting transfers between devices, to_all(): return lax.all_to_all(copies, axes, 0, 0, tiled=True)  25.1 us
    ppermute x10, waiting for transfers between devices, shift_by(): return lax.ppermute(x, axis, [(k, (k + step) % n) for k in range(n)])  17.3 us
    pallas_call x10, Pallas kernels, call(): pl.pallas_call(body, out_shape=outs, in_specs=specs, out_specs=[VMEM] * l...  17.2 us
    all_to_all x1, blocking collectives, to_all(): return lax.all_to_all(copies, axes, 0, 0, tiled=True)  14.3 us
    unnamed x18, local copies, waits for them, and re-layouts  10.7 us
    ppermute x1, waiting for transfers between devices, local(): got2 = lax.ppermute(send2, 'zl', [(0, 1), (1, 0)])  9.37 us
    all_to_all x3, waiting for transfers between devices, to_all(): return lax.all_to_all(copies, axes, 0, 0, tiled=True)  8.68 us
  transfers between devices with their start and end apart: 19, of which 11 were waited for; matrix products, arithmetic and copies ran while one was open for 4% of the time, Pallas kernels for 6%

profile of v4, /device:TPU:2, one launch (start us, length us, event | category | flops | bytes accessed | tf_op | source)
XLA Modules:
  0.0 173.0 jit_solution(413116348934020152)
XLA Ops:
  0.7 1.0 copy-done.7
  1.7 1.0 shard_map.76
  2.6 7.1 %all-to-all-start = ((bf16[8,32,1152]{2,1,0:T(8,128)(2,1)}), bf16[8,32,1152]{2,1,0:T(8,128)(2,1)S(1)}, u32[]{:S(2)}, u32[]{:S(2)}) async-start(bf16[8,32,1152]{2,1,0:T(8,128)(2,1)} %bitcast.9), calls=%async_computation | async-start | bytes 1179648 | tf_op jit(solution)/shard_map/all_to_all | solution.py:48
  9.7 0.9 constant_dynamic-slice_fusion
  10.7 6.1 %collective-permute-start = (bf16[64,1152]{1,0:T(8,128)(2,1)S(1)}, bf16[64,1152]{1,0:T(8,128)(2,1)S(1)}, u32[]{:S(2)}, u32[]{:S(2)}) collective-permute-start(bf16[64,1152]{1,0:T(8,128)(2,1)S(1)} %constant_dynamic-slice_fusion), channel_id=1, source_target_pairs={{0,4},{4,8},{8,12},{12,0},{1,5},{5,9},{9,13},{13,1},{2,6},{6,10},{... | collective-permute-start | bytes 442376 | tf_op jit(solution)/shard_map/ppermute | solution.py:239
  16.7 9.1 %collective-permute-start.1 = (bf16[64,1152]{1,0:T(8,128)(2,1)S(1)}, bf16[64,1152]{1,0:T(8,128)(2,1)S(1)}, u32[]{:S(2)}, u32[]{:S(2)}) collective-permute-start(bf16[64,1152]{1,0:T(8,128)(2,1)S(1)} %constant_dynamic-slice_fusion), channel_id=1, source_target_pairs={{0,8},{4,12},{8,0},{12,4},{1,9},{5,13},{9,1},{13,5},{2,10},{6,14},... | collective-permute-start | bytes 442376 | tf_op jit(solution)/shard_map/ppermute | solution.py:239
  25.9 3.7 %collective-permute-start.2 = (bf16[64,1152]{1,0:T(8,128)(2,1)S(1)}, bf16[64,1152]{1,0:T(8,128)(2,1)S(1)}, u32[]{:S(2)}, u32[]{:S(2)}) collective-permute-start(bf16[64,1152]{1,0:T(8,128)(2,1)S(1)} %constant_dynamic-slice_fusion), channel_id=1, source_target_pairs={{0,12},{4,0},{8,4},{12,8},{1,13},{5,1},{9,5},{13,9},{2,14},{6,2},{... | collective-permute-start | bytes 442376 | tf_op jit(solution)/shard_map/ppermute | solution.py:239
  29.6 7.1 %collective-permute-done.1 = bf16[64,1152]{1,0:T(8,128)(2,1)S(1)} collective-permute-done((bf16[64,1152]{1,0:T(8,128)(2,1)S(1)}, bf16[64,1152]{1,0:T(8,128)(2,1)S(1)}, u32[]{:S(2)}, u32[]{:S(2)}) %collective-permute-start.1) | collective-permute-done | bytes 147488 | tf_op jit(solution)/shard_map/ppermute | solution.py:239
  36.7 2.9 %collective-permute-done.2 = bf16[64,1152]{1,0:T(8,128)(2,1)S(1)} collective-permute-done((bf16[64,1152]{1,0:T(8,128)(2,1)S(1)}, bf16[64,1152]{1,0:T(8,128)(2,1)S(1)}, u32[]{:S(2)}, u32[]{:S(2)}) %collective-permute-start.2) | collective-permute-done | bytes 147488 | tf_op jit(solution)/shard_map/ppermute | solution.py:239
  40.4 3.4 %collective-permute-start.3 = (bf16[256,1152]{1,0:T(8,128)(2,1)S(1)}, bf16[256,1152]{1,0:T(8,128)(2,1)}, u32[]{:S(2)}, u32[]{:S(2)}) collective-permute-start(bf16[256,1152]{1,0:T(8,128)(2,1)S(1)} %bitcast.17), channel_id=1, source_target_pairs={{0,16},{16,32},{32,48},{48,0},{1,17},{17,33},{33,49},{49,1},{2,18}... | collective-permute-start | bytes 1769480 | tf_op jit(solution)/shard_map/ppermute | solution.py:239
  43.8 2.4 %collective-permute-start.4 = (bf16[256,1152]{1,0:T(8,128)(2,1)S(1)}, bf16[256,1152]{1,0:T(8,128)(2,1)}, u32[]{:S(2)}, u32[]{:S(2)}) collective-permute-start(bf16[256,1152]{1,0:T(8,128)(2,1)S(1)} %bitcast.18), channel_id=1, source_target_pairs={{0,48},{16,0},{32,16},{48,32},{1,49},{17,1},{33,17},{49,33},{2,50}... | collective-permute-start | bytes 1769480 | tf_op jit(solution)/shard_map/ppermute | solution.py:239
  46.3 1.9 %collective-permute-start.5 = (bf16[192,1152]{1,0:T(8,128)(2,1)}, bf16[192,1152]{1,0:T(8,128)(2,1)}, u32[]{:S(2)}, u32[]{:S(2)}) collective-permute-start(bf16[192,1152]{1,0:T(8,128)(2,1)} %pad_maximum_fusion.fetched_ref), channel_id=1, source_target_pairs={{0,1},{1,0},{2,3},{3,2},{4,5},{5,4},{6,7},{7,6},{8,9},{9,8},{10,11... | collective-permute-start | bytes 1327112 | tf_op jit(solution)/shard_map/ppermute | solution.py:277
  48.2 3.3 %copy.8 = bf16[1152,1152]{0,1:T(8,128)(2,1)} copy(bf16[1152,1152]{1,0:T(8,128)(2,1)S(1)} %copy-done) | data formatting | bytes 5308416 | tf_op args[1]
  51.6 1.7 %copy-done.2 = bf16[1152,1152]{0,1:T(8,128)(2,1)S(1)} copy-done((bf16[1152,1152]{0,1:T(8,128)(2,1)S(1)}, bf16[1152,1152]{0,1:T(8,128)(2,1)}, u32[]{:S(2)}) %copy-start.2) | copy-done | bytes 2654232
  53.3 1.0 copy-done.5
  54.3 1.0 copy-done.6
  55.3 3.4 %shard_map.77 = (f32[1152,512]{1,0:T(8,128)S(1)}, bf16[1152,512]{1,0:T(8,128)(2,1)S(1)}, f32[1,512]{1,0:T(1,128)S(1)}, f32[288,128]{1,0:T(8,128)S(1)}, f32[288,5...) custom-call(s32[12]{0:T(128)S(1)} %stack.48.at_ref, bf16[1152,1152]{1,0:T(8,128)(2,1)S(1)} %bitcast.16, ...), custom_call_target="tpu_custom_call" | custom-call | flops 1358954496 | bytes 3833904 | tf_op jit(solution)/shard_map/pallas_call | solution.py:24
  58.7 2.0 %collective-permute-done.4.right_ref = bf16[256,1152]{1,0:T(8,128)(2,1)} collective-permute-done((bf16[256,1152]{1,0:T(8,128)(2,1)S(1)}, bf16[256,1152]{1,0:T(8,128)(2,1)}, u32[]{:S(2)}, u32[]{:S(2)}) %collective-permute-start.4) | collective-permute-done | bytes 589856 | tf_op jit(solution)/shard_map/ppermute | solution.py:239
  60.8 1.0 slice.6
  61.8 3.1 %collective-permute-start.6 = (bf16[128,1152]{1,0:T(8,128)(2,1)S(1)}, bf16[128,1152]{1,0:T(8,128)(2,1)S(1)}, u32[]{:S(2)}, u32[]{:S(2)}) collective-permute-start(bf16[128,1152]{1,0:T(8,128)(2,1)S(1)} %slice.6), channel_id=1, source_target_pairs={{0,16},{16,32},{32,48},{48,0},{1,17},{17,33},{33,49},{49,1},{2,18}... | collective-permute-start | bytes 884744 | tf_op jit(solution)/shard_map/ppermute | solution.py:239
  64.9 1.0 slice.7
  65.9 2.7 %collective-permute-start.7 = (bf16[128,1152]{1,0:T(8,128)(2,1)S(1)}, bf16[128,1152]{1,0:T(8,128)(2,1)S(1)}, u32[]{:S(2)}, u32[]{:S(2)}) collective-permute-start(bf16[128,1152]{1,0:T(8,128)(2,1)S(1)} %slice.7), channel_id=1, source_target_pairs={{0,48},{16,0},{32,16},{48,32},{1,49},{17,1},{33,17},{49,33},{2,50}... | collective-permute-start | bytes 884744 | tf_op jit(solution)/shard_map/ppermute | solution.py:239
  70.0 5.2 %shard_map.78 = (f32[1152,512]{1,0:T(8,128)S(1)}, f32[1,512]{1,0:T(1,128)S(1)}) custom-call(s32[12]{0:T(128)S(1)} %stack.48.at_ref, f32[2]{0:T(128)S(1)} %pad_maximum_fusion.1.par_ref, bf16[256,1152]{1,0:T(8,128)(2,1)S(1)} %bitcast.19, bf16[256,1152]{1,0:T(8,128)(2,1)} %collective-permute-done.3.left_ref, ...), custom_call_target="tpu_custom_call" | custom-call | flops 1811939328 | bytes 2949176 | tf_op jit(solution)/shard_map/pallas_call | solution.py:24
  75.2 2.1 %shard_map.79 = (f32[592,512]{1,0:T(8,128)S(1)}, bf16[592,512]{1,0:T(8,128)(2,1)S(1)}) custom-call(s32[12]{0:T(128)S(1)} %stack.48.at_ref, f32[2]{0:T(128)S(1)} %pad_maximum_fusion.1.par_ref, bf16[128,1152]{1,0:T(8,128)(2,1)S(1)} %collective-permute-done.6.a_ref, bf16[128,1152]{1,0:T(8,128)(2,1)S(1)} %collective-permute-done.7.b_ref, ...), custom_call_target="tpu_custom_call" | custom-call | flops 603979776 | bytes 6490168 | tf_op jit(solution)/shard_map/pallas_call | solution.py:24
  77.3 1.9 %collective-permute-start.8 = (bf16[592,512]{1,0:T(8,128)(2,1)S(1)}, bf16[592,512]{1,0:T(8,128)(2,1)S(1)}, u32[]{:S(2)}, u32[]{:S(2)}) collective-permute-start(bf16[592,512]{1,0:T(8,128)(2,1)S(1)} %get-tuple-element.37), channel_id=1, source_target_pairs={{0,1},{1,0},{2,3},{3,2},{4,5},{5,4},{6,7},{7,6},{8,9},{9,8},{10,11... | collective-permute-start | bytes 1818632 | tf_op jit(solution)/shard_map/ppermute | solution.py:329
  79.2 2.0 %collective-permute-done.8.got_ref = bf16[592,512]{1,0:T(8,128)(2,1)S(1)} collective-permute-done((bf16[592,512]{1,0:T(8,128)(2,1)S(1)}, bf16[592,512]{1,0:T(8,128)(2,1)S(1)}, u32[]{:S(2)}, u32[]{:S(2)}) %collective-permute-start.8) | collective-permute-done | bytes 606240 | tf_op jit(solution)/shard_map/ppermute | solution.py:329
  81.9 1.9 %collective-permute-start.9 = (bf16[304,512]{1,0:T(8,128)(2,1)S(1)}, bf16[304,512]{1,0:T(8,128)(2,1)S(1)}, u32[]{:S(2)}, u32[]{:S(2)}) collective-permute-start(bf16[304,512]{1,0:T(8,128)(2,1)S(1)} %get-tuple-element.39), channel_id=1, source_target_pairs={{0,2},{2,0},{1,3},{3,1},{4,6},{6,4},{5,7},{7,5},{8,10},{10,8},{9,1... | collective-permute-start | bytes 933896 | tf_op jit(solution)/shard_map/ppermute | solution.py:338
  83.8 9.4 %collective-permute-done.9.got_ref = bf16[304,512]{1,0:T(8,128)(2,1)S(1)} collective-permute-done((bf16[304,512]{1,0:T(8,128)(2,1)S(1)}, bf16[304,512]{1,0:T(8,128)(2,1)S(1)}, u32[]{:S(2)}, u32[]{:S(2)}) %collective-permute-start.9) | collective-permute-done | bytes 311328 | tf_op jit(solution)/shard_map/ppermute | solution.py:338
  93.2 1.5 shard_map.81
  94.7 11.2 %all-to-all-start.1 = ((bf16[32,96,128]{2,1,0:T(8,128)(2,1)}), bf16[32,96,128]{2,1,0:T(8,128)(2,1)}, u32[]{:S(2)}, u32[]{:S(2)}) async-start(bf16[32,96,128]{2,1,0:T(8,128)(2,1)} %bitcast.12), calls=%async_computation.1 | async-start | bytes 1572864 | tf_op jit(solution)/shard_map/all_to_all | solution.py:48
  105.9 5.5 %collective-permute-start.10 = (bf16[304,128]{1,0:T(8,128)(2,1)S(1)}, bf16[304,128]{1,0:T(8,128)(2,1)S(1)}, u32[]{:S(2)}, u32[]{:S(2)}) collective-permute-start(bf16[304,128]{1,0:T(8,128)(2,1)S(1)} %get-tuple-element.46), channel_id=1, source_target_pairs={{0,12},{4,0},{8,4},{12,8},{1,13},{5,1},{9,5},{13,9},{2,14},{6,2},{... | collective-permute-start | bytes 233480 | tf_op jit(solution)/shard_map/ppermute | solution.py:239
  111.4 2.6 %collective-permute-start.11 = (bf16[304,128]{1,0:T(8,128)(2,1)S(1)}, bf16[304,128]{1,0:T(8,128)(2,1)S(1)}, u32[]{:S(2)}, u32[]{:S(2)}) collective-permute-start(bf16[304,128]{1,0:T(8,128)(2,1)S(1)} %get-tuple-element.47), channel_id=1, source_target_pairs={{0,8},{4,12},{8,0},{12,4},{1,9},{5,13},{9,1},{13,5},{2,10},{6,14},... | collective-permute-start | bytes 233480 | tf_op jit(solution)/shard_map/ppermute | solution.py:239
  113.9 4.4 %collective-permute-start.12 = (bf16[304,128]{1,0:T(8,128)(2,1)S(1)}, bf16[304,128]{1,0:T(8,128)(2,1)S(1)}, u32[]{:S(2)}, u32[]{:S(2)}) collective-permute-start(bf16[304,128]{1,0:T(8,128)(2,1)S(1)} %get-tuple-element.48), channel_id=1, source_target_pairs={{0,4},{4,8},{8,12},{12,0},{1,5},{5,9},{9,13},{13,1},{2,6},{6,10},{... | collective-permute-start | bytes 233480 | tf_op jit(solution)/shard_map/ppermute | solution.py:239
  118.4 3.6 %collective-permute-done.11.refs_2_ = bf16[304,128]{1,0:T(8,128)(2,1)S(1)} collective-permute-done((bf16[304,128]{1,0:T(8,128)(2,1)S(1)}, bf16[304,128]{1,0:T(8,128)(2,1)S(1)}, u32[]{:S(2)}, u32[]{:S(2)}) %collective-permute-start.11) | collective-permute-done | bytes 77856 | tf_op jit(solution)/shard_map/ppermute | solution.py:239
  122.0 1.5 collective-permute-done.12.refs_3_
  124.2 3.6 %all-to-all-done.1.parts_ref = bf16[32,96,128]{2,1,0:T(8,128)(2,1)} async-done(((bf16[32,96,128]{2,1,0:T(8,128)(2,1)}), bf16[32,96,128]{2,1,0:T(8,128)(2,1)}, u32[]{:S(2)}, u32[]{:S(2)}) %all-to-all-start.1) | async-done | bytes 786464 | tf_op jit(solution)/shard_map/all_to_all | solution.py:48
  127.9 2.0 %shard_map.83 = f32[4,96,128]{2,1,0:T(8,128)} custom-call(bf16[32,96,128]{2,1,0:T(8,128)(2,1)} %all-to-all-done.1.parts_ref, bf16[288,128]{1,0:T(8,128)(2,1)} %copy-done.3), custom_call_target="tpu_custom_call" | custom-call | tf_op jit(solution)/shard_map/pallas_call | solution.py:354
  129.9 14.3 %all_to_all.34.parts_ref = f32[4,96,128]{2,1,0:T(8,128)S(1)} all-to-all(f32[4,96,128]{2,1,0:T(8,128)} %shard_map.83), channel_id=1, replica_groups=mesh['y'=8,'x'=4,'zh'=4,'zl'=2,'c'=2] {'zh'}, dimensions={0} | all-to-all | bytes 393216 | tf_op jit(solution)/shard_map/all_to_all | solution.py:48
  144.8 0.9 copy-done.1
  145.7 6.8 %all-to-all-start.3 = ((bf16[32,96,128]{2,1,0:T(8,128)(2,1)}), bf16[32,96,128]{2,1,0:T(8,128)(2,1)S(1)}, u32[]{:S(2)}, u32[]{:S(2)}) async-start(bf16[32,96,128]{2,1,0:T(8,128)(2,1)} %copy-done.1), calls=%async_computation.3 | async-start | bytes 1572864 | tf_op jit(solution)/shard_map/all_to_all | solution.py:48
  152.5 1.9 %collective-permute-start.13 = (bf16[288,128]{1,0:T(8,128)(2,1)S(1)}, bf16[288,128]{1,0:T(8,128)(2,1)S(1)}, u32[]{:S(2)}, u32[]{:S(2)}) collective-permute-start(bf16[288,128]{1,0:T(8,128)(2,1)S(1)} %copy-done.4), channel_id=1, source_target_pairs={{0,1},{1,0},{2,3},{3,2},{4,5},{5,4},{6,7},{7,6},{8,9},{9,8},{10,11... | collective-permute-start | bytes 221192 | tf_op jit(solution)/shard_map/ppermute | solution.py:372
  154.4 3.4 %collective-permute-start.14 = (bf16[288,128]{1,0:T(8,128)(2,1)S(1)}, bf16[288,128]{1,0:T(8,128)(2,1)S(1)}, u32[]{:S(2)}, u32[]{:S(2)}) collective-permute-start(bf16[288,128]{1,0:T(8,128)(2,1)S(1)} %copy-done.4), channel_id=1, source_target_pairs={{0,2},{1,3},{2,0},{3,1},{4,6},{5,7},{6,4},{7,5},{8,10},{9,11},{10,... | collective-permute-start | bytes 221192 | tf_op jit(solution)/shard_map/ppermute | solution.py:372
  157.9 2.2 %collective-permute-start.15 = (bf16[288,128]{1,0:T(8,128)(2,1)S(1)}, bf16[288,128]{1,0:T(8,128)(2,1)S(1)}, u32[]{:S(2)}, u32[]{:S(2)}) collective-permute-start(bf16[288,128]{1,0:T(8,128)(2,1)S(1)} %copy-done.4), channel_id=1, source_target_pairs={{0,3},{1,2},{2,1},{3,0},{4,7},{5,6},{6,5},{7,4},{8,11},{9,10},{10,... | collective-permute-start | bytes 221192 | tf_op jit(solution)/shard_map/ppermute | solution.py:372
  160.1 0.9 collective-permute-done.14.refs_2_
  161.0 3.0 %collective-permute-done.15.refs_3_ = bf16[288,128]{1,0:T(8,128)(2,1)S(1)} collective-permute-done((bf16[288,128]{1,0:T(8,128)(2,1)S(1)}, bf16[288,128]{1,0:T(8,128)(2,1)S(1)}, u32[]{:S(2)}, u32[]{:S(2)}) %collective-permute-start.15) | collective-permute-done | bytes 73760 | tf_op jit(solution)/shard_map/ppermute | solution.py:372
  164.0 2.2 %shard_map.86 = bf16[128,1152]{1,0:T(8,128)(2,1)} custom-call(s32[12]{0:T(128)S(1)} %stack.48.at_ref, bf16[1152,1152]{1,0:T(8,128)(2,1)S(1)} %copy-done, bf16[288,128]{1,0:T(8,128)(2,1)S(1)} %copy-done.4, bf16[288,128]{1,0:T(8,128)(2,1)S(1)} %collective-permute-done.13.refs_1_, bf16[288,128]{1,0:T(8,128)(2,1)S(1)} %collective-permute-done.14.refs_2_, ...), custom_call_target="tpu_custom_call" | custom-call | flops 339738624 | bytes 2949168 | tf_op jit(solution)/shard_map/pallas_call | solution.py:24
  166.2 5.0 %all-to-all-done.3 = bf16[32,96,128]{2,1,0:T(8,128)(2,1)S(1)} async-done(((bf16[32,96,128]{2,1,0:T(8,128)(2,1)}), bf16[32,96,128]{2,1,0:T(8,128)(2,1)S(1)}, u32[]{:S(2)}, u32[]{:S(2)}) %all-to-all-start.3) | async-done | bytes 786464 | tf_op jit(solution)/shard_map/all_to_all | solution.py:48
  171.9 1.1 copy.9
  (26 shorter events, 3.6 us)
Async XLA Ops:
  0.6 47.6 %copy-start = (bf16[1152,1152]{1,0:T(8,128)(2,1)S(1)}, bf16[1152,1152]{1,0:T(8,128)(2,1)}, u32[]{:S(2)}) copy-start(bf16[1152,1152]{1,0:T(8,128)(2,1)} %weight_ref.1) | copy-start | bytes 7962628
  0.6 1.0 copy-start.7
  2.6 37.8 %all-to-all-start = ((bf16[8,32,1152]{2,1,0:T(8,128)(2,1)}), bf16[8,32,1152]{2,1,0:T(8,128)(2,1)S(1)}, u32[]{:S(2)}, u32[]{:S(2)}) async-start(bf16[8,32,1152]{2,1,0:T(8,128)(2,1)} %bitcast.9), calls=%async_computation | async-start | bytes 1179648 | tf_op jit(solution)/shard_map/all_to_all | solution.py:48
  10.7 18.9 %collective-permute-start = (bf16[64,1152]{1,0:T(8,128)(2,1)S(1)}, bf16[64,1152]{1,0:T(8,128)(2,1)S(1)}, u32[]{:S(2)}, u32[]{:S(2)}) collective-permute-start(bf16[64,1152]{1,0:T(8,128)(2,1)S(1)} %constant_dynamic-slice_fusion), channel_id=1, source_target_pairs={{0,4},{4,8},{8,12},{12,0},{1,5},{5,9},{9,13},{13,1},{2,6},{6,10},{... | collective-permute-start | bytes 442376 | tf_op jit(solution)/shard_map/ppermute | solution.py:239
  16.7 19.9 %collective-permute-start.1 = (bf16[64,1152]{1,0:T(8,128)(2,1)S(1)}, bf16[64,1152]{1,0:T(8,128)(2,1)S(1)}, u32[]{:S(2)}, u32[]{:S(2)}) collective-permute-start(bf16[64,1152]{1,0:T(8,128)(2,1)S(1)} %constant_dynamic-slice_fusion), channel_id=1, source_target_pairs={{0,8},{4,12},{8,0},{12,4},{1,9},{5,13},{9,1},{13,5},{2,10},{6,14},... | collective-permute-start | bytes 442376 | tf_op jit(solution)/shard_map/ppermute | solution.py:239
  25.9 13.7 %collective-permute-start.2 = (bf16[64,1152]{1,0:T(8,128)(2,1)S(1)}, bf16[64,1152]{1,0:T(8,128)(2,1)S(1)}, u32[]{:S(2)}, u32[]{:S(2)}) collective-permute-start(bf16[64,1152]{1,0:T(8,128)(2,1)S(1)} %constant_dynamic-slice_fusion), channel_id=1, source_target_pairs={{0,12},{4,0},{8,4},{12,8},{1,13},{5,1},{9,5},{13,9},{2,14},{6,2},{... | collective-permute-start | bytes 442376 | tf_op jit(solution)/shard_map/ppermute | solution.py:239
  40.4 18.3 %collective-permute-start.3 = (bf16[256,1152]{1,0:T(8,128)(2,1)S(1)}, bf16[256,1152]{1,0:T(8,128)(2,1)}, u32[]{:S(2)}, u32[]{:S(2)}) collective-permute-start(bf16[256,1152]{1,0:T(8,128)(2,1)S(1)} %bitcast.17), channel_id=1, source_target_pairs={{0,16},{16,32},{32,48},{48,0},{1,17},{17,33},{33,49},{49,1},{2,18}... | collective-permute-start | bytes 1769480 | tf_op jit(solution)/shard_map/ppermute | solution.py:239
  43.8 17.0 %collective-permute-start.4 = (bf16[256,1152]{1,0:T(8,128)(2,1)S(1)}, bf16[256,1152]{1,0:T(8,128)(2,1)}, u32[]{:S(2)}, u32[]{:S(2)}) collective-permute-start(bf16[256,1152]{1,0:T(8,128)(2,1)S(1)} %bitcast.18), channel_id=1, source_target_pairs={{0,48},{16,0},{32,16},{48,32},{1,49},{17,1},{33,17},{49,33},{2,50}... | collective-permute-start | bytes 1769480 | tf_op jit(solution)/shard_map/ppermute | solution.py:239
  46.3 5.3 %collective-permute-start.5 = (bf16[192,1152]{1,0:T(8,128)(2,1)}, bf16[192,1152]{1,0:T(8,128)(2,1)}, u32[]{:S(2)}, u32[]{:S(2)}) collective-permute-start(bf16[192,1152]{1,0:T(8,128)(2,1)} %pad_maximum_fusion.fetched_ref), channel_id=1, source_target_pairs={{0,1},{1,0},{2,3},{3,2},{4,5},{5,4},{6,7},{7,6},{8,9},{9,8},{10,11... | collective-permute-start | bytes 1327112 | tf_op jit(solution)/shard_map/ppermute | solution.py:277
  51.6 1.8 %copy-start.2 = (bf16[1152,1152]{0,1:T(8,128)(2,1)S(1)}, bf16[1152,1152]{0,1:T(8,128)(2,1)}, u32[]{:S(2)}) copy-start(bf16[1152,1152]{0,1:T(8,128)(2,1)} %copy.8) | copy-start | bytes 7962628
  53.3 1.0 copy-start.5
  54.3 1.0 copy-start.6
  61.8 13.4 %collective-permute-start.6 = (bf16[128,1152]{1,0:T(8,128)(2,1)S(1)}, bf16[128,1152]{1,0:T(8,128)(2,1)S(1)}, u32[]{:S(2)}, u32[]{:S(2)}) collective-permute-start(bf16[128,1152]{1,0:T(8,128)(2,1)S(1)} %slice.6), channel_id=1, source_target_pairs={{0,16},{16,32},{32,48},{48,0},{1,17},{17,33},{33,49},{49,1},{2,18}... | collective-permute-start | bytes 884744 | tf_op jit(solution)/shard_map/ppermute | solution.py:239
  65.9 9.4 %collective-permute-start.7 = (bf16[128,1152]{1,0:T(8,128)(2,1)S(1)}, bf16[128,1152]{1,0:T(8,128)(2,1)S(1)}, u32[]{:S(2)}, u32[]{:S(2)}) collective-permute-start(bf16[128,1152]{1,0:T(8,128)(2,1)S(1)} %slice.7), channel_id=1, source_target_pairs={{0,48},{16,0},{32,16},{48,32},{1,49},{17,1},{33,17},{49,33},{2,50}... | collective-permute-start | bytes 884744 | tf_op jit(solution)/shard_map/ppermute | solution.py:239
  77.3 3.9 %collective-permute-start.8 = (bf16[592,512]{1,0:T(8,128)(2,1)S(1)}, bf16[592,512]{1,0:T(8,128)(2,1)S(1)}, u32[]{:S(2)}, u32[]{:S(2)}) collective-permute-start(bf16[592,512]{1,0:T(8,128)(2,1)S(1)} %get-tuple-element.37), channel_id=1, source_target_pairs={{0,1},{1,0},{2,3},{3,2},{4,5},{5,4},{6,7},{7,6},{8,9},{9,8},{10,11... | collective-permute-start | bytes 1818632 | tf_op jit(solution)/shard_map/ppermute | solution.py:329
  81.9 11.3 %collective-permute-start.9 = (bf16[304,512]{1,0:T(8,128)(2,1)S(1)}, bf16[304,512]{1,0:T(8,128)(2,1)S(1)}, u32[]{:S(2)}, u32[]{:S(2)}) collective-permute-start(bf16[304,512]{1,0:T(8,128)(2,1)S(1)} %get-tuple-element.39), channel_id=1, source_target_pairs={{0,2},{2,0},{1,3},{3,1},{4,6},{6,4},{5,7},{7,5},{8,10},{10,8},{9,1... | collective-permute-start | bytes 933896 | tf_op jit(solution)/shard_map/ppermute | solution.py:338
  94.7 33.2 %all-to-all-start.1 = ((bf16[32,96,128]{2,1,0:T(8,128)(2,1)}), bf16[32,96,128]{2,1,0:T(8,128)(2,1)}, u32[]{:S(2)}, u32[]{:S(2)}) async-start(bf16[32,96,128]{2,1,0:T(8,128)(2,1)} %bitcast.12), calls=%async_computation.1 | async-start | bytes 1572864 | tf_op jit(solution)/shard_map/all_to_all | solution.py:48
  105.9 12.5 %collective-permute-start.10 = (bf16[304,128]{1,0:T(8,128)(2,1)S(1)}, bf16[304,128]{1,0:T(8,128)(2,1)S(1)}, u32[]{:S(2)}, u32[]{:S(2)}) collective-permute-start(bf16[304,128]{1,0:T(8,128)(2,1)S(1)} %get-tuple-element.46), channel_id=1, source_target_pairs={{0,12},{4,0},{8,4},{12,8},{1,13},{5,1},{9,5},{13,9},{2,14},{6,2},{... | collective-permute-start | bytes 233480 | tf_op jit(solution)/shard_map/ppermute | solution.py:239
  111.4 10.6 %collective-permute-start.11 = (bf16[304,128]{1,0:T(8,128)(2,1)S(1)}, bf16[304,128]{1,0:T(8,128)(2,1)S(1)}, u32[]{:S(2)}, u32[]{:S(2)}) collective-permute-start(bf16[304,128]{1,0:T(8,128)(2,1)S(1)} %get-tuple-element.47), channel_id=1, source_target_pairs={{0,8},{4,12},{8,0},{12,4},{1,9},{5,13},{9,1},{13,5},{2,10},{6,14},... | collective-permute-start | bytes 233480 | tf_op jit(solution)/shard_map/ppermute | solution.py:239
  113.9 9.6 %collective-permute-start.12 = (bf16[304,128]{1,0:T(8,128)(2,1)S(1)}, bf16[304,128]{1,0:T(8,128)(2,1)S(1)}, u32[]{:S(2)}, u32[]{:S(2)}) collective-permute-start(bf16[304,128]{1,0:T(8,128)(2,1)S(1)} %get-tuple-element.48), channel_id=1, source_target_pairs={{0,4},{4,8},{8,12},{12,0},{1,5},{5,9},{9,13},{13,1},{2,6},{6,10},{... | collective-permute-start | bytes 233480 | tf_op jit(solution)/shard_map/ppermute | solution.py:239
  123.6 0.6 copy-start.3
  127.9 24.6 %copy-start.4 = (bf16[288,128]{1,0:T(8,128)(2,1)S(1)}, bf16[288,128]{1,0:T(8,128)(2,1)}, u32[]{:S(2)}) copy-start(bf16[288,128]{1,0:T(8,128)(2,1)} %copy-done.3) | copy-start | bytes 221188
  144.8 0.9 copy-start.1
  145.7 25.6 %all-to-all-start.3 = ((bf16[32,96,128]{2,1,0:T(8,128)(2,1)}), bf16[32,96,128]{2,1,0:T(8,128)(2,1)S(1)}, u32[]{:S(2)}, u32[]{:S(2)}) async-start(bf16[32,96,128]{2,1,0:T(8,128)(2,1)} %copy-done.1), calls=%async_computation.3 | async-start | bytes 1572864 | tf_op jit(solution)/shard_map/all_to_all | solution.py:48
  152.5 7.6 %collective-permute-start.13 = (bf16[288,128]{1,0:T(8,128)(2,1)S(1)}, bf16[288,128]{1,0:T(8,128)(2,1)S(1)}, u32[]{:S(2)}, u32[]{:S(2)}) collective-permute-start(bf16[288,128]{1,0:T(8,128)(2,1)S(1)} %copy-done.4), channel_id=1, source_target_pairs={{0,1},{1,0},{2,3},{3,2},{4,5},{5,4},{6,7},{7,6},{8,9},{9,8},{10,11... | collective-permute-start | bytes 221192 | tf_op jit(solution)/shard_map/ppermute | solution.py:372
  154.4 6.6 %collective-permute-start.14 = (bf16[288,128]{1,0:T(8,128)(2,1)S(1)}, bf16[288,128]{1,0:T(8,128)(2,1)S(1)}, u32[]{:S(2)}, u32[]{:S(2)}) collective-permute-start(bf16[288,128]{1,0:T(8,128)(2,1)S(1)} %copy-done.4), channel_id=1, source_target_pairs={{0,2},{1,3},{2,0},{3,1},{4,6},{5,7},{6,4},{7,5},{8,10},{9,11},{10,... | collective-permute-start | bytes 221192 | tf_op jit(solution)/shard_map/ppermute | solution.py:372
  157.9 6.1 %collective-permute-start.15 = (bf16[288,128]{1,0:T(8,128)(2,1)S(1)}, bf16[288,128]{1,0:T(8,128)(2,1)S(1)}, u32[]{:S(2)}, u32[]{:S(2)}) collective-permute-start(bf16[288,128]{1,0:T(8,128)(2,1)S(1)} %copy-done.4), channel_id=1, source_target_pairs={{0,3},{1,2},{2,1},{3,0},{4,7},{5,6},{6,5},{7,4},{8,11},{9,10},{10,... | collective-permute-start | bytes 221192 | tf_op jit(solution)/shard_map/ppermute | solution.py:372

commit v5 on v4

--- a/solution.py
+++ b/solution.py
@@ -63,11 +63,9 @@
     part = rows // 2
     c = at_ref[5]
     feats_ref[:rows] = own_ref[...]
-    for k in range(fetched_ref.shape[0] // part):
-        base = (k + 1) * rows
-        block = pl.ds(k * part, part)
-        feats_ref[pl.ds(pl.multiple_of(base + c * part, 16), part), :] = fetched_ref[block, :]
-        feats_ref[pl.ds(pl.multiple_of(base + (1 - c) * part, 16), part), :] = swapped_ref[block, :]
+    for k, ref in ((c, fetched_ref), (1 - c, swapped_ref)):
+        feats_ref[pl.ds(pl.multiple_of((1 + 2 * k) * rows, 16), rows), :] = ref[:rows]
+        feats_ref[pl.ds(pl.multiple_of(2 * rows + k * part, 16), part), :] = ref[rows:]
     head = lax.dot_general(
         wt_ref[...], feats_ref[...], (((1,), (1,)), ((), ())), preferred_element_type=F32
     )
@@ -113,9 +111,9 @@
     loss_ref[...] = loss
 
 
-def second_kernel(at_ref, par_ref, a_ref, b_ref, low_ref, unit_ref, acc_ref, loss_ref, keep_ref, send_ref, sum_ref):
+def second_kernel(at_ref, par_ref, far_ref, low_ref, unit_ref, acc_ref, loss_ref, keep_ref, send_ref, sum_ref):
     scale = par_ref[0]
-    texts = jnp.concatenate([a_ref[...], b_ref[...]], axis=0)
+    texts = far_ref[...]
     slope, loss = pairs(par_ref, texts, low_ref)
     loss = loss_ref[...] + loss
     total = scale * (acc_ref[...] + turn(texts, slope))
@@ -270,13 +268,18 @@
 
     copies = call(text_kernel, shape((ny * quarter, width), BF16), text_embed)
     part = rows // nc
+    near = [(z * nc + c, (z + 1 - 2 * c) % nzh * nc + c) for z in range(nzh) for c in range(nc)]
     half_rows = lax.dynamic_slice_in_dim(img_feat, c_at * part, part, 0)
-    fetched = jnp.concatenate([shift_by(half_rows, "zh", s) for s in range(1, nzh)], axis=0)
+    fetched = jnp.concatenate(
+        [lax.ppermute(img_feat, ("zh", "c"), near), shift_by(half_rows, "zh", 2)], axis=0
+    )
     own = to_all(copies, "y")
     own, fetched = lax.optimization_barrier((own, fetched))
-    swapped = lax.ppermute(fetched, "c", [(0, 1), (1, 0)])
+    far = shift_by(own, "x", 2)
     left = shift_by(own, "x", 1)
     right = shift_by(own, "x", -1)
+    swapped = lax.ppermute(fetched, "c", [(0, 1), (1, 0)])
+
     unit, low, inv, own_unit, col_unit, feats = call(
         image_kernel,
         [
@@ -295,10 +298,6 @@
         smem=1,
         flops=2 * width * width * images,
     )
-    left, right, low = lax.optimization_barrier((left, right, low))
-    half = own.shape[0] // 2
-    far_a = shift_by(left[:half], "x", 1)
-    far_b = shift_by(right[half:], "x", -1)
     acc, loss_row = call(
         first_kernel,
         [shape((width, images), F32), shape((1, images), F32)],
@@ -316,8 +315,7 @@
         [shape((2 * cols + EXTRA, images), F32), shape((2 * cols + EXTRA, images), BF16)],
         at,
         par,
-        far_a,
-        far_b,
+        far,
         low,
         unit,
         acc,

time: 174 us -> 171 us (0.983)
  local copies, waits for them, and re-layouts: 13.7 us -> 10.7 us
  starting transfers between devices: 81.5 us -> 79.7 us
    ppermute x10 -> x7, starting transfers between devices: 43 us -> 30.3 us  [shift_by(): return lax.ppermute(x, axis, [(k, (k + step) % n) for k in range(n)])]
    ppermute x0 -> x1, starting transfers between devices: none -> 6.08 us  [local(): lax.ppermute(img_feat, ('zh', 'c'), near)]
    ppermute x10 -> x7, waiting for transfers between devices: 17.3 us -> 20.7 us  [shift_by(): return lax.ppermute(x, axis, [(k, (k + step) % n) for k in range(n)])]
    all_to_all x3, starting transfers between devices: 25.1 us -> 28.4 us  [to_all(): return lax.all_to_all(copies, axes, 0, 0, tiled=True)]
    slice x2 -> x0, local copies, waits for them, and re-layouts: 1.97 us -> none  [the longest x1 0.99 us: local(): far_b = shift_by(right[half:], 'x', -1)]
    unnamed x18 -> x16, local copies, waits for them, and re-layouts: 10.7 us -> 9.7 us
  transfers between devices with their start and end apart: 19 -> 17, of which waited for: 11 -> 9; matrix products, arithmetic and copies ran while one was open for 4% -> 3% of each run, Pallas kernels for 6% -> 7%
where the time goes in v5:
time: 171 us; the launch traced here: 169 us
  starting transfers between devices  79.7 us (47%)
  waiting for transfers between devices  42.6 us (25%)
  Pallas kernels  19.6 us (11%)
  blocking collectives  13.7 us (8%)
  local copies, waits for them, and re-layouts  10.7 us (6%)
  between operations  2.26 us (1%)
    ppermute x7, starting transfers between devices, shift_by(): return lax.ppermute(x, axis, [(k, (k + step) % n) for k in range(n)])  30.3 us
    all_to_all x3, starting transfers between devices, to_all(): return lax.all_to_all(copies, axes, 0, 0, tiled=True)  28.4 us
    ppermute x7, waiting for transfers between devices, shift_by(): return lax.ppermute(x, axis, [(k, (k + step) % n) for k in range(n)])  20.7 us
    pallas_call x10, Pallas kernels, call(): pl.pallas_call(body, out_shape=outs, in_specs=specs, out_specs=[VMEM] * l...  17.6 us
    all_to_all x1, blocking collectives, to_all(): return lax.all_to_all(copies, axes, 0, 0, tiled=True)  13.7 us
    unnamed x16, local copies, waits for them, and re-layouts  9.7 us
    all_to_all x3, waiting for transfers between devices, to_all(): return lax.all_to_all(copies, axes, 0, 0, tiled=True)  8.6 us
    ppermute x1, waiting for transfers between devices, local(): got2 = lax.ppermute(send2, 'zl', [(0, 1), (1, 0)])  7.74 us
  transfers between devices with their start and end apart: 17, of which 9 were waited for; matrix products, arithmetic and copies ran while one was open for 3% of the time, Pallas kernels for 7%

profile of v5, /device:TPU:2, one launch (start us, length us, event | category | flops | bytes accessed | tf_op | source)
XLA Modules:
  0.0 169.5 jit_solution(9835318413497179497)
XLA Ops:
  0.7 1.0 copy-done.6
  1.7 1.0 shard_map.76
  2.6 7.1 %all-to-all-start = ((bf16[8,32,1152]{2,1,0:T(8,128)(2,1)}), bf16[8,32,1152]{2,1,0:T(8,128)(2,1)}, u32[]{:S(2)}, u32[]{:S(2)}) async-start(bf16[8,32,1152]{2,1,0:T(8,128)(2,1)} %bitcast.9), calls=%async_computation | async-start | bytes 1179648 | tf_op jit(solution)/shard_map/all_to_all | solution.py:48
  9.7 6.1 %collective-permute-start = (bf16[128,1152]{1,0:T(8,128)(2,1)}, bf16[128,1152]{1,0:T(8,128)(2,1)S(1)}, u32[]{:S(2)}, u32[]{:S(2)}) collective-permute-start(bf16[128,1152]{1,0:T(8,128)(2,1)} %own_ref.1), channel_id=1, source_target_pairs={{0,4},{1,13},{4,8},{5,1},{8,12},{9,5},{12,0},{13,9},{2,6},{3,15},{... | collective-permute-start | bytes 884744 | tf_op jit(solution)/shard_map/ppermute | solution.py:274
  15.8 0.9 constant_dynamic-slice_fusion
  16.8 9.1 %collective-permute-start.1 = (bf16[64,1152]{1,0:T(8,128)(2,1)S(1)}, bf16[64,1152]{1,0:T(8,128)(2,1)S(1)}, u32[]{:S(2)}, u32[]{:S(2)}) collective-permute-start(bf16[64,1152]{1,0:T(8,128)(2,1)S(1)} %constant_dynamic-slice_fusion), channel_id=1, source_target_pairs={{0,8},{4,12},{8,0},{12,4},{1,9},{5,13},{9,1},{13,5},{2,10},{6,14},... | collective-permute-start | bytes 442376 | tf_op jit(solution)/shard_map/ppermute | solution.py:237
  25.9 9.8 %collective-permute-done.1 = bf16[64,1152]{1,0:T(8,128)(2,1)S(1)} collective-permute-done((bf16[64,1152]{1,0:T(8,128)(2,1)S(1)}, bf16[64,1152]{1,0:T(8,128)(2,1)S(1)}, u32[]{:S(2)}, u32[]{:S(2)}) %collective-permute-start.1) | collective-permute-done | bytes 147488 | tf_op jit(solution)/shard_map/ppermute | solution.py:237
  35.7 0.8 pad_maximum_fusion.fetched_ref
  36.5 3.4 %collective-permute-start.4 = (bf16[256,1152]{1,0:T(8,128)(2,1)}, bf16[256,1152]{1,0:T(8,128)(2,1)}, u32[]{:S(2)}, u32[]{:S(2)}) collective-permute-start(bf16[256,1152]{1,0:T(8,128)(2,1)} %bitcast.10.own_ref), channel_id=1, source_target_pairs={{0,16},{16,32},{32,48},{48,0},{1,17},{17,33},{33,49},{49,1},{2,18}... | collective-permute-start | bytes 1769480 | tf_op jit(solution)/shard_map/ppermute | solution.py:237
  39.9 2.4 %collective-permute-start.5 = (bf16[256,1152]{1,0:T(8,128)(2,1)}, bf16[256,1152]{1,0:T(8,128)(2,1)}, u32[]{:S(2)}, u32[]{:S(2)}) collective-permute-start(bf16[256,1152]{1,0:T(8,128)(2,1)} %bitcast.10.own_ref), channel_id=1, source_target_pairs={{0,48},{16,0},{32,16},{48,32},{1,49},{17,1},{33,17},{49,33},{2,50}... | collective-permute-start | bytes 1769480 | tf_op jit(solution)/shard_map/ppermute | solution.py:237
  42.3 1.9 %collective-permute-start.3 = (bf16[192,1152]{1,0:T(8,128)(2,1)}, bf16[192,1152]{1,0:T(8,128)(2,1)}, u32[]{:S(2)}, u32[]{:S(2)}) collective-permute-start(bf16[192,1152]{1,0:T(8,128)(2,1)} %pad_maximum_fusion.fetched_ref), channel_id=1, source_target_pairs={{0,1},{1,0},{2,3},{3,2},{4,5},{5,4},{6,7},{7,6},{8,9},{9,8},{10,11... | collective-permute-start | bytes 1327112 | tf_op jit(solution)/shard_map/ppermute | solution.py:281
  44.3 4.0 %collective-permute-start.2 = (bf16[256,1152]{1,0:T(8,128)(2,1)}, bf16[256,1152]{1,0:T(8,128)(2,1)S(1)}, u32[]{:S(2)}, u32[]{:S(2)}) collective-permute-start(bf16[256,1152]{1,0:T(8,128)(2,1)} %bitcast.10.own_ref), channel_id=1, source_target_pairs={{0,32},{16,48},{32,0},{48,16},{1,33},{17,49},{33,1},{49,17},{2,34}... | collective-permute-start | bytes 1769480 | tf_op jit(solution)/shard_map/ppermute | solution.py:237
  48.3 3.3 %copy.8 = bf16[1152,1152]{0,1:T(8,128)(2,1)} copy(bf16[1152,1152]{1,0:T(8,128)(2,1)S(1)} %copy-done) | data formatting | bytes 5308416 | tf_op args[1]
  53.0 0.1 stack.48.at_ref
  53.0 0.1 pad_maximum_fusion.1.par_ref
  53.1 1.8 %copy-done.2 = bf16[1152,1152]{0,1:T(8,128)(2,1)S(1)} copy-done((bf16[1152,1152]{0,1:T(8,128)(2,1)S(1)}, bf16[1152,1152]{0,1:T(8,128)(2,1)}, u32[]{:S(2)}) %copy-start.2) | copy-done | bytes 2654232
  54.9 1.0 copy-done.5
  55.8 3.6 %shard_map.77 = (f32[1152,512]{1,0:T(8,128)S(1)}, bf16[1152,512]{1,0:T(8,128)(2,1)S(1)}, f32[1,512]{1,0:T(1,128)S(1)}, f32[288,128]{1,0:T(8,128)S(1)}, f32[288,5...) custom-call(s32[12]{0:T(128)S(1)} %stack.48.at_ref, bf16[1152,1152]{1,0:T(8,128)(2,1)S(1)} %bitcast.16, ...), custom_call_target="tpu_custom_call" | custom-call | flops 1358954496 | bytes 3833904 | tf_op jit(solution)/shard_map/pallas_call | solution.py:24
  59.4 5.4 %shard_map.78 = (f32[1152,512]{1,0:T(8,128)S(1)}, f32[1,512]{1,0:T(1,128)S(1)}) custom-call(s32[12]{0:T(128)S(1)} %stack.48.at_ref, f32[2]{0:T(128)S(1)} %pad_maximum_fusion.1.par_ref, bf16[256,1152]{1,0:T(8,128)(2,1)} %bitcast.10.own_ref, bf16[256,1152]{1,0:T(8,128)(2,1)} %collective-permute-done.4.left_ref, ...), custom_call_target="tpu_custom_call" | custom-call | flops 1811939328 | bytes 2949176 | tf_op jit(solution)/shard_map/pallas_call | solution.py:24
  64.8 4.1 %collective-permute-done.2.far_ref = bf16[256,1152]{1,0:T(8,128)(2,1)S(1)} collective-permute-done((bf16[256,1152]{1,0:T(8,128)(2,1)}, bf16[256,1152]{1,0:T(8,128)(2,1)S(1)}, u32[]{:S(2)}, u32[]{:S(2)}) %collective-permute-start.2) | collective-permute-done | bytes 589856 | tf_op jit(solution)/shard_map/ppermute | solution.py:237
  68.9 2.1 %shard_map.79 = (f32[592,512]{1,0:T(8,128)S(1)}, bf16[592,512]{1,0:T(8,128)(2,1)S(1)}) custom-call(s32[12]{0:T(128)S(1)} %stack.48.at_ref, f32[2]{0:T(128)S(1)} %pad_maximum_fusion.1.par_ref, bf16[256,1152]{1,0:T(8,128)(2,1)S(1)} %collective-permute-done.2.far_ref, bf16[1152,512]{1,0:T(8,128)(2,1)S(1)} %get-tuple-element.26.low_ref, ...), custom_call_target="tpu_custom_call" | custom-call | flops 603979776 | bytes 6490168 | tf_op jit(solution)/shard_map/pallas_call | solution.py:24
  71.0 1.9 %collective-permute-start.6 = (bf16[592,512]{1,0:T(8,128)(2,1)S(1)}, bf16[592,512]{1,0:T(8,128)(2,1)S(1)}, u32[]{:S(2)}, u32[]{:S(2)}) collective-permute-start(bf16[592,512]{1,0:T(8,128)(2,1)S(1)} %get-tuple-element.31), channel_id=1, source_target_pairs={{0,1},{1,0},{2,3},{3,2},{4,5},{5,4},{6,7},{7,6},{8,9},{9,8},{10,11... | collective-permute-start | bytes 1818632 | tf_op jit(solution)/shard_map/ppermute | solution.py:327
  72.9 2.0 %collective-permute-done.6.got_ref = bf16[592,512]{1,0:T(8,128)(2,1)S(1)} collective-permute-done((bf16[592,512]{1,0:T(8,128)(2,1)S(1)}, bf16[592,512]{1,0:T(8,128)(2,1)S(1)}, u32[]{:S(2)}, u32[]{:S(2)}) %collective-permute-start.6) | collective-permute-done | bytes 606240 | tf_op jit(solution)/shard_map/ppermute | solution.py:327
  74.9 0.7 shard_map.80
  75.6 3.5 %collective-permute-start.7 = (bf16[304,512]{1,0:T(8,128)(2,1)S(1)}, bf16[304,512]{1,0:T(8,128)(2,1)S(1)}, u32[]{:S(2)}, u32[]{:S(2)}) collective-permute-start(bf16[304,512]{1,0:T(8,128)(2,1)S(1)} %get-tuple-element.33), channel_id=1, source_target_pairs={{0,2},{2,0},{1,3},{3,1},{4,6},{6,4},{5,7},{7,5},{8,10},{10,8},{9,1... | collective-permute-start | bytes 933896 | tf_op jit(solution)/shard_map/ppermute | solution.py:336
  79.1 7.7 %collective-permute-done.7.got_ref = bf16[304,512]{1,0:T(8,128)(2,1)S(1)} collective-permute-done((bf16[304,512]{1,0:T(8,128)(2,1)S(1)}, bf16[304,512]{1,0:T(8,128)(2,1)S(1)}, u32[]{:S(2)}, u32[]{:S(2)}) %collective-permute-start.7) | collective-permute-done | bytes 311328 | tf_op jit(solution)/shard_map/ppermute | solution.py:336
  86.9 1.5 shard_map.81
  88.4 15.2 %all-to-all-start.1 = ((bf16[32,96,128]{2,1,0:T(8,128)(2,1)}), bf16[32,96,128]{2,1,0:T(8,128)(2,1)}, u32[]{:S(2)}, u32[]{:S(2)}) async-start(bf16[32,96,128]{2,1,0:T(8,128)(2,1)} %bitcast.12), calls=%async_computation.1 | async-start | bytes 1572864 | tf_op jit(solution)/shard_map/all_to_all | solution.py:48
  103.7 1.9 %collective-permute-start.10 = (bf16[304,128]{1,0:T(8,128)(2,1)S(1)}, bf16[304,128]{1,0:T(8,128)(2,1)S(1)}, u32[]{:S(2)}, u32[]{:S(2)}) collective-permute-start(bf16[304,128]{1,0:T(8,128)(2,1)S(1)} %get-tuple-element.42), channel_id=1, source_target_pairs={{0,4},{4,8},{8,12},{12,0},{1,5},{5,9},{9,13},{13,1},{2,6},{6,10},{... | collective-permute-start | bytes 233480 | tf_op jit(solution)/shard_map/ppermute | solution.py:237
  105.6 6.0 %collective-permute-start.8 = (bf16[304,128]{1,0:T(8,128)(2,1)S(1)}, bf16[304,128]{1,0:T(8,128)(2,1)S(1)}, u32[]{:S(2)}, u32[]{:S(2)}) collective-permute-start(bf16[304,128]{1,0:T(8,128)(2,1)S(1)} %get-tuple-element.40), channel_id=1, source_target_pairs={{0,12},{4,0},{8,4},{12,8},{1,13},{5,1},{9,5},{13,9},{2,14},{6,2},{... | collective-permute-start | bytes 233480 | tf_op jit(solution)/shard_map/ppermute | solution.py:237
  111.6 3.3 %collective-permute-start.9 = (bf16[304,128]{1,0:T(8,128)(2,1)S(1)}, bf16[304,128]{1,0:T(8,128)(2,1)S(1)}, u32[]{:S(2)}, u32[]{:S(2)}) collective-permute-start(bf16[304,128]{1,0:T(8,128)(2,1)S(1)} %get-tuple-element.41), channel_id=1, source_target_pairs={{0,8},{4,12},{8,0},{12,4},{1,9},{5,13},{9,1},{13,5},{2,10},{6,14},... | collective-permute-start | bytes 233480 | tf_op jit(solution)/shard_map/ppermute | solution.py:237
  115.0 6.8 %collective-permute-done.9.refs_2_ = bf16[304,128]{1,0:T(8,128)(2,1)S(1)} collective-permute-done((bf16[304,128]{1,0:T(8,128)(2,1)S(1)}, bf16[304,128]{1,0:T(8,128)(2,1)S(1)}, u32[]{:S(2)}, u32[]{:S(2)}) %collective-permute-start.9) | collective-permute-done | bytes 77856 | tf_op jit(solution)/shard_map/ppermute | solution.py:237
  121.9 0.6 copy-done.3
  122.5 3.1 %all-to-all-done.1.parts_ref = bf16[32,96,128]{2,1,0:T(8,128)(2,1)} async-done(((bf16[32,96,128]{2,1,0:T(8,128)(2,1)}), bf16[32,96,128]{2,1,0:T(8,128)(2,1)}, u32[]{:S(2)}, u32[]{:S(2)}) %all-to-all-start.1) | async-done | bytes 786464 | tf_op jit(solution)/shard_map/all_to_all | solution.py:48
  125.7 2.0 %shard_map.83 = f32[4,96,128]{2,1,0:T(8,128)} custom-call(bf16[32,96,128]{2,1,0:T(8,128)(2,1)} %all-to-all-done.1.parts_ref, bf16[288,128]{1,0:T(8,128)(2,1)} %copy-done.3), custom_call_target="tpu_custom_call" | custom-call | tf_op jit(solution)/shard_map/pallas_call | solution.py:352
  127.6 13.7 %all_to_all.34.parts_ref = f32[4,96,128]{2,1,0:T(8,128)S(1)} all-to-all(f32[4,96,128]{2,1,0:T(8,128)} %shard_map.83), channel_id=1, replica_groups=mesh['y'=8,'x'=4,'zh'=4,'zl'=2,'c'=2] {'zh'}, dimensions={0} | all-to-all | bytes 393216 | tf_op jit(solution)/shard_map/all_to_all | solution.py:48
  141.3 0.6 shard_map.84
  141.9 0.9 copy-done.1
  142.8 6.1 %all-to-all-start.3 = ((bf16[32,96,128]{2,1,0:T(8,128)(2,1)}), bf16[32,96,128]{2,1,0:T(8,128)(2,1)S(1)}, u32[]{:S(2)}, u32[]{:S(2)}) async-start(bf16[32,96,128]{2,1,0:T(8,128)(2,1)} %copy-done.1), calls=%async_computation.3 | async-start | bytes 1572864 | tf_op jit(solution)/shard_map/all_to_all | solution.py:48
  148.9 1.9 %collective-permute-start.11 = (bf16[288,128]{1,0:T(8,128)(2,1)S(1)}, bf16[288,128]{1,0:T(8,128)(2,1)S(1)}, u32[]{:S(2)}, u32[]{:S(2)}) collective-permute-start(bf16[288,128]{1,0:T(8,128)(2,1)S(1)} %copy-done.4), channel_id=1, source_target_pairs={{0,1},{1,0},{2,3},{3,2},{4,5},{5,4},{6,7},{7,6},{8,9},{9,8},{10,11... | collective-permute-start | bytes 221192 | tf_op jit(solution)/shard_map/ppermute | solution.py:370
  150.9 3.1 %collective-permute-start.12 = (bf16[288,128]{1,0:T(8,128)(2,1)S(1)}, bf16[288,128]{1,0:T(8,128)(2,1)S(1)}, u32[]{:S(2)}, u32[]{:S(2)}) collective-permute-start(bf16[288,128]{1,0:T(8,128)(2,1)S(1)} %copy-done.4), channel_id=1, source_target_pairs={{0,2},{1,3},{2,0},{3,1},{4,6},{5,7},{6,4},{7,5},{8,10},{9,11},{10,... | collective-permute-start | bytes 221192 | tf_op jit(solution)/shard_map/ppermute | solution.py:370
  154.0 2.6 %collective-permute-start.13 = (bf16[288,128]{1,0:T(8,128)(2,1)S(1)}, bf16[288,128]{1,0:T(8,128)(2,1)S(1)}, u32[]{:S(2)}, u32[]{:S(2)}) collective-permute-start(bf16[288,128]{1,0:T(8,128)(2,1)S(1)} %copy-done.4), channel_id=1, source_target_pairs={{0,3},{1,2},{2,1},{3,0},{4,7},{5,6},{6,5},{7,4},{8,11},{9,10},{10,... | collective-permute-start | bytes 221192 | tf_op jit(solution)/shard_map/ppermute | solution.py:370
  156.5 0.9 collective-permute-done.12.refs_2_
  157.4 2.7 %collective-permute-done.13.refs_3_ = bf16[288,128]{1,0:T(8,128)(2,1)S(1)} collective-permute-done((bf16[288,128]{1,0:T(8,128)(2,1)S(1)}, bf16[288,128]{1,0:T(8,128)(2,1)S(1)}, u32[]{:S(2)}, u32[]{:S(2)}) %collective-permute-start.13) | collective-permute-done | bytes 73760 | tf_op jit(solution)/shard_map/ppermute | solution.py:370
  160.1 2.2 %shard_map.86 = bf16[128,1152]{1,0:T(8,128)(2,1)} custom-call(s32[12]{0:T(128)S(1)} %stack.48.at_ref, bf16[1152,1152]{1,0:T(8,128)(2,1)S(1)} %copy-done, bf16[288,128]{1,0:T(8,128)(2,1)S(1)} %copy-done.4, bf16[288,128]{1,0:T(8,128)(2,1)S(1)} %collective-permute-done.11.refs_1_, bf16[288,128]{1,0:T(8,128)(2,1)S(1)} %collective-permute-done.12.refs_2_, ...), custom_call_target="tpu_custom_call" | custom-call | flops 339738624 | bytes 2949168 | tf_op jit(solution)/shard_map/pallas_call | solution.py:24
  162.3 5.5 %all-to-all-done.3 = bf16[32,96,128]{2,1,0:T(8,128)(2,1)S(1)} async-done(((bf16[32,96,128]{2,1,0:T(8,128)(2,1)}), bf16[32,96,128]{2,1,0:T(8,128)(2,1)S(1)}, u32[]{:S(2)}, u32[]{:S(2)}) %all-to-all-start.3) | async-done | bytes 786464 | tf_op jit(solution)/shard_map/all_to_all | solution.py:48
  167.8 0.6 shard_map.85
  168.4 1.1 copy.9
  (18 shorter events, 0.1 us)
Async XLA Ops:
  0.6 47.7 %copy-start = (bf16[1152,1152]{1,0:T(8,128)(2,1)S(1)}, bf16[1152,1152]{1,0:T(8,128)(2,1)}, u32[]{:S(2)}) copy-start(bf16[1152,1152]{1,0:T(8,128)(2,1)} %weight_ref.1) | copy-start | bytes 7962628
  0.6 1.0 copy-start.6
  2.6 33.8 %all-to-all-start = ((bf16[8,32,1152]{2,1,0:T(8,128)(2,1)}), bf16[8,32,1152]{2,1,0:T(8,128)(2,1)}, u32[]{:S(2)}, u32[]{:S(2)}) async-start(bf16[8,32,1152]{2,1,0:T(8,128)(2,1)} %bitcast.9), calls=%async_computation | async-start | bytes 1179648 | tf_op jit(solution)/shard_map/all_to_all | solution.py:48
  9.7 26.0 %collective-permute-start = (bf16[128,1152]{1,0:T(8,128)(2,1)}, bf16[128,1152]{1,0:T(8,128)(2,1)S(1)}, u32[]{:S(2)}, u32[]{:S(2)}) collective-permute-start(bf16[128,1152]{1,0:T(8,128)(2,1)} %own_ref.1), channel_id=1, source_target_pairs={{0,4},{1,13},{4,8},{5,1},{8,12},{9,5},{12,0},{13,9},{2,6},{3,15},{... | collective-permute-start | bytes 884744 | tf_op jit(solution)/shard_map/ppermute | solution.py:274
  16.8 18.9 %collective-permute-start.1 = (bf16[64,1152]{1,0:T(8,128)(2,1)S(1)}, bf16[64,1152]{1,0:T(8,128)(2,1)S(1)}, u32[]{:S(2)}, u32[]{:S(2)}) collective-permute-start(bf16[64,1152]{1,0:T(8,128)(2,1)S(1)} %constant_dynamic-slice_fusion), channel_id=1, source_target_pairs={{0,8},{4,12},{8,0},{12,4},{1,9},{5,13},{9,1},{13,5},{2,10},{6,14},... | collective-permute-start | bytes 442376 | tf_op jit(solution)/shard_map/ppermute | solution.py:237
  36.5 22.9 %collective-permute-start.4 = (bf16[256,1152]{1,0:T(8,128)(2,1)}, bf16[256,1152]{1,0:T(8,128)(2,1)}, u32[]{:S(2)}, u32[]{:S(2)}) collective-permute-start(bf16[256,1152]{1,0:T(8,128)(2,1)} %bitcast.10.own_ref), channel_id=1, source_target_pairs={{0,16},{16,32},{32,48},{48,0},{1,17},{17,33},{33,49},{49,1},{2,18}... | collective-permute-start | bytes 1769480 | tf_op jit(solution)/shard_map/ppermute | solution.py:237
  39.9 19.6 %collective-permute-start.5 = (bf16[256,1152]{1,0:T(8,128)(2,1)}, bf16[256,1152]{1,0:T(8,128)(2,1)}, u32[]{:S(2)}, u32[]{:S(2)}) collective-permute-start(bf16[256,1152]{1,0:T(8,128)(2,1)} %bitcast.10.own_ref), channel_id=1, source_target_pairs={{0,48},{16,0},{32,16},{48,32},{1,49},{17,1},{33,17},{49,33},{2,50}... | collective-permute-start | bytes 1769480 | tf_op jit(solution)/shard_map/ppermute | solution.py:237
  42.3 10.8 %collective-permute-start.3 = (bf16[192,1152]{1,0:T(8,128)(2,1)}, bf16[192,1152]{1,0:T(8,128)(2,1)}, u32[]{:S(2)}, u32[]{:S(2)}) collective-permute-start(bf16[192,1152]{1,0:T(8,128)(2,1)} %pad_maximum_fusion.fetched_ref), channel_id=1, source_target_pairs={{0,1},{1,0},{2,3},{3,2},{4,5},{5,4},{6,7},{7,6},{8,9},{9,8},{10,11... | collective-permute-start | bytes 1327112 | tf_op jit(solution)/shard_map/ppermute | solution.py:281
  44.3 24.6 %collective-permute-start.2 = (bf16[256,1152]{1,0:T(8,128)(2,1)}, bf16[256,1152]{1,0:T(8,128)(2,1)S(1)}, u32[]{:S(2)}, u32[]{:S(2)}) collective-permute-start(bf16[256,1152]{1,0:T(8,128)(2,1)} %bitcast.10.own_ref), channel_id=1, source_target_pairs={{0,32},{16,48},{32,0},{48,16},{1,33},{17,49},{33,1},{49,17},{2,34}... | collective-permute-start | bytes 1769480 | tf_op jit(solution)/shard_map/ppermute | solution.py:237
  53.1 1.8 %copy-start.2 = (bf16[1152,1152]{0,1:T(8,128)(2,1)S(1)}, bf16[1152,1152]{0,1:T(8,128)(2,1)}, u32[]{:S(2)}) copy-start(bf16[1152,1152]{0,1:T(8,128)(2,1)} %copy.8) | copy-start | bytes 7962628
  54.9 1.0 copy-start.5
  71.0 3.9 %collective-permute-start.6 = (bf16[592,512]{1,0:T(8,128)(2,1)S(1)}, bf16[592,512]{1,0:T(8,128)(2,1)S(1)}, u32[]{:S(2)}, u32[]{:S(2)}) collective-permute-start(bf16[592,512]{1,0:T(8,128)(2,1)S(1)} %get-tuple-element.31), channel_id=1, source_target_pairs={{0,1},{1,0},{2,3},{3,2},{4,5},{5,4},{6,7},{7,6},{8,9},{9,8},{10,11... | collective-permute-start | bytes 1818632 | tf_op jit(solution)/shard_map/ppermute | solution.py:327
  75.6 11.3 %collective-permute-start.7 = (bf16[304,512]{1,0:T(8,128)(2,1)S(1)}, bf16[304,512]{1,0:T(8,128)(2,1)S(1)}, u32[]{:S(2)}, u32[]{:S(2)}) collective-permute-start(bf16[304,512]{1,0:T(8,128)(2,1)S(1)} %get-tuple-element.33), channel_id=1, source_target_pairs={{0,2},{2,0},{1,3},{3,1},{4,6},{6,4},{5,7},{7,5},{8,10},{10,8},{9,1... | collective-permute-start | bytes 933896 | tf_op jit(solution)/shard_map/ppermute | solution.py:336
  88.4 37.3 %all-to-all-start.1 = ((bf16[32,96,128]{2,1,0:T(8,128)(2,1)}), bf16[32,96,128]{2,1,0:T(8,128)(2,1)}, u32[]{:S(2)}, u32[]{:S(2)}) async-start(bf16[32,96,128]{2,1,0:T(8,128)(2,1)} %bitcast.12), calls=%async_computation.1 | async-start | bytes 1572864 | tf_op jit(solution)/shard_map/all_to_all | solution.py:48
  103.7 11.3 %collective-permute-start.10 = (bf16[304,128]{1,0:T(8,128)(2,1)S(1)}, bf16[304,128]{1,0:T(8,128)(2,1)S(1)}, u32[]{:S(2)}, u32[]{:S(2)}) collective-permute-start(bf16[304,128]{1,0:T(8,128)(2,1)S(1)} %get-tuple-element.42), channel_id=1, source_target_pairs={{0,4},{4,8},{8,12},{12,0},{1,5},{5,9},{9,13},{13,1},{2,6},{6,10},{... | collective-permute-start | bytes 233480 | tf_op jit(solution)/shard_map/ppermute | solution.py:237
  105.6 9.4 %collective-permute-start.8 = (bf16[304,128]{1,0:T(8,128)(2,1)S(1)}, bf16[304,128]{1,0:T(8,128)(2,1)S(1)}, u32[]{:S(2)}, u32[]{:S(2)}) collective-permute-start(bf16[304,128]{1,0:T(8,128)(2,1)S(1)} %get-tuple-element.40), channel_id=1, source_target_pairs={{0,12},{4,0},{8,4},{12,8},{1,13},{5,1},{9,5},{13,9},{2,14},{6,2},{... | collective-permute-start | bytes 233480 | tf_op jit(solution)/shard_map/ppermute | solution.py:237
  111.6 10.2 %collective-permute-start.9 = (bf16[304,128]{1,0:T(8,128)(2,1)S(1)}, bf16[304,128]{1,0:T(8,128)(2,1)S(1)}, u32[]{:S(2)}, u32[]{:S(2)}) collective-permute-start(bf16[304,128]{1,0:T(8,128)(2,1)S(1)} %get-tuple-element.41), channel_id=1, source_target_pairs={{0,8},{4,12},{8,0},{12,4},{1,9},{5,13},{9,1},{13,5},{2,10},{6,14},... | collective-permute-start | bytes 233480 | tf_op jit(solution)/shard_map/ppermute | solution.py:237
  121.9 0.6 copy-start.3
  125.7 23.3 %copy-start.4 = (bf16[288,128]{1,0:T(8,128)(2,1)S(1)}, bf16[288,128]{1,0:T(8,128)(2,1)}, u32[]{:S(2)}) copy-start(bf16[288,128]{1,0:T(8,128)(2,1)} %copy-done.3) | copy-start | bytes 221188
  141.9 0.9 copy-start.1
  142.8 25.0 %all-to-all-start.3 = ((bf16[32,96,128]{2,1,0:T(8,128)(2,1)}), bf16[32,96,128]{2,1,0:T(8,128)(2,1)S(1)}, u32[]{:S(2)}, u32[]{:S(2)}) async-start(bf16[32,96,128]{2,1,0:T(8,128)(2,1)} %copy-done.1), calls=%async_computation.3 | async-start | bytes 1572864 | tf_op jit(solution)/shard_map/all_to_all | solution.py:48
  148.9 7.6 %collective-permute-start.11 = (bf16[288,128]{1,0:T(8,128)(2,1)S(1)}, bf16[288,128]{1,0:T(8,128)(2,1)S(1)}, u32[]{:S(2)}, u32[]{:S(2)}) collective-permute-start(bf16[288,128]{1,0:T(8,128)(2,1)S(1)} %copy-done.4), channel_id=1, source_target_pairs={{0,1},{1,0},{2,3},{3,2},{4,5},{5,4},{6,7},{7,6},{8,9},{9,8},{10,11... | collective-permute-start | bytes 221192 | tf_op jit(solution)/shard_map/ppermute | solution.py:370
  150.9 6.6 %collective-permute-start.12 = (bf16[288,128]{1,0:T(8,128)(2,1)S(1)}, bf16[288,128]{1,0:T(8,128)(2,1)S(1)}, u32[]{:S(2)}, u32[]{:S(2)}) collective-permute-start(bf16[288,128]{1,0:T(8,128)(2,1)S(1)} %copy-done.4), channel_id=1, source_target_pairs={{0,2},{1,3},{2,0},{3,1},{4,6},{5,7},{6,4},{7,5},{8,10},{9,11},{10,... | collective-permute-start | bytes 221192 | tf_op jit(solution)/shard_map/ppermute | solution.py:370
  154.0 6.1 %collective-permute-start.13 = (bf16[288,128]{1,0:T(8,128)(2,1)S(1)}, bf16[288,128]{1,0:T(8,128)(2,1)S(1)}, u32[]{:S(2)}, u32[]{:S(2)}) collective-permute-start(bf16[288,128]{1,0:T(8,128)(2,1)S(1)} %copy-done.4), channel_id=1, source_target_pairs={{0,3},{1,2},{2,1},{3,0},{4,7},{5,6},{6,5},{7,4},{8,11},{9,10},{10,... | collective-permute-start | bytes 221192 | tf_op jit(solution)/shard_map/ppermute | solution.py:370

commit v6 on v5

--- a/solution.py
+++ b/solution.py
@@ -17,7 +17,7 @@
 SMEM = pl.BlockSpec(memory_space=pltpu.SMEM)
 
 
-def call(body, outs, *args, smem=0, flops=0, **kwargs):
+def call(body, outs, *args, smem=0, flops=0, limit=12, **kwargs):
     many = isinstance(outs, (tuple, list))
     specs = [SMEM] * smem + [VMEM] * (len(args) - smem)
     size = sum(a.size * a.dtype.itemsize for a in args)
@@ -27,7 +27,7 @@
         in_specs=specs,
         out_specs=[VMEM] * len(outs) if many else VMEM,
         cost_estimate=pl.CostEstimate(flops=flops, bytes_accessed=size, transcendentals=0),
-        compiler_params=pltpu.CompilerParams(vmem_limit_bytes=40 * 2**20),
+        compiler_params=pltpu.CompilerParams(vmem_limit_bytes=limit * 2**20),
         **kwargs,
     )(*args)
 
@@ -46,6 +46,11 @@
 
 def to_all(copies, axes):
     return lax.all_to_all(copies, axes, 0, 0, tiled=True)
+
+
+def spread(block, axes):
+    n = lax.axis_size(axes)
+    return to_all(jnp.broadcast_to(block[None], (n,) + block.shape), axes).reshape(n * block.shape[0], block.shape[1])
 
 
 def text_kernel(text_ref, out_ref):
@@ -80,16 +85,15 @@
     own_unit_ref[...] = unit_ref[pl.ds(start, cols), :rows]
 
 
-def pairs(par_ref, texts, low_ref, own=None):
-    z = par_ref[0] * jnp.dot(texts, low_ref[...], preferred_element_type=F32) + par_ref[1]
-    v = z if own is None else jnp.where(own, -z, z)
+def pairs(z, own):
+    v = jnp.where(own, -z, z)
     e = jnp.exp(-jnp.abs(v))
     one = 1.0 + e
     series = e * (1.0 - e * (0.5 - e * (1.0 / 3.0 - e * (0.25 - e * 0.2))))
     log1p = jnp.where(e < 0.03, series, jnp.log(one))
     soft = jnp.maximum(v, 0.0) + log1p
     s = jnp.where(v >= 0.0, 1.0, e) / one
-    slope = (s if own is None else jnp.where(own, -s, s)).astype(BF16)
+    slope = jnp.where(own, -s, s).astype(BF16)
     return slope, jnp.sum(soft, axis=0, keepdims=True)
 
 
@@ -97,36 +101,50 @@
     return lax.dot_general(texts, slope, (((0,), (0,)), ((), ())), preferred_element_type=F32)
 
 
-def first_kernel(at_ref, par_ref, own_ref, left_ref, right_ref, low_ref, acc_ref, loss_ref):
-    size = (own_ref.shape[0], low_ref.shape[1])
-    col = lax.broadcasted_iota(jnp.int32, size, 0) - at_ref[2]
+def pair_kernel(
+    steps, at_ref, par_ref, texts_ref, low_in, unit_in, keep_ref, send_ref, held_ref, acc_ref, low_ref, unit_ref, sems
+):
+    chunk = texts_ref.shape[0] // steps
+    low_copy = pltpu.make_async_copy(low_in, low_ref, sems.at[steps])
+    unit_copy = pltpu.make_async_copy(unit_in, unit_ref, sems.at[steps + 1])
+    low_copy.start()
+    copies = []
+    for k in range(steps):
+        block = pl.ds(k * chunk, chunk)
+        copies.append(pltpu.make_async_copy(texts_ref.at[block], held_ref.at[block], sems.at[k]))
+        copies[-1].start()
+    unit_copy.start()
+    low_copy.wait()
+    size = (chunk, low_ref.shape[1])
     row = lax.broadcasted_iota(jnp.int32, size, 1) - at_ref[3]
-    own = (row == col) & (col >= 0) & (col < at_ref[4])
-    slope, loss = pairs(par_ref, own_ref[...], low_ref, own)
-    acc_ref[...] = turn(own_ref[...], slope)
-    for ref in (left_ref, right_ref):
-        slope, more = pairs(par_ref, ref[...], low_ref)
-        acc_ref[...] += turn(ref[...], slope)
-        loss = loss + more
-    loss_ref[...] = loss
-
-
-def second_kernel(at_ref, par_ref, far_ref, low_ref, unit_ref, acc_ref, loss_ref, keep_ref, send_ref, sum_ref):
+
+    def logits(k):
+        copies[k].wait()
+        texts = held_ref[k * chunk : (k + 1) * chunk]
+        return par_ref[0] * jnp.dot(texts, low_ref[...], preferred_element_type=F32) + par_ref[1]
+
+    z = logits(0)
+    total_loss = None
+    for k in range(steps):
+        after = logits(k + 1) if k + 1 < steps else None
+        col = lax.broadcasted_iota(jnp.int32, size, 0) + (k * chunk - at_ref[2])
+        own = (row == col) & (col >= 0) & (col < at_ref[4])
+        slope, loss = pairs(z, own)
+        term = turn(held_ref[k * chunk : (k + 1) * chunk], slope)
+        acc_ref[...] = term if k == 0 else acc_ref[...] + term
+        total_loss = loss if k == 0 else total_loss + loss
+        z = after
+    unit_copy.wait()
     scale = par_ref[0]
-    texts = far_ref[...]
-    slope, loss = pairs(par_ref, texts, low_ref)
-    loss = loss_ref[...] + loss
-    total = scale * (acc_ref[...] + turn(texts, slope))
-    sum_ref[...] = total
-    dots = jnp.sum(unit_ref[...] * total, axis=0, keepdims=True)
+    dots = scale * jnp.sum(unit_ref[...] * acc_ref[...], axis=0, keepdims=True)
     cols = (keep_ref.shape[0] - EXTRA) // 2
     c = at_ref[5]
     for k in range(2):
         mine = pl.multiple_of((2 * k + c) * cols, 16)
         other = pl.multiple_of((2 * k + 1 - c) * cols, 16)
-        keep_ref[k * cols : (k + 1) * cols] = sum_ref[pl.ds(mine, cols), :]
-        send_ref[k * cols : (k + 1) * cols] = sum_ref[pl.ds(other, cols), :].astype(BF16)
-    pack(keep_ref, send_ref, 2 * cols, dots, loss)
+        keep_ref[k * cols : (k + 1) * cols] = scale * acc_ref[pl.ds(mine, cols), :]
+        send_ref[k * cols : (k + 1) * cols] = (scale * acc_ref[pl.ds(other, cols), :]).astype(BF16)
+    pack(keep_ref, send_ref, 2 * cols, dots, total_loss)
 
 
 def pack(keep_ref, send_ref, at, dots, loss):
@@ -223,10 +241,10 @@
 
 
 def final_kernel(pairs, full_ref, head_ref, loss_ref):
-    width, cols = head_ref.shape
+    cols, width = head_ref.shape
     tiles = width // LANES
     for k in range(tiles):
-        head_ref[k * LANES : (k + 1) * LANES] = full_ref[k * cols : (k + 1) * cols].astype(F32).T.astype(BF16)
+        head_ref[:, k * LANES : (k + 1) * LANES] = full_ref[k * cols : (k + 1) * cols]
     at = tiles * cols
     total = jnp.sum(full_ref[at : at + EXTRA].astype(F32), axis=0, keepdims=True)
     loss_ref[...] = jnp.sum(total, axis=1, keepdims=True) / pairs
@@ -255,7 +273,7 @@
         [
             rep_at,
             0 * rep_at,
-            y_at * quarter,
+            (x_at * ny + y_at) * quarter,
             rep_at * quarter,
             quarter + 0 * rep_at,
             c_at,
@@ -270,14 +288,11 @@
     part = rows // nc
     near = [(z * nc + c, (z + 1 - 2 * c) % nzh * nc + c) for z in range(nzh) for c in range(nc)]
     half_rows = lax.dynamic_slice_in_dim(img_feat, c_at * part, part, 0)
-    fetched = jnp.concatenate(
-        [lax.ppermute(img_feat, ("zh", "c"), near), shift_by(half_rows, "zh", 2)], axis=0
-    )
+    beside = lax.ppermute(img_feat, ("zh", "c"), near)
     own = to_all(copies, "y")
-    own, fetched = lax.optimization_barrier((own, fetched))
-    far = shift_by(own, "x", 2)
-    left = shift_by(own, "x", 1)
-    right = shift_by(own, "x", -1)
+    own, beside = lax.optimization_barrier((own, beside))
+    texts = spread(own, "x")
+    fetched = jnp.concatenate([beside, shift_by(half_rows, "zh", 2)], axis=0)
     swapped = lax.ppermute(fetched, "c", [(0, 1), (1, 0)])
 
     unit, low, inv, own_unit, col_unit, feats = call(
@@ -298,32 +313,24 @@
         smem=1,
         flops=2 * width * width * images,
     )
-    acc, loss_row = call(
-        first_kernel,
-        [shape((width, images), F32), shape((1, images), F32)],
-        at,
-        par,
-        own,
-        left,
-        right,
-        low,
-        smem=2,
-        flops=4 * width * images * 3 * own.shape[0],
-    )
-    keep, send = call(
-        second_kernel,
-        [shape((2 * cols + EXTRA, images), F32), shape((2 * cols + EXTRA, images), BF16)],
-        at,
-        par,
-        far,
-        low,
-        unit,
-        acc,
-        loss_row,
-        smem=2,
-        flops=4 * width * images * own.shape[0],
-        scratch_shapes=[pltpu.VMEM((width, images), F32)],
-    )
+    steps = 4
+    keep, send = pl.pallas_call(
+        functools.partial(pair_kernel, steps),
+        out_shape=[shape((2 * cols + EXTRA, images), F32), shape((2 * cols + EXTRA, images), BF16)],
+        in_specs=[SMEM, SMEM] + [pl.BlockSpec(memory_space=pl.ANY)] * 3,
+        out_specs=[VMEM, VMEM],
+        scratch_shapes=[
+            pltpu.VMEM(texts.shape, BF16),
+            pltpu.VMEM((width, images), F32),
+            pltpu.VMEM((width, images), BF16),
+            pltpu.VMEM((width, images), F32),
+            pltpu.SemaphoreType.DMA((steps + 2,)),
+        ],
+        cost_estimate=pl.CostEstimate(
+            flops=4 * width * images * texts.shape[0], bytes_accessed=texts.size * 2, transcendentals=0
+        ),
+        compiler_params=pltpu.CompilerParams(vmem_limit_bytes=20 * 2**20),
+    )(at, par, texts, low, unit)
     got = lax.ppermute(send, "c", [(0, 1), (1, 0)])
     keep2, send2 = call(
         middle_kernel,
@@ -361,7 +368,7 @@
     group = rows * plane * nzh
     head_grad, loss = call(
         functools.partial(final_kernel, float(group) * float(group)),
-        [shape((width, cols), BF16), shape((1, 1), F32)],
+        [shape((cols, width), BF16), shape((1, 1), F32)],
         full,
     )
 
@@ -378,7 +385,7 @@
         flops=2 * rows * width * width,
         scratch_shapes=[pltpu.VMEM((width, rows), BF16)],
     )
-    return (loss.reshape(1), feat_grad, head_grad)
+    return (loss.reshape(1), feat_grad, head_grad.T)
 
 
 def solution(mesh):

time: 171 us -> 176 us (1.029)
  local copies, waits for them, and re-layouts: 10.7 us -> 19.6 us
  starting transfers between devices: 79.7 us -> 73.7 us
  blocking collectives: 13.7 us -> 16.6 us
    ppermute x7 -> x4, waiting for transfers between devices: 20.7 us -> 9.6 us  [shift_by(): return lax.ppermute(x, axis, [(k, (k + step) % n) for k in range(n)])]
    ppermute x1, waiting for transfers between devices: 0.01 us -> 9.88 us  [local(): beside = lax.ppermute(img_feat, ('zh', 'c'), near)]
    unnamed x16 -> x40, local copies, waits for them, and re-layouts: 9.7 us -> 17.9 us
    pallas_call x0 -> x1, Pallas kernels: none -> 7.31 us  [local(): pl.pallas_call(functools.partial(pair_kernel, steps), out_shape=[shape((2...]
    pallas_call x10 -> x8, Pallas kernels: 17.6 us -> 10.4 us  [call(): pl.pallas_call(body, out_shape=outs, in_specs=specs, out_specs=[VMEM] * l...]
    all_to_all x3 -> x4, starting transfers between devices: 28.4 us -> 23.3 us  [to_all(): return lax.all_to_all(copies, axes, 0, 0, tiled=True)]
    ppermute x7 -> x4, starting transfers between devices: 30.3 us -> 25.3 us  [shift_by(): return lax.ppermute(x, axis, [(k, (k + step) % n) for k in range(n)])]
    ppermute x1, starting transfers between devices: 3.54 us -> 6.61 us  [local(): got2 = lax.ppermute(send2, 'zl', [(0, 1), (1, 0)])]
  transfers between devices with their start and end apart: 17 -> 15, of which waited for: 9 -> 9; matrix products, arithmetic and copies ran while one was open for 3% -> 2% of each run, Pallas kernels for 7% -> 3%
where the time goes in v6:
time: 176 us; the launch traced here: 175 us
  starting transfers between devices  73.7 us (42%)
  waiting for transfers between devices  43 us (24%)
  local copies, waits for them, and re-layouts  19.6 us (11%)
  Pallas kernels  19.6 us (11%)
  blocking collectives  16.6 us (9%)
  between operations  2.25 us (1%)
    ppermute x4, starting transfers between devices, shift_by(): return lax.ppermute(x, axis, [(k, (k + step) % n) for k in range(n)])  25.3 us
    all_to_all x4, starting transfers between devices, to_all(): return lax.all_to_all(copies, axes, 0, 0, tiled=True)  23.3 us
    unnamed x40, local copies, waits for them, and re-layouts  17.9 us
    all_to_all x1, blocking collectives, to_all(): return lax.all_to_all(copies, axes, 0, 0, tiled=True)  16.6 us
    all_to_all x4, waiting for transfers between devices, to_all(): return lax.all_to_all(copies, axes, 0, 0, tiled=True)  10.7 us
    pallas_call x8, Pallas kernels, call(): pl.pallas_call(body, out_shape=outs, in_specs=specs, out_specs=[VMEM] * l...  10.4 us
    ppermute x1, waiting for transfers between devices, local(): beside = lax.ppermute(img_feat, ('zh', 'c'), near)  9.88 us
    ppermute x4, waiting for transfers between devices, shift_by(): return lax.ppermute(x, axis, [(k, (k + step) % n) for k in range(n)])  9.6 us
  transfers between devices with their start and end apart: 15, of which 9 were waited for; matrix products, arithmetic and copies ran while one was open for 2% of the time, Pallas kernels for 3%

profile of v6, /device:TPU:2, one launch (start us, length us, event | category | flops | bytes accessed | tf_op | source)
XLA Modules:
  0.0 174.8 jit_solution(15739588828748994285)
XLA Ops:
  0.6 0.9 copy-done.11
  1.5 1.0 shard_map.76
  2.5 7.1 %all-to-all-start = ((bf16[8,32,1152]{2,1,0:T(8,128)(2,1)}), bf16[8,32,1152]{2,1,0:T(8,128)(2,1)S(1)}, u32[]{:S(2)}, u32[]{:S(2)}) async-start(bf16[8,32,1152]{2,1,0:T(8,128)(2,1)} %bitcast.9), calls=%async_computation | async-start | bytes 1179648 | tf_op jit(solution)/shard_map/all_to_all | solution.py:48
  9.6 6.1 %collective-permute-start = (bf16[128,1152]{1,0:T(8,128)(2,1)}, bf16[128,1152]{1,0:T(8,128)(2,1)S(1)}, u32[]{:S(2)}, u32[]{:S(2)}) collective-permute-start(bf16[128,1152]{1,0:T(8,128)(2,1)} %own_ref.1), channel_id=1, source_target_pairs={{0,4},{1,13},{4,8},{5,1},{8,12},{9,5},{12,0},{13,9},{2,6},{3,15},{... | collective-permute-start | bytes 884744 | tf_op jit(solution)/shard_map/ppermute | solution.py:291
  15.7 9.9 %collective-permute-done = bf16[128,1152]{1,0:T(8,128)(2,1)S(1)} collective-permute-done((bf16[128,1152]{1,0:T(8,128)(2,1)}, bf16[128,1152]{1,0:T(8,128)(2,1)S(1)}, u32[]{:S(2)}, u32[]{:S(2)}) %collective-permute-start) | collective-permute-done | bytes 294944 | tf_op jit(solution)/shard_map/ppermute | solution.py:291
  25.5 2.9 %all-to-all-done = bf16[8,32,1152]{2,1,0:T(8,128)(2,1)S(1)} async-done(((bf16[8,32,1152]{2,1,0:T(8,128)(2,1)}), bf16[8,32,1152]{2,1,0:T(8,128)(2,1)S(1)}, u32[]{:S(2)}, u32[]{:S(2)}) %all-to-all-start) | async-done | bytes 589856 | tf_op jit(solution)/shard_map/all_to_all | solution.py:48
  28.5 1.6 broadcast_in_dim.2
  30.1 5.3 %all-to-all-start.1 = ((bf16[4,256,1152]{2,1,0:T(8,128)(2,1)}), bf16[4,256,1152]{2,1,0:T(8,128)(2,1)}, u32[]{:S(2)}, u32[]{:S(2)}) async-start(bf16[4,256,1152]{2,1,0:T(8,128)(2,1)} %broadcast_in_dim.2), calls=%async_computation.1 | async-start | bytes 4718592 | tf_op jit(solution)/shard_map/all_to_all | solution.py:48
  35.4 10.9 %collective-permute-start.1 = (bf16[64,1152]{1,0:T(8,128)(2,1)S(1)}, bf16[64,1152]{1,0:T(8,128)(2,1)S(1)}, u32[]{:S(2)}, u32[]{:S(2)}) collective-permute-start(bf16[64,1152]{1,0:T(8,128)(2,1)S(1)} %constant_dynamic-slice_fusion), channel_id=1, source_target_pairs={{0,8},{4,12},{8,0},{12,4},{1,9},{5,13},{9,1},{13,5},{2,10},{6,14},... | collective-permute-start | bytes 442376 | tf_op jit(solution)/shard_map/ppermute | solution.py:255
  46.3 3.8 %collective-permute-done.1 = bf16[64,1152]{1,0:T(8,128)(2,1)S(1)} collective-permute-done((bf16[64,1152]{1,0:T(8,128)(2,1)S(1)}, bf16[64,1152]{1,0:T(8,128)(2,1)S(1)}, u32[]{:S(2)}, u32[]{:S(2)}) %collective-permute-start.1) | collective-permute-done | bytes 147488 | tf_op jit(solution)/shard_map/ppermute | solution.py:255
  50.1 1.9 %collective-permute-start.2 = (bf16[192,1152]{1,0:T(8,128)(2,1)S(1)}, bf16[192,1152]{1,0:T(8,128)(2,1)}, u32[]{:S(2)}, u32[]{:S(2)}) collective-permute-start(bf16[192,1152]{1,0:T(8,128)(2,1)S(1)} %constant_dynamic-update-slice_fusion.fetched_ref), channel_id=1, source_target_pairs={{0,1},{1,0},{2,3},{3,2},{4,5},{5,4},{6,7},{7,6},{8,9},{9,8},{10,11... | collective-permute-start | bytes 1327112 | tf_op jit(solution)/shard_map/ppermute | solution.py:296
  52.1 3.3 %copy.8 = bf16[1152,1152]{0,1:T(8,128)(2,1)} copy(bf16[1152,1152]{1,0:T(8,128)(2,1)S(1)} %copy-done) | data formatting | bytes 5308416 | tf_op args[1]
  56.9 1.8 %copy-done.2 = bf16[1152,1152]{0,1:T(8,128)(2,1)S(1)} copy-done((bf16[1152,1152]{0,1:T(8,128)(2,1)S(1)}, bf16[1152,1152]{0,1:T(8,128)(2,1)}, u32[]{:S(2)}) %copy-start.2) | copy-done | bytes 2654232
  58.7 1.0 copy-done.8
  59.7 1.0 copy-done.10
  60.6 3.4 %shard_map.77 = (f32[1152,512]{1,0:T(8,128)S(1)}, bf16[1152,512]{1,0:T(8,128)(2,1)S(1)}, f32[1,512]{1,0:T(1,128)S(1)}, f32[288,128]{1,0:T(8,128)S(1)}, f32[288,5...) custom-call(s32[12]{0:T(128)S(1)} %stack.48.at_ref, bf16[1152,1152]{1,0:T(8,128)(2,1)S(1)} %bitcast.18, ...), custom_call_target="tpu_custom_call" | custom-call | flops 1358954496 | bytes 3833904 | tf_op jit(solution)/shard_map/pallas_call | solution.py:24
  64.1 1.1 copy-done.3
  65.1 1.5 copy-done.15
  66.6 1.0 copy-done.17
  67.6 1.7 copy-done.16
  69.3 1.3 copy-done.18
  70.6 7.3 %shard_map.78 = (f32[592,512]{1,0:T(8,128)S(1)}, bf16[592,512]{1,0:T(8,128)(2,1)S(1)}) custom-call(s32[12]{0:T(128)S(1)} %stack.48.at_ref, f32[2]{0:T(128)S(1)} %pad_maximum_fusion.par_ref, bf16[1024,1152]{1,0:T(8,128)(2,1)} %bitcast.11.texts_ref, bf16[1152,512]{1,0:T(8,128)(2,1)S(1)} %copy-done.18, f32[1152,512]{1,0:T(8,128)S(1)} %copy-done.16), custom_call_target="tpu_custom_call" | custom-call | flops 2415919104 | bytes 2359296 | tf_op jit(solution)/shard_map/pallas_call | solution.py:317
  77.9 2.5 %collective-permute-start.3 = (bf16[592,512]{1,0:T(8,128)(2,1)S(1)}, bf16[592,512]{1,0:T(8,128)(2,1)S(1)}, u32[]{:S(2)}, u32[]{:S(2)}) collective-permute-start(bf16[592,512]{1,0:T(8,128)(2,1)S(1)} %get-tuple-element.27), channel_id=1, source_target_pairs={{0,1},{1,0},{2,3},{3,2},{4,5},{5,4},{6,7},{7,6},{8,9},{9,8},{10,11... | collective-permute-start | bytes 1818632 | tf_op jit(solution)/shard_map/ppermute | solution.py:334
  80.4 1.6 collective-permute-done.3.got_ref
  82.1 0.7 shard_map.79
  82.7 6.6 %collective-permute-start.4 = (bf16[304,512]{1,0:T(8,128)(2,1)S(1)}, bf16[304,512]{1,0:T(8,128)(2,1)S(1)}, u32[]{:S(2)}, u32[]{:S(2)}) collective-permute-start(bf16[304,512]{1,0:T(8,128)(2,1)S(1)} %get-tuple-element.29), channel_id=1, source_target_pairs={{0,2},{2,0},{1,3},{3,1},{4,6},{6,4},{5,7},{7,5},{8,10},{10,8},{9,1... | collective-permute-start | bytes 933896 | tf_op jit(solution)/shard_map/ppermute | solution.py:343
  89.4 7.9 %collective-permute-done.4.got_ref = bf16[304,512]{1,0:T(8,128)(2,1)S(1)} collective-permute-done((bf16[304,512]{1,0:T(8,128)(2,1)S(1)}, bf16[304,512]{1,0:T(8,128)(2,1)S(1)}, u32[]{:S(2)}, u32[]{:S(2)}) %collective-permute-start.4) | collective-permute-done | bytes 311328 | tf_op jit(solution)/shard_map/ppermute | solution.py:343
  97.2 1.5 shard_map.80
  98.7 0.6 copy-done.12
  99.4 0.6 copy-done.13
  100.0 0.6 copy-done.14
  100.6 5.0 %all-to-all-start.2 = ((bf16[32,96,128]{2,1,0:T(8,128)(2,1)}), bf16[32,96,128]{2,1,0:T(8,128)(2,1)}, u32[]{:S(2)}, u32[]{:S(2)}) async-start(bf16[32,96,128]{2,1,0:T(8,128)(2,1)} %bitcast.13), calls=%async_computation.2 | async-start | bytes 1572864 | tf_op jit(solution)/shard_map/all_to_all | solution.py:48
  105.7 7.5 %collective-permute-start.5 = (bf16[304,128]{1,0:T(8,128)(2,1)}, bf16[304,128]{1,0:T(8,128)(2,1)S(1)}, u32[]{:S(2)}, u32[]{:S(2)}) collective-permute-start(bf16[304,128]{1,0:T(8,128)(2,1)} %copy-done.14), channel_id=1, source_target_pairs={{0,12},{4,0},{8,4},{12,8},{1,13},{5,1},{9,5},{13,9},{2,14},{6,2},{... | collective-permute-start | bytes 233480 | tf_op jit(solution)/shard_map/ppermute | solution.py:255
  113.2 2.4 %collective-permute-start.6 = (bf16[304,128]{1,0:T(8,128)(2,1)}, bf16[304,128]{1,0:T(8,128)(2,1)S(1)}, u32[]{:S(2)}, u32[]{:S(2)}) collective-permute-start(bf16[304,128]{1,0:T(8,128)(2,1)} %copy-done.13), channel_id=1, source_target_pairs={{0,8},{4,12},{8,0},{12,4},{1,9},{5,13},{9,1},{13,5},{2,10},{6,14},... | collective-permute-start | bytes 233480 | tf_op jit(solution)/shard_map/ppermute | solution.py:255
  115.6 4.4 %collective-permute-start.7 = (bf16[304,128]{1,0:T(8,128)(2,1)}, bf16[304,128]{1,0:T(8,128)(2,1)S(1)}, u32[]{:S(2)}, u32[]{:S(2)}) collective-permute-start(bf16[304,128]{1,0:T(8,128)(2,1)} %copy-done.12), channel_id=1, source_target_pairs={{0,4},{4,8},{8,12},{12,0},{1,5},{5,9},{9,13},{13,1},{2,6},{6,10},{... | collective-permute-start | bytes 233480 | tf_op jit(solution)/shard_map/ppermute | solution.py:255
  120.1 5.8 %collective-permute-done.6.refs_2_ = bf16[304,128]{1,0:T(8,128)(2,1)S(1)} collective-permute-done((bf16[304,128]{1,0:T(8,128)(2,1)}, bf16[304,128]{1,0:T(8,128)(2,1)S(1)}, u32[]{:S(2)}, u32[]{:S(2)}) %collective-permute-start.6) | collective-permute-done | bytes 77856 | tf_op jit(solution)/shard_map/ppermute | solution.py:255
  126.6 1.5 all-to-all-done.2.parts_ref
  128.1 2.0 %shard_map.82 = f32[4,96,128]{2,1,0:T(8,128)} custom-call(bf16[32,96,128]{2,1,0:T(8,128)(2,1)} %all-to-all-done.2.parts_ref, bf16[288,128]{1,0:T(8,128)(2,1)} %copy-done.5), custom_call_target="tpu_custom_call" | custom-call | tf_op jit(solution)/shard_map/pallas_call | solution.py:359
  130.1 16.6 %all_to_all.39.parts_ref = f32[4,96,128]{2,1,0:T(8,128)S(1)} all-to-all(f32[4,96,128]{2,1,0:T(8,128)} %shard_map.82), channel_id=1, replica_groups=mesh['y'=8,'x'=4,'zh'=4,'zl'=2,'c'=2] {'zh'}, dimensions={0} | all-to-all | bytes 393216 | tf_op jit(solution)/shard_map/all_to_all | solution.py:48
  147.3 0.9 copy-done.1
  148.2 6.0 %all-to-all-start.4 = ((bf16[32,96,128]{2,1,0:T(8,128)(2,1)}), bf16[32,96,128]{2,1,0:T(8,128)(2,1)S(1)}, u32[]{:S(2)}, u32[]{:S(2)}) async-start(bf16[32,96,128]{2,1,0:T(8,128)(2,1)} %copy-done.1), calls=%async_computation.4 | async-start | bytes 1572864 | tf_op jit(solution)/shard_map/all_to_all | solution.py:48
  154.2 1.9 %collective-permute-start.10 = (bf16[288,128]{1,0:T(8,128)(2,1)S(1)}, bf16[288,128]{1,0:T(8,128)(2,1)S(1)}, u32[]{:S(2)}, u32[]{:S(2)}) collective-permute-start(bf16[288,128]{1,0:T(8,128)(2,1)S(1)} %copy-done.6), channel_id=1, source_target_pairs={{0,3},{1,2},{2,1},{3,0},{4,7},{5,6},{6,5},{7,4},{8,11},{9,10},{10,... | collective-permute-start | bytes 221192 | tf_op jit(solution)/shard_map/ppermute | solution.py:377
  156.1 3.0 %collective-permute-start.8 = (bf16[288,128]{1,0:T(8,128)(2,1)S(1)}, bf16[288,128]{1,0:T(8,128)(2,1)S(1)}, u32[]{:S(2)}, u32[]{:S(2)}) collective-permute-start(bf16[288,128]{1,0:T(8,128)(2,1)S(1)} %copy-done.6), channel_id=1, source_target_pairs={{0,1},{1,0},{2,3},{3,2},{4,5},{5,4},{6,7},{7,6},{8,9},{9,8},{10,11... | collective-permute-start | bytes 221192 | tf_op jit(solution)/shard_map/ppermute | solution.py:377
  159.1 2.9 %collective-permute-start.9 = (bf16[288,128]{1,0:T(8,128)(2,1)S(1)}, bf16[288,128]{1,0:T(8,128)(2,1)S(1)}, u32[]{:S(2)}, u32[]{:S(2)}) collective-permute-start(bf16[288,128]{1,0:T(8,128)(2,1)S(1)} %copy-done.6), channel_id=1, source_target_pairs={{0,2},{1,3},{2,0},{3,1},{4,6},{5,7},{6,4},{7,5},{8,10},{9,11},{10,... | collective-permute-start | bytes 221192 | tf_op jit(solution)/shard_map/ppermute | solution.py:377
  162.1 3.3 %collective-permute-done.9.refs_2_ = bf16[288,128]{1,0:T(8,128)(2,1)S(1)} collective-permute-done((bf16[288,128]{1,0:T(8,128)(2,1)S(1)}, bf16[288,128]{1,0:T(8,128)(2,1)S(1)}, u32[]{:S(2)}, u32[]{:S(2)}) %collective-permute-start.9) | collective-permute-done | bytes 73760 | tf_op jit(solution)/shard_map/ppermute | solution.py:377
  165.4 2.2 %shard_map.85 = bf16[128,1152]{1,0:T(8,128)(2,1)} custom-call(s32[12]{0:T(128)S(1)} %stack.48.at_ref, bf16[1152,1152]{1,0:T(8,128)(2,1)S(1)} %copy-done, bf16[288,128]{1,0:T(8,128)(2,1)S(1)} %copy-done.6, bf16[288,128]{1,0:T(8,128)(2,1)S(1)} %collective-permute-done.8.refs_1_, bf16[288,128]{1,0:T(8,128)(2,1)S(1)} %collective-permute-done.9.refs_2_, ...), custom_call_target="tpu_custom_call" | custom-call | flops 339738624 | bytes 2949168 | tf_op jit(solution)/shard_map/pallas_call | solution.py:24
  167.6 6.2 %all-to-all-done.4 = bf16[32,96,128]{2,1,0:T(8,128)(2,1)S(1)} async-done(((bf16[32,96,128]{2,1,0:T(8,128)(2,1)}), bf16[32,96,128]{2,1,0:T(8,128)(2,1)S(1)}, u32[]{:S(2)}, u32[]{:S(2)}) %all-to-all-start.4) | async-done | bytes 786464 | tf_op jit(solution)/shard_map/all_to_all | solution.py:48
  173.8 1.0 shard_map.84
  (38 shorter events, 1.6 us)
Async XLA Ops:
  0.6 0.9 copy-start.11
  2.5 26.0 %all-to-all-start = ((bf16[8,32,1152]{2,1,0:T(8,128)(2,1)}), bf16[8,32,1152]{2,1,0:T(8,128)(2,1)S(1)}, u32[]{:S(2)}, u32[]{:S(2)}) async-start(bf16[8,32,1152]{2,1,0:T(8,128)(2,1)} %bitcast.9), calls=%async_computation | async-start | bytes 1179648 | tf_op jit(solution)/shard_map/all_to_all | solution.py:48
  9.6 16.0 %collective-permute-start = (bf16[128,1152]{1,0:T(8,128)(2,1)}, bf16[128,1152]{1,0:T(8,128)(2,1)S(1)}, u32[]{:S(2)}, u32[]{:S(2)}) collective-permute-start(bf16[128,1152]{1,0:T(8,128)(2,1)} %own_ref.1), channel_id=1, source_target_pairs={{0,4},{1,13},{4,8},{5,1},{8,12},{9,5},{12,0},{13,9},{2,6},{3,15},{... | collective-permute-start | bytes 884744 | tf_op jit(solution)/shard_map/ppermute | solution.py:291
  30.1 5.3 %copy-start.9 = (bf16[128,1152]{1,0:T(8,128)(2,1)S(1)}, bf16[128,1152]{1,0:T(8,128)(2,1)}, u32[]{:S(2)}) copy-start(bf16[128,1152]{1,0:T(8,128)(2,1)} %own_ref.1) | copy-start | bytes 884740
  30.1 22.0 %copy-start = (bf16[1152,1152]{1,0:T(8,128)(2,1)S(1)}, bf16[1152,1152]{1,0:T(8,128)(2,1)}, u32[]{:S(2)}) copy-start(bf16[1152,1152]{1,0:T(8,128)(2,1)} %weight_ref.1) | copy-start | bytes 7962628
  30.1 37.6 %all-to-all-start.1 = ((bf16[4,256,1152]{2,1,0:T(8,128)(2,1)}), bf16[4,256,1152]{2,1,0:T(8,128)(2,1)}, u32[]{:S(2)}, u32[]{:S(2)}) async-start(bf16[4,256,1152]{2,1,0:T(8,128)(2,1)} %broadcast_in_dim.2), calls=%async_computation.1 | async-start | bytes 4718592 | tf_op jit(solution)/shard_map/all_to_all | solution.py:48
  35.4 14.8 %collective-permute-start.1 = (bf16[64,1152]{1,0:T(8,128)(2,1)S(1)}, bf16[64,1152]{1,0:T(8,128)(2,1)S(1)}, u32[]{:S(2)}, u32[]{:S(2)}) collective-permute-start(bf16[64,1152]{1,0:T(8,128)(2,1)S(1)} %constant_dynamic-slice_fusion), channel_id=1, source_target_pairs={{0,8},{4,12},{8,0},{12,4},{1,9},{5,13},{9,1},{13,5},{2,10},{6,14},... | collective-permute-start | bytes 442376 | tf_op jit(solution)/shard_map/ppermute | solution.py:255
  50.1 5.3 %copy-start.7 = (bf16[192,1152]{1,0:T(8,128)(2,1)}, bf16[192,1152]{1,0:T(8,128)(2,1)S(1)}, u32[]{:S(2)}) copy-start(bf16[192,1152]{1,0:T(8,128)(2,1)S(1)} %constant_dynamic-update-slice_fusion.fetched_ref) | copy-start | bytes 1327108
  50.1 6.8 %collective-permute-start.2 = (bf16[192,1152]{1,0:T(8,128)(2,1)S(1)}, bf16[192,1152]{1,0:T(8,128)(2,1)}, u32[]{:S(2)}, u32[]{:S(2)}) collective-permute-start(bf16[192,1152]{1,0:T(8,128)(2,1)S(1)} %constant_dynamic-update-slice_fusion.fetched_ref), channel_id=1, source_target_pairs={{0,1},{1,0},{2,3},{3,2},{4,5},{5,4},{6,7},{7,6},{8,9},{9,8},{10,11... | collective-permute-start | bytes 1327112 | tf_op jit(solution)/shard_map/ppermute | solution.py:296
  56.9 1.8 %copy-start.2 = (bf16[1152,1152]{0,1:T(8,128)(2,1)S(1)}, bf16[1152,1152]{0,1:T(8,128)(2,1)}, u32[]{:S(2)}) copy-start(bf16[1152,1152]{0,1:T(8,128)(2,1)} %copy.8) | copy-start | bytes 7962628
  58.7 1.0 copy-start.8
  59.7 1.0 copy-start.10
  64.1 1.1 copy-start.3
  65.1 1.5 copy-start.15
  66.6 1.0 copy-start.17
  67.6 1.7 copy-start.16
  69.3 1.3 copy-start.18
  77.9 19.3 %copy-start.4 = (bf16[512,1152]{1,0:T(8,128)(2,1)S(1)}, bf16[512,1152]{1,0:T(8,128)(2,1)}, u32[]{:S(2)}) copy-start(bf16[512,1152]{1,0:T(8,128)(2,1)} %copy-done.3) | copy-start | bytes 3538948
  77.9 4.2 %collective-permute-start.3 = (bf16[592,512]{1,0:T(8,128)(2,1)S(1)}, bf16[592,512]{1,0:T(8,128)(2,1)S(1)}, u32[]{:S(2)}, u32[]{:S(2)}) collective-permute-start(bf16[592,512]{1,0:T(8,128)(2,1)S(1)} %get-tuple-element.27), channel_id=1, source_target_pairs={{0,1},{1,0},{2,3},{3,2},{4,5},{5,4},{6,7},{7,6},{8,9},{9,8},{10,11... | collective-permute-start | bytes 1818632 | tf_op jit(solution)/shard_map/ppermute | solution.py:334
  82.7 14.5 %collective-permute-start.4 = (bf16[304,512]{1,0:T(8,128)(2,1)S(1)}, bf16[304,512]{1,0:T(8,128)(2,1)S(1)}, u32[]{:S(2)}, u32[]{:S(2)}) collective-permute-start(bf16[304,512]{1,0:T(8,128)(2,1)S(1)} %get-tuple-element.29), channel_id=1, source_target_pairs={{0,2},{2,0},{1,3},{3,1},{4,6},{6,4},{5,7},{7,5},{8,10},{10,8},{9,1... | collective-permute-start | bytes 933896 | tf_op jit(solution)/shard_map/ppermute | solution.py:343
  98.7 0.6 copy-start.12
  99.4 0.6 copy-start.13
  100.0 0.6 copy-start.14
  100.6 27.5 %all-to-all-start.2 = ((bf16[32,96,128]{2,1,0:T(8,128)(2,1)}), bf16[32,96,128]{2,1,0:T(8,128)(2,1)}, u32[]{:S(2)}, u32[]{:S(2)}) async-start(bf16[32,96,128]{2,1,0:T(8,128)(2,1)} %bitcast.13), calls=%async_computation.2 | async-start | bytes 1572864 | tf_op jit(solution)/shard_map/all_to_all | solution.py:48
  105.7 14.4 %collective-permute-start.5 = (bf16[304,128]{1,0:T(8,128)(2,1)}, bf16[304,128]{1,0:T(8,128)(2,1)S(1)}, u32[]{:S(2)}, u32[]{:S(2)}) collective-permute-start(bf16[304,128]{1,0:T(8,128)(2,1)} %copy-done.14), channel_id=1, source_target_pairs={{0,12},{4,0},{8,4},{12,8},{1,13},{5,1},{9,5},{13,9},{2,14},{6,2},{... | collective-permute-start | bytes 233480 | tf_op jit(solution)/shard_map/ppermute | solution.py:255
  113.2 12.7 %collective-permute-start.6 = (bf16[304,128]{1,0:T(8,128)(2,1)}, bf16[304,128]{1,0:T(8,128)(2,1)S(1)}, u32[]{:S(2)}, u32[]{:S(2)}) collective-permute-start(bf16[304,128]{1,0:T(8,128)(2,1)} %copy-done.13), channel_id=1, source_target_pairs={{0,8},{4,12},{8,0},{12,4},{1,9},{5,13},{9,1},{13,5},{2,10},{6,14},... | collective-permute-start | bytes 233480 | tf_op jit(solution)/shard_map/ppermute | solution.py:255
  115.6 10.3 %collective-permute-start.7 = (bf16[304,128]{1,0:T(8,128)(2,1)}, bf16[304,128]{1,0:T(8,128)(2,1)S(1)}, u32[]{:S(2)}, u32[]{:S(2)}) collective-permute-start(bf16[304,128]{1,0:T(8,128)(2,1)} %copy-done.12), channel_id=1, source_target_pairs={{0,4},{4,8},{8,12},{12,0},{1,5},{5,9},{9,13},{13,1},{2,6},{6,10},{... | collective-permute-start | bytes 233480 | tf_op jit(solution)/shard_map/ppermute | solution.py:255
  126.0 0.6 copy-start.5
  128.1 26.0 %copy-start.6 = (bf16[288,128]{1,0:T(8,128)(2,1)S(1)}, bf16[288,128]{1,0:T(8,128)(2,1)}, u32[]{:S(2)}) copy-start(bf16[288,128]{1,0:T(8,128)(2,1)} %copy-done.5) | copy-start | bytes 221188
  147.3 0.9 copy-start.1
  148.2 25.7 %all-to-all-start.4 = ((bf16[32,96,128]{2,1,0:T(8,128)(2,1)}), bf16[32,96,128]{2,1,0:T(8,128)(2,1)S(1)}, u32[]{:S(2)}, u32[]{:S(2)}) async-start(bf16[32,96,128]{2,1,0:T(8,128)(2,1)} %copy-done.1), calls=%async_computation.4 | async-start | bytes 1572864 | tf_op jit(solution)/shard_map/all_to_all | solution.py:48
  154.2 7.9 %collective-permute-start.10 = (bf16[288,128]{1,0:T(8,128)(2,1)S(1)}, bf16[288,128]{1,0:T(8,128)(2,1)S(1)}, u32[]{:S(2)}, u32[]{:S(2)}) collective-permute-start(bf16[288,128]{1,0:T(8,128)(2,1)S(1)} %copy-done.6), channel_id=1, source_target_pairs={{0,3},{1,2},{2,1},{3,0},{4,7},{5,6},{6,5},{7,4},{8,11},{9,10},{10,... | collective-permute-start | bytes 221192 | tf_op jit(solution)/shard_map/ppermute | solution.py:377
  156.1 6.0 %collective-permute-start.8 = (bf16[288,128]{1,0:T(8,128)(2,1)S(1)}, bf16[288,128]{1,0:T(8,128)(2,1)S(1)}, u32[]{:S(2)}, u32[]{:S(2)}) collective-permute-start(bf16[288,128]{1,0:T(8,128)(2,1)S(1)} %copy-done.6), channel_id=1, source_target_pairs={{0,1},{1,0},{2,3},{3,2},{4,5},{5,4},{6,7},{7,6},{8,9},{9,8},{10,11... | collective-permute-start | bytes 221192 | tf_op jit(solution)/shard_map/ppermute | solution.py:377
  159.1 6.2 %collective-permute-start.9 = (bf16[288,128]{1,0:T(8,128)(2,1)S(1)}, bf16[288,128]{1,0:T(8,128)(2,1)S(1)}, u32[]{:S(2)}, u32[]{:S(2)}) collective-permute-start(bf16[288,128]{1,0:T(8,128)(2,1)S(1)} %copy-done.6), channel_id=1, source_target_pairs={{0,2},{1,3},{2,0},{3,1},{4,6},{5,7},{6,4},{7,5},{8,10},{9,11},{10,... | collective-permute-start | bytes 221192 | tf_op jit(solution)/shard_map/ppermute | solution.py:377

commit v7 on v5

--- a/solution.py
+++ b/solution.py
@@ -17,7 +17,7 @@
 SMEM = pl.BlockSpec(memory_space=pltpu.SMEM)
 
 
-def call(body, outs, *args, smem=0, flops=0, **kwargs):
+def call(body, outs, *args, smem=0, flops=0, limit=16, **kwargs):
     many = isinstance(outs, (tuple, list))
     specs = [SMEM] * smem + [VMEM] * (len(args) - smem)
     size = sum(a.size * a.dtype.itemsize for a in args)
@@ -27,7 +27,7 @@
         in_specs=specs,
         out_specs=[VMEM] * len(outs) if many else VMEM,
         cost_estimate=pl.CostEstimate(flops=flops, bytes_accessed=size, transcendentals=0),
-        compiler_params=pltpu.CompilerParams(vmem_limit_bytes=40 * 2**20),
+        compiler_params=pltpu.CompilerParams(vmem_limit_bytes=limit * 2**20),
         **kwargs,
     )(*args)
 
@@ -97,26 +97,23 @@
     return lax.dot_general(texts, slope, (((0,), (0,)), ((), ())), preferred_element_type=F32)
 
 
-def first_kernel(at_ref, par_ref, own_ref, left_ref, right_ref, low_ref, acc_ref, loss_ref):
+def first_kernel(at_ref, par_ref, own_ref, left_ref, low_ref, acc_ref, loss_ref):
     size = (own_ref.shape[0], low_ref.shape[1])
     col = lax.broadcasted_iota(jnp.int32, size, 0) - at_ref[2]
     row = lax.broadcasted_iota(jnp.int32, size, 1) - at_ref[3]
     own = (row == col) & (col >= 0) & (col < at_ref[4])
     slope, loss = pairs(par_ref, own_ref[...], low_ref, own)
-    acc_ref[...] = turn(own_ref[...], slope)
-    for ref in (left_ref, right_ref):
-        slope, more = pairs(par_ref, ref[...], low_ref)
-        acc_ref[...] += turn(ref[...], slope)
-        loss = loss + more
-    loss_ref[...] = loss
-
-
-def second_kernel(at_ref, par_ref, far_ref, low_ref, unit_ref, acc_ref, loss_ref, keep_ref, send_ref, sum_ref):
+    more_slope, more = pairs(par_ref, left_ref[...], low_ref)
+    acc_ref[...] = turn(own_ref[...], slope) + turn(left_ref[...], more_slope)
+    loss_ref[...] = loss + more
+
+
+def second_kernel(at_ref, par_ref, right_ref, far_ref, low_ref, unit_ref, acc_ref, loss_ref, keep_ref, send_ref, sum_ref):
     scale = par_ref[0]
-    texts = far_ref[...]
-    slope, loss = pairs(par_ref, texts, low_ref)
-    loss = loss_ref[...] + loss
-    total = scale * (acc_ref[...] + turn(texts, slope))
+    slope, loss = pairs(par_ref, right_ref[...], low_ref)
+    more_slope, more = pairs(par_ref, far_ref[...], low_ref)
+    loss = loss_ref[...] + loss + more
+    total = scale * (acc_ref[...] + turn(right_ref[...], slope) + turn(far_ref[...], more_slope))
     sum_ref[...] = total
     dots = jnp.sum(unit_ref[...] * total, axis=0, keepdims=True)
     cols = (keep_ref.shape[0] - EXTRA) // 2
@@ -158,7 +155,7 @@
     pack(keep2_ref, send2_ref, cols, dots, loss)
 
 
-def head_kernel(keep_ref, got_ref, unit_ref, inv_ref, feats_ref, flat_ref, *dir_refs):
+def head_kernel(at_loss, keep_ref, got_ref, unit_ref, inv_ref, feats_ref, flat_ref, *dir_refs):
     cols = keep_ref.shape[0] - EXTRA
     dots, loss = unpack(keep_ref, got_ref, cols)
     total = keep_ref[:cols] + got_ref[:cols].astype(F32)
@@ -172,9 +169,10 @@
         part = part + loss[:, k * LANES : (k + 1) * LANES]
     terms = [t.astype(F32) for t in split3(part)]
     tail = jnp.concatenate(terms + [jnp.zeros((EXTRA - 3, LANES), F32)], axis=0)
-    at = tiles * cols
-    flat_ref[at : at + EXTRA] = tail.astype(BF16)
-    flat_ref[at + EXTRA :] = jnp.zeros((flat_ref.shape[0] - at - EXTRA, LANES), BF16)
+    end = tiles * cols
+    flat_ref[end:at_loss] = jnp.zeros((at_loss - end, LANES), BF16)
+    flat_ref[at_loss : at_loss + EXTRA] = tail.astype(BF16)
+    flat_ref[at_loss + EXTRA :] = jnp.zeros((flat_ref.shape[0] - at_loss - EXTRA, LANES), BF16)
     low = total.astype(BF16)
     terms = [t.astype(F32) for t in split3(dots)]
     lines = jnp.concatenate(terms + [jnp.zeros((EXTRA - 3, dots.shape[1]), F32)], axis=0).astype(BF16)
@@ -222,13 +220,12 @@
         out_ref[k, EXTRA:] = low[EXTRA:]
 
 
-def final_kernel(pairs, full_ref, head_ref, loss_ref):
-    width, cols = head_ref.shape
+def final_kernel(at_loss, pairs, full_ref, head_ref, loss_ref):
+    cols, width = head_ref.shape
     tiles = width // LANES
     for k in range(tiles):
-        head_ref[k * LANES : (k + 1) * LANES] = full_ref[k * cols : (k + 1) * cols].astype(F32).T.astype(BF16)
-    at = tiles * cols
-    total = jnp.sum(full_ref[at : at + EXTRA].astype(F32), axis=0, keepdims=True)
+        head_ref[:, k * LANES : (k + 1) * LANES] = full_ref[k * cols : (k + 1) * cols]
+    total = jnp.sum(full_ref[at_loss : at_loss + EXTRA].astype(F32), axis=0, keepdims=True)
     loss_ref[...] = jnp.sum(total, axis=1, keepdims=True) / pairs
 
 
@@ -248,9 +245,9 @@
     tiles = width // LANES
     y_at, x_at, zl_at, c_at = (lax.axis_index(a) for a in ("y", "x", "zl", "c"))
     rep_at = zl_at * nc + c_at
-    at_loss = tiles * cols
-    piece = -(-(at_loss + EXTRA) // (plane * 16)) * 16
-    assert at_loss % piece == 0
+    piece = -(-(tiles * cols) // (plane * 8)) * 8
+    at_loss = -(-(tiles * cols) // piece) * piece
+    assert at_loss < plane * piece
     at = jnp.stack(
         [
             rep_at,
@@ -268,11 +265,21 @@
 
     copies = call(text_kernel, shape((ny * quarter, width), BF16), text_embed)
     part = rows // nc
-    near = [(z * nc + c, (z + 1 - 2 * c) % nzh * nc + c) for z in range(nzh) for c in range(nc)]
+    def place(z, low, core):
+        return (z % nzh * nzl + low) * nc + core
+
+    near = []
+    cross = []
+    for z in range(nzh):
+        near += [(place(z, 1, k), place(z + 1, k, 0)) for k in range(nc)]
+        near += [(place(z, 0, k), place(z - 1, k, 1)) for k in range(nc)]
+        cross += [(place(z, 1, k), place(z + 2, 0, k)) for k in range(nc)]
+        cross += [(place(z, 0, k), place(z - 2, 1, k)) for k in range(nc)]
     half_rows = lax.dynamic_slice_in_dim(img_feat, c_at * part, part, 0)
-    fetched = jnp.concatenate(
-        [lax.ppermute(img_feat, ("zh", "c"), near), shift_by(half_rows, "zh", 2)], axis=0
-    )
+    line = ("zh", "zl", "c")
+    across = lax.ppermute(half_rows, line, cross)
+    beside = lax.ppermute(img_feat, line, near)
+    fetched = jnp.concatenate([beside, across], axis=0)
     own = to_all(copies, "y")
     own, fetched = lax.optimization_barrier((own, fetched))
     far = shift_by(own, "x", 2)
@@ -305,23 +312,23 @@
         par,
         own,
         left,
-        right,
         low,
         smem=2,
-        flops=4 * width * images * 3 * own.shape[0],
+        flops=8 * width * images * own.shape[0],
     )
     keep, send = call(
         second_kernel,
         [shape((2 * cols + EXTRA, images), F32), shape((2 * cols + EXTRA, images), BF16)],
         at,
         par,
+        right,
         far,
         low,
         unit,
         acc,
         loss_row,
         smem=2,
-        flops=4 * width * images * own.shape[0],
+        flops=8 * width * images * own.shape[0],
         scratch_shapes=[pltpu.VMEM((width, images), F32)],
     )
     got = lax.ppermute(send, "c", [(0, 1), (1, 0)])
@@ -335,7 +342,7 @@
     )
     got2 = lax.ppermute(send2, "zl", [(0, 1), (1, 0)])
     flat, *dirs = call(
-        head_kernel,
+        functools.partial(head_kernel, at_loss),
         [shape((plane * piece, LANES), BF16)] + [shape((cols + EXTRA, rows), BF16)] * nzh,
         keep2,
         got2,
@@ -360,8 +367,8 @@
     full = to_all(low_part.reshape(plane * piece, LANES), ("y", "x"))
     group = rows * plane * nzh
     head_grad, loss = call(
-        functools.partial(final_kernel, float(group) * float(group)),
-        [shape((width, cols), BF16), shape((1, 1), F32)],
+        functools.partial(final_kernel, at_loss, float(group) * float(group)),
+        [shape((cols, width), BF16), shape((1, 1), F32)],
         full,
     )
 
@@ -378,7 +385,7 @@
         flops=2 * rows * width * width,
         scratch_shapes=[pltpu.VMEM((width, rows), BF16)],
     )
-    return (loss.reshape(1), feat_grad, head_grad)
+    return (loss.reshape(1), feat_grad, head_grad.T)
 
 
 def solution(mesh):

time: 171 us -> 168 us (0.982)
  waiting for transfers between devices: 42.6 us -> 40 us
  blocking collectives: 13.7 us -> 15.8 us
    ppermute x1 -> x2, starting transfers between devices: 6.08 us -> 14.3 us  [the longest x1 10.1 us: local(): beside = lax.ppermute(img_feat, line, near)]
    ppermute x1 -> x2, waiting for transfers between devices: 0.01 us -> 8.19 us  [the longest x1 8.19 us: local(): across = lax.ppermute(half_rows, line, cross)]
    ppermute x7 -> x6, waiting for transfers between devices: 20.7 us -> 13.3 us  [shift_by(): return lax.ppermute(x, axis, [(k, (k + step) % n) for k in range(n)])]
    ppermute x7 -> x6, starting transfers between devices: 30.3 us -> 24.7 us  [shift_by(): return lax.ppermute(x, axis, [(k, (k + step) % n) for k in range(n)])]
    all_to_all x3, waiting for transfers between devices: 8.6 us -> 4.75 us  [to_all(): return lax.all_to_all(copies, axes, 0, 0, tiled=True)]
    all_to_all x3, starting transfers between devices: 28.4 us -> 24.9 us  [to_all(): return lax.all_to_all(copies, axes, 0, 0, tiled=True)]
    all_to_all x1, blocking collectives: 13.7 us -> 15.8 us  [to_all(): return lax.all_to_all(copies, axes, 0, 0, tiled=True)]
    unnamed x16 -> x17, local copies, waits for them, and re-layouts: 9.7 us -> 9.54 us
  transfers between devices with their start and end apart: 17 -> 17, of which waited for: 9 -> 9; matrix products, arithmetic and copies ran while one was open for 3% -> 3% of each run, Pallas kernels for 7% -> 5%
where the time goes in v7:
time: 168 us; the launch traced here: 167 us
  starting transfers between devices  78.6 us (47%)
  waiting for transfers between devices  40 us (24%)
  Pallas kernels  19.3 us (11%)
  blocking collectives  15.8 us (9%)
  local copies, waits for them, and re-layouts  10.6 us (6%)
  between operations  2.26 us (1%)
    all_to_all x3, starting transfers between devices, to_all(): return lax.all_to_all(copies, axes, 0, 0, tiled=True)  24.9 us
    ppermute x6, starting transfers between devices, shift_by(): return lax.ppermute(x, axis, [(k, (k + step) % n) for k in range(n)])  24.7 us
    pallas_call x10, Pallas kernels, call(): pl.pallas_call(body, out_shape=outs, in_specs=specs, out_specs=[VMEM] * l...  17.4 us
    all_to_all x1, blocking collectives, to_all(): return lax.all_to_all(copies, axes, 0, 0, tiled=True)  15.8 us
    ppermute x6, waiting for transfers between devices, shift_by(): return lax.ppermute(x, axis, [(k, (k + step) % n) for k in range(n)])  13.3 us
    ppermute x1, starting transfers between devices, local(): beside = lax.ppermute(img_feat, line, near)  10.1 us
    unnamed x17, local copies, waits for them, and re-layouts  9.54 us
    ppermute x1, waiting for transfers between devices, local(): across = lax.ppermute(half_rows, line, cross)  8.19 us
  transfers between devices with their start and end apart: 17, of which 9 were waited for; matrix products, arithmetic and copies ran while one was open for 3% of the time, Pallas kernels for 5%

profile of v7, /device:TPU:2, one launch (start us, length us, event | category | flops | bytes accessed | tf_op | source)
XLA Modules:
  0.0 167.3 jit_solution(5827696139541452790)
XLA Ops:
  0.7 1.0 copy-done.7
  1.7 1.0 shard_map.76
  2.6 7.1 %all-to-all-start = ((bf16[8,32,1152]{2,1,0:T(8,128)(2,1)}), bf16[8,32,1152]{2,1,0:T(8,128)(2,1)S(1)}, u32[]{:S(2)}, u32[]{:S(2)}) async-start(bf16[8,32,1152]{2,1,0:T(8,128)(2,1)} %bitcast.9), calls=%async_computation | async-start | bytes 1179648 | tf_op jit(solution)/shard_map/all_to_all | solution.py:48
  9.7 10.1 %collective-permute-start = (bf16[128,1152]{1,0:T(8,128)(2,1)}, bf16[128,1152]{1,0:T(8,128)(2,1)S(1)}, u32[]{:S(2)}, u32[]{:S(2)}) collective-permute-start(bf16[128,1152]{1,0:T(8,128)(2,1)} %own_ref.1), channel_id=1, source_target_pairs={{2,4},{3,6},{0,13},{1,15},{6,8},{7,10},{4,1},{5,3},{10,12},{11,14}... | collective-permute-start | bytes 884744 | tf_op jit(solution)/shard_map/ppermute | solution.py:281
  19.8 0.9 constant_dynamic-slice_fusion
  20.8 4.2 %collective-permute-start.1 = (bf16[64,1152]{1,0:T(8,128)(2,1)S(1)}, bf16[64,1152]{1,0:T(8,128)(2,1)S(1)}, u32[]{:S(2)}, u32[]{:S(2)}) collective-permute-start(bf16[64,1152]{1,0:T(8,128)(2,1)S(1)} %constant_dynamic-slice_fusion), channel_id=1, source_target_pairs={{2,8},{3,9},{0,10},{1,11},{6,12},{7,13},{4,14},{5,15},{10,0},{11,1... | collective-permute-start | bytes 442376 | tf_op jit(solution)/shard_map/ppermute | solution.py:280
  25.0 8.2 %collective-permute-done.1 = bf16[64,1152]{1,0:T(8,128)(2,1)S(1)} collective-permute-done((bf16[64,1152]{1,0:T(8,128)(2,1)S(1)}, bf16[64,1152]{1,0:T(8,128)(2,1)S(1)}, u32[]{:S(2)}, u32[]{:S(2)}) %collective-permute-start.1) | collective-permute-done | bytes 147488 | tf_op jit(solution)/shard_map/ppermute | solution.py:280
  33.2 0.8 pad_maximum_fusion.fetched_ref
  34.0 3.4 %collective-permute-start.5 = (bf16[256,1152]{1,0:T(8,128)(2,1)S(1)}, bf16[256,1152]{1,0:T(8,128)(2,1)}, u32[]{:S(2)}, u32[]{:S(2)}) collective-permute-start(bf16[256,1152]{1,0:T(8,128)(2,1)S(1)} %bitcast.18), channel_id=1, source_target_pairs={{0,16},{16,32},{32,48},{48,0},{1,17},{17,33},{33,49},{49,1},{2,18}... | collective-permute-start | bytes 1769480 | tf_op jit(solution)/shard_map/ppermute | solution.py:234
  37.4 1.9 %collective-permute-start.4 = (bf16[192,1152]{1,0:T(8,128)(2,1)}, bf16[192,1152]{1,0:T(8,128)(2,1)}, u32[]{:S(2)}, u32[]{:S(2)}) collective-permute-start(bf16[192,1152]{1,0:T(8,128)(2,1)} %pad_maximum_fusion.fetched_ref), channel_id=1, source_target_pairs={{0,1},{1,0},{2,3},{3,2},{4,5},{5,4},{6,7},{7,6},{8,9},{9,8},{10,11... | collective-permute-start | bytes 1327112 | tf_op jit(solution)/shard_map/ppermute | solution.py:288
  39.3 2.4 %collective-permute-start.2 = (bf16[256,1152]{1,0:T(8,128)(2,1)S(1)}, bf16[256,1152]{1,0:T(8,128)(2,1)}, u32[]{:S(2)}, u32[]{:S(2)}) collective-permute-start(bf16[256,1152]{1,0:T(8,128)(2,1)S(1)} %bitcast.19), channel_id=1, source_target_pairs={{0,48},{16,0},{32,16},{48,32},{1,49},{17,1},{33,17},{49,33},{2,50}... | collective-permute-start | bytes 1769480 | tf_op jit(solution)/shard_map/ppermute | solution.py:234
  41.8 4.0 %collective-permute-start.3 = (bf16[256,1152]{1,0:T(8,128)(2,1)S(1)}, bf16[256,1152]{1,0:T(8,128)(2,1)}, u32[]{:S(2)}, u32[]{:S(2)}) collective-permute-start(bf16[256,1152]{1,0:T(8,128)(2,1)S(1)} %bitcast.20), channel_id=1, source_target_pairs={{0,32},{16,48},{32,0},{48,16},{1,33},{17,49},{33,1},{49,17},{2,34}... | collective-permute-start | bytes 1769480 | tf_op jit(solution)/shard_map/ppermute | solution.py:234
  45.8 3.3 %copy.8 = bf16[1152,1152]{0,1:T(8,128)(2,1)} copy(bf16[1152,1152]{1,0:T(8,128)(2,1)S(1)} %copy-done) | data formatting | bytes 5308416 | tf_op args[1]
  50.5 0.1 stack.48.at_ref
  50.5 0.1 pad_maximum_fusion.1.par_ref
  50.6 1.8 %copy-done.2 = bf16[1152,1152]{0,1:T(8,128)(2,1)S(1)} copy-done((bf16[1152,1152]{0,1:T(8,128)(2,1)S(1)}, bf16[1152,1152]{0,1:T(8,128)(2,1)}, u32[]{:S(2)}) %copy-start.2) | copy-done | bytes 2654232
  52.4 1.0 copy-done.5
  53.4 1.0 copy-done.6
  54.4 3.4 %shard_map.77 = (f32[1152,512]{1,0:T(8,128)S(1)}, bf16[1152,512]{1,0:T(8,128)(2,1)S(1)}, f32[1,512]{1,0:T(1,128)S(1)}, f32[288,128]{1,0:T(8,128)S(1)}, f32[288,5...) custom-call(s32[12]{0:T(128)S(1)} %stack.48.at_ref, bf16[1152,1152]{1,0:T(8,128)(2,1)S(1)} %bitcast.17, ...), custom_call_target="tpu_custom_call" | custom-call | flops 1358954496 | bytes 3833904 | tf_op jit(solution)/shard_map/pallas_call | solution.py:24
  57.8 3.5 %shard_map.78 = (f32[1152,512]{1,0:T(8,128)S(1)}, f32[1,512]{1,0:T(1,128)S(1)}) custom-call(s32[12]{0:T(128)S(1)} %stack.48.at_ref, f32[2]{0:T(128)S(1)} %pad_maximum_fusion.1.par_ref, bf16[256,1152]{1,0:T(8,128)(2,1)S(1)} %bitcast.21, bf16[256,1152]{1,0:T(8,128)(2,1)} %collective-permute-done.5.left_ref, bf16[1152,512]{1,0:T(8,128)(2,1)S(1)} %get-tuple-element.26.low_ref), custom_call_target="tpu_custom_call" | custom-call | flops 1207959552 | bytes 2359352 | tf_op jit(solution)/shard_map/pallas_call | solution.py:24
  61.3 9.0 %collective-permute-done.3.far_ref = bf16[256,1152]{1,0:T(8,128)(2,1)} collective-permute-done((bf16[256,1152]{1,0:T(8,128)(2,1)S(1)}, bf16[256,1152]{1,0:T(8,128)(2,1)}, u32[]{:S(2)}, u32[]{:S(2)}) %collective-permute-start.3) | collective-permute-done | bytes 589856 | tf_op jit(solution)/shard_map/ppermute | solution.py:234
  70.3 3.5 %shard_map.79 = (f32[592,512]{1,0:T(8,128)S(1)}, bf16[592,512]{1,0:T(8,128)(2,1)S(1)}) custom-call(s32[12]{0:T(128)S(1)} %stack.48.at_ref, f32[2]{0:T(128)S(1)} %pad_maximum_fusion.1.par_ref, bf16[256,1152]{1,0:T(8,128)(2,1)} %collective-permute-done.2.right_ref, bf16[256,1152]{1,0:T(8,128)(2,1)} %collective-permute-done.3.far_ref, ...), custom_call_target="tpu_custom_call" | custom-call | flops 1207959552 | bytes 7079992 | tf_op jit(solution)/shard_map/pallas_call | solution.py:24
  73.8 1.9 %collective-permute-start.6 = (bf16[592,512]{1,0:T(8,128)(2,1)S(1)}, bf16[592,512]{1,0:T(8,128)(2,1)S(1)}, u32[]{:S(2)}, u32[]{:S(2)}) collective-permute-start(bf16[592,512]{1,0:T(8,128)(2,1)S(1)} %get-tuple-element.31), channel_id=1, source_target_pairs={{0,1},{1,0},{2,3},{3,2},{4,5},{5,4},{6,7},{7,6},{8,9},{9,8},{10,11... | collective-permute-start | bytes 1818632 | tf_op jit(solution)/shard_map/ppermute | solution.py:334
  75.8 2.0 %collective-permute-done.6.got_ref = bf16[592,512]{1,0:T(8,128)(2,1)S(1)} collective-permute-done((bf16[592,512]{1,0:T(8,128)(2,1)S(1)}, bf16[592,512]{1,0:T(8,128)(2,1)S(1)}, u32[]{:S(2)}, u32[]{:S(2)}) %collective-permute-start.6) | collective-permute-done | bytes 606240 | tf_op jit(solution)/shard_map/ppermute | solution.py:334
  77.8 0.7 shard_map.80
  78.4 3.2 %collective-permute-start.7 = (bf16[304,512]{1,0:T(8,128)(2,1)S(1)}, bf16[304,512]{1,0:T(8,128)(2,1)S(1)}, u32[]{:S(2)}, u32[]{:S(2)}) collective-permute-start(bf16[304,512]{1,0:T(8,128)(2,1)S(1)} %get-tuple-element.33), channel_id=1, source_target_pairs={{0,2},{2,0},{1,3},{3,1},{4,6},{6,4},{5,7},{7,5},{8,10},{10,8},{9,1... | collective-permute-start | bytes 933896 | tf_op jit(solution)/shard_map/ppermute | solution.py:343
  81.6 8.1 %collective-permute-done.7.got_ref = bf16[304,512]{1,0:T(8,128)(2,1)S(1)} collective-permute-done((bf16[304,512]{1,0:T(8,128)(2,1)S(1)}, bf16[304,512]{1,0:T(8,128)(2,1)S(1)}, u32[]{:S(2)}, u32[]{:S(2)}) %collective-permute-start.7) | collective-permute-done | bytes 311328 | tf_op jit(solution)/shard_map/ppermute | solution.py:343
  89.7 1.5 shard_map.81
  91.2 9.6 %all-to-all-start.1 = ((bf16[32,88,128]{2,1,0:T(8,128)(2,1)}), bf16[32,88,128]{2,1,0:T(8,128)(2,1)}, u32[]{:S(2)}, u32[]{:S(2)}) async-start(bf16[32,88,128]{2,1,0:T(8,128)(2,1)} %bitcast.12), calls=%async_computation.1 | async-start | bytes 1441792 | tf_op jit(solution)/shard_map/all_to_all | solution.py:48
  100.9 4.8 %collective-permute-start.10 = (bf16[304,128]{1,0:T(8,128)(2,1)S(1)}, bf16[304,128]{1,0:T(8,128)(2,1)S(1)}, u32[]{:S(2)}, u32[]{:S(2)}) collective-permute-start(bf16[304,128]{1,0:T(8,128)(2,1)S(1)} %get-tuple-element.42), channel_id=1, source_target_pairs={{0,4},{4,8},{8,12},{12,0},{1,5},{5,9},{9,13},{13,1},{2,6},{6,10},{... | collective-permute-start | bytes 233480 | tf_op jit(solution)/shard_map/ppermute | solution.py:234
  105.7 3.8 %collective-permute-start.8 = (bf16[304,128]{1,0:T(8,128)(2,1)S(1)}, bf16[304,128]{1,0:T(8,128)(2,1)S(1)}, u32[]{:S(2)}, u32[]{:S(2)}) collective-permute-start(bf16[304,128]{1,0:T(8,128)(2,1)S(1)} %get-tuple-element.40), channel_id=1, source_target_pairs={{0,12},{4,0},{8,4},{12,8},{1,13},{5,1},{9,5},{13,9},{2,14},{6,2},{... | collective-permute-start | bytes 233480 | tf_op jit(solution)/shard_map/ppermute | solution.py:234
  109.5 6.2 %collective-permute-start.9 = (bf16[304,128]{1,0:T(8,128)(2,1)S(1)}, bf16[304,128]{1,0:T(8,128)(2,1)S(1)}, u32[]{:S(2)}, u32[]{:S(2)}) collective-permute-start(bf16[304,128]{1,0:T(8,128)(2,1)S(1)} %get-tuple-element.41), channel_id=1, source_target_pairs={{0,8},{4,12},{8,0},{12,4},{1,9},{5,13},{9,1},{13,5},{2,10},{6,14},... | collective-permute-start | bytes 233480 | tf_op jit(solution)/shard_map/ppermute | solution.py:234
  115.8 4.3 %collective-permute-done.9.refs_2_ = bf16[304,128]{1,0:T(8,128)(2,1)S(1)} collective-permute-done((bf16[304,128]{1,0:T(8,128)(2,1)S(1)}, bf16[304,128]{1,0:T(8,128)(2,1)S(1)}, u32[]{:S(2)}, u32[]{:S(2)}) %collective-permute-start.9) | collective-permute-done | bytes 77856 | tf_op jit(solution)/shard_map/ppermute | solution.py:234
  120.2 0.6 copy-done.3
  120.8 0.6 all-to-all-done.1.parts_ref
  121.4 1.9 %shard_map.83 = f32[4,88,128]{2,1,0:T(8,128)} custom-call(bf16[32,88,128]{2,1,0:T(8,128)(2,1)} %all-to-all-done.1.parts_ref, bf16[288,128]{1,0:T(8,128)(2,1)} %copy-done.3), custom_call_target="tpu_custom_call" | custom-call | tf_op jit(solution)/shard_map/pallas_call | solution.py:359
  123.4 15.8 %all_to_all.34.parts_ref = f32[4,88,128]{2,1,0:T(8,128)S(1)} all-to-all(f32[4,88,128]{2,1,0:T(8,128)} %shard_map.83), channel_id=1, replica_groups=mesh['y'=8,'x'=4,'zh'=4,'zl'=2,'c'=2] {'zh'}, dimensions={0} | all-to-all | bytes 360448 | tf_op jit(solution)/shard_map/all_to_all | solution.py:48
  139.2 0.6 shard_map.84
  139.8 0.9 copy-done.1
  140.6 8.2 %all-to-all-start.3 = ((bf16[32,88,128]{2,1,0:T(8,128)(2,1)}), bf16[32,88,128]{2,1,0:T(8,128)(2,1)S(1)}, u32[]{:S(2)}, u32[]{:S(2)}) async-start(bf16[32,88,128]{2,1,0:T(8,128)(2,1)} %copy-done.1), calls=%async_computation.3 | async-start | bytes 1441792 | tf_op jit(solution)/shard_map/all_to_all | solution.py:48
  148.8 1.9 %collective-permute-start.11 = (bf16[288,128]{1,0:T(8,128)(2,1)S(1)}, bf16[288,128]{1,0:T(8,128)(2,1)S(1)}, u32[]{:S(2)}, u32[]{:S(2)}) collective-permute-start(bf16[288,128]{1,0:T(8,128)(2,1)S(1)} %copy-done.4), channel_id=1, source_target_pairs={{0,1},{1,0},{2,3},{3,2},{4,5},{5,4},{6,7},{7,6},{8,9},{9,8},{10,11... | collective-permute-start | bytes 221192 | tf_op jit(solution)/shard_map/ppermute | solution.py:377
  150.8 3.1 %collective-permute-start.12 = (bf16[288,128]{1,0:T(8,128)(2,1)S(1)}, bf16[288,128]{1,0:T(8,128)(2,1)S(1)}, u32[]{:S(2)}, u32[]{:S(2)}) collective-permute-start(bf16[288,128]{1,0:T(8,128)(2,1)S(1)} %copy-done.4), channel_id=1, source_target_pairs={{0,2},{1,3},{2,0},{3,1},{4,6},{5,7},{6,4},{7,5},{8,10},{9,11},{10,... | collective-permute-start | bytes 221192 | tf_op jit(solution)/shard_map/ppermute | solution.py:377
  153.9 2.5 %collective-permute-start.13 = (bf16[288,128]{1,0:T(8,128)(2,1)S(1)}, bf16[288,128]{1,0:T(8,128)(2,1)S(1)}, u32[]{:S(2)}, u32[]{:S(2)}) collective-permute-start(bf16[288,128]{1,0:T(8,128)(2,1)S(1)} %copy-done.4), channel_id=1, source_target_pairs={{0,3},{1,2},{2,1},{3,0},{4,7},{5,6},{6,5},{7,4},{8,11},{9,10},{10,... | collective-permute-start | bytes 221192 | tf_op jit(solution)/shard_map/ppermute | solution.py:377
  156.5 0.9 collective-permute-done.12.refs_2_
  157.3 2.7 %collective-permute-done.13.refs_3_ = bf16[288,128]{1,0:T(8,128)(2,1)S(1)} collective-permute-done((bf16[288,128]{1,0:T(8,128)(2,1)S(1)}, bf16[288,128]{1,0:T(8,128)(2,1)S(1)}, u32[]{:S(2)}, u32[]{:S(2)}) %collective-permute-start.13) | collective-permute-done | bytes 73760 | tf_op jit(solution)/shard_map/ppermute | solution.py:377
  160.0 2.2 %shard_map.86 = bf16[128,1152]{1,0:T(8,128)(2,1)} custom-call(s32[12]{0:T(128)S(1)} %stack.48.at_ref, bf16[1152,1152]{1,0:T(8,128)(2,1)S(1)} %copy-done, bf16[288,128]{1,0:T(8,128)(2,1)S(1)} %copy-done.4, bf16[288,128]{1,0:T(8,128)(2,1)S(1)} %collective-permute-done.11.refs_1_, bf16[288,128]{1,0:T(8,128)(2,1)S(1)} %collective-permute-done.12.refs_2_, ...), custom_call_target="tpu_custom_call" | custom-call | flops 339738624 | bytes 2949168 | tf_op jit(solution)/shard_map/pallas_call | solution.py:24
  162.2 4.1 %all-to-all-done.3 = bf16[32,88,128]{2,1,0:T(8,128)(2,1)S(1)} async-done(((bf16[32,88,128]{2,1,0:T(8,128)(2,1)}), bf16[32,88,128]{2,1,0:T(8,128)(2,1)S(1)}, u32[]{:S(2)}, u32[]{:S(2)}) %all-to-all-start.3) | async-done | bytes 720928 | tf_op jit(solution)/shard_map/all_to_all | solution.py:48
  166.4 1.0 shard_map.85
  (19 shorter events, 0.1 us)
Async XLA Ops:
  0.6 45.2 %copy-start = (bf16[1152,1152]{1,0:T(8,128)(2,1)S(1)}, bf16[1152,1152]{1,0:T(8,128)(2,1)}, u32[]{:S(2)}) copy-start(bf16[1152,1152]{1,0:T(8,128)(2,1)} %weight_ref.1) | copy-start | bytes 7962628
  0.6 1.0 copy-start.7
  2.6 31.4 %all-to-all-start = ((bf16[8,32,1152]{2,1,0:T(8,128)(2,1)}), bf16[8,32,1152]{2,1,0:T(8,128)(2,1)S(1)}, u32[]{:S(2)}, u32[]{:S(2)}) async-start(bf16[8,32,1152]{2,1,0:T(8,128)(2,1)} %bitcast.9), calls=%async_computation | async-start | bytes 1179648 | tf_op jit(solution)/shard_map/all_to_all | solution.py:48
  9.7 23.4 %collective-permute-start = (bf16[128,1152]{1,0:T(8,128)(2,1)}, bf16[128,1152]{1,0:T(8,128)(2,1)S(1)}, u32[]{:S(2)}, u32[]{:S(2)}) collective-permute-start(bf16[128,1152]{1,0:T(8,128)(2,1)} %own_ref.1), channel_id=1, source_target_pairs={{2,4},{3,6},{0,13},{1,15},{6,8},{7,10},{4,1},{5,3},{10,12},{11,14}... | collective-permute-start | bytes 884744 | tf_op jit(solution)/shard_map/ppermute | solution.py:281
  20.8 12.4 %collective-permute-start.1 = (bf16[64,1152]{1,0:T(8,128)(2,1)S(1)}, bf16[64,1152]{1,0:T(8,128)(2,1)S(1)}, u32[]{:S(2)}, u32[]{:S(2)}) collective-permute-start(bf16[64,1152]{1,0:T(8,128)(2,1)S(1)} %constant_dynamic-slice_fusion), channel_id=1, source_target_pairs={{2,8},{3,9},{0,10},{1,11},{6,12},{7,13},{4,14},{5,15},{10,0},{11,1... | collective-permute-start | bytes 442376 | tf_op jit(solution)/shard_map/ppermute | solution.py:280
  34.0 23.8 %collective-permute-start.5 = (bf16[256,1152]{1,0:T(8,128)(2,1)S(1)}, bf16[256,1152]{1,0:T(8,128)(2,1)}, u32[]{:S(2)}, u32[]{:S(2)}) collective-permute-start(bf16[256,1152]{1,0:T(8,128)(2,1)S(1)} %bitcast.18), channel_id=1, source_target_pairs={{0,16},{16,32},{32,48},{48,0},{1,17},{17,33},{33,49},{49,1},{2,18}... | collective-permute-start | bytes 1769480 | tf_op jit(solution)/shard_map/ppermute | solution.py:234
  37.4 13.3 %collective-permute-start.4 = (bf16[192,1152]{1,0:T(8,128)(2,1)}, bf16[192,1152]{1,0:T(8,128)(2,1)}, u32[]{:S(2)}, u32[]{:S(2)}) collective-permute-start(bf16[192,1152]{1,0:T(8,128)(2,1)} %pad_maximum_fusion.fetched_ref), channel_id=1, source_target_pairs={{0,1},{1,0},{2,3},{3,2},{4,5},{5,4},{6,7},{7,6},{8,9},{9,8},{10,11... | collective-permute-start | bytes 1327112 | tf_op jit(solution)/shard_map/ppermute | solution.py:288
  39.3 22.0 %collective-permute-start.2 = (bf16[256,1152]{1,0:T(8,128)(2,1)S(1)}, bf16[256,1152]{1,0:T(8,128)(2,1)}, u32[]{:S(2)}, u32[]{:S(2)}) collective-permute-start(bf16[256,1152]{1,0:T(8,128)(2,1)S(1)} %bitcast.19), channel_id=1, source_target_pairs={{0,48},{16,0},{32,16},{48,32},{1,49},{17,1},{33,17},{49,33},{2,50}... | collective-permute-start | bytes 1769480 | tf_op jit(solution)/shard_map/ppermute | solution.py:234
  41.8 28.6 %collective-permute-start.3 = (bf16[256,1152]{1,0:T(8,128)(2,1)S(1)}, bf16[256,1152]{1,0:T(8,128)(2,1)}, u32[]{:S(2)}, u32[]{:S(2)}) collective-permute-start(bf16[256,1152]{1,0:T(8,128)(2,1)S(1)} %bitcast.20), channel_id=1, source_target_pairs={{0,32},{16,48},{32,0},{48,16},{1,33},{17,49},{33,1},{49,17},{2,34}... | collective-permute-start | bytes 1769480 | tf_op jit(solution)/shard_map/ppermute | solution.py:234
  50.6 1.8 %copy-start.2 = (bf16[1152,1152]{0,1:T(8,128)(2,1)S(1)}, bf16[1152,1152]{0,1:T(8,128)(2,1)}, u32[]{:S(2)}) copy-start(bf16[1152,1152]{0,1:T(8,128)(2,1)} %copy.8) | copy-start | bytes 7962628
  52.4 1.0 copy-start.5
  53.4 1.0 copy-start.6
  73.8 3.9 %collective-permute-start.6 = (bf16[592,512]{1,0:T(8,128)(2,1)S(1)}, bf16[592,512]{1,0:T(8,128)(2,1)S(1)}, u32[]{:S(2)}, u32[]{:S(2)}) collective-permute-start(bf16[592,512]{1,0:T(8,128)(2,1)S(1)} %get-tuple-element.31), channel_id=1, source_target_pairs={{0,1},{1,0},{2,3},{3,2},{4,5},{5,4},{6,7},{7,6},{8,9},{9,8},{10,11... | collective-permute-start | bytes 1818632 | tf_op jit(solution)/shard_map/ppermute | solution.py:334
  78.4 11.3 %collective-permute-start.7 = (bf16[304,512]{1,0:T(8,128)(2,1)S(1)}, bf16[304,512]{1,0:T(8,128)(2,1)S(1)}, u32[]{:S(2)}, u32[]{:S(2)}) collective-permute-start(bf16[304,512]{1,0:T(8,128)(2,1)S(1)} %get-tuple-element.33), channel_id=1, source_target_pairs={{0,2},{2,0},{1,3},{3,1},{4,6},{6,4},{5,7},{7,5},{8,10},{10,8},{9,1... | collective-permute-start | bytes 933896 | tf_op jit(solution)/shard_map/ppermute | solution.py:343
  91.2 30.2 %all-to-all-start.1 = ((bf16[32,88,128]{2,1,0:T(8,128)(2,1)}), bf16[32,88,128]{2,1,0:T(8,128)(2,1)}, u32[]{:S(2)}, u32[]{:S(2)}) async-start(bf16[32,88,128]{2,1,0:T(8,128)(2,1)} %bitcast.12), calls=%async_computation.1 | async-start | bytes 1441792 | tf_op jit(solution)/shard_map/all_to_all | solution.py:48
  100.9 14.9 %collective-permute-start.10 = (bf16[304,128]{1,0:T(8,128)(2,1)S(1)}, bf16[304,128]{1,0:T(8,128)(2,1)S(1)}, u32[]{:S(2)}, u32[]{:S(2)}) collective-permute-start(bf16[304,128]{1,0:T(8,128)(2,1)S(1)} %get-tuple-element.42), channel_id=1, source_target_pairs={{0,4},{4,8},{8,12},{12,0},{1,5},{5,9},{9,13},{13,1},{2,6},{6,10},{... | collective-permute-start | bytes 233480 | tf_op jit(solution)/shard_map/ppermute | solution.py:234
  105.7 10.1 %collective-permute-start.8 = (bf16[304,128]{1,0:T(8,128)(2,1)S(1)}, bf16[304,128]{1,0:T(8,128)(2,1)S(1)}, u32[]{:S(2)}, u32[]{:S(2)}) collective-permute-start(bf16[304,128]{1,0:T(8,128)(2,1)S(1)} %get-tuple-element.40), channel_id=1, source_target_pairs={{0,12},{4,0},{8,4},{12,8},{1,13},{5,1},{9,5},{13,9},{2,14},{6,2},{... | collective-permute-start | bytes 233480 | tf_op jit(solution)/shard_map/ppermute | solution.py:234
  109.5 10.6 %collective-permute-start.9 = (bf16[304,128]{1,0:T(8,128)(2,1)S(1)}, bf16[304,128]{1,0:T(8,128)(2,1)S(1)}, u32[]{:S(2)}, u32[]{:S(2)}) collective-permute-start(bf16[304,128]{1,0:T(8,128)(2,1)S(1)} %get-tuple-element.41), channel_id=1, source_target_pairs={{0,8},{4,12},{8,0},{12,4},{1,9},{5,13},{9,1},{13,5},{2,10},{6,14},... | collective-permute-start | bytes 233480 | tf_op jit(solution)/shard_map/ppermute | solution.py:234
  120.2 0.6 copy-start.3
  121.4 27.4 %copy-start.4 = (bf16[288,128]{1,0:T(8,128)(2,1)S(1)}, bf16[288,128]{1,0:T(8,128)(2,1)}, u32[]{:S(2)}) copy-start(bf16[288,128]{1,0:T(8,128)(2,1)} %copy-done.3) | copy-start | bytes 221188
  139.8 0.9 copy-start.1
  140.6 25.7 %all-to-all-start.3 = ((bf16[32,88,128]{2,1,0:T(8,128)(2,1)}), bf16[32,88,128]{2,1,0:T(8,128)(2,1)S(1)}, u32[]{:S(2)}, u32[]{:S(2)}) async-start(bf16[32,88,128]{2,1,0:T(8,128)(2,1)} %copy-done.1), calls=%async_computation.3 | async-start | bytes 1441792 | tf_op jit(solution)/shard_map/all_to_all | solution.py:48
  148.8 7.6 %collective-permute-start.11 = (bf16[288,128]{1,0:T(8,128)(2,1)S(1)}, bf16[288,128]{1,0:T(8,128)(2,1)S(1)}, u32[]{:S(2)}, u32[]{:S(2)}) collective-permute-start(bf16[288,128]{1,0:T(8,128)(2,1)S(1)} %copy-done.4), channel_id=1, source_target_pairs={{0,1},{1,0},{2,3},{3,2},{4,5},{5,4},{6,7},{7,6},{8,9},{9,8},{10,11... | collective-permute-start | bytes 221192 | tf_op jit(solution)/shard_map/ppermute | solution.py:377
  150.8 6.6 %collective-permute-start.12 = (bf16[288,128]{1,0:T(8,128)(2,1)S(1)}, bf16[288,128]{1,0:T(8,128)(2,1)S(1)}, u32[]{:S(2)}, u32[]{:S(2)}) collective-permute-start(bf16[288,128]{1,0:T(8,128)(2,1)S(1)} %copy-done.4), channel_id=1, source_target_pairs={{0,2},{1,3},{2,0},{3,1},{4,6},{5,7},{6,4},{7,5},{8,10},{9,11},{10,... | collective-permute-start | bytes 221192 | tf_op jit(solution)/shard_map/ppermute | solution.py:377
  153.9 6.1 %collective-permute-start.13 = (bf16[288,128]{1,0:T(8,128)(2,1)S(1)}, bf16[288,128]{1,0:T(8,128)(2,1)S(1)}, u32[]{:S(2)}, u32[]{:S(2)}) collective-permute-start(bf16[288,128]{1,0:T(8,128)(2,1)S(1)} %copy-done.4), channel_id=1, source_target_pairs={{0,3},{1,2},{2,1},{3,0},{4,7},{5,6},{6,5},{7,4},{8,11},{9,10},{10,... | collective-permute-start | bytes 221192 | tf_op jit(solution)/shard_map/ppermute | solution.py:377

commit v8 on v7

--- a/solution.py
+++ b/solution.py
@@ -60,12 +60,24 @@
 def image_kernel(at_ref, wt_ref, own_ref, fetched_ref, swapped_ref, *refs):
     unit_ref, low_ref, inv_ref, own_unit_ref, cols_ref, feats_ref = refs
     rows = own_ref.shape[0]
-    part = rows // 2
-    c = at_ref[5]
+    low = at_ref[6]
+    beside = pl.multiple_of((1 + 2 * low) * rows, 16)
+    beyond = pl.multiple_of((3 - 2 * low) * rows, 16)
     feats_ref[:rows] = own_ref[...]
-    for k, ref in ((c, fetched_ref), (1 - c, swapped_ref)):
-        feats_ref[pl.ds(pl.multiple_of((1 + 2 * k) * rows, 16), rows), :] = ref[:rows]
-        feats_ref[pl.ds(pl.multiple_of(2 * rows + k * part, 16), part), :] = ref[rows:]
+
+    def place(ends_ref, middle_ref):
+        feats_ref[pl.ds(beside, rows), :] = ends_ref[:rows]
+        feats_ref[pl.ds(beyond, rows), :] = ends_ref[rows:]
+        feats_ref[2 * rows : 3 * rows] = middle_ref[:rows]
+
+    @pl.when(at_ref[5] == 0)
+    def _():
+        place(fetched_ref, swapped_ref)
+
+    @pl.when(at_ref[5] != 0)
+    def _():
+        place(swapped_ref, fetched_ref)
+
     head = lax.dot_general(
         wt_ref[...], feats_ref[...], (((1,), (1,)), ((), ())), preferred_element_type=F32
     )
@@ -264,28 +276,23 @@
     par = jnp.stack([jnp.exp(log_temp[0]), logit_bias[0]])
 
     copies = call(text_kernel, shape((ny * quarter, width), BF16), text_embed)
-    part = rows // nc
     def place(z, low, core):
         return (z % nzh * nzl + low) * nc + core
 
-    near = []
-    cross = []
+    line = ("zh", "zl", "c")
+    fetch = []
     for z in range(nzh):
-        near += [(place(z, 1, k), place(z + 1, k, 0)) for k in range(nc)]
-        near += [(place(z, 0, k), place(z - 1, k, 1)) for k in range(nc)]
-        cross += [(place(z, 1, k), place(z + 2, 0, k)) for k in range(nc)]
-        cross += [(place(z, 0, k), place(z - 2, 1, k)) for k in range(nc)]
-    half_rows = lax.dynamic_slice_in_dim(img_feat, c_at * part, part, 0)
-    line = ("zh", "zl", "c")
-    across = lax.ppermute(half_rows, line, cross)
-    beside = lax.ppermute(img_feat, line, near)
-    fetched = jnp.concatenate([beside, across], axis=0)
+        fetch += [(place(z - 1, 1, 0), place(z, 0, 0)), (place(z + 1, 0, 0), place(z, 1, 0))]
+        fetch += [(place(z - 2, 1, 1), place(z, 0, 1)), (place(z + 2, 0, 1), place(z, 1, 1))]
+    fetched = lax.ppermute(img_feat, line, fetch)
+    across = lax.ppermute(fetched, ("zl", "c"), [(0, 2), (2, 0)])
     own = to_all(copies, "y")
-    own, fetched = lax.optimization_barrier((own, fetched))
+    own, fetched, across = lax.optimization_barrier((own, fetched, across))
+    fetched = jnp.concatenate([fetched, across], axis=0)
+    swapped = lax.ppermute(fetched, "c", [(0, 1), (1, 0)])
     far = shift_by(own, "x", 2)
     left = shift_by(own, "x", 1)
     right = shift_by(own, "x", -1)
-    swapped = lax.ppermute(fetched, "c", [(0, 1), (1, 0)])
 
     unit, low, inv, own_unit, col_unit, feats = call(
         image_kernel,

time: 168 us -> 175 us (1.042)
  waiting for transfers between devices: 40 us -> 50.5 us
  starting transfers between devices: 78.6 us -> 75.2 us
    ppermute x2, waiting for transfers between devices: 8.19 us -> 16.9 us  [the longest x1 10.1 us: local(): fetched = lax.ppermute(img_feat, line, fetch)]
    unnamed x17 -> x16, local copies, waits for them, and re-layouts: 9.54 us -> 9.28 us
  transfers between devices with their start and end apart: 17 -> 17, of which waited for: 9 -> 10; matrix products, arithmetic and copies ran while one was open for 3% -> 2% of each run, Pallas kernels for 5% -> 5%
where the time goes in v8:
time: 175 us; the launch traced here: 174 us
  starting transfers between devices  75.2 us (43%)
  waiting for transfers between devices  50.5 us (29%)
  Pallas kernels  19.6 us (11%)
  blocking collectives  14.9 us (9%)
  local copies, waits for them, and re-layouts  11.1 us (6%)
  between operations  2.25 us (1%)
    all_to_all x3, starting transfers between devices, to_all(): return lax.all_to_all(copies, axes, 0, 0, tiled=True)  24.7 us
    ppermute x6, starting transfers between devices, shift_by(): return lax.ppermute(x, axis, [(k, (k + step) % n) for k in range(n)])  24.2 us
    pallas_call x10, Pallas kernels, call(): pl.pallas_call(body, out_shape=outs, in_specs=specs, out_specs=[VMEM] * l...  17.7 us
    all_to_all x1, blocking collectives, to_all(): return lax.all_to_all(copies, axes, 0, 0, tiled=True)  14.9 us
    ppermute x6, waiting for transfers between devices, shift_by(): return lax.ppermute(x, axis, [(k, (k + step) % n) for k in range(n)])  13.2 us
    ppermute x1, starting transfers between devices, local(): fetched = lax.ppermute(img_feat, line, fetch)  10.9 us
    ppermute x1, waiting for transfers between devices, local(): fetched = lax.ppermute(img_feat, line, fetch)  10.1 us
    ppermute x1, waiting for transfers between devices, local(): got2 = lax.ppermute(send2, 'zl', [(0, 1), (1, 0)])  9.36 us
  transfers between devices with their start and end apart: 17, of which 10 were waited for; matrix products, arithmetic and copies ran while one was open for 2% of the time, Pallas kernels for 5%

profile of v8, /device:TPU:2, one launch (start us, length us, event | category | flops | bytes accessed | tf_op | source)
XLA Modules:
  0.0 173.6 jit_solution(15657467250281165696)
XLA Ops:
  0.7 1.0 copy-done.5
  1.7 1.0 shard_map.76
  2.6 7.1 %all-to-all-start = ((bf16[8,32,1152]{2,1,0:T(8,128)(2,1)}), bf16[8,32,1152]{2,1,0:T(8,128)(2,1)S(1)}, u32[]{:S(2)}, u32[]{:S(2)}) async-start(bf16[8,32,1152]{2,1,0:T(8,128)(2,1)} %bitcast.9), calls=%async_computation | async-start | bytes 1179648 | tf_op jit(solution)/shard_map/all_to_all | solution.py:48
  9.7 10.9 %collective-permute-start = (bf16[128,1152]{1,0:T(8,128)(2,1)}, bf16[128,1152]{1,0:T(8,128)(2,1)S(1)}, u32[]{:S(2)}, u32[]{:S(2)}) collective-permute-start(bf16[128,1152]{1,0:T(8,128)(2,1)} %own_ref.1), channel_id=1, source_target_pairs={{14,0},{4,2},{11,1},{9,3},{2,4},{8,6},{15,5},{13,7},{6,8},{12,10},... | collective-permute-start | bytes 884744 | tf_op jit(solution)/shard_map/ppermute | solution.py:287
  20.7 10.1 %collective-permute-done = bf16[128,1152]{1,0:T(8,128)(2,1)S(1)} collective-permute-done((bf16[128,1152]{1,0:T(8,128)(2,1)}, bf16[128,1152]{1,0:T(8,128)(2,1)S(1)}, u32[]{:S(2)}, u32[]{:S(2)}) %collective-permute-start) | collective-permute-done | bytes 294944 | tf_op jit(solution)/shard_map/ppermute | solution.py:287
  30.7 1.9 %collective-permute-start.1 = (bf16[128,1152]{1,0:T(8,128)(2,1)S(1)}, bf16[128,1152]{1,0:T(8,128)(2,1)}, u32[]{:S(2)}, u32[]{:S(2)}) collective-permute-start(bf16[128,1152]{1,0:T(8,128)(2,1)S(1)} %collective-permute-done), channel_id=1, source_target_pairs={{0,2},{2,0},{4,6},{6,4},{8,10},{10,8},{12,14},{14,12},{16,18},{18,... | collective-permute-start | bytes 884744 | tf_op jit(solution)/shard_map/ppermute | solution.py:288
  32.7 6.8 %collective-permute-done.1 = bf16[128,1152]{1,0:T(8,128)(2,1)} collective-permute-done((bf16[128,1152]{1,0:T(8,128)(2,1)S(1)}, bf16[128,1152]{1,0:T(8,128)(2,1)}, u32[]{:S(2)}, u32[]{:S(2)}) %collective-permute-start.1) | collective-permute-done | bytes 294944 | tf_op jit(solution)/shard_map/ppermute | solution.py:288
  39.5 0.7 constant_dynamic-update-slice_fusion.1
  40.2 1.7 constant_dynamic-update-slice_fusion.fetched_ref
  41.9 1.9 %collective-permute-start.4 = (bf16[256,1152]{1,0:T(8,128)(2,1)}, bf16[256,1152]{1,0:T(8,128)(2,1)}, u32[]{:S(2)}, u32[]{:S(2)}) collective-permute-start(bf16[256,1152]{1,0:T(8,128)(2,1)} %constant_dynamic-update-slice_fusion.fetched_ref), channel_id=1, source_target_pairs={{0,1},{1,0},{2,3},{3,2},{4,5},{5,4},{6,7},{7,6},{8,9},{9,8},{10,11... | collective-permute-start | bytes 1769480 | tf_op jit(solution)/shard_map/ppermute | solution.py:292
  43.8 3.4 %collective-permute-start.5 = (bf16[256,1152]{1,0:T(8,128)(2,1)S(1)}, bf16[256,1152]{1,0:T(8,128)(2,1)}, u32[]{:S(2)}, u32[]{:S(2)}) collective-permute-start(bf16[256,1152]{1,0:T(8,128)(2,1)S(1)} %bitcast.18), channel_id=1, source_target_pairs={{0,16},{16,32},{32,48},{48,0},{1,17},{17,33},{33,49},{49,1},{2,18}... | collective-permute-start | bytes 1769480 | tf_op jit(solution)/shard_map/ppermute | solution.py:246
  47.2 2.4 %collective-permute-start.2 = (bf16[256,1152]{1,0:T(8,128)(2,1)S(1)}, bf16[256,1152]{1,0:T(8,128)(2,1)}, u32[]{:S(2)}, u32[]{:S(2)}) collective-permute-start(bf16[256,1152]{1,0:T(8,128)(2,1)S(1)} %bitcast.19), channel_id=1, source_target_pairs={{0,48},{16,0},{32,16},{48,32},{1,49},{17,1},{33,17},{49,33},{2,50}... | collective-permute-start | bytes 1769480 | tf_op jit(solution)/shard_map/ppermute | solution.py:246
  49.7 4.0 %collective-permute-start.3 = (bf16[256,1152]{1,0:T(8,128)(2,1)S(1)}, bf16[256,1152]{1,0:T(8,128)(2,1)}, u32[]{:S(2)}, u32[]{:S(2)}) collective-permute-start(bf16[256,1152]{1,0:T(8,128)(2,1)S(1)} %bitcast.20), channel_id=1, source_target_pairs={{0,32},{16,48},{32,0},{48,16},{1,33},{17,49},{33,1},{49,17},{2,34}... | collective-permute-start | bytes 1769480 | tf_op jit(solution)/shard_map/ppermute | solution.py:246
  53.7 3.3 %copy.8 = bf16[1152,1152]{0,1:T(8,128)(2,1)} copy(bf16[1152,1152]{1,0:T(8,128)(2,1)S(1)} %copy-done) | data formatting | bytes 5308416 | tf_op args[1]
  58.4 0.1 stack.48.at_ref
  58.5 0.1 pad_maximum_fusion.par_ref
  58.5 1.8 %copy-done.2 = bf16[1152,1152]{0,1:T(8,128)(2,1)S(1)} copy-done((bf16[1152,1152]{0,1:T(8,128)(2,1)S(1)}, bf16[1152,1152]{0,1:T(8,128)(2,1)}, u32[]{:S(2)}) %copy-start.2) | copy-done | bytes 2654232
  60.3 1.0 copy-done.6
  61.3 3.7 %shard_map.77 = (f32[1152,512]{1,0:T(8,128)S(1)}, bf16[1152,512]{1,0:T(8,128)(2,1)S(1)}, f32[1,512]{1,0:T(1,128)S(1)}, f32[288,128]{1,0:T(8,128)S(1)}, f32[288,5...) custom-call(s32[12]{0:T(128)S(1)} %stack.48.at_ref, bf16[1152,1152]{1,0:T(8,128)(2,1)S(1)} %bitcast.17, ...), custom_call_target="tpu_custom_call" | custom-call | flops 1358954496 | bytes 4128816 | tf_op jit(solution)/shard_map/pallas_call | solution.py:24
  64.9 3.5 %shard_map.78 = (f32[1152,512]{1,0:T(8,128)S(1)}, f32[1,512]{1,0:T(1,128)S(1)}) custom-call(s32[12]{0:T(128)S(1)} %stack.48.at_ref, f32[2]{0:T(128)S(1)} %pad_maximum_fusion.par_ref, bf16[256,1152]{1,0:T(8,128)(2,1)S(1)} %bitcast.21, bf16[256,1152]{1,0:T(8,128)(2,1)} %collective-permute-done.5.left_ref, bf16[1152,512]{1,0:T(8,128)(2,1)S(1)} %get-tuple-element.28.low_ref), custom_call_target="tpu_custom_call" | custom-call | flops 1207959552 | bytes 2359352 | tf_op jit(solution)/shard_map/pallas_call | solution.py:24
  68.5 9.5 %collective-permute-done.3.far_ref = bf16[256,1152]{1,0:T(8,128)(2,1)} collective-permute-done((bf16[256,1152]{1,0:T(8,128)(2,1)S(1)}, bf16[256,1152]{1,0:T(8,128)(2,1)}, u32[]{:S(2)}, u32[]{:S(2)}) %collective-permute-start.3) | collective-permute-done | bytes 589856 | tf_op jit(solution)/shard_map/ppermute | solution.py:246
  77.9 3.6 %shard_map.79 = (f32[592,512]{1,0:T(8,128)S(1)}, bf16[592,512]{1,0:T(8,128)(2,1)S(1)}) custom-call(s32[12]{0:T(128)S(1)} %stack.48.at_ref, f32[2]{0:T(128)S(1)} %pad_maximum_fusion.par_ref, bf16[256,1152]{1,0:T(8,128)(2,1)} %collective-permute-done.2.right_ref, bf16[256,1152]{1,0:T(8,128)(2,1)} %collective-permute-done.3.far_ref, ...), custom_call_target="tpu_custom_call" | custom-call | flops 1207959552 | bytes 7079992 | tf_op jit(solution)/shard_map/pallas_call | solution.py:24
  81.5 1.9 %collective-permute-start.6 = (bf16[592,512]{1,0:T(8,128)(2,1)S(1)}, bf16[592,512]{1,0:T(8,128)(2,1)S(1)}, u32[]{:S(2)}, u32[]{:S(2)}) collective-permute-start(bf16[592,512]{1,0:T(8,128)(2,1)S(1)} %get-tuple-element.33), channel_id=1, source_target_pairs={{0,1},{1,0},{2,3},{3,2},{4,5},{5,4},{6,7},{7,6},{8,9},{9,8},{10,11... | collective-permute-start | bytes 1818632 | tf_op jit(solution)/shard_map/ppermute | solution.py:341
  83.4 2.0 %collective-permute-done.6.got_ref = bf16[592,512]{1,0:T(8,128)(2,1)S(1)} collective-permute-done((bf16[592,512]{1,0:T(8,128)(2,1)S(1)}, bf16[592,512]{1,0:T(8,128)(2,1)S(1)}, u32[]{:S(2)}, u32[]{:S(2)}) %collective-permute-start.6) | collective-permute-done | bytes 606240 | tf_op jit(solution)/shard_map/ppermute | solution.py:341
  85.4 0.7 shard_map.80
  86.1 1.9 %collective-permute-start.7 = (bf16[304,512]{1,0:T(8,128)(2,1)S(1)}, bf16[304,512]{1,0:T(8,128)(2,1)S(1)}, u32[]{:S(2)}, u32[]{:S(2)}) collective-permute-start(bf16[304,512]{1,0:T(8,128)(2,1)S(1)} %get-tuple-element.35), channel_id=1, source_target_pairs={{0,2},{2,0},{1,3},{3,1},{4,6},{6,4},{5,7},{7,5},{8,10},{10,8},{9,1... | collective-permute-start | bytes 933896 | tf_op jit(solution)/shard_map/ppermute | solution.py:350
  88.1 9.4 %collective-permute-done.7.got_ref = bf16[304,512]{1,0:T(8,128)(2,1)S(1)} collective-permute-done((bf16[304,512]{1,0:T(8,128)(2,1)S(1)}, bf16[304,512]{1,0:T(8,128)(2,1)S(1)}, u32[]{:S(2)}, u32[]{:S(2)}) %collective-permute-start.7) | collective-permute-done | bytes 311328 | tf_op jit(solution)/shard_map/ppermute | solution.py:350
  97.4 1.5 shard_map.81
  98.9 9.4 %all-to-all-start.1 = ((bf16[32,88,128]{2,1,0:T(8,128)(2,1)}), bf16[32,88,128]{2,1,0:T(8,128)(2,1)}, u32[]{:S(2)}, u32[]{:S(2)}) async-start(bf16[32,88,128]{2,1,0:T(8,128)(2,1)} %bitcast.12), calls=%async_computation.1 | async-start | bytes 1441792 | tf_op jit(solution)/shard_map/all_to_all | solution.py:48
  108.3 2.2 %collective-permute-start.10 = (bf16[304,128]{1,0:T(8,128)(2,1)S(1)}, bf16[304,128]{1,0:T(8,128)(2,1)S(1)}, u32[]{:S(2)}, u32[]{:S(2)}) collective-permute-start(bf16[304,128]{1,0:T(8,128)(2,1)S(1)} %get-tuple-element.44), channel_id=1, source_target_pairs={{0,4},{4,8},{8,12},{12,0},{1,5},{5,9},{9,13},{13,1},{2,6},{6,10},{... | collective-permute-start | bytes 233480 | tf_op jit(solution)/shard_map/ppermute | solution.py:246
  110.6 5.7 %collective-permute-start.8 = (bf16[304,128]{1,0:T(8,128)(2,1)S(1)}, bf16[304,128]{1,0:T(8,128)(2,1)S(1)}, u32[]{:S(2)}, u32[]{:S(2)}) collective-permute-start(bf16[304,128]{1,0:T(8,128)(2,1)S(1)} %get-tuple-element.42), channel_id=1, source_target_pairs={{0,12},{4,0},{8,4},{12,8},{1,13},{5,1},{9,5},{13,9},{2,14},{6,2},{... | collective-permute-start | bytes 233480 | tf_op jit(solution)/shard_map/ppermute | solution.py:246
  116.3 6.4 %collective-permute-start.9 = (bf16[304,128]{1,0:T(8,128)(2,1)S(1)}, bf16[304,128]{1,0:T(8,128)(2,1)S(1)}, u32[]{:S(2)}, u32[]{:S(2)}) collective-permute-start(bf16[304,128]{1,0:T(8,128)(2,1)S(1)} %get-tuple-element.43), channel_id=1, source_target_pairs={{0,8},{4,12},{8,0},{12,4},{1,9},{5,13},{9,1},{13,5},{2,10},{6,14},... | collective-permute-start | bytes 233480 | tf_op jit(solution)/shard_map/ppermute | solution.py:246
  122.8 3.8 %collective-permute-done.9.refs_2_ = bf16[304,128]{1,0:T(8,128)(2,1)S(1)} collective-permute-done((bf16[304,128]{1,0:T(8,128)(2,1)S(1)}, bf16[304,128]{1,0:T(8,128)(2,1)S(1)}, u32[]{:S(2)}, u32[]{:S(2)}) %collective-permute-start.9) | collective-permute-done | bytes 77856 | tf_op jit(solution)/shard_map/ppermute | solution.py:246
  126.6 0.6 copy-done.3
  127.2 1.7 all-to-all-done.1.parts_ref
  128.9 1.9 %shard_map.83 = f32[4,88,128]{2,1,0:T(8,128)} custom-call(bf16[32,88,128]{2,1,0:T(8,128)(2,1)} %all-to-all-done.1.parts_ref, bf16[288,128]{1,0:T(8,128)(2,1)} %copy-done.3), custom_call_target="tpu_custom_call" | custom-call | tf_op jit(solution)/shard_map/pallas_call | solution.py:366
  130.9 14.9 %all_to_all.34.parts_ref = f32[4,88,128]{2,1,0:T(8,128)S(1)} all-to-all(f32[4,88,128]{2,1,0:T(8,128)} %shard_map.83), channel_id=1, replica_groups=mesh['y'=8,'x'=4,'zh'=4,'zl'=2,'c'=2] {'zh'}, dimensions={0} | all-to-all | bytes 360448 | tf_op jit(solution)/shard_map/all_to_all | solution.py:48
  145.8 0.6 shard_map.84
  146.4 0.9 copy-done.1
  147.2 8.2 %all-to-all-start.3 = ((bf16[32,88,128]{2,1,0:T(8,128)(2,1)}), bf16[32,88,128]{2,1,0:T(8,128)(2,1)S(1)}, u32[]{:S(2)}, u32[]{:S(2)}) async-start(bf16[32,88,128]{2,1,0:T(8,128)(2,1)} %copy-done.1), calls=%async_computation.3 | async-start | bytes 1441792 | tf_op jit(solution)/shard_map/all_to_all | solution.py:48
  155.5 1.9 %collective-permute-start.11 = (bf16[288,128]{1,0:T(8,128)(2,1)S(1)}, bf16[288,128]{1,0:T(8,128)(2,1)S(1)}, u32[]{:S(2)}, u32[]{:S(2)}) collective-permute-start(bf16[288,128]{1,0:T(8,128)(2,1)S(1)} %copy-done.4), channel_id=1, source_target_pairs={{0,1},{1,0},{2,3},{3,2},{4,5},{5,4},{6,7},{7,6},{8,9},{9,8},{10,11... | collective-permute-start | bytes 221192 | tf_op jit(solution)/shard_map/ppermute | solution.py:384
  157.4 3.0 %collective-permute-start.12 = (bf16[288,128]{1,0:T(8,128)(2,1)S(1)}, bf16[288,128]{1,0:T(8,128)(2,1)S(1)}, u32[]{:S(2)}, u32[]{:S(2)}) collective-permute-start(bf16[288,128]{1,0:T(8,128)(2,1)S(1)} %copy-done.4), channel_id=1, source_target_pairs={{0,2},{1,3},{2,0},{3,1},{4,6},{5,7},{6,4},{7,5},{8,10},{9,11},{10,... | collective-permute-start | bytes 221192 | tf_op jit(solution)/shard_map/ppermute | solution.py:384
  160.4 2.7 %collective-permute-start.13 = (bf16[288,128]{1,0:T(8,128)(2,1)S(1)}, bf16[288,128]{1,0:T(8,128)(2,1)S(1)}, u32[]{:S(2)}, u32[]{:S(2)}) collective-permute-start(bf16[288,128]{1,0:T(8,128)(2,1)S(1)} %copy-done.4), channel_id=1, source_target_pairs={{0,3},{1,2},{2,1},{3,0},{4,7},{5,6},{6,5},{7,4},{8,11},{9,10},{10,... | collective-permute-start | bytes 221192 | tf_op jit(solution)/shard_map/ppermute | solution.py:384
  163.1 0.9 collective-permute-done.12.refs_2_
  164.0 2.6 %collective-permute-done.13.refs_3_ = bf16[288,128]{1,0:T(8,128)(2,1)S(1)} collective-permute-done((bf16[288,128]{1,0:T(8,128)(2,1)S(1)}, bf16[288,128]{1,0:T(8,128)(2,1)S(1)}, u32[]{:S(2)}, u32[]{:S(2)}) %collective-permute-start.13) | collective-permute-done | bytes 73760 | tf_op jit(solution)/shard_map/ppermute | solution.py:384
  166.6 2.2 %shard_map.86 = bf16[128,1152]{1,0:T(8,128)(2,1)} custom-call(s32[12]{0:T(128)S(1)} %stack.48.at_ref, bf16[1152,1152]{1,0:T(8,128)(2,1)S(1)} %copy-done, bf16[288,128]{1,0:T(8,128)(2,1)S(1)} %copy-done.4, bf16[288,128]{1,0:T(8,128)(2,1)S(1)} %collective-permute-done.11.refs_1_, bf16[288,128]{1,0:T(8,128)(2,1)S(1)} %collective-permute-done.12.refs_2_, ...), custom_call_target="tpu_custom_call" | custom-call | flops 339738624 | bytes 2949168 | tf_op jit(solution)/shard_map/pallas_call | solution.py:24
  168.8 3.9 %all-to-all-done.3 = bf16[32,88,128]{2,1,0:T(8,128)(2,1)S(1)} async-done(((bf16[32,88,128]{2,1,0:T(8,128)(2,1)}), bf16[32,88,128]{2,1,0:T(8,128)(2,1)S(1)}, u32[]{:S(2)}, u32[]{:S(2)}) %all-to-all-start.3) | async-done | bytes 720928 | tf_op jit(solution)/shard_map/all_to_all | solution.py:48
  172.7 1.0 shard_map.85
  (17 shorter events, 0.1 us)
Async XLA Ops:
  0.6 53.1 %copy-start = (bf16[1152,1152]{1,0:T(8,128)(2,1)S(1)}, bf16[1152,1152]{1,0:T(8,128)(2,1)}, u32[]{:S(2)}) copy-start(bf16[1152,1152]{1,0:T(8,128)(2,1)} %weight_ref.1) | copy-start | bytes 7962628
  0.6 1.0 copy-start.5
  2.6 36.8 %all-to-all-start = ((bf16[8,32,1152]{2,1,0:T(8,128)(2,1)}), bf16[8,32,1152]{2,1,0:T(8,128)(2,1)S(1)}, u32[]{:S(2)}, u32[]{:S(2)}) async-start(bf16[8,32,1152]{2,1,0:T(8,128)(2,1)} %bitcast.9), calls=%async_computation | async-start | bytes 1179648 | tf_op jit(solution)/shard_map/all_to_all | solution.py:48
  9.7 21.0 %collective-permute-start = (bf16[128,1152]{1,0:T(8,128)(2,1)}, bf16[128,1152]{1,0:T(8,128)(2,1)S(1)}, u32[]{:S(2)}, u32[]{:S(2)}) collective-permute-start(bf16[128,1152]{1,0:T(8,128)(2,1)} %own_ref.1), channel_id=1, source_target_pairs={{14,0},{4,2},{11,1},{9,3},{2,4},{8,6},{15,5},{13,7},{6,8},{12,10},... | collective-permute-start | bytes 884744 | tf_op jit(solution)/shard_map/ppermute | solution.py:287
  30.7 8.7 %collective-permute-start.1 = (bf16[128,1152]{1,0:T(8,128)(2,1)S(1)}, bf16[128,1152]{1,0:T(8,128)(2,1)}, u32[]{:S(2)}, u32[]{:S(2)}) collective-permute-start(bf16[128,1152]{1,0:T(8,128)(2,1)S(1)} %collective-permute-done), channel_id=1, source_target_pairs={{0,2},{2,0},{4,6},{6,4},{8,10},{10,8},{12,14},{14,12},{16,18},{18,... | collective-permute-start | bytes 884744 | tf_op jit(solution)/shard_map/ppermute | solution.py:288
  41.9 16.7 %collective-permute-start.4 = (bf16[256,1152]{1,0:T(8,128)(2,1)}, bf16[256,1152]{1,0:T(8,128)(2,1)}, u32[]{:S(2)}, u32[]{:S(2)}) collective-permute-start(bf16[256,1152]{1,0:T(8,128)(2,1)} %constant_dynamic-update-slice_fusion.fetched_ref), channel_id=1, source_target_pairs={{0,1},{1,0},{2,3},{3,2},{4,5},{5,4},{6,7},{7,6},{8,9},{9,8},{10,11... | collective-permute-start | bytes 1769480 | tf_op jit(solution)/shard_map/ppermute | solution.py:292
  43.8 21.1 %collective-permute-start.5 = (bf16[256,1152]{1,0:T(8,128)(2,1)S(1)}, bf16[256,1152]{1,0:T(8,128)(2,1)}, u32[]{:S(2)}, u32[]{:S(2)}) collective-permute-start(bf16[256,1152]{1,0:T(8,128)(2,1)S(1)} %bitcast.18), channel_id=1, source_target_pairs={{0,16},{16,32},{32,48},{48,0},{1,17},{17,33},{33,49},{49,1},{2,18}... | collective-permute-start | bytes 1769480 | tf_op jit(solution)/shard_map/ppermute | solution.py:246
  47.2 21.3 %collective-permute-start.2 = (bf16[256,1152]{1,0:T(8,128)(2,1)S(1)}, bf16[256,1152]{1,0:T(8,128)(2,1)}, u32[]{:S(2)}, u32[]{:S(2)}) collective-permute-start(bf16[256,1152]{1,0:T(8,128)(2,1)S(1)} %bitcast.19), channel_id=1, source_target_pairs={{0,48},{16,0},{32,16},{48,32},{1,49},{17,1},{33,17},{49,33},{2,50}... | collective-permute-start | bytes 1769480 | tf_op jit(solution)/shard_map/ppermute | solution.py:246
  49.7 28.3 %collective-permute-start.3 = (bf16[256,1152]{1,0:T(8,128)(2,1)S(1)}, bf16[256,1152]{1,0:T(8,128)(2,1)}, u32[]{:S(2)}, u32[]{:S(2)}) collective-permute-start(bf16[256,1152]{1,0:T(8,128)(2,1)S(1)} %bitcast.20), channel_id=1, source_target_pairs={{0,32},{16,48},{32,0},{48,16},{1,33},{17,49},{33,1},{49,17},{2,34}... | collective-permute-start | bytes 1769480 | tf_op jit(solution)/shard_map/ppermute | solution.py:246
  58.5 1.8 %copy-start.2 = (bf16[1152,1152]{0,1:T(8,128)(2,1)S(1)}, bf16[1152,1152]{0,1:T(8,128)(2,1)}, u32[]{:S(2)}) copy-start(bf16[1152,1152]{0,1:T(8,128)(2,1)} %copy.8) | copy-start | bytes 7962628
  60.3 1.0 copy-start.6
  81.5 3.9 %collective-permute-start.6 = (bf16[592,512]{1,0:T(8,128)(2,1)S(1)}, bf16[592,512]{1,0:T(8,128)(2,1)S(1)}, u32[]{:S(2)}, u32[]{:S(2)}) collective-permute-start(bf16[592,512]{1,0:T(8,128)(2,1)S(1)} %get-tuple-element.33), channel_id=1, source_target_pairs={{0,1},{1,0},{2,3},{3,2},{4,5},{5,4},{6,7},{7,6},{8,9},{9,8},{10,11... | collective-permute-start | bytes 1818632 | tf_op jit(solution)/shard_map/ppermute | solution.py:341
  86.1 11.3 %collective-permute-start.7 = (bf16[304,512]{1,0:T(8,128)(2,1)S(1)}, bf16[304,512]{1,0:T(8,128)(2,1)S(1)}, u32[]{:S(2)}, u32[]{:S(2)}) collective-permute-start(bf16[304,512]{1,0:T(8,128)(2,1)S(1)} %get-tuple-element.35), channel_id=1, source_target_pairs={{0,2},{2,0},{1,3},{3,1},{4,6},{6,4},{5,7},{7,5},{8,10},{10,8},{9,1... | collective-permute-start | bytes 933896 | tf_op jit(solution)/shard_map/ppermute | solution.py:350
  98.9 30.0 %all-to-all-start.1 = ((bf16[32,88,128]{2,1,0:T(8,128)(2,1)}), bf16[32,88,128]{2,1,0:T(8,128)(2,1)}, u32[]{:S(2)}, u32[]{:S(2)}) async-start(bf16[32,88,128]{2,1,0:T(8,128)(2,1)} %bitcast.12), calls=%async_computation.1 | async-start | bytes 1441792 | tf_op jit(solution)/shard_map/all_to_all | solution.py:48
  108.3 14.4 %collective-permute-start.10 = (bf16[304,128]{1,0:T(8,128)(2,1)S(1)}, bf16[304,128]{1,0:T(8,128)(2,1)S(1)}, u32[]{:S(2)}, u32[]{:S(2)}) collective-permute-start(bf16[304,128]{1,0:T(8,128)(2,1)S(1)} %get-tuple-element.44), channel_id=1, source_target_pairs={{0,4},{4,8},{8,12},{12,0},{1,5},{5,9},{9,13},{13,1},{2,6},{6,10},{... | collective-permute-start | bytes 233480 | tf_op jit(solution)/shard_map/ppermute | solution.py:246
  110.6 12.2 %collective-permute-start.8 = (bf16[304,128]{1,0:T(8,128)(2,1)S(1)}, bf16[304,128]{1,0:T(8,128)(2,1)S(1)}, u32[]{:S(2)}, u32[]{:S(2)}) collective-permute-start(bf16[304,128]{1,0:T(8,128)(2,1)S(1)} %get-tuple-element.42), channel_id=1, source_target_pairs={{0,12},{4,0},{8,4},{12,8},{1,13},{5,1},{9,5},{13,9},{2,14},{6,2},{... | collective-permute-start | bytes 233480 | tf_op jit(solution)/shard_map/ppermute | solution.py:246
  116.3 10.2 %collective-permute-start.9 = (bf16[304,128]{1,0:T(8,128)(2,1)S(1)}, bf16[304,128]{1,0:T(8,128)(2,1)S(1)}, u32[]{:S(2)}, u32[]{:S(2)}) collective-permute-start(bf16[304,128]{1,0:T(8,128)(2,1)S(1)} %get-tuple-element.43), channel_id=1, source_target_pairs={{0,8},{4,12},{8,0},{12,4},{1,9},{5,13},{9,1},{13,5},{2,10},{6,14},... | collective-permute-start | bytes 233480 | tf_op jit(solution)/shard_map/ppermute | solution.py:246
  126.6 0.6 copy-start.3
  128.9 26.5 %copy-start.4 = (bf16[288,128]{1,0:T(8,128)(2,1)S(1)}, bf16[288,128]{1,0:T(8,128)(2,1)}, u32[]{:S(2)}) copy-start(bf16[288,128]{1,0:T(8,128)(2,1)} %copy-done.3) | copy-start | bytes 221188
  146.4 0.9 copy-start.1
  147.2 25.4 %all-to-all-start.3 = ((bf16[32,88,128]{2,1,0:T(8,128)(2,1)}), bf16[32,88,128]{2,1,0:T(8,128)(2,1)S(1)}, u32[]{:S(2)}, u32[]{:S(2)}) async-start(bf16[32,88,128]{2,1,0:T(8,128)(2,1)} %copy-done.1), calls=%async_computation.3 | async-start | bytes 1441792 | tf_op jit(solution)/shard_map/all_to_all | solution.py:48
  155.5 7.6 %collective-permute-start.11 = (bf16[288,128]{1,0:T(8,128)(2,1)S(1)}, bf16[288,128]{1,0:T(8,128)(2,1)S(1)}, u32[]{:S(2)}, u32[]{:S(2)}) collective-permute-start(bf16[288,128]{1,0:T(8,128)(2,1)S(1)} %copy-done.4), channel_id=1, source_target_pairs={{0,1},{1,0},{2,3},{3,2},{4,5},{5,4},{6,7},{7,6},{8,9},{9,8},{10,11... | collective-permute-start | bytes 221192 | tf_op jit(solution)/shard_map/ppermute | solution.py:384
  157.4 6.6 %collective-permute-start.12 = (bf16[288,128]{1,0:T(8,128)(2,1)S(1)}, bf16[288,128]{1,0:T(8,128)(2,1)S(1)}, u32[]{:S(2)}, u32[]{:S(2)}) collective-permute-start(bf16[288,128]{1,0:T(8,128)(2,1)S(1)} %copy-done.4), channel_id=1, source_target_pairs={{0,2},{1,3},{2,0},{3,1},{4,6},{5,7},{6,4},{7,5},{8,10},{9,11},{10,... | collective-permute-start | bytes 221192 | tf_op jit(solution)/shard_map/ppermute | solution.py:384
  160.4 6.1 %collective-permute-start.13 = (bf16[288,128]{1,0:T(8,128)(2,1)S(1)}, bf16[288,128]{1,0:T(8,128)(2,1)S(1)}, u32[]{:S(2)}, u32[]{:S(2)}) collective-permute-start(bf16[288,128]{1,0:T(8,128)(2,1)S(1)} %copy-done.4), channel_id=1, source_target_pairs={{0,3},{1,2},{2,1},{3,0},{4,7},{5,6},{6,5},{7,4},{8,11},{9,10},{10,... | collective-permute-start | bytes 221192 | tf_op jit(solution)/shard_map/ppermute | solution.py:384

commit v9 on v7

--- a/solution.py
+++ b/solution.py
@@ -281,7 +281,6 @@
     beside = lax.ppermute(img_feat, line, near)
     fetched = jnp.concatenate([beside, across], axis=0)
     own = to_all(copies, "y")
-    own, fetched = lax.optimization_barrier((own, fetched))
     far = shift_by(own, "x", 2)
     left = shift_by(own, "x", 1)
     right = shift_by(own, "x", -1)
@@ -303,7 +302,7 @@
         fetched,
         swapped,
         smem=1,
-        flops=2 * width * width * images,
+        flops=2 * width,
     )
     acc, loss_row = call(
         first_kernel,

time: 168 us -> 159 us (0.946)
  waiting for transfers between devices: 40 us -> 33.4 us
    ppermute x1, waiting for transfers between devices: 8.19 us -> 0.01 us  [local(): across = lax.ppermute(half_rows, line, cross)]
    ppermute x1, waiting for transfers between devices: 0.01 us -> 3.99 us  [local(): beside = lax.ppermute(img_feat, line, near)]
    all_to_all x3, starting transfers between devices: 24.9 us -> 22.6 us  [to_all(): return lax.all_to_all(copies, axes, 0, 0, tiled=True)]
    unnamed x17 -> x16, local copies, waits for them, and re-layouts: 9.54 us -> 7.61 us
  transfers between devices with their start and end apart: 17 -> 17, of which waited for: 9 -> 8; matrix products, arithmetic and copies ran while one was open for 3% -> 3% of each run, Pallas kernels for 5% -> 6%
where the time goes in v9:
time: 159 us; the launch traced here: 158 us
  starting transfers between devices  77.2 us (49%)
  waiting for transfers between devices  33.4 us (21%)
  Pallas kernels  19.5 us (12%)
  blocking collectives  15.8 us (10%)
  local copies, waits for them, and re-layouts  9.56 us (6%)
  between operations  2.29 us (1%)
    ppermute x6, starting transfers between devices, shift_by(): return lax.ppermute(x, axis, [(k, (k + step) % n) for k in range(n)])  24.5 us
    all_to_all x3, starting transfers between devices, to_all(): return lax.all_to_all(copies, axes, 0, 0, tiled=True)  22.6 us
    pallas_call x10, Pallas kernels, call(): pl.pallas_call(body, out_shape=outs, in_specs=specs, out_specs=[VMEM] * l...  17.6 us
    all_to_all x1, blocking collectives, to_all(): return lax.all_to_all(copies, axes, 0, 0, tiled=True)  15.8 us
    ppermute x6, waiting for transfers between devices, shift_by(): return lax.ppermute(x, axis, [(k, (k + step) % n) for k in range(n)])  12.3 us
    ppermute x1, starting transfers between devices, local(): beside = lax.ppermute(img_feat, line, near)  10.1 us
    ppermute x3, starting transfers between devices, local(): lax.ppermute(back, ('zl', 'c'), [(k, k ^ d) for k in range(nrep)])  7.67 us
    ppermute x1, waiting for transfers between devices, local(): got2 = lax.ppermute(send2, 'zl', [(0, 1), (1, 0)])  7.64 us
  transfers between devices with their start and end apart: 17, of which 8 were waited for; matrix products, arithmetic and copies ran while one was open for 3% of the time, Pallas kernels for 6%

profile of v9, /device:TPU:2, one launch (start us, length us, event | category | flops | bytes accessed | tf_op | source)
XLA Modules:
  0.0 157.9 jit_solution(12107121347721905910)
XLA Ops:
  0.7 1.0 copy-done.6
  1.7 1.0 shard_map.76
  2.6 7.1 %all-to-all-start = ((bf16[8,32,1152]{2,1,0:T(8,128)(2,1)}), bf16[8,32,1152]{2,1,0:T(8,128)(2,1)}, u32[]{:S(2)}, u32[]{:S(2)}) async-start(bf16[8,32,1152]{2,1,0:T(8,128)(2,1)} %bitcast.9), calls=%async_computation | async-start | bytes 1179648 | tf_op jit(solution)/shard_map/all_to_all | solution.py:48
  9.7 10.1 %collective-permute-start.2 = (bf16[128,1152]{1,0:T(8,128)(2,1)}, bf16[128,1152]{1,0:T(8,128)(2,1)S(1)}, u32[]{:S(2)}, u32[]{:S(2)}) collective-permute-start(bf16[128,1152]{1,0:T(8,128)(2,1)} %own_ref.1), channel_id=1, source_target_pairs={{2,4},{3,6},{0,13},{1,15},{6,8},{7,10},{4,1},{5,3},{10,12},{11,14}... | collective-permute-start | bytes 884744 | tf_op jit(solution)/shard_map/ppermute | solution.py:281
  19.8 0.9 constant_dynamic-slice_fusion
  20.8 4.2 %collective-permute-start.3 = (bf16[64,1152]{1,0:T(8,128)(2,1)S(1)}, bf16[64,1152]{1,0:T(8,128)(2,1)}, u32[]{:S(2)}, u32[]{:S(2)}) collective-permute-start(bf16[64,1152]{1,0:T(8,128)(2,1)S(1)} %constant_dynamic-slice_fusion), channel_id=1, source_target_pairs={{2,8},{3,9},{0,10},{1,11},{6,12},{7,13},{4,14},{5,15},{10,0},{11,1... | collective-permute-start | bytes 442376 | tf_op jit(solution)/shard_map/ppermute | solution.py:280
  25.0 4.0 %collective-permute-done.2 = bf16[128,1152]{1,0:T(8,128)(2,1)S(1)} collective-permute-done((bf16[128,1152]{1,0:T(8,128)(2,1)}, bf16[128,1152]{1,0:T(8,128)(2,1)S(1)}, u32[]{:S(2)}, u32[]{:S(2)}) %collective-permute-start.2) | collective-permute-done | bytes 294944 | tf_op jit(solution)/shard_map/ppermute | solution.py:281
  29.0 3.4 %collective-permute-start.5 = (bf16[256,1152]{1,0:T(8,128)(2,1)}, bf16[256,1152]{1,0:T(8,128)(2,1)}, u32[]{:S(2)}, u32[]{:S(2)}) collective-permute-start(bf16[256,1152]{1,0:T(8,128)(2,1)} %bitcast.10.own_ref), channel_id=1, source_target_pairs={{0,16},{16,32},{32,48},{48,0},{1,17},{17,33},{33,49},{49,1},{2,18}... | collective-permute-start | bytes 1769480 | tf_op jit(solution)/shard_map/ppermute | solution.py:234
  32.4 2.4 %collective-permute-start = (bf16[256,1152]{1,0:T(8,128)(2,1)}, bf16[256,1152]{1,0:T(8,128)(2,1)}, u32[]{:S(2)}, u32[]{:S(2)}) collective-permute-start(bf16[256,1152]{1,0:T(8,128)(2,1)} %bitcast.10.own_ref), channel_id=1, source_target_pairs={{0,48},{16,0},{32,16},{48,32},{1,49},{17,1},{33,17},{49,33},{2,50}... | collective-permute-start | bytes 1769480 | tf_op jit(solution)/shard_map/ppermute | solution.py:234
  34.9 4.0 %collective-permute-start.1 = (bf16[256,1152]{1,0:T(8,128)(2,1)}, bf16[256,1152]{1,0:T(8,128)(2,1)}, u32[]{:S(2)}, u32[]{:S(2)}) collective-permute-start(bf16[256,1152]{1,0:T(8,128)(2,1)} %bitcast.10.own_ref), channel_id=1, source_target_pairs={{0,32},{16,48},{32,0},{48,16},{1,33},{17,49},{33,1},{49,17},{2,34}... | collective-permute-start | bytes 1769480 | tf_op jit(solution)/shard_map/ppermute | solution.py:234
  38.9 0.9 constant_dynamic-update-slice_fusion.fetched_ref
  39.9 1.9 %collective-permute-start.4 = (bf16[192,1152]{1,0:T(8,128)(2,1)S(1)}, bf16[192,1152]{1,0:T(8,128)(2,1)}, u32[]{:S(2)}, u32[]{:S(2)}) collective-permute-start(bf16[192,1152]{1,0:T(8,128)(2,1)S(1)} %constant_dynamic-update-slice_fusion.fetched_ref), channel_id=1, source_target_pairs={{0,1},{1,0},{2,3},{3,2},{4,5},{5,4},{6,7},{7,6},{8,9},{9,8},{10,11... | collective-permute-start | bytes 1327112 | tf_op jit(solution)/shard_map/ppermute | solution.py:287
  41.8 0.0 copy-start.3
  41.8 3.3 %copy.8 = bf16[1152,1152]{0,1:T(8,128)(2,1)} copy(bf16[1152,1152]{1,0:T(8,128)(2,1)S(1)} %copy-done) | data formatting | bytes 5308416 | tf_op args[1]
  46.5 0.1 stack.48.at_ref
  46.5 0.1 pad_maximum_fusion.par_ref
  46.6 1.8 %copy-done.1 = bf16[1152,1152]{0,1:T(8,128)(2,1)S(1)} copy-done((bf16[1152,1152]{0,1:T(8,128)(2,1)S(1)}, bf16[1152,1152]{0,1:T(8,128)(2,1)}, u32[]{:S(2)}) %copy-start.1) | copy-done | bytes 2654232
  48.4 3.4 %shard_map.77 = (f32[1152,512]{1,0:T(8,128)S(1)}, bf16[1152,512]{1,0:T(8,128)(2,1)S(1)}, f32[1,512]{1,0:T(1,128)S(1)}, f32[288,128]{1,0:T(8,128)S(1)}, f32[288,5...) custom-call(s32[12]{0:T(128)S(1)} %stack.48.at_ref, bf16[1152,1152]{1,0:T(8,128)(2,1)S(1)} %bitcast.16, ...), custom_call_target="tpu_custom_call" | custom-call | flops 2304 | bytes 3833904 | tf_op jit(solution)/shard_map/pallas_call | solution.py:24
  51.8 3.7 %shard_map.78 = (f32[1152,512]{1,0:T(8,128)S(1)}, f32[1,512]{1,0:T(1,128)S(1)}) custom-call(s32[12]{0:T(128)S(1)} %stack.48.at_ref, f32[2]{0:T(128)S(1)} %pad_maximum_fusion.par_ref, bf16[256,1152]{1,0:T(8,128)(2,1)} %bitcast.10.own_ref, bf16[256,1152]{1,0:T(8,128)(2,1)} %collective-permute-done.5.left_ref, bf16[1152,512]{1,0:T(8,128)(2,1)S(1)} %get-tuple-element.22.low_ref), custom_call_target="tpu_custom_call" | custom-call | flops 1207959552 | bytes 2359352 | tf_op jit(solution)/shard_map/pallas_call | solution.py:24
  55.5 7.0 %collective-permute-done.1.far_ref = bf16[256,1152]{1,0:T(8,128)(2,1)} collective-permute-done((bf16[256,1152]{1,0:T(8,128)(2,1)}, bf16[256,1152]{1,0:T(8,128)(2,1)}, u32[]{:S(2)}, u32[]{:S(2)}) %collective-permute-start.1) | collective-permute-done | bytes 589856 | tf_op jit(solution)/shard_map/ppermute | solution.py:234
  62.6 3.5 %shard_map.79 = (f32[592,512]{1,0:T(8,128)S(1)}, bf16[592,512]{1,0:T(8,128)(2,1)S(1)}) custom-call(s32[12]{0:T(128)S(1)} %stack.48.at_ref, f32[2]{0:T(128)S(1)} %pad_maximum_fusion.par_ref, bf16[256,1152]{1,0:T(8,128)(2,1)} %collective-permute-done.right_ref, bf16[256,1152]{1,0:T(8,128)(2,1)} %collective-permute-done.1.far_ref, ...), custom_call_target="tpu_custom_call" | custom-call | flops 1207959552 | bytes 7079992 | tf_op jit(solution)/shard_map/pallas_call | solution.py:24
  66.1 1.9 %collective-permute-start.6 = (bf16[592,512]{1,0:T(8,128)(2,1)S(1)}, bf16[592,512]{1,0:T(8,128)(2,1)S(1)}, u32[]{:S(2)}, u32[]{:S(2)}) collective-permute-start(bf16[592,512]{1,0:T(8,128)(2,1)S(1)} %get-tuple-element.27), channel_id=1, source_target_pairs={{0,1},{1,0},{2,3},{3,2},{4,5},{5,4},{6,7},{7,6},{8,9},{9,8},{10,11... | collective-permute-start | bytes 1818632 | tf_op jit(solution)/shard_map/ppermute | solution.py:333
  68.1 2.0 %collective-permute-done.6.got_ref = bf16[592,512]{1,0:T(8,128)(2,1)S(1)} collective-permute-done((bf16[592,512]{1,0:T(8,128)(2,1)S(1)}, bf16[592,512]{1,0:T(8,128)(2,1)S(1)}, u32[]{:S(2)}, u32[]{:S(2)}) %collective-permute-start.6) | collective-permute-done | bytes 606240 | tf_op jit(solution)/shard_map/ppermute | solution.py:333
  70.0 0.7 shard_map.80
  70.7 4.3 %collective-permute-start.7 = (bf16[304,512]{1,0:T(8,128)(2,1)S(1)}, bf16[304,512]{1,0:T(8,128)(2,1)S(1)}, u32[]{:S(2)}, u32[]{:S(2)}) collective-permute-start(bf16[304,512]{1,0:T(8,128)(2,1)S(1)} %get-tuple-element.29), channel_id=1, source_target_pairs={{0,2},{2,0},{1,3},{3,1},{4,6},{6,4},{5,7},{7,5},{8,10},{10,8},{9,1... | collective-permute-start | bytes 933896 | tf_op jit(solution)/shard_map/ppermute | solution.py:342
  75.0 7.6 %collective-permute-done.7.got_ref = bf16[304,512]{1,0:T(8,128)(2,1)S(1)} collective-permute-done((bf16[304,512]{1,0:T(8,128)(2,1)S(1)}, bf16[304,512]{1,0:T(8,128)(2,1)S(1)}, u32[]{:S(2)}, u32[]{:S(2)}) %collective-permute-start.7) | collective-permute-done | bytes 311328 | tf_op jit(solution)/shard_map/ppermute | solution.py:342
  82.7 1.5 shard_map.81
  84.1 8.0 %all-to-all-start.1 = ((bf16[32,88,128]{2,1,0:T(8,128)(2,1)}), bf16[32,88,128]{2,1,0:T(8,128)(2,1)}, u32[]{:S(2)}, u32[]{:S(2)}) async-start(bf16[32,88,128]{2,1,0:T(8,128)(2,1)} %bitcast.12), calls=%async_computation.1 | async-start | bytes 1441792 | tf_op jit(solution)/shard_map/all_to_all | solution.py:48
  92.2 5.6 %collective-permute-start.10 = (bf16[304,128]{1,0:T(8,128)(2,1)S(1)}, bf16[304,128]{1,0:T(8,128)(2,1)S(1)}, u32[]{:S(2)}, u32[]{:S(2)}) collective-permute-start(bf16[304,128]{1,0:T(8,128)(2,1)S(1)} %get-tuple-element.38), channel_id=1, source_target_pairs={{0,4},{4,8},{8,12},{12,0},{1,5},{5,9},{9,13},{13,1},{2,6},{6,10},{... | collective-permute-start | bytes 233480 | tf_op jit(solution)/shard_map/ppermute | solution.py:234
  97.8 3.7 %collective-permute-start.8 = (bf16[304,128]{1,0:T(8,128)(2,1)S(1)}, bf16[304,128]{1,0:T(8,128)(2,1)S(1)}, u32[]{:S(2)}, u32[]{:S(2)}) collective-permute-start(bf16[304,128]{1,0:T(8,128)(2,1)S(1)} %get-tuple-element.36), channel_id=1, source_target_pairs={{0,12},{4,0},{8,4},{12,8},{1,13},{5,1},{9,5},{13,9},{2,14},{6,2},{... | collective-permute-start | bytes 233480 | tf_op jit(solution)/shard_map/ppermute | solution.py:234
  101.5 5.3 %collective-permute-start.9 = (bf16[304,128]{1,0:T(8,128)(2,1)S(1)}, bf16[304,128]{1,0:T(8,128)(2,1)S(1)}, u32[]{:S(2)}, u32[]{:S(2)}) collective-permute-start(bf16[304,128]{1,0:T(8,128)(2,1)S(1)} %get-tuple-element.37), channel_id=1, source_target_pairs={{0,8},{4,12},{8,0},{12,4},{1,9},{5,13},{9,1},{13,5},{2,10},{6,14},... | collective-permute-start | bytes 233480 | tf_op jit(solution)/shard_map/ppermute | solution.py:234
  106.8 5.3 %collective-permute-done.9.refs_2_ = bf16[304,128]{1,0:T(8,128)(2,1)S(1)} collective-permute-done((bf16[304,128]{1,0:T(8,128)(2,1)S(1)}, bf16[304,128]{1,0:T(8,128)(2,1)S(1)}, u32[]{:S(2)}, u32[]{:S(2)}) %collective-permute-start.9) | collective-permute-done | bytes 77856 | tf_op jit(solution)/shard_map/ppermute | solution.py:234
  112.1 0.1 shard_map.82.after_ref.refs_0_
  112.2 0.0 copy-start.4
  112.2 0.6 copy-done.4
  112.8 1.9 %shard_map.83 = f32[4,88,128]{2,1,0:T(8,128)} custom-call(bf16[32,88,128]{2,1,0:T(8,128)(2,1)} %all-to-all-done.1.parts_ref, bf16[288,128]{1,0:T(8,128)(2,1)} %copy-done.4), custom_call_target="tpu_custom_call" | custom-call | tf_op jit(solution)/shard_map/pallas_call | solution.py:358
  114.7 15.8 %all_to_all.33.parts_ref = f32[4,88,128]{2,1,0:T(8,128)S(1)} all-to-all(f32[4,88,128]{2,1,0:T(8,128)} %shard_map.83), channel_id=1, replica_groups=mesh['y'=8,'x'=4,'zh'=4,'zl'=2,'c'=2] {'zh'}, dimensions={0} | all-to-all | bytes 360448 | tf_op jit(solution)/shard_map/all_to_all | solution.py:48
  130.6 0.6 shard_map.84
  131.2 0.9 copy-done.2
  132.0 7.5 %all-to-all-start.3 = ((bf16[32,88,128]{2,1,0:T(8,128)(2,1)}), bf16[32,88,128]{2,1,0:T(8,128)(2,1)S(1)}, u32[]{:S(2)}, u32[]{:S(2)}) async-start(bf16[32,88,128]{2,1,0:T(8,128)(2,1)} %copy-done.2), calls=%async_computation.3 | async-start | bytes 1441792 | tf_op jit(solution)/shard_map/all_to_all | solution.py:48
  139.5 1.9 %collective-permute-start.11 = (bf16[288,128]{1,0:T(8,128)(2,1)S(1)}, bf16[288,128]{1,0:T(8,128)(2,1)S(1)}, u32[]{:S(2)}, u32[]{:S(2)}) collective-permute-start(bf16[288,128]{1,0:T(8,128)(2,1)S(1)} %copy-done.5), channel_id=1, source_target_pairs={{0,1},{1,0},{2,3},{3,2},{4,5},{5,4},{6,7},{7,6},{8,9},{9,8},{10,11... | collective-permute-start | bytes 221192 | tf_op jit(solution)/shard_map/ppermute | solution.py:376
  141.4 3.7 %collective-permute-start.12 = (bf16[288,128]{1,0:T(8,128)(2,1)S(1)}, bf16[288,128]{1,0:T(8,128)(2,1)S(1)}, u32[]{:S(2)}, u32[]{:S(2)}) collective-permute-start(bf16[288,128]{1,0:T(8,128)(2,1)S(1)} %copy-done.5), channel_id=1, source_target_pairs={{0,2},{1,3},{2,0},{3,1},{4,6},{5,7},{6,4},{7,5},{8,10},{9,11},{10,... | collective-permute-start | bytes 221192 | tf_op jit(solution)/shard_map/ppermute | solution.py:376
  145.2 2.0 %collective-permute-start.13 = (bf16[288,128]{1,0:T(8,128)(2,1)S(1)}, bf16[288,128]{1,0:T(8,128)(2,1)S(1)}, u32[]{:S(2)}, u32[]{:S(2)}) collective-permute-start(bf16[288,128]{1,0:T(8,128)(2,1)S(1)} %copy-done.5), channel_id=1, source_target_pairs={{0,3},{1,2},{2,1},{3,0},{4,7},{5,6},{6,5},{7,4},{8,11},{9,10},{10,... | collective-permute-start | bytes 221192 | tf_op jit(solution)/shard_map/ppermute | solution.py:376
  147.2 0.9 collective-permute-done.12.refs_2_
  148.1 3.2 %collective-permute-done.13.refs_3_ = bf16[288,128]{1,0:T(8,128)(2,1)S(1)} collective-permute-done((bf16[288,128]{1,0:T(8,128)(2,1)S(1)}, bf16[288,128]{1,0:T(8,128)(2,1)S(1)}, u32[]{:S(2)}, u32[]{:S(2)}) %collective-permute-start.13) | collective-permute-done | bytes 73760 | tf_op jit(solution)/shard_map/ppermute | solution.py:376
  151.3 2.2 %shard_map.86 = bf16[128,1152]{1,0:T(8,128)(2,1)} custom-call(s32[12]{0:T(128)S(1)} %stack.48.at_ref, bf16[1152,1152]{1,0:T(8,128)(2,1)S(1)} %copy-done, bf16[288,128]{1,0:T(8,128)(2,1)S(1)} %copy-done.5, bf16[288,128]{1,0:T(8,128)(2,1)S(1)} %collective-permute-done.11.refs_1_, bf16[288,128]{1,0:T(8,128)(2,1)S(1)} %collective-permute-done.12.refs_2_, ...), custom_call_target="tpu_custom_call" | custom-call | flops 339738624 | bytes 2949168 | tf_op jit(solution)/shard_map/pallas_call | solution.py:24
  153.5 3.4 %all-to-all-done.3 = bf16[32,88,128]{2,1,0:T(8,128)(2,1)S(1)} async-done(((bf16[32,88,128]{2,1,0:T(8,128)(2,1)}), bf16[32,88,128]{2,1,0:T(8,128)(2,1)S(1)}, u32[]{:S(2)}, u32[]{:S(2)}) %all-to-all-start.3) | async-done | bytes 720928 | tf_op jit(solution)/shard_map/all_to_all | solution.py:48
  156.9 1.0 shard_map.85
  (18 shorter events, 0.1 us)
Async XLA Ops:
  0.6 41.2 %copy-start = (bf16[1152,1152]{1,0:T(8,128)(2,1)S(1)}, bf16[1152,1152]{1,0:T(8,128)(2,1)}, u32[]{:S(2)}) copy-start(bf16[1152,1152]{1,0:T(8,128)(2,1)} %weight_ref.1) | copy-start | bytes 7962628
  0.6 1.0 copy-start.6
  2.6 26.4 %all-to-all-start = ((bf16[8,32,1152]{2,1,0:T(8,128)(2,1)}), bf16[8,32,1152]{2,1,0:T(8,128)(2,1)}, u32[]{:S(2)}, u32[]{:S(2)}) async-start(bf16[8,32,1152]{2,1,0:T(8,128)(2,1)} %bitcast.9), calls=%async_computation | async-start | bytes 1179648 | tf_op jit(solution)/shard_map/all_to_all | solution.py:48
  9.7 19.2 %collective-permute-start.2 = (bf16[128,1152]{1,0:T(8,128)(2,1)}, bf16[128,1152]{1,0:T(8,128)(2,1)S(1)}, u32[]{:S(2)}, u32[]{:S(2)}) collective-permute-start(bf16[128,1152]{1,0:T(8,128)(2,1)} %own_ref.1), channel_id=1, source_target_pairs={{2,4},{3,6},{0,13},{1,15},{6,8},{7,10},{4,1},{5,3},{10,12},{11,14}... | collective-permute-start | bytes 884744 | tf_op jit(solution)/shard_map/ppermute | solution.py:281
  20.8 18.2 %collective-permute-start.3 = (bf16[64,1152]{1,0:T(8,128)(2,1)S(1)}, bf16[64,1152]{1,0:T(8,128)(2,1)}, u32[]{:S(2)}, u32[]{:S(2)}) collective-permute-start(bf16[64,1152]{1,0:T(8,128)(2,1)S(1)} %constant_dynamic-slice_fusion), channel_id=1, source_target_pairs={{2,8},{3,9},{0,10},{1,11},{6,12},{7,13},{4,14},{5,15},{10,0},{11,1... | collective-permute-start | bytes 442376 | tf_op jit(solution)/shard_map/ppermute | solution.py:280
  29.0 22.8 %collective-permute-start.5 = (bf16[256,1152]{1,0:T(8,128)(2,1)}, bf16[256,1152]{1,0:T(8,128)(2,1)}, u32[]{:S(2)}, u32[]{:S(2)}) collective-permute-start(bf16[256,1152]{1,0:T(8,128)(2,1)} %bitcast.10.own_ref), channel_id=1, source_target_pairs={{0,16},{16,32},{32,48},{48,0},{1,17},{17,33},{33,49},{49,1},{2,18}... | collective-permute-start | bytes 1769480 | tf_op jit(solution)/shard_map/ppermute | solution.py:234
  32.4 23.1 %collective-permute-start = (bf16[256,1152]{1,0:T(8,128)(2,1)}, bf16[256,1152]{1,0:T(8,128)(2,1)}, u32[]{:S(2)}, u32[]{:S(2)}) collective-permute-start(bf16[256,1152]{1,0:T(8,128)(2,1)} %bitcast.10.own_ref), channel_id=1, source_target_pairs={{0,48},{16,0},{32,16},{48,32},{1,49},{17,1},{33,17},{49,33},{2,50}... | collective-permute-start | bytes 1769480 | tf_op jit(solution)/shard_map/ppermute | solution.py:234
  34.9 27.7 %collective-permute-start.1 = (bf16[256,1152]{1,0:T(8,128)(2,1)}, bf16[256,1152]{1,0:T(8,128)(2,1)}, u32[]{:S(2)}, u32[]{:S(2)}) collective-permute-start(bf16[256,1152]{1,0:T(8,128)(2,1)} %bitcast.10.own_ref), channel_id=1, source_target_pairs={{0,32},{16,48},{32,0},{48,16},{1,33},{17,49},{33,1},{49,17},{2,34}... | collective-permute-start | bytes 1769480 | tf_op jit(solution)/shard_map/ppermute | solution.py:234
  39.9 6.8 %collective-permute-start.4 = (bf16[192,1152]{1,0:T(8,128)(2,1)S(1)}, bf16[192,1152]{1,0:T(8,128)(2,1)}, u32[]{:S(2)}, u32[]{:S(2)}) collective-permute-start(bf16[192,1152]{1,0:T(8,128)(2,1)S(1)} %constant_dynamic-update-slice_fusion.fetched_ref), channel_id=1, source_target_pairs={{0,1},{1,0},{2,3},{3,2},{4,5},{5,4},{6,7},{7,6},{8,9},{9,8},{10,11... | collective-permute-start | bytes 1327112 | tf_op jit(solution)/shard_map/ppermute | solution.py:287
  41.8 4.8 %copy-start.3 = (bf16[128,1152]{1,0:T(8,128)(2,1)S(1)}, bf16[128,1152]{1,0:T(8,128)(2,1)}, u32[]{:S(2)}) copy-start(bf16[128,1152]{1,0:T(8,128)(2,1)} %own_ref.1) | copy-start | bytes 884740
  46.6 1.8 %copy-start.1 = (bf16[1152,1152]{0,1:T(8,128)(2,1)S(1)}, bf16[1152,1152]{0,1:T(8,128)(2,1)}, u32[]{:S(2)}) copy-start(bf16[1152,1152]{0,1:T(8,128)(2,1)} %copy.8) | copy-start | bytes 7962628
  66.1 3.9 %collective-permute-start.6 = (bf16[592,512]{1,0:T(8,128)(2,1)S(1)}, bf16[592,512]{1,0:T(8,128)(2,1)S(1)}, u32[]{:S(2)}, u32[]{:S(2)}) collective-permute-start(bf16[592,512]{1,0:T(8,128)(2,1)S(1)} %get-tuple-element.27), channel_id=1, source_target_pairs={{0,1},{1,0},{2,3},{3,2},{4,5},{5,4},{6,7},{7,6},{8,9},{9,8},{10,11... | collective-permute-start | bytes 1818632 | tf_op jit(solution)/shard_map/ppermute | solution.py:333
  70.7 11.9 %collective-permute-start.7 = (bf16[304,512]{1,0:T(8,128)(2,1)S(1)}, bf16[304,512]{1,0:T(8,128)(2,1)S(1)}, u32[]{:S(2)}, u32[]{:S(2)}) collective-permute-start(bf16[304,512]{1,0:T(8,128)(2,1)S(1)} %get-tuple-element.29), channel_id=1, source_target_pairs={{0,2},{2,0},{1,3},{3,1},{4,6},{6,4},{5,7},{7,5},{8,10},{10,8},{9,1... | collective-permute-start | bytes 933896 | tf_op jit(solution)/shard_map/ppermute | solution.py:342
  84.1 28.7 %all-to-all-start.1 = ((bf16[32,88,128]{2,1,0:T(8,128)(2,1)}), bf16[32,88,128]{2,1,0:T(8,128)(2,1)}, u32[]{:S(2)}, u32[]{:S(2)}) async-start(bf16[32,88,128]{2,1,0:T(8,128)(2,1)} %bitcast.12), calls=%async_computation.1 | async-start | bytes 1441792 | tf_op jit(solution)/shard_map/all_to_all | solution.py:48
  92.2 14.6 %collective-permute-start.10 = (bf16[304,128]{1,0:T(8,128)(2,1)S(1)}, bf16[304,128]{1,0:T(8,128)(2,1)S(1)}, u32[]{:S(2)}, u32[]{:S(2)}) collective-permute-start(bf16[304,128]{1,0:T(8,128)(2,1)S(1)} %get-tuple-element.38), channel_id=1, source_target_pairs={{0,4},{4,8},{8,12},{12,0},{1,5},{5,9},{9,13},{13,1},{2,6},{6,10},{... | collective-permute-start | bytes 233480 | tf_op jit(solution)/shard_map/ppermute | solution.py:234
  97.8 9.1 %collective-permute-start.8 = (bf16[304,128]{1,0:T(8,128)(2,1)S(1)}, bf16[304,128]{1,0:T(8,128)(2,1)S(1)}, u32[]{:S(2)}, u32[]{:S(2)}) collective-permute-start(bf16[304,128]{1,0:T(8,128)(2,1)S(1)} %get-tuple-element.36), channel_id=1, source_target_pairs={{0,12},{4,0},{8,4},{12,8},{1,13},{5,1},{9,5},{13,9},{2,14},{6,2},{... | collective-permute-start | bytes 233480 | tf_op jit(solution)/shard_map/ppermute | solution.py:234
  101.5 10.6 %collective-permute-start.9 = (bf16[304,128]{1,0:T(8,128)(2,1)S(1)}, bf16[304,128]{1,0:T(8,128)(2,1)S(1)}, u32[]{:S(2)}, u32[]{:S(2)}) collective-permute-start(bf16[304,128]{1,0:T(8,128)(2,1)S(1)} %get-tuple-element.37), channel_id=1, source_target_pairs={{0,8},{4,12},{8,0},{12,4},{1,9},{5,13},{9,1},{13,5},{2,10},{6,14},... | collective-permute-start | bytes 233480 | tf_op jit(solution)/shard_map/ppermute | solution.py:234
  112.2 0.6 copy-start.4
  112.8 26.7 %copy-start.5 = (bf16[288,128]{1,0:T(8,128)(2,1)S(1)}, bf16[288,128]{1,0:T(8,128)(2,1)}, u32[]{:S(2)}) copy-start(bf16[288,128]{1,0:T(8,128)(2,1)} %copy-done.4) | copy-start | bytes 221188
  131.2 0.9 copy-start.2
  132.0 24.9 %all-to-all-start.3 = ((bf16[32,88,128]{2,1,0:T(8,128)(2,1)}), bf16[32,88,128]{2,1,0:T(8,128)(2,1)S(1)}, u32[]{:S(2)}, u32[]{:S(2)}) async-start(bf16[32,88,128]{2,1,0:T(8,128)(2,1)} %copy-done.2), calls=%async_computation.3 | async-start | bytes 1441792 | tf_op jit(solution)/shard_map/all_to_all | solution.py:48
  139.5 7.7 %collective-permute-start.11 = (bf16[288,128]{1,0:T(8,128)(2,1)S(1)}, bf16[288,128]{1,0:T(8,128)(2,1)S(1)}, u32[]{:S(2)}, u32[]{:S(2)}) collective-permute-start(bf16[288,128]{1,0:T(8,128)(2,1)S(1)} %copy-done.5), channel_id=1, source_target_pairs={{0,1},{1,0},{2,3},{3,2},{4,5},{5,4},{6,7},{7,6},{8,9},{9,8},{10,11... | collective-permute-start | bytes 221192 | tf_op jit(solution)/shard_map/ppermute | solution.py:376
  141.4 6.7 %collective-permute-start.12 = (bf16[288,128]{1,0:T(8,128)(2,1)S(1)}, bf16[288,128]{1,0:T(8,128)(2,1)S(1)}, u32[]{:S(2)}, u32[]{:S(2)}) collective-permute-start(bf16[288,128]{1,0:T(8,128)(2,1)S(1)} %copy-done.5), channel_id=1, source_target_pairs={{0,2},{1,3},{2,0},{3,1},{4,6},{5,7},{6,4},{7,5},{8,10},{9,11},{10,... | collective-permute-start | bytes 221192 | tf_op jit(solution)/shard_map/ppermute | solution.py:376
  145.2 6.1 %collective-permute-start.13 = (bf16[288,128]{1,0:T(8,128)(2,1)S(1)}, bf16[288,128]{1,0:T(8,128)(2,1)S(1)}, u32[]{:S(2)}, u32[]{:S(2)}) collective-permute-start(bf16[288,128]{1,0:T(8,128)(2,1)S(1)} %copy-done.5), channel_id=1, source_target_pairs={{0,3},{1,2},{2,1},{3,0},{4,7},{5,6},{6,5},{7,4},{8,11},{9,10},{10,... | collective-permute-start | bytes 221192 | tf_op jit(solution)/shard_map/ppermute | solution.py:376

commit v10 on v9

--- a/solution.py
+++ b/solution.py
@@ -108,12 +108,17 @@
     loss_ref[...] = loss + more
 
 
-def second_kernel(at_ref, par_ref, right_ref, far_ref, low_ref, unit_ref, acc_ref, loss_ref, keep_ref, send_ref, sum_ref):
+def next_kernel(par_ref, texts_ref, low_ref, acc_in_ref, loss_in_ref, acc_ref, loss_ref):
+    slope, loss = pairs(par_ref, texts_ref[...], low_ref)
+    acc_ref[...] = acc_in_ref[...] + turn(texts_ref[...], slope)
+    loss_ref[...] = loss_in_ref[...] + loss
+
+
+def last_kernel(at_ref, par_ref, texts_ref, low_ref, unit_ref, acc_ref, loss_ref, keep_ref, send_ref, sum_ref):
     scale = par_ref[0]
-    slope, loss = pairs(par_ref, right_ref[...], low_ref)
-    more_slope, more = pairs(par_ref, far_ref[...], low_ref)
-    loss = loss_ref[...] + loss + more
-    total = scale * (acc_ref[...] + turn(right_ref[...], slope) + turn(far_ref[...], more_slope))
+    slope, loss = pairs(par_ref, texts_ref[...], low_ref)
+    loss = loss_ref[...] + loss
+    total = scale * (acc_ref[...] + turn(texts_ref[...], slope))
     sum_ref[...] = total
     dots = jnp.sum(unit_ref[...] * total, axis=0, keepdims=True)
     cols = (keep_ref.shape[0] - EXTRA) // 2
@@ -192,10 +197,18 @@
     out_ref[...] = ((total[:cols] - unit_ref[...] * dots) * inv_ref[:, :rows]).astype(BF16)
 
 
-def sum_kernel(parts_ref, after_ref, out_ref):
-    total = jnp.sum(parts_ref[...].astype(F32), axis=0)
+def to_low(at_ref, total):
+    first = total[:EXTRA]
+    terms = [t.astype(F32) for t in split3(first[0:1] + first[1:2] + first[2:3])]
+    row = jnp.concatenate(terms + [jnp.zeros((EXTRA - 3, LANES), F32)], axis=0)
+    return jnp.where(at_ref[7] > 0, row, first).astype(BF16), total[EXTRA:].astype(BF16)
+
+
+def sum_kernel(at_ref, parts_ref, after_ref, out_ref):
+    first, rest = to_low(at_ref, jnp.sum(parts_ref[...].astype(F32), axis=0))
     for k in range(out_ref.shape[0]):
-        out_ref[k] = total
+        out_ref[k, :EXTRA] = first
+        out_ref[k, EXTRA:] = rest
 
 
 def feat_kernel(at_ref, weight_ref, *refs):
@@ -206,18 +219,6 @@
     out_ref[...] = lax.dot_general(
         back_ref[...], weight_ref[...], (((0,), (1,)), ((), ())), preferred_element_type=F32
     ).astype(BF16)
-
-
-def last_sum_kernel(at_ref, parts_ref, out_ref):
-    total = jnp.sum(parts_ref[...], axis=0)
-    low = total.astype(BF16)
-    first = total[:EXTRA]
-    terms = [t.astype(F32) for t in split3(first[0:1] + first[1:2] + first[2:3])]
-    row = jnp.concatenate(terms + [jnp.zeros((EXTRA - 3, LANES), F32)], axis=0).astype(BF16)
-    first = jnp.where(at_ref[7] > 0, row.astype(F32), first).astype(BF16)
-    for k in range(out_ref.shape[0]):
-        out_ref[k, :EXTRA] = first
-        out_ref[k, EXTRA:] = low[EXTRA:]
 
 
 def final_kernel(at_loss, pairs, full_ref, head_ref, loss_ref):
@@ -313,21 +314,31 @@
         left,
         low,
         smem=2,
-        flops=8 * width * images * own.shape[0],
+        flops=2 * 4 * width * images * own.shape[0],
+    )
+    acc, loss_row = call(
+        next_kernel,
+        [shape((width, images), F32), shape((1, images), F32)],
+        par,
+        right,
+        low,
+        acc,
+        loss_row,
+        smem=1,
+        flops=width,
     )
     keep, send = call(
-        second_kernel,
+        last_kernel,
         [shape((2 * cols + EXTRA, images), F32), shape((2 * cols + EXTRA, images), BF16)],
         at,
         par,
-        right,
         far,
         low,
         unit,
         acc,
         loss_row,
         smem=2,
-        flops=8 * width * images * own.shape[0],
+        flops=4 * width * images * own.shape[0],
         scratch_shapes=[pltpu.VMEM((width, images), F32)],
     )
     got = lax.ppermute(send, "c", [(0, 1), (1, 0)])
@@ -357,12 +368,17 @@
     parts = to_all(flat, ("y", "x")).reshape(plane, piece, LANES)
     part = pl.pallas_call(
         sum_kernel,
-        out_shape=shape((nzh, piece, LANES), F32),
-        in_specs=[VMEM, pl.BlockSpec(memory_space=pl.ANY)],
+        out_shape=shape((nzh, piece, LANES), BF16),
+        in_specs=[SMEM, VMEM, pl.BlockSpec(memory_space=pl.ANY)],
         out_specs=VMEM,
-    )(parts, back)
+    )(at, parts, back)
     part = to_all(part, "zh")
-    low_part = call(last_sum_kernel, shape((plane, piece, LANES), BF16), at, part, smem=1)
+    low_part = pl.pallas_call(
+        sum_kernel,
+        out_shape=shape((plane, piece, LANES), BF16),
+        in_specs=[SMEM, VMEM, pl.BlockSpec(memory_space=pl.ANY)],
+        out_specs=VMEM,
+    )(at, part, back)
     full = to_all(low_part.reshape(plane * piece, LANES), ("y", "x"))
     group = rows * plane * nzh
     head_grad, loss = call(

time: 159 us -> 161 us (1.013)
  Pallas kernels: 19.5 us -> 22.3 us
  starting transfers between devices: 77.2 us -> 79.6 us
    all_to_all x3, starting transfers between devices: 22.6 us -> 26.2 us  [to_all(): return lax.all_to_all(copies, axes, 0, 0, tiled=True)]
    ppermute x3, waiting for transfers between devices: 4.11 us -> 1.28 us  [local(): lax.ppermute(back, ('zl', 'c'), [(k, k ^ d) for k in range(nrep)])]
    all_to_all x3, waiting for transfers between devices: 3.37 us -> 6.11 us  [to_all(): return lax.all_to_all(copies, axes, 0, 0, tiled=True)]
    pallas_call x1 -> x2, Pallas kernels: 1.93 us -> 3.74 us  [the longest x1 1.9 us: local(): pl.pallas_call(sum_kernel, out_shape=shape((nzh, piece, LANES), BF16), in...]
    unnamed x16 -> x18, local copies, waits for them, and re-layouts: 7.61 us -> 6.59 us
  transfers between devices with their start and end apart: 17 -> 17, of which waited for: 8 -> 8; matrix products, arithmetic and copies ran while one was open for 3% -> 3% of each run, Pallas kernels for 6% -> 7%
where the time goes in v10:
time: 161 us; the launch traced here: 160 us
  starting transfers between devices  79.6 us (49%)
  waiting for transfers between devices  32 us (20%)
  Pallas kernels  22.3 us (14%)
  blocking collectives  15.1 us (9%)
  local copies, waits for them, and re-layouts  8.53 us (5%)
  between operations  2.27 us (1%)
    all_to_all x3, starting transfers between devices, to_all(): return lax.all_to_all(copies, axes, 0, 0, tiled=True)  26.2 us
    ppermute x6, starting transfers between devices, shift_by(): return lax.ppermute(x, axis, [(k, (k + step) % n) for k in range(n)])  23.4 us
    pallas_call x10, Pallas kernels, call(): pl.pallas_call(body, out_shape=outs, in_specs=specs, out_specs=[VMEM] * l...  18.6 us
    all_to_all x1, blocking collectives, to_all(): return lax.all_to_all(copies, axes, 0, 0, tiled=True)  15.1 us
    ppermute x6, waiting for transfers between devices, shift_by(): return lax.ppermute(x, axis, [(k, (k + step) % n) for k in range(n)])  11 us
    ppermute x1, starting transfers between devices, local(): beside = lax.ppermute(img_feat, line, near)  10.1 us
    ppermute x1, waiting for transfers between devices, local(): got2 = lax.ppermute(send2, 'zl', [(0, 1), (1, 0)])  7.64 us
    ppermute x3, starting transfers between devices, local(): lax.ppermute(back, ('zl', 'c'), [(k, k ^ d) for k in range(nrep)])  7.59 us
  transfers between devices with their start and end apart: 17, of which 8 were waited for; matrix products, arithmetic and copies ran while one was open for 3% of the time, Pallas kernels for 7%

profile of v10, /device:TPU:2, one launch (start us, length us, event | category | flops | bytes accessed | tf_op | source)
XLA Modules:
  0.0 159.9 jit_solution(3531161069064605446)
XLA Ops:
  0.6 0.9 copy-done.5
  1.5 1.0 shard_map.76
  2.5 7.2 %all-to-all-start = ((bf16[8,32,1152]{2,1,0:T(8,128)(2,1)}), bf16[8,32,1152]{2,1,0:T(8,128)(2,1)}, u32[]{:S(2)}, u32[]{:S(2)}) async-start(bf16[8,32,1152]{2,1,0:T(8,128)(2,1)} %bitcast.9), calls=%async_computation | async-start | bytes 1179648 | tf_op jit(solution)/shard_map/all_to_all | solution.py:48
  9.7 10.1 %collective-permute-start.1 = (bf16[128,1152]{1,0:T(8,128)(2,1)}, bf16[128,1152]{1,0:T(8,128)(2,1)S(1)}, u32[]{:S(2)}, u32[]{:S(2)}) collective-permute-start(bf16[128,1152]{1,0:T(8,128)(2,1)} %own_ref.1), channel_id=1, source_target_pairs={{2,4},{3,6},{0,13},{1,15},{6,8},{7,10},{4,1},{5,3},{10,12},{11,14}... | collective-permute-start | bytes 884744 | tf_op jit(solution)/shard_map/ppermute | solution.py:282
  19.8 0.9 constant_dynamic-slice_fusion
  20.7 4.2 %collective-permute-start.2 = (bf16[64,1152]{1,0:T(8,128)(2,1)S(1)}, bf16[64,1152]{1,0:T(8,128)(2,1)}, u32[]{:S(2)}, u32[]{:S(2)}) collective-permute-start(bf16[64,1152]{1,0:T(8,128)(2,1)S(1)} %constant_dynamic-slice_fusion), channel_id=1, source_target_pairs={{2,8},{3,9},{0,10},{1,11},{6,12},{7,13},{4,14},{5,15},{10,0},{11,1... | collective-permute-start | bytes 442376 | tf_op jit(solution)/shard_map/ppermute | solution.py:281
  25.0 4.0 %collective-permute-done.1 = bf16[128,1152]{1,0:T(8,128)(2,1)S(1)} collective-permute-done((bf16[128,1152]{1,0:T(8,128)(2,1)}, bf16[128,1152]{1,0:T(8,128)(2,1)S(1)}, u32[]{:S(2)}, u32[]{:S(2)}) %collective-permute-start.1) | collective-permute-done | bytes 294944 | tf_op jit(solution)/shard_map/ppermute | solution.py:282
  29.0 3.4 %collective-permute-start.5 = (bf16[256,1152]{1,0:T(8,128)(2,1)}, bf16[256,1152]{1,0:T(8,128)(2,1)}, u32[]{:S(2)}, u32[]{:S(2)}) collective-permute-start(bf16[256,1152]{1,0:T(8,128)(2,1)} %bitcast.10.own_ref), channel_id=1, source_target_pairs={{0,16},{16,32},{32,48},{48,0},{1,17},{17,33},{33,49},{49,1},{2,18}... | collective-permute-start | bytes 1769480 | tf_op jit(solution)/shard_map/ppermute | solution.py:235
  32.4 2.4 %collective-permute-start.4 = (bf16[256,1152]{1,0:T(8,128)(2,1)}, bf16[256,1152]{1,0:T(8,128)(2,1)}, u32[]{:S(2)}, u32[]{:S(2)}) collective-permute-start(bf16[256,1152]{1,0:T(8,128)(2,1)} %bitcast.10.own_ref), channel_id=1, source_target_pairs={{0,48},{16,0},{32,16},{48,32},{1,49},{17,1},{33,17},{49,33},{2,50}... | collective-permute-start | bytes 1769480 | tf_op jit(solution)/shard_map/ppermute | solution.py:235
  34.8 4.0 %collective-permute-start = (bf16[256,1152]{1,0:T(8,128)(2,1)}, bf16[256,1152]{1,0:T(8,128)(2,1)}, u32[]{:S(2)}, u32[]{:S(2)}) collective-permute-start(bf16[256,1152]{1,0:T(8,128)(2,1)} %bitcast.10.own_ref), channel_id=1, source_target_pairs={{0,32},{16,48},{32,0},{48,16},{1,33},{17,49},{33,1},{49,17},{2,34}... | collective-permute-start | bytes 1769480 | tf_op jit(solution)/shard_map/ppermute | solution.py:235
  38.9 0.9 constant_dynamic-update-slice_fusion.fetched_ref
  39.8 1.9 %collective-permute-start.3 = (bf16[192,1152]{1,0:T(8,128)(2,1)S(1)}, bf16[192,1152]{1,0:T(8,128)(2,1)}, u32[]{:S(2)}, u32[]{:S(2)}) collective-permute-start(bf16[192,1152]{1,0:T(8,128)(2,1)S(1)} %constant_dynamic-update-slice_fusion.fetched_ref), channel_id=1, source_target_pairs={{0,1},{1,0},{2,3},{3,2},{4,5},{5,4},{6,7},{7,6},{8,9},{9,8},{10,11... | collective-permute-start | bytes 1327112 | tf_op jit(solution)/shard_map/ppermute | solution.py:288
  43.1 0.0 copy-start.4
  43.1 3.3 %copy.8 = bf16[1152,1152]{0,1:T(8,128)(2,1)} copy(bf16[1152,1152]{1,0:T(8,128)(2,1)S(1)} %copy-done) | data formatting | bytes 5308416 | tf_op args[1]
  46.4 0.1 stack.48.at_ref
  46.5 0.0 copy-start.6
  46.5 0.1 pad_maximum_fusion.par_ref
  46.6 1.7 %copy-done.1 = bf16[1152,1152]{0,1:T(8,128)(2,1)S(1)} copy-done((bf16[1152,1152]{0,1:T(8,128)(2,1)S(1)}, bf16[1152,1152]{0,1:T(8,128)(2,1)}, u32[]{:S(2)}) %copy-start.1) | copy-done | bytes 2654232
  48.4 3.4 %shard_map.77 = (f32[1152,512]{1,0:T(8,128)S(1)}, bf16[1152,512]{1,0:T(8,128)(2,1)S(1)}, f32[1,512]{1,0:T(1,128)S(1)}, f32[288,128]{1,0:T(8,128)S(1)}, f32[288,5...) custom-call(s32[12]{0:T(128)S(1)} %stack.48.at_ref, bf16[1152,1152]{1,0:T(8,128)(2,1)S(1)} %bitcast.16, ...), custom_call_target="tpu_custom_call" | custom-call | flops 2304 | bytes 3833904 | tf_op jit(solution)/shard_map/pallas_call | solution.py:24
  51.8 3.7 %shard_map.78 = (f32[1152,512]{1,0:T(8,128)S(1)}, f32[1,512]{1,0:T(1,128)S(1)}) custom-call(s32[12]{0:T(128)S(1)} %stack.48.at_ref, f32[2]{0:T(128)S(1)} %pad_maximum_fusion.par_ref, bf16[256,1152]{1,0:T(8,128)(2,1)} %bitcast.10.own_ref, bf16[256,1152]{1,0:T(8,128)(2,1)} %collective-permute-done.5.left_ref, bf16[1152,512]{1,0:T(8,128)(2,1)S(1)} %get-tuple-element.24.low_ref), custom_call_target="tpu_custom_call" | custom-call | flops 1207959552 | bytes 2359352 | tf_op jit(solution)/shard_map/pallas_call | solution.py:24
  55.5 2.5 %shard_map.79 = (f32[1152,512]{1,0:T(8,128)S(1)}, f32[1,512]{1,0:T(1,128)S(1)}) custom-call(f32[2]{0:T(128)S(1)} %pad_maximum_fusion.par_ref, bf16[256,1152]{1,0:T(8,128)(2,1)} %collective-permute-done.4.texts_ref, bf16[1152,512]{1,0:T(8,128)(2,1)S(1)} %get-tuple-element.24.low_ref, f32[1152,512]{1,0:T(8,128)S(1)} %get-tuple-element.26.acc_in_ref, ...), custom_call_target="tpu_custom_call" | custom-call | flops 1152 | bytes 4130824 | tf_op jit(solution)/shard_map/pallas_call | solution.py:24
  58.0 4.6 %collective-permute-done.texts_ref = bf16[256,1152]{1,0:T(8,128)(2,1)} collective-permute-done((bf16[256,1152]{1,0:T(8,128)(2,1)}, bf16[256,1152]{1,0:T(8,128)(2,1)}, u32[]{:S(2)}, u32[]{:S(2)}) %collective-permute-start) | collective-permute-done | bytes 589856 | tf_op jit(solution)/shard_map/ppermute | solution.py:235
  62.6 2.6 %shard_map.80 = (f32[592,512]{1,0:T(8,128)S(1)}, bf16[592,512]{1,0:T(8,128)(2,1)S(1)}) custom-call(s32[12]{0:T(128)S(1)} %stack.48.at_ref, f32[2]{0:T(128)S(1)} %pad_maximum_fusion.par_ref, bf16[256,1152]{1,0:T(8,128)(2,1)} %collective-permute-done.texts_ref, bf16[1152,512]{1,0:T(8,128)(2,1)S(1)} %get-tuple-element.24.low_ref, ...), custom_call_target="tpu_custom_call" | custom-call | flops 603979776 | bytes 6490168 | tf_op jit(solution)/shard_map/pallas_call | solution.py:24
  65.2 1.9 %collective-permute-start.6 = (bf16[592,512]{1,0:T(8,128)(2,1)S(1)}, bf16[592,512]{1,0:T(8,128)(2,1)S(1)}, u32[]{:S(2)}, u32[]{:S(2)}) collective-permute-start(bf16[592,512]{1,0:T(8,128)(2,1)S(1)} %get-tuple-element.31), channel_id=1, source_target_pairs={{0,1},{1,0},{2,3},{3,2},{4,5},{5,4},{6,7},{7,6},{8,9},{9,8},{10,11... | collective-permute-start | bytes 1818632 | tf_op jit(solution)/shard_map/ppermute | solution.py:344
  67.1 2.0 %collective-permute-done.6.got_ref = bf16[592,512]{1,0:T(8,128)(2,1)S(1)} collective-permute-done((bf16[592,512]{1,0:T(8,128)(2,1)S(1)}, bf16[592,512]{1,0:T(8,128)(2,1)S(1)}, u32[]{:S(2)}, u32[]{:S(2)}) %collective-permute-start.6) | collective-permute-done | bytes 606240 | tf_op jit(solution)/shard_map/ppermute | solution.py:344
  69.1 0.7 shard_map.81
  69.8 4.3 %collective-permute-start.7 = (bf16[304,512]{1,0:T(8,128)(2,1)S(1)}, bf16[304,512]{1,0:T(8,128)(2,1)S(1)}, u32[]{:S(2)}, u32[]{:S(2)}) collective-permute-start(bf16[304,512]{1,0:T(8,128)(2,1)S(1)} %get-tuple-element.33), channel_id=1, source_target_pairs={{0,2},{2,0},{1,3},{3,1},{4,6},{6,4},{5,7},{7,5},{8,10},{10,8},{9,1... | collective-permute-start | bytes 933896 | tf_op jit(solution)/shard_map/ppermute | solution.py:353
  74.1 7.6 %collective-permute-done.7.got_ref = bf16[304,512]{1,0:T(8,128)(2,1)S(1)} collective-permute-done((bf16[304,512]{1,0:T(8,128)(2,1)S(1)}, bf16[304,512]{1,0:T(8,128)(2,1)S(1)}, u32[]{:S(2)}, u32[]{:S(2)}) %collective-permute-start.7) | collective-permute-done | bytes 311328 | tf_op jit(solution)/shard_map/ppermute | solution.py:353
  81.7 1.5 shard_map.82
  83.2 10.7 %all-to-all-start.1 = ((bf16[32,88,128]{2,1,0:T(8,128)(2,1)}), bf16[32,88,128]{2,1,0:T(8,128)(2,1)}, u32[]{:S(2)}, u32[]{:S(2)}) async-start(bf16[32,88,128]{2,1,0:T(8,128)(2,1)} %bitcast.12), calls=%async_computation.1 | async-start | bytes 1441792 | tf_op jit(solution)/shard_map/all_to_all | solution.py:48
  93.9 7.4 %collective-permute-start.8 = (bf16[304,128]{1,0:T(8,128)(2,1)S(1)}, bf16[304,128]{1,0:T(8,128)(2,1)S(1)}, u32[]{:S(2)}, u32[]{:S(2)}) collective-permute-start(bf16[304,128]{1,0:T(8,128)(2,1)S(1)} %get-tuple-element.40), channel_id=1, source_target_pairs={{0,12},{4,0},{8,4},{12,8},{1,13},{5,1},{9,5},{13,9},{2,14},{6,2},{... | collective-permute-start | bytes 233480 | tf_op jit(solution)/shard_map/ppermute | solution.py:235
  101.3 3.7 %collective-permute-start.9 = (bf16[304,128]{1,0:T(8,128)(2,1)S(1)}, bf16[304,128]{1,0:T(8,128)(2,1)S(1)}, u32[]{:S(2)}, u32[]{:S(2)}) collective-permute-start(bf16[304,128]{1,0:T(8,128)(2,1)S(1)} %get-tuple-element.41), channel_id=1, source_target_pairs={{0,8},{4,12},{8,0},{12,4},{1,9},{5,13},{9,1},{13,5},{2,10},{6,14},... | collective-permute-start | bytes 233480 | tf_op jit(solution)/shard_map/ppermute | solution.py:235
  105.0 2.5 %collective-permute-start.10 = (bf16[304,128]{1,0:T(8,128)(2,1)S(1)}, bf16[304,128]{1,0:T(8,128)(2,1)S(1)}, u32[]{:S(2)}, u32[]{:S(2)}) collective-permute-start(bf16[304,128]{1,0:T(8,128)(2,1)S(1)} %get-tuple-element.42), channel_id=1, source_target_pairs={{0,4},{4,8},{8,12},{12,0},{1,5},{5,9},{9,13},{13,1},{2,6},{6,10},{... | collective-permute-start | bytes 233480 | tf_op jit(solution)/shard_map/ppermute | solution.py:235
  107.5 5.2 %collective-permute-done.9.refs_2_ = bf16[304,128]{1,0:T(8,128)(2,1)S(1)} collective-permute-done((bf16[304,128]{1,0:T(8,128)(2,1)S(1)}, bf16[304,128]{1,0:T(8,128)(2,1)S(1)}, u32[]{:S(2)}, u32[]{:S(2)}) %collective-permute-start.9) | collective-permute-done | bytes 77856 | tf_op jit(solution)/shard_map/ppermute | solution.py:235
  112.7 1.2 collective-permute-done.10.refs_3_
  113.9 0.1 shard_map.83.after_ref.refs_0_
  114.0 0.6 copy-done.2
  114.6 1.9 %shard_map.84 = bf16[4,88,128]{2,1,0:T(8,128)(2,1)} custom-call(s32[12]{0:T(128)} %copy-done.6, bf16[32,88,128]{2,1,0:T(8,128)(2,1)} %all-to-all-done.1.parts_ref, bf16[288,128]{1,0:T(8,128)(2,1)} %copy-done.2), custom_call_target="tpu_custom_call" | custom-call | tf_op jit(solution)/shard_map/pallas_call | solution.py:369
  116.5 15.1 %all_to_all.33.parts_ref = bf16[4,88,128]{2,1,0:T(8,128)(2,1)} all-to-all(bf16[4,88,128]{2,1,0:T(8,128)(2,1)} %shard_map.84), channel_id=1, replica_groups=mesh['y'=8,'x'=4,'zh'=4,'zl'=2,'c'=2] {'zh'}, dimensions={0} | all-to-all | bytes 180224 | tf_op jit(solution)/shard_map/all_to_all | solution.py:48
  131.6 1.8 %shard_map.85 = bf16[32,88,128]{2,1,0:T(8,128)(2,1)} custom-call(s32[12]{0:T(128)} %copy-done.6, bf16[4,88,128]{2,1,0:T(8,128)(2,1)} %all_to_all.33.parts_ref, bf16[288,128]{1,0:T(8,128)(2,1)} %copy-done.2), custom_call_target="tpu_custom_call" | custom-call | tf_op jit(solution)/shard_map/pallas_call | solution.py:376
  133.4 8.3 %all-to-all-start.3 = ((bf16[32,88,128]{2,1,0:T(8,128)(2,1)}), bf16[32,88,128]{2,1,0:T(8,128)(2,1)S(1)}, u32[]{:S(2)}, u32[]{:S(2)}) async-start(bf16[32,88,128]{2,1,0:T(8,128)(2,1)} %shard_map.85), calls=%async_computation.3 | async-start | bytes 1441792 | tf_op jit(solution)/shard_map/all_to_all | solution.py:48
  141.7 1.9 %collective-permute-start.13 = (bf16[288,128]{1,0:T(8,128)(2,1)S(1)}, bf16[288,128]{1,0:T(8,128)(2,1)S(1)}, u32[]{:S(2)}, u32[]{:S(2)}) collective-permute-start(bf16[288,128]{1,0:T(8,128)(2,1)S(1)} %copy-done.3), channel_id=1, source_target_pairs={{0,3},{1,2},{2,1},{3,0},{4,7},{5,6},{6,5},{7,4},{8,11},{9,10},{10,... | collective-permute-start | bytes 221192 | tf_op jit(solution)/shard_map/ppermute | solution.py:392
  143.6 2.8 %collective-permute-start.12 = (bf16[288,128]{1,0:T(8,128)(2,1)S(1)}, bf16[288,128]{1,0:T(8,128)(2,1)S(1)}, u32[]{:S(2)}, u32[]{:S(2)}) collective-permute-start(bf16[288,128]{1,0:T(8,128)(2,1)S(1)} %copy-done.3), channel_id=1, source_target_pairs={{0,2},{1,3},{2,0},{3,1},{4,6},{5,7},{6,4},{7,5},{8,10},{9,11},{10,... | collective-permute-start | bytes 221192 | tf_op jit(solution)/shard_map/ppermute | solution.py:392
  146.5 2.8 %collective-permute-start.11 = (bf16[288,128]{1,0:T(8,128)(2,1)S(1)}, bf16[288,128]{1,0:T(8,128)(2,1)S(1)}, u32[]{:S(2)}, u32[]{:S(2)}) collective-permute-start(bf16[288,128]{1,0:T(8,128)(2,1)S(1)} %copy-done.3), channel_id=1, source_target_pairs={{0,1},{1,0},{2,3},{3,2},{4,5},{5,4},{6,7},{7,6},{8,9},{9,8},{10,11... | collective-permute-start | bytes 221192 | tf_op jit(solution)/shard_map/ppermute | solution.py:392
  149.3 1.3 collective-permute-done.12.refs_2_
  150.6 2.2 %shard_map.87 = bf16[128,1152]{1,0:T(8,128)(2,1)} custom-call(s32[12]{0:T(128)S(1)} %copy-done.7, bf16[1152,1152]{1,0:T(8,128)(2,1)S(1)} %copy-done, bf16[288,128]{1,0:T(8,128)(2,1)S(1)} %copy-done.3, bf16[288,128]{1,0:T(8,128)(2,1)S(1)} %collective-permute-done.11.refs_1_, bf16[288,128]{1,0:T(8,128)(2,1)S(1)} %collective-permute-done.12.refs_2_, ...), custom_call_target="tpu_custom_call" | custom-call | flops 339738624 | bytes 2949168 | tf_op jit(solution)/shard_map/pallas_call | solution.py:24
  152.8 6.1 %all-to-all-done.3 = bf16[32,88,128]{2,1,0:T(8,128)(2,1)S(1)} async-done(((bf16[32,88,128]{2,1,0:T(8,128)(2,1)}), bf16[32,88,128]{2,1,0:T(8,128)(2,1)S(1)}, u32[]{:S(2)}, u32[]{:S(2)}) %all-to-all-start.3) | async-done | bytes 720928 | tf_op jit(solution)/shard_map/all_to_all | solution.py:48
  158.9 1.0 shard_map.86
  (21 shorter events, 0.1 us)
Async XLA Ops:
  0.6 0.9 copy-start.5
  1.5 41.6 %copy-start = (bf16[1152,1152]{1,0:T(8,128)(2,1)S(1)}, bf16[1152,1152]{1,0:T(8,128)(2,1)}, u32[]{:S(2)}) copy-start(bf16[1152,1152]{1,0:T(8,128)(2,1)} %weight_ref.1) | copy-start | bytes 7962628
  2.5 26.5 %all-to-all-start = ((bf16[8,32,1152]{2,1,0:T(8,128)(2,1)}), bf16[8,32,1152]{2,1,0:T(8,128)(2,1)}, u32[]{:S(2)}, u32[]{:S(2)}) async-start(bf16[8,32,1152]{2,1,0:T(8,128)(2,1)} %bitcast.9), calls=%async_computation | async-start | bytes 1179648 | tf_op jit(solution)/shard_map/all_to_all | solution.py:48
  9.7 19.2 %collective-permute-start.1 = (bf16[128,1152]{1,0:T(8,128)(2,1)}, bf16[128,1152]{1,0:T(8,128)(2,1)S(1)}, u32[]{:S(2)}, u32[]{:S(2)}) collective-permute-start(bf16[128,1152]{1,0:T(8,128)(2,1)} %own_ref.1), channel_id=1, source_target_pairs={{2,4},{3,6},{0,13},{1,15},{6,8},{7,10},{4,1},{5,3},{10,12},{11,14}... | collective-permute-start | bytes 884744 | tf_op jit(solution)/shard_map/ppermute | solution.py:282
  20.7 18.2 %collective-permute-start.2 = (bf16[64,1152]{1,0:T(8,128)(2,1)S(1)}, bf16[64,1152]{1,0:T(8,128)(2,1)}, u32[]{:S(2)}, u32[]{:S(2)}) collective-permute-start(bf16[64,1152]{1,0:T(8,128)(2,1)S(1)} %constant_dynamic-slice_fusion), channel_id=1, source_target_pairs={{2,8},{3,9},{0,10},{1,11},{6,12},{7,13},{4,14},{5,15},{10,0},{11,1... | collective-permute-start | bytes 442376 | tf_op jit(solution)/shard_map/ppermute | solution.py:281
  29.0 22.8 %collective-permute-start.5 = (bf16[256,1152]{1,0:T(8,128)(2,1)}, bf16[256,1152]{1,0:T(8,128)(2,1)}, u32[]{:S(2)}, u32[]{:S(2)}) collective-permute-start(bf16[256,1152]{1,0:T(8,128)(2,1)} %bitcast.10.own_ref), channel_id=1, source_target_pairs={{0,16},{16,32},{32,48},{48,0},{1,17},{17,33},{33,49},{49,1},{2,18}... | collective-permute-start | bytes 1769480 | tf_op jit(solution)/shard_map/ppermute | solution.py:235
  32.4 23.1 %collective-permute-start.4 = (bf16[256,1152]{1,0:T(8,128)(2,1)}, bf16[256,1152]{1,0:T(8,128)(2,1)}, u32[]{:S(2)}, u32[]{:S(2)}) collective-permute-start(bf16[256,1152]{1,0:T(8,128)(2,1)} %bitcast.10.own_ref), channel_id=1, source_target_pairs={{0,48},{16,0},{32,16},{48,32},{1,49},{17,1},{33,17},{49,33},{2,50}... | collective-permute-start | bytes 1769480 | tf_op jit(solution)/shard_map/ppermute | solution.py:235
  34.8 27.7 %collective-permute-start = (bf16[256,1152]{1,0:T(8,128)(2,1)}, bf16[256,1152]{1,0:T(8,128)(2,1)}, u32[]{:S(2)}, u32[]{:S(2)}) collective-permute-start(bf16[256,1152]{1,0:T(8,128)(2,1)} %bitcast.10.own_ref), channel_id=1, source_target_pairs={{0,32},{16,48},{32,0},{48,16},{1,33},{17,49},{33,1},{49,17},{2,34}... | collective-permute-start | bytes 1769480 | tf_op jit(solution)/shard_map/ppermute | solution.py:235
  39.8 6.8 %collective-permute-start.3 = (bf16[192,1152]{1,0:T(8,128)(2,1)S(1)}, bf16[192,1152]{1,0:T(8,128)(2,1)}, u32[]{:S(2)}, u32[]{:S(2)}) collective-permute-start(bf16[192,1152]{1,0:T(8,128)(2,1)S(1)} %constant_dynamic-update-slice_fusion.fetched_ref), channel_id=1, source_target_pairs={{0,1},{1,0},{2,3},{3,2},{4,5},{5,4},{6,7},{7,6},{8,9},{9,8},{10,11... | collective-permute-start | bytes 1327112 | tf_op jit(solution)/shard_map/ppermute | solution.py:288
  43.1 3.5 %copy-start.4 = (bf16[128,1152]{1,0:T(8,128)(2,1)S(1)}, bf16[128,1152]{1,0:T(8,128)(2,1)}, u32[]{:S(2)}) copy-start(bf16[128,1152]{1,0:T(8,128)(2,1)} %own_ref.1) | copy-start | bytes 884740
  46.5 22.6 %copy-start.6 = (s32[12]{0:T(128)}, s32[12]{0:T(128)S(1)}, u32[]{:S(2)}) copy-start(s32[12]{0:T(128)S(1)} %stack.48.at_ref) | copy-start | bytes 148
  46.6 1.8 %copy-start.1 = (bf16[1152,1152]{0,1:T(8,128)(2,1)S(1)}, bf16[1152,1152]{0,1:T(8,128)(2,1)}, u32[]{:S(2)}) copy-start(bf16[1152,1152]{0,1:T(8,128)(2,1)} %copy.8) | copy-start | bytes 7962628
  65.2 3.9 %collective-permute-start.6 = (bf16[592,512]{1,0:T(8,128)(2,1)S(1)}, bf16[592,512]{1,0:T(8,128)(2,1)S(1)}, u32[]{:S(2)}, u32[]{:S(2)}) collective-permute-start(bf16[592,512]{1,0:T(8,128)(2,1)S(1)} %get-tuple-element.31), channel_id=1, source_target_pairs={{0,1},{1,0},{2,3},{3,2},{4,5},{5,4},{6,7},{7,6},{8,9},{9,8},{10,11... | collective-permute-start | bytes 1818632 | tf_op jit(solution)/shard_map/ppermute | solution.py:344
  69.8 11.9 %collective-permute-start.7 = (bf16[304,512]{1,0:T(8,128)(2,1)S(1)}, bf16[304,512]{1,0:T(8,128)(2,1)S(1)}, u32[]{:S(2)}, u32[]{:S(2)}) collective-permute-start(bf16[304,512]{1,0:T(8,128)(2,1)S(1)} %get-tuple-element.33), channel_id=1, source_target_pairs={{0,2},{2,0},{1,3},{3,1},{4,6},{6,4},{5,7},{7,5},{8,10},{10,8},{9,1... | collective-permute-start | bytes 933896 | tf_op jit(solution)/shard_map/ppermute | solution.py:353
  83.2 67.4 %copy-start.7 = (s32[12]{0:T(128)S(1)}, s32[12]{0:T(128)}, u32[]{:S(2)}) copy-start(s32[12]{0:T(128)} %copy-done.6) | copy-start | bytes 148
  83.2 31.4 %all-to-all-start.1 = ((bf16[32,88,128]{2,1,0:T(8,128)(2,1)}), bf16[32,88,128]{2,1,0:T(8,128)(2,1)}, u32[]{:S(2)}, u32[]{:S(2)}) async-start(bf16[32,88,128]{2,1,0:T(8,128)(2,1)} %bitcast.12), calls=%async_computation.1 | async-start | bytes 1441792 | tf_op jit(solution)/shard_map/all_to_all | solution.py:48
  93.9 13.6 %collective-permute-start.8 = (bf16[304,128]{1,0:T(8,128)(2,1)S(1)}, bf16[304,128]{1,0:T(8,128)(2,1)S(1)}, u32[]{:S(2)}, u32[]{:S(2)}) collective-permute-start(bf16[304,128]{1,0:T(8,128)(2,1)S(1)} %get-tuple-element.40), channel_id=1, source_target_pairs={{0,12},{4,0},{8,4},{12,8},{1,13},{5,1},{9,5},{13,9},{2,14},{6,2},{... | collective-permute-start | bytes 233480 | tf_op jit(solution)/shard_map/ppermute | solution.py:235
  101.3 11.4 %collective-permute-start.9 = (bf16[304,128]{1,0:T(8,128)(2,1)S(1)}, bf16[304,128]{1,0:T(8,128)(2,1)S(1)}, u32[]{:S(2)}, u32[]{:S(2)}) collective-permute-start(bf16[304,128]{1,0:T(8,128)(2,1)S(1)} %get-tuple-element.41), channel_id=1, source_target_pairs={{0,8},{4,12},{8,0},{12,4},{1,9},{5,13},{9,1},{13,5},{2,10},{6,14},... | collective-permute-start | bytes 233480 | tf_op jit(solution)/shard_map/ppermute | solution.py:235
  105.0 8.9 %collective-permute-start.10 = (bf16[304,128]{1,0:T(8,128)(2,1)S(1)}, bf16[304,128]{1,0:T(8,128)(2,1)S(1)}, u32[]{:S(2)}, u32[]{:S(2)}) collective-permute-start(bf16[304,128]{1,0:T(8,128)(2,1)S(1)} %get-tuple-element.42), channel_id=1, source_target_pairs={{0,4},{4,8},{8,12},{12,0},{1,5},{5,9},{9,13},{13,1},{2,6},{6,10},{... | collective-permute-start | bytes 233480 | tf_op jit(solution)/shard_map/ppermute | solution.py:235
  113.9 0.6 copy-start.2
  114.6 27.1 %copy-start.3 = (bf16[288,128]{1,0:T(8,128)(2,1)S(1)}, bf16[288,128]{1,0:T(8,128)(2,1)}, u32[]{:S(2)}) copy-start(bf16[288,128]{1,0:T(8,128)(2,1)} %copy-done.2) | copy-start | bytes 221188
  133.4 25.5 %all-to-all-start.3 = ((bf16[32,88,128]{2,1,0:T(8,128)(2,1)}), bf16[32,88,128]{2,1,0:T(8,128)(2,1)S(1)}, u32[]{:S(2)}, u32[]{:S(2)}) async-start(bf16[32,88,128]{2,1,0:T(8,128)(2,1)} %shard_map.85), calls=%async_computation.3 | async-start | bytes 1441792 | tf_op jit(solution)/shard_map/all_to_all | solution.py:48
  141.7 7.6 %collective-permute-start.13 = (bf16[288,128]{1,0:T(8,128)(2,1)S(1)}, bf16[288,128]{1,0:T(8,128)(2,1)S(1)}, u32[]{:S(2)}, u32[]{:S(2)}) collective-permute-start(bf16[288,128]{1,0:T(8,128)(2,1)S(1)} %copy-done.3), channel_id=1, source_target_pairs={{0,3},{1,2},{2,1},{3,0},{4,7},{5,6},{6,5},{7,4},{8,11},{9,10},{10,... | collective-permute-start | bytes 221192 | tf_op jit(solution)/shard_map/ppermute | solution.py:392
  143.6 7.0 %collective-permute-start.12 = (bf16[288,128]{1,0:T(8,128)(2,1)S(1)}, bf16[288,128]{1,0:T(8,128)(2,1)S(1)}, u32[]{:S(2)}, u32[]{:S(2)}) collective-permute-start(bf16[288,128]{1,0:T(8,128)(2,1)S(1)} %copy-done.3), channel_id=1, source_target_pairs={{0,2},{1,3},{2,0},{3,1},{4,6},{5,7},{6,4},{7,5},{8,10},{9,11},{10,... | collective-permute-start | bytes 221192 | tf_op jit(solution)/shard_map/ppermute | solution.py:392
  146.5 4.1 %collective-permute-start.11 = (bf16[288,128]{1,0:T(8,128)(2,1)S(1)}, bf16[288,128]{1,0:T(8,128)(2,1)S(1)}, u32[]{:S(2)}, u32[]{:S(2)}) collective-permute-start(bf16[288,128]{1,0:T(8,128)(2,1)S(1)} %copy-done.3), channel_id=1, source_target_pairs={{0,1},{1,0},{2,3},{3,2},{4,5},{5,4},{6,7},{7,6},{8,9},{9,8},{10,11... | collective-permute-start | bytes 221192 | tf_op jit(solution)/shard_map/ppermute | solution.py:392

commit v11 on v10

--- a/solution.py
+++ b/solution.py
@@ -204,7 +204,8 @@
     return jnp.where(at_ref[7] > 0, row, first).astype(BF16), total[EXTRA:].astype(BF16)
 
 
-def sum_kernel(at_ref, parts_ref, after_ref, out_ref):
+def sum_kernel(at_ref, parts_ref, *refs):
+    out_ref = refs[-1]
     first, rest = to_low(at_ref, jnp.sum(parts_ref[...].astype(F32), axis=0))
     for k in range(out_ref.shape[0]):
         out_ref[k, :EXTRA] = first
@@ -363,22 +364,12 @@
     )
 
     dirs = [dirs[0]] + [shift_by(dirs[s], "zh", -s) for s in range(1, nzh)]
-    back = call(back_kernel, shape((cols, rows), BF16), own_unit, inv, *dirs)
+    back = call(back_kernel, shape((cols, rows), BF16), own_unit, inv, *dirs, flops=2 * 10**10)
 
     parts = to_all(flat, ("y", "x")).reshape(plane, piece, LANES)
-    part = pl.pallas_call(
-        sum_kernel,
-        out_shape=shape((nzh, piece, LANES), BF16),
-        in_specs=[SMEM, VMEM, pl.BlockSpec(memory_space=pl.ANY)],
-        out_specs=VMEM,
-    )(at, parts, back)
+    part = call(sum_kernel, shape((nzh, piece, LANES), BF16), at, parts, smem=1)
     part = to_all(part, "zh")
-    low_part = pl.pallas_call(
-        sum_kernel,
-        out_shape=shape((plane, piece, LANES), BF16),
-        in_specs=[SMEM, VMEM, pl.BlockSpec(memory_space=pl.ANY)],
-        out_specs=VMEM,
-    )(at, part, back)
+    low_part = call(sum_kernel, shape((plane, piece, LANES), BF16), at, part, smem=1)
     full = to_all(low_part.reshape(plane * piece, LANES), ("y", "x"))
     group = rows * plane * nzh
     head_grad, loss = call(

time: 161 us -> 165 us (1.025)
  blocking collectives: 15.1 us -> 30.8 us
  waiting for transfers between devices: 32 us -> 25 us
  starting transfers between devices: 79.6 us -> 74 us
  local copies, waits for them, and re-layouts: 8.53 us -> 10.3 us
    all_to_all x1, blocking collectives: 15.1 us -> 30.8 us  [to_all(): return lax.all_to_all(copies, axes, 0, 0, tiled=True)]
    all_to_all x3, starting transfers between devices: 26.2 us -> 19.5 us  [to_all(): return lax.all_to_all(copies, axes, 0, 0, tiled=True)]
    ppermute x6, waiting for transfers between devices: 11 us -> 4.62 us  [shift_by(): return lax.ppermute(x, axis, [(k, (k + step) % n) for k in range(n)])]
    pallas_call x2 -> x0, Pallas kernels: 3.74 us -> none  [the longest x1 1.9 us: local(): pl.pallas_call(sum_kernel, out_shape=shape((nzh, piece, LANES), BF16), in...]
    pallas_call x10 -> x12, Pallas kernels: 18.6 us -> 21.1 us  [call(): pl.pallas_call(body, out_shape=outs, in_specs=specs, out_specs=[VMEM] * l...]
    unnamed x18 -> x16, local copies, waits for them, and re-layouts: 6.59 us -> 8.33 us
  transfers between devices with their start and end apart: 17 -> 17, of which waited for: 8 -> 6; matrix products, arithmetic and copies ran while one was open for 3% -> 3% of each run, Pallas kernels for 7% -> 8%
where the time goes in v11:
time: 165 us; the launch traced here: 164 us
  starting transfers between devices  74 us (45%)
  blocking collectives  30.8 us (19%)
  waiting for transfers between devices  25 us (15%)
  Pallas kernels  21.1 us (13%)
  local copies, waits for them, and re-layouts  10.3 us (6%)
  between operations  2.29 us (1%)
    all_to_all x1, blocking collectives, to_all(): return lax.all_to_all(copies, axes, 0, 0, tiled=True)  30.8 us
    ppermute x6, starting transfers between devices, shift_by(): return lax.ppermute(x, axis, [(k, (k + step) % n) for k in range(n)])  24.5 us
    pallas_call x12, Pallas kernels, call(): pl.pallas_call(body, out_shape=outs, in_specs=specs, out_specs=[VMEM] * l...  21.1 us
    all_to_all x3, starting transfers between devices, to_all(): return lax.all_to_all(copies, axes, 0, 0, tiled=True)  19.5 us
    ppermute x1, starting transfers between devices, local(): beside = lax.ppermute(img_feat, line, near)  10.1 us
    unnamed x16, local copies, waits for them, and re-layouts  8.33 us
    ppermute x1, waiting for transfers between devices, local(): got2 = lax.ppermute(send2, 'zl', [(0, 1), (1, 0)])  7.64 us
    ppermute x3, starting transfers between devices, local(): lax.ppermute(back, ('zl', 'c'), [(k, k ^ d) for k in range(nrep)])  7.59 us
  transfers between devices with their start and end apart: 17, of which 6 were waited for; matrix products, arithmetic and copies ran while one was open for 3% of the time, Pallas kernels for 8%

profile of v11, /device:TPU:2, one launch (start us, length us, event | category | flops | bytes accessed | tf_op | source)
XLA Modules:
  0.0 163.5 jit_solution(11493358178046871280)
XLA Ops:
  0.6 0.9 copy-done.4
  1.5 1.0 shard_map.76
  2.5 7.2 %all-to-all-start = ((bf16[8,32,1152]{2,1,0:T(8,128)(2,1)}), bf16[8,32,1152]{2,1,0:T(8,128)(2,1)}, u32[]{:S(2)}, u32[]{:S(2)}) async-start(bf16[8,32,1152]{2,1,0:T(8,128)(2,1)} %bitcast.9), calls=%async_computation | async-start | bytes 1179648 | tf_op jit(solution)/shard_map/all_to_all | solution.py:48
  9.7 10.1 %collective-permute-start.1 = (bf16[128,1152]{1,0:T(8,128)(2,1)}, bf16[128,1152]{1,0:T(8,128)(2,1)S(1)}, u32[]{:S(2)}, u32[]{:S(2)}) collective-permute-start(bf16[128,1152]{1,0:T(8,128)(2,1)} %own_ref.1), channel_id=1, source_target_pairs={{2,4},{3,6},{0,13},{1,15},{6,8},{7,10},{4,1},{5,3},{10,12},{11,14}... | collective-permute-start | bytes 884744 | tf_op jit(solution)/shard_map/ppermute | solution.py:283
  19.8 0.9 constant_dynamic-slice_fusion
  20.7 4.2 %collective-permute-start.2 = (bf16[64,1152]{1,0:T(8,128)(2,1)S(1)}, bf16[64,1152]{1,0:T(8,128)(2,1)}, u32[]{:S(2)}, u32[]{:S(2)}) collective-permute-start(bf16[64,1152]{1,0:T(8,128)(2,1)S(1)} %constant_dynamic-slice_fusion), channel_id=1, source_target_pairs={{2,8},{3,9},{0,10},{1,11},{6,12},{7,13},{4,14},{5,15},{10,0},{11,1... | collective-permute-start | bytes 442376 | tf_op jit(solution)/shard_map/ppermute | solution.py:282
  25.0 4.0 %collective-permute-done.1 = bf16[128,1152]{1,0:T(8,128)(2,1)S(1)} collective-permute-done((bf16[128,1152]{1,0:T(8,128)(2,1)}, bf16[128,1152]{1,0:T(8,128)(2,1)S(1)}, u32[]{:S(2)}, u32[]{:S(2)}) %collective-permute-start.1) | collective-permute-done | bytes 294944 | tf_op jit(solution)/shard_map/ppermute | solution.py:283
  29.0 0.0 all-to-all-done
  29.0 3.4 %collective-permute-start.5 = (bf16[256,1152]{1,0:T(8,128)(2,1)}, bf16[256,1152]{1,0:T(8,128)(2,1)}, u32[]{:S(2)}, u32[]{:S(2)}) collective-permute-start(bf16[256,1152]{1,0:T(8,128)(2,1)} %bitcast.10.own_ref), channel_id=1, source_target_pairs={{0,16},{16,32},{32,48},{48,0},{1,17},{17,33},{33,49},{49,1},{2,18}... | collective-permute-start | bytes 1769480 | tf_op jit(solution)/shard_map/ppermute | solution.py:236
  32.4 2.4 %collective-permute-start.4 = (bf16[256,1152]{1,0:T(8,128)(2,1)}, bf16[256,1152]{1,0:T(8,128)(2,1)}, u32[]{:S(2)}, u32[]{:S(2)}) collective-permute-start(bf16[256,1152]{1,0:T(8,128)(2,1)} %bitcast.10.own_ref), channel_id=1, source_target_pairs={{0,48},{16,0},{32,16},{48,32},{1,49},{17,1},{33,17},{49,33},{2,50}... | collective-permute-start | bytes 1769480 | tf_op jit(solution)/shard_map/ppermute | solution.py:236
  34.8 4.0 %collective-permute-start = (bf16[256,1152]{1,0:T(8,128)(2,1)}, bf16[256,1152]{1,0:T(8,128)(2,1)}, u32[]{:S(2)}, u32[]{:S(2)}) collective-permute-start(bf16[256,1152]{1,0:T(8,128)(2,1)} %bitcast.10.own_ref), channel_id=1, source_target_pairs={{0,32},{16,48},{32,0},{48,16},{1,33},{17,49},{33,1},{49,17},{2,34}... | collective-permute-start | bytes 1769480 | tf_op jit(solution)/shard_map/ppermute | solution.py:236
  38.9 0.9 constant_dynamic-update-slice_fusion.fetched_ref
  39.8 1.9 %collective-permute-start.3 = (bf16[192,1152]{1,0:T(8,128)(2,1)S(1)}, bf16[192,1152]{1,0:T(8,128)(2,1)}, u32[]{:S(2)}, u32[]{:S(2)}) collective-permute-start(bf16[192,1152]{1,0:T(8,128)(2,1)S(1)} %constant_dynamic-update-slice_fusion.fetched_ref), channel_id=1, source_target_pairs={{0,1},{1,0},{2,3},{3,2},{4,5},{5,4},{6,7},{7,6},{8,9},{9,8},{10,11... | collective-permute-start | bytes 1327112 | tf_op jit(solution)/shard_map/ppermute | solution.py:289
  43.1 0.0 copy-start.3
  43.1 3.3 %copy.8 = bf16[1152,1152]{0,1:T(8,128)(2,1)} copy(bf16[1152,1152]{1,0:T(8,128)(2,1)S(1)} %copy-done) | data formatting | bytes 5308416 | tf_op args[1]
  46.4 0.1 stack.48.at_ref
  46.5 0.1 pad_maximum_fusion.par_ref
  46.6 1.8 %copy-done.1 = bf16[1152,1152]{0,1:T(8,128)(2,1)S(1)} copy-done((bf16[1152,1152]{0,1:T(8,128)(2,1)S(1)}, bf16[1152,1152]{0,1:T(8,128)(2,1)}, u32[]{:S(2)}) %copy-start.1) | copy-done | bytes 2654232
  48.3 3.4 %shard_map.77 = (f32[1152,512]{1,0:T(8,128)S(1)}, bf16[1152,512]{1,0:T(8,128)(2,1)S(1)}, f32[1,512]{1,0:T(1,128)S(1)}, f32[288,128]{1,0:T(8,128)S(1)}, f32[288,5...) custom-call(s32[12]{0:T(128)S(1)} %stack.48.at_ref, bf16[1152,1152]{1,0:T(8,128)(2,1)S(1)} %bitcast.16, ...), custom_call_target="tpu_custom_call" | custom-call | flops 2304 | bytes 3833904 | tf_op jit(solution)/shard_map/pallas_call | solution.py:24
  51.8 3.7 %shard_map.78 = (f32[1152,512]{1,0:T(8,128)S(1)}, f32[1,512]{1,0:T(1,128)S(1)}) custom-call(s32[12]{0:T(128)S(1)} %stack.48.at_ref, f32[2]{0:T(128)S(1)} %pad_maximum_fusion.par_ref, bf16[256,1152]{1,0:T(8,128)(2,1)} %bitcast.10.own_ref, bf16[256,1152]{1,0:T(8,128)(2,1)} %collective-permute-done.5.left_ref, bf16[1152,512]{1,0:T(8,128)(2,1)S(1)} %get-tuple-element.24.low_ref), custom_call_target="tpu_custom_call" | custom-call | flops 1207959552 | bytes 2359352 | tf_op jit(solution)/shard_map/pallas_call | solution.py:24
  55.5 2.4 %shard_map.79 = (f32[1152,512]{1,0:T(8,128)S(1)}, f32[1,512]{1,0:T(1,128)S(1)}) custom-call(f32[2]{0:T(128)S(1)} %pad_maximum_fusion.par_ref, bf16[256,1152]{1,0:T(8,128)(2,1)} %collective-permute-done.4.texts_ref, bf16[1152,512]{1,0:T(8,128)(2,1)S(1)} %get-tuple-element.24.low_ref, f32[1152,512]{1,0:T(8,128)S(1)} %get-tuple-element.26.acc_in_ref, ...), custom_call_target="tpu_custom_call" | custom-call | flops 1152 | bytes 4130824 | tf_op jit(solution)/shard_map/pallas_call | solution.py:24
  57.9 4.6 %collective-permute-done.texts_ref = bf16[256,1152]{1,0:T(8,128)(2,1)} collective-permute-done((bf16[256,1152]{1,0:T(8,128)(2,1)}, bf16[256,1152]{1,0:T(8,128)(2,1)}, u32[]{:S(2)}, u32[]{:S(2)}) %collective-permute-start) | collective-permute-done | bytes 589856 | tf_op jit(solution)/shard_map/ppermute | solution.py:236
  62.6 2.6 %shard_map.80 = (f32[592,512]{1,0:T(8,128)S(1)}, bf16[592,512]{1,0:T(8,128)(2,1)S(1)}) custom-call(s32[12]{0:T(128)S(1)} %stack.48.at_ref, f32[2]{0:T(128)S(1)} %pad_maximum_fusion.par_ref, bf16[256,1152]{1,0:T(8,128)(2,1)} %collective-permute-done.texts_ref, bf16[1152,512]{1,0:T(8,128)(2,1)S(1)} %get-tuple-element.24.low_ref, ...), custom_call_target="tpu_custom_call" | custom-call | flops 603979776 | bytes 6490168 | tf_op jit(solution)/shard_map/pallas_call | solution.py:24
  65.2 1.9 %collective-permute-start.6 = (bf16[592,512]{1,0:T(8,128)(2,1)S(1)}, bf16[592,512]{1,0:T(8,128)(2,1)S(1)}, u32[]{:S(2)}, u32[]{:S(2)}) collective-permute-start(bf16[592,512]{1,0:T(8,128)(2,1)S(1)} %get-tuple-element.31), channel_id=1, source_target_pairs={{0,1},{1,0},{2,3},{3,2},{4,5},{5,4},{6,7},{7,6},{8,9},{9,8},{10,11... | collective-permute-start | bytes 1818632 | tf_op jit(solution)/shard_map/ppermute | solution.py:345
  67.1 2.0 %collective-permute-done.6.got_ref = bf16[592,512]{1,0:T(8,128)(2,1)S(1)} collective-permute-done((bf16[592,512]{1,0:T(8,128)(2,1)S(1)}, bf16[592,512]{1,0:T(8,128)(2,1)S(1)}, u32[]{:S(2)}, u32[]{:S(2)}) %collective-permute-start.6) | collective-permute-done | bytes 606240 | tf_op jit(solution)/shard_map/ppermute | solution.py:345
  69.1 0.7 shard_map.81
  69.8 4.3 %collective-permute-start.7 = (bf16[304,512]{1,0:T(8,128)(2,1)S(1)}, bf16[304,512]{1,0:T(8,128)(2,1)S(1)}, u32[]{:S(2)}, u32[]{:S(2)}) collective-permute-start(bf16[304,512]{1,0:T(8,128)(2,1)S(1)} %get-tuple-element.33), channel_id=1, source_target_pairs={{0,2},{2,0},{1,3},{3,1},{4,6},{6,4},{5,7},{7,5},{8,10},{10,8},{9,1... | collective-permute-start | bytes 933896 | tf_op jit(solution)/shard_map/ppermute | solution.py:354
  74.1 7.6 %collective-permute-done.7.got_ref = bf16[304,512]{1,0:T(8,128)(2,1)S(1)} collective-permute-done((bf16[304,512]{1,0:T(8,128)(2,1)S(1)}, bf16[304,512]{1,0:T(8,128)(2,1)S(1)}, u32[]{:S(2)}, u32[]{:S(2)}) %collective-permute-start.7) | collective-permute-done | bytes 311328 | tf_op jit(solution)/shard_map/ppermute | solution.py:354
  81.7 1.2 shard_map.82
  83.0 0.6 copy-done.5
  83.6 30.8 %all_to_all.33.parts_ref = bf16[32,88,128]{2,1,0:T(8,128)(2,1)S(1)} all-to-all(bf16[32,88,128]{2,1,0:T(8,128)(2,1)S(1)} %bitcast.18), channel_id=1, replica_groups=mesh['y'=8,'x'=4,'zh'=4,'zl'=2,'c'=2] {'y','x'}, dimensions={0} | all-to-all | bytes 1441792 | tf_op jit(solution)/shard_map/all_to_all | solution.py:48
  114.4 1.3 shard_map.83
  115.7 6.7 %all-to-all-start.2 = ((bf16[4,88,128]{2,1,0:T(8,128)(2,1)}), bf16[4,88,128]{2,1,0:T(8,128)(2,1)S(1)}, u32[]{:S(2)}, u32[]{:S(2)}) async-start(bf16[4,88,128]{2,1,0:T(8,128)(2,1)} %shard_map.83), calls=%async_computation.2 | async-start | bytes 180224 | tf_op jit(solution)/shard_map/all_to_all | solution.py:48
  122.4 6.0 %collective-permute-start.8 = (bf16[304,128]{1,0:T(8,128)(2,1)}, bf16[304,128]{1,0:T(8,128)(2,1)}, u32[]{:S(2)}, u32[]{:S(2)}) collective-permute-start(bf16[304,128]{1,0:T(8,128)(2,1)} %get-tuple-element.41), channel_id=1, source_target_pairs={{0,12},{4,0},{8,4},{12,8},{1,13},{5,1},{9,5},{13,9},{2,14},{6,2},{... | collective-permute-start | bytes 233480 | tf_op jit(solution)/shard_map/ppermute | solution.py:236
  128.4 4.3 %collective-permute-start.9 = (bf16[304,128]{1,0:T(8,128)(2,1)}, bf16[304,128]{1,0:T(8,128)(2,1)}, u32[]{:S(2)}, u32[]{:S(2)}) collective-permute-start(bf16[304,128]{1,0:T(8,128)(2,1)} %get-tuple-element.42), channel_id=1, source_target_pairs={{0,8},{4,12},{8,0},{12,4},{1,9},{5,13},{9,1},{13,5},{2,10},{6,14},... | collective-permute-start | bytes 233480 | tf_op jit(solution)/shard_map/ppermute | solution.py:236
  132.7 4.3 %collective-permute-start.10 = (bf16[304,128]{1,0:T(8,128)(2,1)}, bf16[304,128]{1,0:T(8,128)(2,1)}, u32[]{:S(2)}, u32[]{:S(2)}) collective-permute-start(bf16[304,128]{1,0:T(8,128)(2,1)} %get-tuple-element.43), channel_id=1, source_target_pairs={{0,4},{4,8},{8,12},{12,0},{1,5},{5,9},{9,13},{13,1},{2,6},{6,10},{... | collective-permute-start | bytes 233480 | tf_op jit(solution)/shard_map/ppermute | solution.py:236
  137.0 0.6 shard_map.84
  137.6 0.9 copy-done.2
  138.5 5.6 %all-to-all-start.3 = ((bf16[32,88,128]{2,1,0:T(8,128)(2,1)}), bf16[32,88,128]{2,1,0:T(8,128)(2,1)S(1)}, u32[]{:S(2)}, u32[]{:S(2)}) async-start(bf16[32,88,128]{2,1,0:T(8,128)(2,1)} %copy-done.2), calls=%async_computation.3 | async-start | bytes 1441792 | tf_op jit(solution)/shard_map/all_to_all | solution.py:48
  144.1 0.9 copy-done.6
  145.0 1.0 shard_map.86.refs_0_
  146.0 1.9 %collective-permute-start.13 = (bf16[288,128]{1,0:T(8,128)(2,1)S(1)}, bf16[288,128]{1,0:T(8,128)(2,1)S(1)}, u32[]{:S(2)}, u32[]{:S(2)}) collective-permute-start(bf16[288,128]{1,0:T(8,128)(2,1)S(1)} %shard_map.86.refs_0_), channel_id=1, source_target_pairs={{0,3},{1,2},{2,1},{3,0},{4,7},{5,6},{6,5},{7,4},{8,11},{9,10},{10,... | collective-permute-start | bytes 221192 | tf_op jit(solution)/shard_map/ppermute | solution.py:383
  147.9 2.6 %collective-permute-start.12 = (bf16[288,128]{1,0:T(8,128)(2,1)S(1)}, bf16[288,128]{1,0:T(8,128)(2,1)S(1)}, u32[]{:S(2)}, u32[]{:S(2)}) collective-permute-start(bf16[288,128]{1,0:T(8,128)(2,1)S(1)} %shard_map.86.refs_0_), channel_id=1, source_target_pairs={{0,2},{1,3},{2,0},{3,1},{4,6},{5,7},{6,4},{7,5},{8,10},{9,11},{10,... | collective-permute-start | bytes 221192 | tf_op jit(solution)/shard_map/ppermute | solution.py:383
  150.5 3.1 %collective-permute-start.11 = (bf16[288,128]{1,0:T(8,128)(2,1)S(1)}, bf16[288,128]{1,0:T(8,128)(2,1)S(1)}, u32[]{:S(2)}, u32[]{:S(2)}) collective-permute-start(bf16[288,128]{1,0:T(8,128)(2,1)S(1)} %shard_map.86.refs_0_), channel_id=1, source_target_pairs={{0,1},{1,0},{2,3},{3,2},{4,5},{5,4},{6,7},{7,6},{8,9},{9,8},{10,11... | collective-permute-start | bytes 221192 | tf_op jit(solution)/shard_map/ppermute | solution.py:383
  153.6 1.2 collective-permute-done.12.refs_2_
  154.8 2.2 %shard_map.87 = bf16[128,1152]{1,0:T(8,128)(2,1)} custom-call(s32[12]{0:T(128)S(1)} %stack.48.at_ref, bf16[1152,1152]{1,0:T(8,128)(2,1)S(1)} %copy-done, bf16[288,128]{1,0:T(8,128)(2,1)S(1)} %shard_map.86.refs_0_, bf16[288,128]{1,0:T(8,128)(2,1)S(1)} %collective-permute-done.11.refs_1_, bf16[288,128]{1,0:T(8,128)(2,1)S(1)} %collective-permute-done.12.refs_2_, ...), custom_call_target="tpu_custom_call" | custom-call | flops 339738624 | bytes 2949168 | tf_op jit(solution)/shard_map/pallas_call | solution.py:24
  157.0 5.6 %all-to-all-done.3 = bf16[32,88,128]{2,1,0:T(8,128)(2,1)S(1)} async-done(((bf16[32,88,128]{2,1,0:T(8,128)(2,1)}), bf16[32,88,128]{2,1,0:T(8,128)(2,1)S(1)}, u32[]{:S(2)}, u32[]{:S(2)}) %all-to-all-start.3) | async-done | bytes 720928 | tf_op jit(solution)/shard_map/all_to_all | solution.py:48
  162.6 1.0 shard_map.85
  (19 shorter events, 0.1 us)
Async XLA Ops:
  0.6 0.9 copy-start.4
  1.5 41.6 %copy-start = (bf16[1152,1152]{1,0:T(8,128)(2,1)S(1)}, bf16[1152,1152]{1,0:T(8,128)(2,1)}, u32[]{:S(2)}) copy-start(bf16[1152,1152]{1,0:T(8,128)(2,1)} %weight_ref.1) | copy-start | bytes 7962628
  2.5 26.5 %all-to-all-start = ((bf16[8,32,1152]{2,1,0:T(8,128)(2,1)}), bf16[8,32,1152]{2,1,0:T(8,128)(2,1)}, u32[]{:S(2)}, u32[]{:S(2)}) async-start(bf16[8,32,1152]{2,1,0:T(8,128)(2,1)} %bitcast.9), calls=%async_computation | async-start | bytes 1179648 | tf_op jit(solution)/shard_map/all_to_all | solution.py:48
  9.7 19.2 %collective-permute-start.1 = (bf16[128,1152]{1,0:T(8,128)(2,1)}, bf16[128,1152]{1,0:T(8,128)(2,1)S(1)}, u32[]{:S(2)}, u32[]{:S(2)}) collective-permute-start(bf16[128,1152]{1,0:T(8,128)(2,1)} %own_ref.1), channel_id=1, source_target_pairs={{2,4},{3,6},{0,13},{1,15},{6,8},{7,10},{4,1},{5,3},{10,12},{11,14}... | collective-permute-start | bytes 884744 | tf_op jit(solution)/shard_map/ppermute | solution.py:283
  20.7 18.2 %collective-permute-start.2 = (bf16[64,1152]{1,0:T(8,128)(2,1)S(1)}, bf16[64,1152]{1,0:T(8,128)(2,1)}, u32[]{:S(2)}, u32[]{:S(2)}) collective-permute-start(bf16[64,1152]{1,0:T(8,128)(2,1)S(1)} %constant_dynamic-slice_fusion), channel_id=1, source_target_pairs={{2,8},{3,9},{0,10},{1,11},{6,12},{7,13},{4,14},{5,15},{10,0},{11,1... | collective-permute-start | bytes 442376 | tf_op jit(solution)/shard_map/ppermute | solution.py:282
  29.0 22.8 %collective-permute-start.5 = (bf16[256,1152]{1,0:T(8,128)(2,1)}, bf16[256,1152]{1,0:T(8,128)(2,1)}, u32[]{:S(2)}, u32[]{:S(2)}) collective-permute-start(bf16[256,1152]{1,0:T(8,128)(2,1)} %bitcast.10.own_ref), channel_id=1, source_target_pairs={{0,16},{16,32},{32,48},{48,0},{1,17},{17,33},{33,49},{49,1},{2,18}... | collective-permute-start | bytes 1769480 | tf_op jit(solution)/shard_map/ppermute | solution.py:236
  32.4 23.1 %collective-permute-start.4 = (bf16[256,1152]{1,0:T(8,128)(2,1)}, bf16[256,1152]{1,0:T(8,128)(2,1)}, u32[]{:S(2)}, u32[]{:S(2)}) collective-permute-start(bf16[256,1152]{1,0:T(8,128)(2,1)} %bitcast.10.own_ref), channel_id=1, source_target_pairs={{0,48},{16,0},{32,16},{48,32},{1,49},{17,1},{33,17},{49,33},{2,50}... | collective-permute-start | bytes 1769480 | tf_op jit(solution)/shard_map/ppermute | solution.py:236
  34.8 27.7 %collective-permute-start = (bf16[256,1152]{1,0:T(8,128)(2,1)}, bf16[256,1152]{1,0:T(8,128)(2,1)}, u32[]{:S(2)}, u32[]{:S(2)}) collective-permute-start(bf16[256,1152]{1,0:T(8,128)(2,1)} %bitcast.10.own_ref), channel_id=1, source_target_pairs={{0,32},{16,48},{32,0},{48,16},{1,33},{17,49},{33,1},{49,17},{2,34}... | collective-permute-start | bytes 1769480 | tf_op jit(solution)/shard_map/ppermute | solution.py:236
  39.8 6.8 %collective-permute-start.3 = (bf16[192,1152]{1,0:T(8,128)(2,1)S(1)}, bf16[192,1152]{1,0:T(8,128)(2,1)}, u32[]{:S(2)}, u32[]{:S(2)}) collective-permute-start(bf16[192,1152]{1,0:T(8,128)(2,1)S(1)} %constant_dynamic-update-slice_fusion.fetched_ref), channel_id=1, source_target_pairs={{0,1},{1,0},{2,3},{3,2},{4,5},{5,4},{6,7},{7,6},{8,9},{9,8},{10,11... | collective-permute-start | bytes 1327112 | tf_op jit(solution)/shard_map/ppermute | solution.py:289
  43.1 3.5 %copy-start.3 = (bf16[128,1152]{1,0:T(8,128)(2,1)S(1)}, bf16[128,1152]{1,0:T(8,128)(2,1)}, u32[]{:S(2)}) copy-start(bf16[128,1152]{1,0:T(8,128)(2,1)} %own_ref.1) | copy-start | bytes 884740
  46.6 1.8 %copy-start.1 = (bf16[1152,1152]{0,1:T(8,128)(2,1)S(1)}, bf16[1152,1152]{0,1:T(8,128)(2,1)}, u32[]{:S(2)}) copy-start(bf16[1152,1152]{0,1:T(8,128)(2,1)} %copy.8) | copy-start | bytes 7962628
  65.2 3.9 %collective-permute-start.6 = (bf16[592,512]{1,0:T(8,128)(2,1)S(1)}, bf16[592,512]{1,0:T(8,128)(2,1)S(1)}, u32[]{:S(2)}, u32[]{:S(2)}) collective-permute-start(bf16[592,512]{1,0:T(8,128)(2,1)S(1)} %get-tuple-element.31), channel_id=1, source_target_pairs={{0,1},{1,0},{2,3},{3,2},{4,5},{5,4},{6,7},{7,6},{8,9},{9,8},{10,11... | collective-permute-start | bytes 1818632 | tf_op jit(solution)/shard_map/ppermute | solution.py:345
  69.8 11.9 %collective-permute-start.7 = (bf16[304,512]{1,0:T(8,128)(2,1)S(1)}, bf16[304,512]{1,0:T(8,128)(2,1)S(1)}, u32[]{:S(2)}, u32[]{:S(2)}) collective-permute-start(bf16[304,512]{1,0:T(8,128)(2,1)S(1)} %get-tuple-element.33), channel_id=1, source_target_pairs={{0,2},{2,0},{1,3},{3,1},{4,6},{6,4},{5,7},{7,5},{8,10},{10,8},{9,1... | collective-permute-start | bytes 933896 | tf_op jit(solution)/shard_map/ppermute | solution.py:354
  83.0 0.6 copy-start.5
  115.7 21.3 %all-to-all-start.2 = ((bf16[4,88,128]{2,1,0:T(8,128)(2,1)}), bf16[4,88,128]{2,1,0:T(8,128)(2,1)S(1)}, u32[]{:S(2)}, u32[]{:S(2)}) async-start(bf16[4,88,128]{2,1,0:T(8,128)(2,1)} %shard_map.83), calls=%async_computation.2 | async-start | bytes 180224 | tf_op jit(solution)/shard_map/all_to_all | solution.py:48
  122.4 21.7 %collective-permute-start.8 = (bf16[304,128]{1,0:T(8,128)(2,1)}, bf16[304,128]{1,0:T(8,128)(2,1)}, u32[]{:S(2)}, u32[]{:S(2)}) collective-permute-start(bf16[304,128]{1,0:T(8,128)(2,1)} %get-tuple-element.41), channel_id=1, source_target_pairs={{0,12},{4,0},{8,4},{12,8},{1,13},{5,1},{9,5},{13,9},{2,14},{6,2},{... | collective-permute-start | bytes 233480 | tf_op jit(solution)/shard_map/ppermute | solution.py:236
  128.4 15.6 %collective-permute-start.9 = (bf16[304,128]{1,0:T(8,128)(2,1)}, bf16[304,128]{1,0:T(8,128)(2,1)}, u32[]{:S(2)}, u32[]{:S(2)}) collective-permute-start(bf16[304,128]{1,0:T(8,128)(2,1)} %get-tuple-element.42), channel_id=1, source_target_pairs={{0,8},{4,12},{8,0},{12,4},{1,9},{5,13},{9,1},{13,5},{2,10},{6,14},... | collective-permute-start | bytes 233480 | tf_op jit(solution)/shard_map/ppermute | solution.py:236
  132.7 11.4 %collective-permute-start.10 = (bf16[304,128]{1,0:T(8,128)(2,1)}, bf16[304,128]{1,0:T(8,128)(2,1)}, u32[]{:S(2)}, u32[]{:S(2)}) collective-permute-start(bf16[304,128]{1,0:T(8,128)(2,1)} %get-tuple-element.43), channel_id=1, source_target_pairs={{0,4},{4,8},{8,12},{12,0},{1,5},{5,9},{9,13},{13,1},{2,6},{6,10},{... | collective-permute-start | bytes 233480 | tf_op jit(solution)/shard_map/ppermute | solution.py:236
  137.6 0.9 copy-start.2
  138.5 24.1 %all-to-all-start.3 = ((bf16[32,88,128]{2,1,0:T(8,128)(2,1)}), bf16[32,88,128]{2,1,0:T(8,128)(2,1)S(1)}, u32[]{:S(2)}, u32[]{:S(2)}) async-start(bf16[32,88,128]{2,1,0:T(8,128)(2,1)} %copy-done.2), calls=%async_computation.3 | async-start | bytes 1441792 | tf_op jit(solution)/shard_map/all_to_all | solution.py:48
  144.1 0.9 copy-start.6
  146.0 7.6 %collective-permute-start.13 = (bf16[288,128]{1,0:T(8,128)(2,1)S(1)}, bf16[288,128]{1,0:T(8,128)(2,1)S(1)}, u32[]{:S(2)}, u32[]{:S(2)}) collective-permute-start(bf16[288,128]{1,0:T(8,128)(2,1)S(1)} %shard_map.86.refs_0_), channel_id=1, source_target_pairs={{0,3},{1,2},{2,1},{3,0},{4,7},{5,6},{6,5},{7,4},{8,11},{9,10},{10,... | collective-permute-start | bytes 221192 | tf_op jit(solution)/shard_map/ppermute | solution.py:383
  147.9 6.9 %collective-permute-start.12 = (bf16[288,128]{1,0:T(8,128)(2,1)S(1)}, bf16[288,128]{1,0:T(8,128)(2,1)S(1)}, u32[]{:S(2)}, u32[]{:S(2)}) collective-permute-start(bf16[288,128]{1,0:T(8,128)(2,1)S(1)} %shard_map.86.refs_0_), channel_id=1, source_target_pairs={{0,2},{1,3},{2,0},{3,1},{4,6},{5,7},{6,4},{7,5},{8,10},{9,11},{10,... | collective-permute-start | bytes 221192 | tf_op jit(solution)/shard_map/ppermute | solution.py:383
  150.5 4.3 %collective-permute-start.11 = (bf16[288,128]{1,0:T(8,128)(2,1)S(1)}, bf16[288,128]{1,0:T(8,128)(2,1)S(1)}, u32[]{:S(2)}, u32[]{:S(2)}) collective-permute-start(bf16[288,128]{1,0:T(8,128)(2,1)S(1)} %shard_map.86.refs_0_), channel_id=1, source_target_pairs={{0,1},{1,0},{2,3},{3,2},{4,5},{5,4},{6,7},{7,6},{8,9},{9,8},{10,11... | collective-permute-start | bytes 221192 | tf_op jit(solution)/shard_map/ppermute | solution.py:383

commit v12 on v9

--- a/solution.py
+++ b/solution.py
@@ -67,7 +67,7 @@
         feats_ref[pl.ds(pl.multiple_of((1 + 2 * k) * rows, 16), rows), :] = ref[:rows]
         feats_ref[pl.ds(pl.multiple_of(2 * rows + k * part, 16), part), :] = ref[rows:]
     head = lax.dot_general(
-        wt_ref[...], feats_ref[...], (((1,), (1,)), ((), ())), preferred_element_type=F32
+        wt_ref[...], feats_ref[...], (((0,), (1,)), ((), ())), preferred_element_type=F32
     )
     inv = lax.rsqrt(jnp.sum(head * head, axis=0, keepdims=True) + EPS)
     unit = head * inv
@@ -192,10 +192,19 @@
     out_ref[...] = ((total[:cols] - unit_ref[...] * dots) * inv_ref[:, :rows]).astype(BF16)
 
 
-def sum_kernel(parts_ref, after_ref, out_ref):
-    total = jnp.sum(parts_ref[...].astype(F32), axis=0)
+def to_low(at_ref, total):
+    first = total[:EXTRA]
+    terms = [t.astype(F32) for t in split3(first[0:1] + first[1:2] + first[2:3])]
+    row = jnp.concatenate(terms + [jnp.zeros((EXTRA - 3, LANES), F32)], axis=0)
+    return jnp.where(at_ref[7] > 0, row, first).astype(BF16), total[EXTRA:].astype(BF16)
+
+
+def sum_kernel(at_ref, parts_ref, *refs):
+    out_ref = refs[-1]
+    first, rest = to_low(at_ref, jnp.sum(parts_ref[...].astype(F32), axis=0))
     for k in range(out_ref.shape[0]):
-        out_ref[k] = total
+        out_ref[k, :EXTRA] = first
+        out_ref[k, EXTRA:] = rest
 
 
 def feat_kernel(at_ref, weight_ref, *refs):
@@ -206,18 +215,6 @@
     out_ref[...] = lax.dot_general(
         back_ref[...], weight_ref[...], (((0,), (1,)), ((), ())), preferred_element_type=F32
     ).astype(BF16)
-
-
-def last_sum_kernel(at_ref, parts_ref, out_ref):
-    total = jnp.sum(parts_ref[...], axis=0)
-    low = total.astype(BF16)
-    first = total[:EXTRA]
-    terms = [t.astype(F32) for t in split3(first[0:1] + first[1:2] + first[2:3])]
-    row = jnp.concatenate(terms + [jnp.zeros((EXTRA - 3, LANES), F32)], axis=0).astype(BF16)
-    first = jnp.where(at_ref[7] > 0, row.astype(F32), first).astype(BF16)
-    for k in range(out_ref.shape[0]):
-        out_ref[k, :EXTRA] = first
-        out_ref[k, EXTRA:] = low[EXTRA:]
 
 
 def final_kernel(at_loss, pairs, full_ref, head_ref, loss_ref):
@@ -297,7 +294,7 @@
             shape((images, width), BF16),
         ],
         at,
-        head_weight.T,
+        head_weight,
         img_feat,
         fetched,
         swapped,
@@ -357,12 +354,12 @@
     parts = to_all(flat, ("y", "x")).reshape(plane, piece, LANES)
     part = pl.pallas_call(
         sum_kernel,
-        out_shape=shape((nzh, piece, LANES), F32),
-        in_specs=[VMEM, pl.BlockSpec(memory_space=pl.ANY)],
+        out_shape=shape((nzh, piece, LANES), BF16),
+        in_specs=[SMEM, VMEM, pl.BlockSpec(memory_space=pl.ANY)],
         out_specs=VMEM,
-    )(parts, back)
+    )(at, parts, back)
     part = to_all(part, "zh")
-    low_part = call(last_sum_kernel, shape((plane, piece, LANES), BF16), at, part, smem=1)
+    low_part = call(sum_kernel, shape((plane, piece, LANES), BF16), at, part, smem=1)
     full = to_all(low_part.reshape(plane * piece, LANES), ("y", "x"))
     group = rows * plane * nzh
     head_grad, loss = call(

time: 159 us -> 160 us (level)
  waiting for transfers between devices: 33.4 us -> 40.2 us
  local copies, waits for them, and re-layouts: 9.56 us -> 5.36 us
  blocking collectives: 15.8 us -> 13.6 us
    ppermute x6, waiting for transfers between devices: 12.3 us -> 19 us  [shift_by(): return lax.ppermute(x, axis, [(k, (k + step) % n) for k in range(n)])]
    unnamed x16 -> x17, local copies, waits for them, and re-layouts: 7.61 us -> 3.42 us
    ppermute x3, waiting for transfers between devices: 4.11 us -> 0.88 us  [local(): lax.ppermute(back, ('zl', 'c'), [(k, k ^ d) for k in range(nrep)])]
    all_to_all x3, waiting for transfers between devices: 3.37 us -> 6.27 us  [to_all(): return lax.all_to_all(copies, axes, 0, 0, tiled=True)]
    all_to_all x3, starting transfers between devices: 22.6 us -> 24.9 us  [to_all(): return lax.all_to_all(copies, axes, 0, 0, tiled=True)]
    all_to_all x1, blocking collectives: 15.8 us -> 13.6 us  [to_all(): return lax.all_to_all(copies, axes, 0, 0, tiled=True)]
  transfers between devices with their start and end apart: 17 -> 17, of which waited for: 8 -> 11; matrix products, arithmetic and copies ran while one was open for 3% -> 2% of each run, Pallas kernels for 6% -> 6%
where the time goes in v12:
time: 160 us; the launch traced here: 159 us
  starting transfers between devices  78.2 us (49%)
  waiting for transfers between devices  40.2 us (25%)
  Pallas kernels  19.5 us (12%)
  blocking collectives  13.6 us (8%)
  local copies, waits for them, and re-layouts  5.36 us (3%)
  between operations  2.26 us (1%)
    all_to_all x3, starting transfers between devices, to_all(): return lax.all_to_all(copies, axes, 0, 0, tiled=True)  24.9 us
    ppermute x6, starting transfers between devices, shift_by(): return lax.ppermute(x, axis, [(k, (k + step) % n) for k in range(n)])  23.4 us
    ppermute x6, waiting for transfers between devices, shift_by(): return lax.ppermute(x, axis, [(k, (k + step) % n) for k in range(n)])  19 us
    pallas_call x10, Pallas kernels, call(): pl.pallas_call(body, out_shape=outs, in_specs=specs, out_specs=[VMEM] * l...  17.6 us
    all_to_all x1, blocking collectives, to_all(): return lax.all_to_all(copies, axes, 0, 0, tiled=True)  13.6 us
    ppermute x1, starting transfers between devices, local(): beside = lax.ppermute(img_feat, line, near)  10.1 us
    ppermute x1, waiting for transfers between devices, local(): got2 = lax.ppermute(send2, 'zl', [(0, 1), (1, 0)])  7.64 us
    ppermute x3, starting transfers between devices, local(): lax.ppermute(back, ('zl', 'c'), [(k, k ^ d) for k in range(nrep)])  7.59 us
  transfers between devices with their start and end apart: 17, of which 11 were waited for; matrix products, arithmetic and copies ran while one was open for 2% of the time, Pallas kernels for 6%

profile of v12, /device:TPU:2, one launch (start us, length us, event | category | flops | bytes accessed | tf_op | source)
XLA Modules:
  0.0 159.2 jit_solution(16570190855139114224)
XLA Ops:
  0.7 0.9 copy-done.5
  1.6 1.0 shard_map.76
  2.5 7.2 %all-to-all-start = ((bf16[8,32,1152]{2,1,0:T(8,128)(2,1)}), bf16[8,32,1152]{2,1,0:T(8,128)(2,1)}, u32[]{:S(2)}, u32[]{:S(2)}) async-start(bf16[8,32,1152]{2,1,0:T(8,128)(2,1)} %bitcast.9), calls=%async_computation | async-start | bytes 1179648 | tf_op jit(solution)/shard_map/all_to_all | solution.py:48
  9.8 10.1 %collective-permute-start.2 = (bf16[128,1152]{1,0:T(8,128)(2,1)}, bf16[128,1152]{1,0:T(8,128)(2,1)}, u32[]{:S(2)}, u32[]{:S(2)}) collective-permute-start(bf16[128,1152]{1,0:T(8,128)(2,1)} %own_ref.1), channel_id=1, source_target_pairs={{2,4},{3,6},{0,13},{1,15},{6,8},{7,10},{4,1},{5,3},{10,12},{11,14}... | collective-permute-start | bytes 884744 | tf_op jit(solution)/shard_map/ppermute | solution.py:278
  19.9 0.9 constant_dynamic-slice_fusion
  20.8 4.2 %collective-permute-start.3 = (bf16[64,1152]{1,0:T(8,128)(2,1)S(1)}, bf16[64,1152]{1,0:T(8,128)(2,1)}, u32[]{:S(2)}, u32[]{:S(2)}) collective-permute-start(bf16[64,1152]{1,0:T(8,128)(2,1)S(1)} %constant_dynamic-slice_fusion), channel_id=1, source_target_pairs={{2,8},{3,9},{0,10},{1,11},{6,12},{7,13},{4,14},{5,15},{10,0},{11,1... | collective-permute-start | bytes 442376 | tf_op jit(solution)/shard_map/ppermute | solution.py:277
  25.0 4.0 %collective-permute-done.2 = bf16[128,1152]{1,0:T(8,128)(2,1)} collective-permute-done((bf16[128,1152]{1,0:T(8,128)(2,1)}, bf16[128,1152]{1,0:T(8,128)(2,1)}, u32[]{:S(2)}, u32[]{:S(2)}) %collective-permute-start.2) | collective-permute-done | bytes 294944 | tf_op jit(solution)/shard_map/ppermute | solution.py:278
  29.0 1.0 constant_dynamic-update-slice_fusion.1
  30.0 3.4 %collective-permute-start.5 = (bf16[256,1152]{1,0:T(8,128)(2,1)}, bf16[256,1152]{1,0:T(8,128)(2,1)}, u32[]{:S(2)}, u32[]{:S(2)}) collective-permute-start(bf16[256,1152]{1,0:T(8,128)(2,1)} %bitcast.10.own_ref), channel_id=1, source_target_pairs={{0,16},{16,32},{32,48},{48,0},{1,17},{17,33},{33,49},{49,1},{2,18}... | collective-permute-start | bytes 1769480 | tf_op jit(solution)/shard_map/ppermute | solution.py:231
  33.4 3.0 %collective-permute-start.1 = (bf16[256,1152]{1,0:T(8,128)(2,1)}, bf16[256,1152]{1,0:T(8,128)(2,1)}, u32[]{:S(2)}, u32[]{:S(2)}) collective-permute-start(bf16[256,1152]{1,0:T(8,128)(2,1)} %bitcast.10.own_ref), channel_id=1, source_target_pairs={{0,32},{16,48},{32,0},{48,16},{1,33},{17,49},{33,1},{49,17},{2,34}... | collective-permute-start | bytes 1769480 | tf_op jit(solution)/shard_map/ppermute | solution.py:231
  36.4 4.1 %collective-permute-start = (bf16[256,1152]{1,0:T(8,128)(2,1)}, bf16[256,1152]{1,0:T(8,128)(2,1)}, u32[]{:S(2)}, u32[]{:S(2)}) collective-permute-start(bf16[256,1152]{1,0:T(8,128)(2,1)} %bitcast.10.own_ref), channel_id=1, source_target_pairs={{0,48},{16,0},{32,16},{48,32},{1,49},{17,1},{33,17},{49,33},{2,50}... | collective-permute-start | bytes 1769480 | tf_op jit(solution)/shard_map/ppermute | solution.py:231
  40.5 0.9 constant_dynamic-update-slice_fusion.fetched_ref
  41.5 1.9 %collective-permute-start.4 = (bf16[192,1152]{1,0:T(8,128)(2,1)S(1)}, bf16[192,1152]{1,0:T(8,128)(2,1)}, u32[]{:S(2)}, u32[]{:S(2)}) collective-permute-start(bf16[192,1152]{1,0:T(8,128)(2,1)S(1)} %constant_dynamic-update-slice_fusion.fetched_ref), channel_id=1, source_target_pairs={{0,1},{1,0},{2,3},{3,2},{4,5},{5,4},{6,7},{7,6},{8,9},{9,8},{10,11... | collective-permute-start | bytes 1327112 | tf_op jit(solution)/shard_map/ppermute | solution.py:284
  44.7 0.1 stack.48.at_ref
  44.8 0.1 pad_maximum_fusion.par_ref
  44.9 0.4 collective-permute-done.4.swapped_ref
  45.3 3.4 %shard_map.77 = (f32[1152,512]{1,0:T(8,128)S(1)}, bf16[1152,512]{1,0:T(8,128)(2,1)S(1)}, f32[1,512]{1,0:T(1,128)S(1)}, f32[288,128]{1,0:T(8,128)S(1)}, f32[288,5...) custom-call(s32[12]{0:T(128)S(1)} %stack.48.at_ref, bf16[1152,1152]{1,0:T(8,128)(2,1)S(1)} %copy-done, ...), custom_call_target="tpu_custom_call" | custom-call | flops 2304 | bytes 3833904 | tf_op jit(solution)/shard_map/pallas_call | solution.py:24
  48.7 3.7 %shard_map.78 = (f32[1152,512]{1,0:T(8,128)S(1)}, f32[1,512]{1,0:T(1,128)S(1)}) custom-call(s32[12]{0:T(128)S(1)} %stack.48.at_ref, f32[2]{0:T(128)S(1)} %pad_maximum_fusion.par_ref, bf16[256,1152]{1,0:T(8,128)(2,1)} %bitcast.10.own_ref, bf16[256,1152]{1,0:T(8,128)(2,1)} %collective-permute-done.5.left_ref, bf16[1152,512]{1,0:T(8,128)(2,1)S(1)} %get-tuple-element.22.low_ref), custom_call_target="tpu_custom_call" | custom-call | flops 1207959552 | bytes 2359352 | tf_op jit(solution)/shard_map/pallas_call | solution.py:24
  52.4 1.0 collective-permute-done.1.far_ref
  53.4 10.2 %collective-permute-done.right_ref = bf16[256,1152]{1,0:T(8,128)(2,1)} collective-permute-done((bf16[256,1152]{1,0:T(8,128)(2,1)}, bf16[256,1152]{1,0:T(8,128)(2,1)}, u32[]{:S(2)}, u32[]{:S(2)}) %collective-permute-start) | collective-permute-done | bytes 589856 | tf_op jit(solution)/shard_map/ppermute | solution.py:231
  63.6 3.5 %shard_map.79 = (f32[592,512]{1,0:T(8,128)S(1)}, bf16[592,512]{1,0:T(8,128)(2,1)S(1)}) custom-call(s32[12]{0:T(128)S(1)} %stack.48.at_ref, f32[2]{0:T(128)S(1)} %pad_maximum_fusion.par_ref, bf16[256,1152]{1,0:T(8,128)(2,1)} %collective-permute-done.right_ref, bf16[256,1152]{1,0:T(8,128)(2,1)} %collective-permute-done.1.far_ref, ...), custom_call_target="tpu_custom_call" | custom-call | flops 1207959552 | bytes 7079992 | tf_op jit(solution)/shard_map/pallas_call | solution.py:24
  67.1 1.9 %collective-permute-start.6 = (bf16[592,512]{1,0:T(8,128)(2,1)S(1)}, bf16[592,512]{1,0:T(8,128)(2,1)S(1)}, u32[]{:S(2)}, u32[]{:S(2)}) collective-permute-start(bf16[592,512]{1,0:T(8,128)(2,1)S(1)} %get-tuple-element.27), channel_id=1, source_target_pairs={{0,1},{1,0},{2,3},{3,2},{4,5},{5,4},{6,7},{7,6},{8,9},{9,8},{10,11... | collective-permute-start | bytes 1818632 | tf_op jit(solution)/shard_map/ppermute | solution.py:330
  69.1 2.0 %collective-permute-done.6.got_ref = bf16[592,512]{1,0:T(8,128)(2,1)S(1)} collective-permute-done((bf16[592,512]{1,0:T(8,128)(2,1)S(1)}, bf16[592,512]{1,0:T(8,128)(2,1)S(1)}, u32[]{:S(2)}, u32[]{:S(2)}) %collective-permute-start.6) | collective-permute-done | bytes 606240 | tf_op jit(solution)/shard_map/ppermute | solution.py:330
  71.1 0.7 shard_map.80
  71.8 4.2 %collective-permute-start.7 = (bf16[304,512]{1,0:T(8,128)(2,1)S(1)}, bf16[304,512]{1,0:T(8,128)(2,1)S(1)}, u32[]{:S(2)}, u32[]{:S(2)}) collective-permute-start(bf16[304,512]{1,0:T(8,128)(2,1)S(1)} %get-tuple-element.29), channel_id=1, source_target_pairs={{0,2},{2,0},{1,3},{3,1},{4,6},{6,4},{5,7},{7,5},{8,10},{10,8},{9,1... | collective-permute-start | bytes 933896 | tf_op jit(solution)/shard_map/ppermute | solution.py:339
  75.9 7.6 %collective-permute-done.7.got_ref = bf16[304,512]{1,0:T(8,128)(2,1)S(1)} collective-permute-done((bf16[304,512]{1,0:T(8,128)(2,1)S(1)}, bf16[304,512]{1,0:T(8,128)(2,1)S(1)}, u32[]{:S(2)}, u32[]{:S(2)}) %collective-permute-start.7) | collective-permute-done | bytes 311328 | tf_op jit(solution)/shard_map/ppermute | solution.py:339
  83.6 1.5 shard_map.81
  85.1 8.8 %all-to-all-start.1 = ((bf16[32,88,128]{2,1,0:T(8,128)(2,1)}), bf16[32,88,128]{2,1,0:T(8,128)(2,1)}, u32[]{:S(2)}, u32[]{:S(2)}) async-start(bf16[32,88,128]{2,1,0:T(8,128)(2,1)} %bitcast.11), calls=%async_computation.1 | async-start | bytes 1441792 | tf_op jit(solution)/shard_map/all_to_all | solution.py:48
  93.9 6.6 %collective-permute-start.8 = (bf16[304,128]{1,0:T(8,128)(2,1)S(1)}, bf16[304,128]{1,0:T(8,128)(2,1)S(1)}, u32[]{:S(2)}, u32[]{:S(2)}) collective-permute-start(bf16[304,128]{1,0:T(8,128)(2,1)S(1)} %get-tuple-element.36), channel_id=1, source_target_pairs={{0,12},{4,0},{8,4},{12,8},{1,13},{5,1},{9,5},{13,9},{2,14},{6,2},{... | collective-permute-start | bytes 233480 | tf_op jit(solution)/shard_map/ppermute | solution.py:231
  100.6 4.4 %collective-permute-start.9 = (bf16[304,128]{1,0:T(8,128)(2,1)S(1)}, bf16[304,128]{1,0:T(8,128)(2,1)S(1)}, u32[]{:S(2)}, u32[]{:S(2)}) collective-permute-start(bf16[304,128]{1,0:T(8,128)(2,1)S(1)} %get-tuple-element.37), channel_id=1, source_target_pairs={{0,8},{4,12},{8,0},{12,4},{1,9},{5,13},{9,1},{13,5},{2,10},{6,14},... | collective-permute-start | bytes 233480 | tf_op jit(solution)/shard_map/ppermute | solution.py:231
  105.0 1.9 %collective-permute-start.10 = (bf16[304,128]{1,0:T(8,128)(2,1)S(1)}, bf16[304,128]{1,0:T(8,128)(2,1)S(1)}, u32[]{:S(2)}, u32[]{:S(2)}) collective-permute-start(bf16[304,128]{1,0:T(8,128)(2,1)S(1)} %get-tuple-element.38), channel_id=1, source_target_pairs={{0,4},{4,8},{8,12},{12,0},{1,5},{5,9},{9,13},{13,1},{2,6},{6,10},{... | collective-permute-start | bytes 233480 | tf_op jit(solution)/shard_map/ppermute | solution.py:231
  106.9 5.1 %collective-permute-done.9.refs_2_ = bf16[304,128]{1,0:T(8,128)(2,1)S(1)} collective-permute-done((bf16[304,128]{1,0:T(8,128)(2,1)S(1)}, bf16[304,128]{1,0:T(8,128)(2,1)S(1)}, u32[]{:S(2)}, u32[]{:S(2)}) %collective-permute-start.9) | collective-permute-done | bytes 77856 | tf_op jit(solution)/shard_map/ppermute | solution.py:231
  112.0 2.8 %collective-permute-done.10.refs_3_ = bf16[304,128]{1,0:T(8,128)(2,1)S(1)} collective-permute-done((bf16[304,128]{1,0:T(8,128)(2,1)S(1)}, bf16[304,128]{1,0:T(8,128)(2,1)S(1)}, u32[]{:S(2)}, u32[]{:S(2)}) %collective-permute-start.10) | collective-permute-done | bytes 77856 | tf_op jit(solution)/shard_map/ppermute | solution.py:231
  114.7 0.1 shard_map.82.refs_0_
  114.8 0.6 copy-done.3
  115.4 1.9 %shard_map.83 = bf16[4,88,128]{2,1,0:T(8,128)(2,1)} custom-call(s32[12]{0:T(128)} %copy-done.6, bf16[32,88,128]{2,1,0:T(8,128)(2,1)} %all-to-all-done.1.parts_ref, bf16[288,128]{1,0:T(8,128)(2,1)} %copy-done.3), custom_call_target="tpu_custom_call" | custom-call | tf_op jit(solution)/shard_map/pallas_call | solution.py:355
  117.4 13.6 %all_to_all.33.parts_ref = bf16[4,88,128]{2,1,0:T(8,128)(2,1)S(1)} all-to-all(bf16[4,88,128]{2,1,0:T(8,128)(2,1)} %shard_map.83), channel_id=1, replica_groups=mesh['y'=8,'x'=4,'zh'=4,'zl'=2,'c'=2] {'zh'}, dimensions={0} | all-to-all | bytes 180224 | tf_op jit(solution)/shard_map/all_to_all | solution.py:48
  131.0 0.6 shard_map.84
  131.6 0.9 copy-done.1
  132.4 8.8 %all-to-all-start.3 = ((bf16[32,88,128]{2,1,0:T(8,128)(2,1)}), bf16[32,88,128]{2,1,0:T(8,128)(2,1)S(1)}, u32[]{:S(2)}, u32[]{:S(2)}) async-start(bf16[32,88,128]{2,1,0:T(8,128)(2,1)} %copy-done.1), calls=%async_computation.3 | async-start | bytes 1441792 | tf_op jit(solution)/shard_map/all_to_all | solution.py:48
  141.3 1.9 %collective-permute-start.13 = (bf16[288,128]{1,0:T(8,128)(2,1)S(1)}, bf16[288,128]{1,0:T(8,128)(2,1)S(1)}, u32[]{:S(2)}, u32[]{:S(2)}) collective-permute-start(bf16[288,128]{1,0:T(8,128)(2,1)S(1)} %copy-done.4), channel_id=1, source_target_pairs={{0,3},{1,2},{2,1},{3,0},{4,7},{5,6},{6,5},{7,4},{8,11},{9,10},{10,... | collective-permute-start | bytes 221192 | tf_op jit(solution)/shard_map/ppermute | solution.py:373
  143.2 1.9 %collective-permute-start.12 = (bf16[288,128]{1,0:T(8,128)(2,1)S(1)}, bf16[288,128]{1,0:T(8,128)(2,1)S(1)}, u32[]{:S(2)}, u32[]{:S(2)}) collective-permute-start(bf16[288,128]{1,0:T(8,128)(2,1)S(1)} %copy-done.4), channel_id=1, source_target_pairs={{0,2},{1,3},{2,0},{3,1},{4,6},{5,7},{6,4},{7,5},{8,10},{9,11},{10,... | collective-permute-start | bytes 221192 | tf_op jit(solution)/shard_map/ppermute | solution.py:373
  145.1 3.7 %collective-permute-start.11 = (bf16[288,128]{1,0:T(8,128)(2,1)S(1)}, bf16[288,128]{1,0:T(8,128)(2,1)S(1)}, u32[]{:S(2)}, u32[]{:S(2)}) collective-permute-start(bf16[288,128]{1,0:T(8,128)(2,1)S(1)} %copy-done.4), channel_id=1, source_target_pairs={{0,1},{1,0},{2,3},{3,2},{4,5},{5,4},{6,7},{7,6},{8,9},{9,8},{10,11... | collective-permute-start | bytes 221192 | tf_op jit(solution)/shard_map/ppermute | solution.py:373
  148.9 0.8 collective-permute-done.12.refs_2_
  149.7 0.1 collective-permute-done.11.refs_1_
  149.8 2.2 %shard_map.86 = bf16[128,1152]{1,0:T(8,128)(2,1)} custom-call(s32[12]{0:T(128)S(1)} %copy-done.7, bf16[1152,1152]{1,0:T(8,128)(2,1)S(1)} %copy-done, bf16[288,128]{1,0:T(8,128)(2,1)S(1)} %copy-done.4, bf16[288,128]{1,0:T(8,128)(2,1)S(1)} %collective-permute-done.11.refs_1_, bf16[288,128]{1,0:T(8,128)(2,1)S(1)} %collective-permute-done.12.refs_2_, ...), custom_call_target="tpu_custom_call" | custom-call | flops 339738624 | bytes 2949168 | tf_op jit(solution)/shard_map/pallas_call | solution.py:24
  152.0 6.3 %all-to-all-done.3 = bf16[32,88,128]{2,1,0:T(8,128)(2,1)S(1)} async-done(((bf16[32,88,128]{2,1,0:T(8,128)(2,1)}), bf16[32,88,128]{2,1,0:T(8,128)(2,1)S(1)}, u32[]{:S(2)}, u32[]{:S(2)}) %all-to-all-start.3) | async-done | bytes 720928 | tf_op jit(solution)/shard_map/all_to_all | solution.py:48
  158.2 1.0 shard_map.85
  (19 shorter events, 0.0 us)
Async XLA Ops:
  0.6 44.6 %copy-start.2 = (bf16[128,1152]{1,0:T(8,128)(2,1)S(1)}, bf16[128,1152]{1,0:T(8,128)(2,1)}, u32[]{:S(2)}) copy-start(bf16[128,1152]{1,0:T(8,128)(2,1)} %own_ref.1) | copy-start | bytes 884740
  0.6 0.9 copy-start.5
  1.6 43.7 %copy-start = (bf16[1152,1152]{1,0:T(8,128)(2,1)S(1)}, bf16[1152,1152]{1,0:T(8,128)(2,1)}, u32[]{:S(2)}) copy-start(bf16[1152,1152]{1,0:T(8,128)(2,1)} %weight_ref.1) | copy-start | bytes 7962628
  2.5 27.5 %all-to-all-start = ((bf16[8,32,1152]{2,1,0:T(8,128)(2,1)}), bf16[8,32,1152]{2,1,0:T(8,128)(2,1)}, u32[]{:S(2)}, u32[]{:S(2)}) async-start(bf16[8,32,1152]{2,1,0:T(8,128)(2,1)} %bitcast.9), calls=%async_computation | async-start | bytes 1179648 | tf_op jit(solution)/shard_map/all_to_all | solution.py:48
  9.8 19.2 %collective-permute-start.2 = (bf16[128,1152]{1,0:T(8,128)(2,1)}, bf16[128,1152]{1,0:T(8,128)(2,1)}, u32[]{:S(2)}, u32[]{:S(2)}) collective-permute-start(bf16[128,1152]{1,0:T(8,128)(2,1)} %own_ref.1), channel_id=1, source_target_pairs={{2,4},{3,6},{0,13},{1,15},{6,8},{7,10},{4,1},{5,3},{10,12},{11,14}... | collective-permute-start | bytes 884744 | tf_op jit(solution)/shard_map/ppermute | solution.py:278
  20.8 19.7 %collective-permute-start.3 = (bf16[64,1152]{1,0:T(8,128)(2,1)S(1)}, bf16[64,1152]{1,0:T(8,128)(2,1)}, u32[]{:S(2)}, u32[]{:S(2)}) collective-permute-start(bf16[64,1152]{1,0:T(8,128)(2,1)S(1)} %constant_dynamic-slice_fusion), channel_id=1, source_target_pairs={{2,8},{3,9},{0,10},{1,11},{6,12},{7,13},{4,14},{5,15},{10,0},{11,1... | collective-permute-start | bytes 442376 | tf_op jit(solution)/shard_map/ppermute | solution.py:277
  30.0 18.7 %collective-permute-start.5 = (bf16[256,1152]{1,0:T(8,128)(2,1)}, bf16[256,1152]{1,0:T(8,128)(2,1)}, u32[]{:S(2)}, u32[]{:S(2)}) collective-permute-start(bf16[256,1152]{1,0:T(8,128)(2,1)} %bitcast.10.own_ref), channel_id=1, source_target_pairs={{0,16},{16,32},{32,48},{48,0},{1,17},{17,33},{33,49},{49,1},{2,18}... | collective-permute-start | bytes 1769480 | tf_op jit(solution)/shard_map/ppermute | solution.py:231
  33.4 20.0 %collective-permute-start.1 = (bf16[256,1152]{1,0:T(8,128)(2,1)}, bf16[256,1152]{1,0:T(8,128)(2,1)}, u32[]{:S(2)}, u32[]{:S(2)}) collective-permute-start(bf16[256,1152]{1,0:T(8,128)(2,1)} %bitcast.10.own_ref), channel_id=1, source_target_pairs={{0,32},{16,48},{32,0},{48,16},{1,33},{17,49},{33,1},{49,17},{2,34}... | collective-permute-start | bytes 1769480 | tf_op jit(solution)/shard_map/ppermute | solution.py:231
  36.4 27.2 %collective-permute-start = (bf16[256,1152]{1,0:T(8,128)(2,1)}, bf16[256,1152]{1,0:T(8,128)(2,1)}, u32[]{:S(2)}, u32[]{:S(2)}) collective-permute-start(bf16[256,1152]{1,0:T(8,128)(2,1)} %bitcast.10.own_ref), channel_id=1, source_target_pairs={{0,48},{16,0},{32,16},{48,32},{1,49},{17,1},{33,17},{49,33},{2,50}... | collective-permute-start | bytes 1769480 | tf_op jit(solution)/shard_map/ppermute | solution.py:231
  41.5 3.8 %collective-permute-start.4 = (bf16[192,1152]{1,0:T(8,128)(2,1)S(1)}, bf16[192,1152]{1,0:T(8,128)(2,1)}, u32[]{:S(2)}, u32[]{:S(2)}) collective-permute-start(bf16[192,1152]{1,0:T(8,128)(2,1)S(1)} %constant_dynamic-update-slice_fusion.fetched_ref), channel_id=1, source_target_pairs={{0,1},{1,0},{2,3},{3,2},{4,5},{5,4},{6,7},{7,6},{8,9},{9,8},{10,11... | collective-permute-start | bytes 1327112 | tf_op jit(solution)/shard_map/ppermute | solution.py:284
  44.8 26.2 %copy-start.6 = (s32[12]{0:T(128)}, s32[12]{0:T(128)S(1)}, u32[]{:S(2)}) copy-start(s32[12]{0:T(128)S(1)} %stack.48.at_ref) | copy-start | bytes 148
  67.1 3.9 %collective-permute-start.6 = (bf16[592,512]{1,0:T(8,128)(2,1)S(1)}, bf16[592,512]{1,0:T(8,128)(2,1)S(1)}, u32[]{:S(2)}, u32[]{:S(2)}) collective-permute-start(bf16[592,512]{1,0:T(8,128)(2,1)S(1)} %get-tuple-element.27), channel_id=1, source_target_pairs={{0,1},{1,0},{2,3},{3,2},{4,5},{5,4},{6,7},{7,6},{8,9},{9,8},{10,11... | collective-permute-start | bytes 1818632 | tf_op jit(solution)/shard_map/ppermute | solution.py:330
  71.8 11.8 %collective-permute-start.7 = (bf16[304,512]{1,0:T(8,128)(2,1)S(1)}, bf16[304,512]{1,0:T(8,128)(2,1)S(1)}, u32[]{:S(2)}, u32[]{:S(2)}) collective-permute-start(bf16[304,512]{1,0:T(8,128)(2,1)S(1)} %get-tuple-element.29), channel_id=1, source_target_pairs={{0,2},{2,0},{1,3},{3,1},{4,6},{6,4},{5,7},{7,5},{8,10},{10,8},{9,1... | collective-permute-start | bytes 933896 | tf_op jit(solution)/shard_map/ppermute | solution.py:339
  83.6 47.4 %copy-start.7 = (s32[12]{0:T(128)S(1)}, s32[12]{0:T(128)}, u32[]{:S(2)}) copy-start(s32[12]{0:T(128)} %copy-done.6) | copy-start | bytes 148
  85.1 30.4 %all-to-all-start.1 = ((bf16[32,88,128]{2,1,0:T(8,128)(2,1)}), bf16[32,88,128]{2,1,0:T(8,128)(2,1)}, u32[]{:S(2)}, u32[]{:S(2)}) async-start(bf16[32,88,128]{2,1,0:T(8,128)(2,1)} %bitcast.11), calls=%async_computation.1 | async-start | bytes 1441792 | tf_op jit(solution)/shard_map/all_to_all | solution.py:48
  93.9 13.0 %collective-permute-start.8 = (bf16[304,128]{1,0:T(8,128)(2,1)S(1)}, bf16[304,128]{1,0:T(8,128)(2,1)S(1)}, u32[]{:S(2)}, u32[]{:S(2)}) collective-permute-start(bf16[304,128]{1,0:T(8,128)(2,1)S(1)} %get-tuple-element.36), channel_id=1, source_target_pairs={{0,12},{4,0},{8,4},{12,8},{1,13},{5,1},{9,5},{13,9},{2,14},{6,2},{... | collective-permute-start | bytes 233480 | tf_op jit(solution)/shard_map/ppermute | solution.py:231
  100.6 11.4 %collective-permute-start.9 = (bf16[304,128]{1,0:T(8,128)(2,1)S(1)}, bf16[304,128]{1,0:T(8,128)(2,1)S(1)}, u32[]{:S(2)}, u32[]{:S(2)}) collective-permute-start(bf16[304,128]{1,0:T(8,128)(2,1)S(1)} %get-tuple-element.37), channel_id=1, source_target_pairs={{0,8},{4,12},{8,0},{12,4},{1,9},{5,13},{9,1},{13,5},{2,10},{6,14},... | collective-permute-start | bytes 233480 | tf_op jit(solution)/shard_map/ppermute | solution.py:231
  105.0 9.8 %collective-permute-start.10 = (bf16[304,128]{1,0:T(8,128)(2,1)S(1)}, bf16[304,128]{1,0:T(8,128)(2,1)S(1)}, u32[]{:S(2)}, u32[]{:S(2)}) collective-permute-start(bf16[304,128]{1,0:T(8,128)(2,1)S(1)} %get-tuple-element.38), channel_id=1, source_target_pairs={{0,4},{4,8},{8,12},{12,0},{1,5},{5,9},{9,13},{13,1},{2,6},{6,10},{... | collective-permute-start | bytes 233480 | tf_op jit(solution)/shard_map/ppermute | solution.py:231
  114.8 0.6 copy-start.3
  115.4 25.8 %copy-start.4 = (bf16[288,128]{1,0:T(8,128)(2,1)S(1)}, bf16[288,128]{1,0:T(8,128)(2,1)}, u32[]{:S(2)}) copy-start(bf16[288,128]{1,0:T(8,128)(2,1)} %copy-done.3) | copy-start | bytes 221188
  131.6 0.9 copy-start.1
  132.4 25.8 %all-to-all-start.3 = ((bf16[32,88,128]{2,1,0:T(8,128)(2,1)}), bf16[32,88,128]{2,1,0:T(8,128)(2,1)S(1)}, u32[]{:S(2)}, u32[]{:S(2)}) async-start(bf16[32,88,128]{2,1,0:T(8,128)(2,1)} %copy-done.1), calls=%async_computation.3 | async-start | bytes 1441792 | tf_op jit(solution)/shard_map/all_to_all | solution.py:48
  141.3 7.6 %collective-permute-start.13 = (bf16[288,128]{1,0:T(8,128)(2,1)S(1)}, bf16[288,128]{1,0:T(8,128)(2,1)S(1)}, u32[]{:S(2)}, u32[]{:S(2)}) collective-permute-start(bf16[288,128]{1,0:T(8,128)(2,1)S(1)} %copy-done.4), channel_id=1, source_target_pairs={{0,3},{1,2},{2,1},{3,0},{4,7},{5,6},{6,5},{7,4},{8,11},{9,10},{10,... | collective-permute-start | bytes 221192 | tf_op jit(solution)/shard_map/ppermute | solution.py:373
  143.2 6.5 %collective-permute-start.12 = (bf16[288,128]{1,0:T(8,128)(2,1)S(1)}, bf16[288,128]{1,0:T(8,128)(2,1)S(1)}, u32[]{:S(2)}, u32[]{:S(2)}) collective-permute-start(bf16[288,128]{1,0:T(8,128)(2,1)S(1)} %copy-done.4), channel_id=1, source_target_pairs={{0,2},{1,3},{2,0},{3,1},{4,6},{5,7},{6,4},{7,5},{8,10},{9,11},{10,... | collective-permute-start | bytes 221192 | tf_op jit(solution)/shard_map/ppermute | solution.py:373
  145.1 4.6 %collective-permute-start.11 = (bf16[288,128]{1,0:T(8,128)(2,1)S(1)}, bf16[288,128]{1,0:T(8,128)(2,1)S(1)}, u32[]{:S(2)}, u32[]{:S(2)}) collective-permute-start(bf16[288,128]{1,0:T(8,128)(2,1)S(1)} %copy-done.4), channel_id=1, source_target_pairs={{0,1},{1,0},{2,3},{3,2},{4,5},{5,4},{6,7},{7,6},{8,9},{9,8},{10,11... | collective-permute-start | bytes 221192 | tf_op jit(solution)/shard_map/ppermute | solution.py:373

commit v13 on v11

--- a/solution.py
+++ b/solution.py
@@ -57,6 +57,11 @@
         out_ref[k * n : (k + 1) * n] = low
 
 
+def join_kernel(a_ref, b_ref, out_ref):
+    out_ref[: a_ref.shape[0]] = a_ref[...]
+    out_ref[a_ref.shape[0] :] = b_ref[...]
+
+
 def image_kernel(at_ref, wt_ref, own_ref, fetched_ref, swapped_ref, *refs):
     unit_ref, low_ref, inv_ref, own_unit_ref, cols_ref, feats_ref = refs
     rows = own_ref.shape[0]
@@ -67,7 +72,7 @@
         feats_ref[pl.ds(pl.multiple_of((1 + 2 * k) * rows, 16), rows), :] = ref[:rows]
         feats_ref[pl.ds(pl.multiple_of(2 * rows + k * part, 16), part), :] = ref[rows:]
     head = lax.dot_general(
-        wt_ref[...], feats_ref[...], (((1,), (1,)), ((), ())), preferred_element_type=F32
+        wt_ref[...], feats_ref[...], (((0,), (1,)), ((), ())), preferred_element_type=F32
     )
     inv = lax.rsqrt(jnp.sum(head * head, axis=0, keepdims=True) + EPS)
     unit = head * inv
@@ -281,7 +286,9 @@
     line = ("zh", "zl", "c")
     across = lax.ppermute(half_rows, line, cross)
     beside = lax.ppermute(img_feat, line, near)
-    fetched = jnp.concatenate([beside, across], axis=0)
+    fetched = call(
+        join_kernel, shape((beside.shape[0] + across.shape[0], width), BF16), beside, across
+    )
     own = to_all(copies, "y")
     far = shift_by(own, "x", 2)
     left = shift_by(own, "x", 1)
@@ -299,7 +306,7 @@
             shape((images, width), BF16),
         ],
         at,
-        head_weight.T,
+        head_weight,
         img_feat,
         fetched,
         swapped,
@@ -315,7 +322,7 @@
         left,
         low,
         smem=2,
-        flops=2 * 4 * width * images * own.shape[0],
+        flops=width,
     )
     acc, loss_row = call(
         next_kernel,
@@ -364,10 +371,15 @@
     )
 
     dirs = [dirs[0]] + [shift_by(dirs[s], "zh", -s) for s in range(1, nzh)]
-    back = call(back_kernel, shape((cols, rows), BF16), own_unit, inv, *dirs, flops=2 * 10**10)
+    back = call(back_kernel, shape((cols, rows), BF16), own_unit, inv, *dirs)
 
     parts = to_all(flat, ("y", "x")).reshape(plane, piece, LANES)
-    part = call(sum_kernel, shape((nzh, piece, LANES), BF16), at, parts, smem=1)
+    part = pl.pallas_call(
+        sum_kernel,
+        out_shape=shape((nzh, piece, LANES), BF16),
+        in_specs=[SMEM, VMEM, pl.BlockSpec(memory_space=pl.ANY)],
+        out_specs=VMEM,
+    )(at, parts, back)
     part = to_all(part, "zh")
     low_part = call(sum_kernel, shape((plane, piece, LANES), BF16), at, part, smem=1)
     full = to_all(low_part.reshape(plane * piece, LANES), ("y", "x"))

time: 165 us -> 160 us (0.970)
  blocking collectives: 30.8 us -> 15.8 us
  waiting for transfers between devices: 25 us -> 34.3 us
  local copies, waits for them, and re-layouts: 10.3 us -> 4.12 us
  starting transfers between devices: 74 us -> 79.5 us
  Pallas kernels: 21.1 us -> 22.9 us
    all_to_all x1, blocking collectives: 30.8 us -> 15.8 us  [to_all(): return lax.all_to_all(copies, axes, 0, 0, tiled=True)]
    ppermute x6, waiting for transfers between devices: 4.62 us -> 12.9 us  [shift_by(): return lax.ppermute(x, axis, [(k, (k + step) % n) for k in range(n)])]
    unnamed x16 -> x20, local copies, waits for them, and re-layouts: 8.33 us -> 2.45 us
    all_to_all x3, starting transfers between devices: 19.5 us -> 24.3 us  [to_all(): return lax.all_to_all(copies, axes, 0, 0, tiled=True)]
    all_to_all x3, waiting for transfers between devices: 5.58 us -> 10 us  [to_all(): return lax.all_to_all(copies, axes, 0, 0, tiled=True)]
    ppermute x1, waiting for transfers between devices: 3.99 us -> 0.01 us  [local(): beside = lax.ppermute(img_feat, line, near)]
    pallas_call x0 -> x1, Pallas kernels: none -> 1.9 us  [local(): pl.pallas_call(sum_kernel, out_shape=shape((nzh, piece, LANES), BF16), in...]
  transfers between devices with their start and end apart: 17 -> 17, of which waited for: 6 -> 10; matrix products, arithmetic and copies ran while one was open for 3% -> 1% of each run, Pallas kernels for 8% -> 9%
where the time goes in v13:
time: 160 us; the launch traced here: 159 us
  starting transfers between devices  79.5 us (50%)
  waiting for transfers between devices  34.3 us (21%)
  Pallas kernels  22.9 us (14%)
  blocking collectives  15.8 us (10%)
  local copies, waits for them, and re-layouts  4.12 us (3%)
  between operations  2.29 us (1%)
    ppermute x6, starting transfers between devices, shift_by(): return lax.ppermute(x, axis, [(k, (k + step) % n) for k in range(n)])  24.4 us
    all_to_all x3, starting transfers between devices, to_all(): return lax.all_to_all(copies, axes, 0, 0, tiled=True)  24.3 us
    pallas_call x12, Pallas kernels, call(): pl.pallas_call(body, out_shape=outs, in_specs=specs, out_specs=[VMEM] * l...  21 us
    all_to_all x1, blocking collectives, to_all(): return lax.all_to_all(copies, axes, 0, 0, tiled=True)  15.8 us
    ppermute x6, waiting for transfers between devices, shift_by(): return lax.ppermute(x, axis, [(k, (k + step) % n) for k in range(n)])  12.9 us
    ppermute x1, starting transfers between devices, local(): beside = lax.ppermute(img_feat, line, near)  10.1 us
    all_to_all x3, waiting for transfers between devices, to_all(): return lax.all_to_all(copies, axes, 0, 0, tiled=True)  10 us
    ppermute x3, starting transfers between devices, local(): lax.ppermute(back, ('zl', 'c'), [(k, k ^ d) for k in range(nrep)])  8.26 us
  transfers between devices with their start and end apart: 17, of which 10 were waited for; matrix products, arithmetic and copies ran while one was open for 1% of the time, Pallas kernels for 9%

profile of v13, /device:TPU:2, one launch (start us, length us, event | category | flops | bytes accessed | tf_op | source)
XLA Modules:
  0.0 158.9 jit_solution(14238247041948171639)
XLA Ops:
  0.7 0.9 copy-done.7
  1.6 1.0 shard_map.76
  2.5 7.2 %all-to-all-start = ((bf16[8,32,1152]{2,1,0:T(8,128)(2,1)}), bf16[8,32,1152]{2,1,0:T(8,128)(2,1)S(1)}, u32[]{:S(2)}, u32[]{:S(2)}) async-start(bf16[8,32,1152]{2,1,0:T(8,128)(2,1)} %bitcast.9), calls=%async_computation | async-start | bytes 1179648 | tf_op jit(solution)/shard_map/all_to_all | solution.py:48
  9.8 10.1 %collective-permute-start.1 = (bf16[128,1152]{1,0:T(8,128)(2,1)}, bf16[128,1152]{1,0:T(8,128)(2,1)}, u32[]{:S(2)}, u32[]{:S(2)}) collective-permute-start(bf16[128,1152]{1,0:T(8,128)(2,1)} %own_ref.1), channel_id=1, source_target_pairs={{2,4},{3,6},{0,13},{1,15},{6,8},{7,10},{4,1},{5,3},{10,12},{11,14}... | collective-permute-start | bytes 884744 | tf_op jit(solution)/shard_map/ppermute | solution.py:288
  19.9 1.6 constant_dynamic-slice_fusion
  21.4 4.2 %collective-permute-start.2 = (bf16[64,1152]{1,0:T(8,128)(2,1)}, bf16[64,1152]{1,0:T(8,128)(2,1)}, u32[]{:S(2)}, u32[]{:S(2)}) collective-permute-start(bf16[64,1152]{1,0:T(8,128)(2,1)} %constant_dynamic-slice_fusion), channel_id=1, source_target_pairs={{2,8},{3,9},{0,10},{1,11},{6,12},{7,13},{4,14},{5,15},{10,0},{11,1... | collective-permute-start | bytes 442376 | tf_op jit(solution)/shard_map/ppermute | solution.py:287
  25.7 3.0 %all-to-all-done = bf16[8,32,1152]{2,1,0:T(8,128)(2,1)S(1)} async-done(((bf16[8,32,1152]{2,1,0:T(8,128)(2,1)}), bf16[8,32,1152]{2,1,0:T(8,128)(2,1)S(1)}, u32[]{:S(2)}, u32[]{:S(2)}) %all-to-all-start) | async-done | bytes 589856 | tf_op jit(solution)/shard_map/all_to_all | solution.py:48
  28.7 3.4 %collective-permute-start.5 = (bf16[256,1152]{1,0:T(8,128)(2,1)S(1)}, bf16[256,1152]{1,0:T(8,128)(2,1)}, u32[]{:S(2)}, u32[]{:S(2)}) collective-permute-start(bf16[256,1152]{1,0:T(8,128)(2,1)S(1)} %bitcast.16), channel_id=1, source_target_pairs={{0,16},{16,32},{32,48},{48,0},{1,17},{17,33},{33,49},{49,1},{2,18}... | collective-permute-start | bytes 1769480 | tf_op jit(solution)/shard_map/ppermute | solution.py:241
  32.1 2.4 %collective-permute-start.4 = (bf16[256,1152]{1,0:T(8,128)(2,1)S(1)}, bf16[256,1152]{1,0:T(8,128)(2,1)}, u32[]{:S(2)}, u32[]{:S(2)}) collective-permute-start(bf16[256,1152]{1,0:T(8,128)(2,1)S(1)} %bitcast.17), channel_id=1, source_target_pairs={{0,48},{16,0},{32,16},{48,32},{1,49},{17,1},{33,17},{49,33},{2,50}... | collective-permute-start | bytes 1769480 | tf_op jit(solution)/shard_map/ppermute | solution.py:241
  34.5 4.0 %collective-permute-start = (bf16[256,1152]{1,0:T(8,128)(2,1)S(1)}, bf16[256,1152]{1,0:T(8,128)(2,1)}, u32[]{:S(2)}, u32[]{:S(2)}) collective-permute-start(bf16[256,1152]{1,0:T(8,128)(2,1)S(1)} %bitcast.18), channel_id=1, source_target_pairs={{0,32},{16,48},{32,0},{48,16},{1,33},{17,49},{33,1},{49,17},{2,34}... | collective-permute-start | bytes 1769480 | tf_op jit(solution)/shard_map/ppermute | solution.py:241
  38.6 1.8 %shard_map.77.fetched_ref = bf16[192,1152]{1,0:T(8,128)(2,1)} custom-call(bf16[128,1152]{1,0:T(8,128)(2,1)} %collective-permute-done.1.a_ref, bf16[64,1152]{1,0:T(8,128)(2,1)} %collective-permute-done.2.b_ref), custom_call_target="tpu_custom_call" | custom-call | bytes 442368 | tf_op jit(solution)/shard_map/pallas_call | solution.py:24
  40.4 1.9 %collective-permute-start.3 = (bf16[192,1152]{1,0:T(8,128)(2,1)}, bf16[192,1152]{1,0:T(8,128)(2,1)}, u32[]{:S(2)}, u32[]{:S(2)}) collective-permute-start(bf16[192,1152]{1,0:T(8,128)(2,1)} %shard_map.77.fetched_ref), channel_id=1, source_target_pairs={{0,1},{1,0},{2,3},{3,2},{4,5},{5,4},{6,7},{7,6},{8,9},{9,8},{10,11... | collective-permute-start | bytes 1327112 | tf_op jit(solution)/shard_map/ppermute | solution.py:296
  43.6 0.1 stack.48.at_ref
  43.7 0.0 copy-start.8
  43.7 0.1 pad_maximum_fusion.par_ref
  43.8 0.6 collective-permute-done.3.swapped_ref
  44.4 3.6 %shard_map.78 = (f32[1152,512]{1,0:T(8,128)S(1)}, bf16[1152,512]{1,0:T(8,128)(2,1)S(1)}, f32[1,512]{1,0:T(1,128)S(1)}, f32[288,128]{1,0:T(8,128)S(1)}, f32[288,5...) custom-call(s32[12]{0:T(128)S(1)} %stack.48.at_ref, bf16[1152,1152]{1,0:T(8,128)(2,1)S(1)} %copy-done, ...), custom_call_target="tpu_custom_call" | custom-call | flops 2304 | bytes 3833904 | tf_op jit(solution)/shard_map/pallas_call | solution.py:24
  48.0 3.6 %shard_map.79 = (f32[1152,512]{1,0:T(8,128)S(1)}, f32[1,512]{1,0:T(1,128)S(1)}) custom-call(s32[12]{0:T(128)S(1)} %stack.48.at_ref, f32[2]{0:T(128)S(1)} %pad_maximum_fusion.par_ref, bf16[256,1152]{1,0:T(8,128)(2,1)S(1)} %bitcast.19, bf16[256,1152]{1,0:T(8,128)(2,1)} %collective-permute-done.5.left_ref, bf16[1152,512]{1,0:T(8,128)(2,1)S(1)} %get-tuple-element.24.low_ref), custom_call_target="tpu_custom_call" | custom-call | flops 1152 | bytes 2359352 | tf_op jit(solution)/shard_map/pallas_call | solution.py:24
  51.6 2.5 %shard_map.80 = (f32[1152,512]{1,0:T(8,128)S(1)}, f32[1,512]{1,0:T(1,128)S(1)}) custom-call(f32[2]{0:T(128)S(1)} %pad_maximum_fusion.par_ref, bf16[256,1152]{1,0:T(8,128)(2,1)} %collective-permute-done.4.texts_ref, bf16[1152,512]{1,0:T(8,128)(2,1)S(1)} %get-tuple-element.24.low_ref, f32[1152,512]{1,0:T(8,128)S(1)} %get-tuple-element.26.acc_in_ref, ...), custom_call_target="tpu_custom_call" | custom-call | flops 1152 | bytes 4130824 | tf_op jit(solution)/shard_map/pallas_call | solution.py:24
  54.0 8.3 %collective-permute-done.texts_ref = bf16[256,1152]{1,0:T(8,128)(2,1)} collective-permute-done((bf16[256,1152]{1,0:T(8,128)(2,1)S(1)}, bf16[256,1152]{1,0:T(8,128)(2,1)}, u32[]{:S(2)}, u32[]{:S(2)}) %collective-permute-start) | collective-permute-done | bytes 589856 | tf_op jit(solution)/shard_map/ppermute | solution.py:241
  62.3 2.6 %shard_map.81 = (f32[592,512]{1,0:T(8,128)S(1)}, bf16[592,512]{1,0:T(8,128)(2,1)S(1)}) custom-call(s32[12]{0:T(128)S(1)} %stack.48.at_ref, f32[2]{0:T(128)S(1)} %pad_maximum_fusion.par_ref, bf16[256,1152]{1,0:T(8,128)(2,1)} %collective-permute-done.texts_ref, bf16[1152,512]{1,0:T(8,128)(2,1)S(1)} %get-tuple-element.24.low_ref, ...), custom_call_target="tpu_custom_call" | custom-call | flops 603979776 | bytes 6490168 | tf_op jit(solution)/shard_map/pallas_call | solution.py:24
  64.9 1.9 %collective-permute-start.6 = (bf16[592,512]{1,0:T(8,128)(2,1)S(1)}, bf16[592,512]{1,0:T(8,128)(2,1)S(1)}, u32[]{:S(2)}, u32[]{:S(2)}) collective-permute-start(bf16[592,512]{1,0:T(8,128)(2,1)S(1)} %get-tuple-element.31), channel_id=1, source_target_pairs={{0,1},{1,0},{2,3},{3,2},{4,5},{5,4},{6,7},{7,6},{8,9},{9,8},{10,11... | collective-permute-start | bytes 1818632 | tf_op jit(solution)/shard_map/ppermute | solution.py:352
  66.9 2.0 %collective-permute-done.6.got_ref = bf16[592,512]{1,0:T(8,128)(2,1)S(1)} collective-permute-done((bf16[592,512]{1,0:T(8,128)(2,1)S(1)}, bf16[592,512]{1,0:T(8,128)(2,1)S(1)}, u32[]{:S(2)}, u32[]{:S(2)}) %collective-permute-start.6) | collective-permute-done | bytes 606240 | tf_op jit(solution)/shard_map/ppermute | solution.py:352
  68.9 0.7 shard_map.82
  69.6 4.4 %collective-permute-start.7 = (bf16[304,512]{1,0:T(8,128)(2,1)S(1)}, bf16[304,512]{1,0:T(8,128)(2,1)S(1)}, u32[]{:S(2)}, u32[]{:S(2)}) collective-permute-start(bf16[304,512]{1,0:T(8,128)(2,1)S(1)} %get-tuple-element.33), channel_id=1, source_target_pairs={{0,2},{2,0},{1,3},{3,1},{4,6},{6,4},{5,7},{7,5},{8,10},{10,8},{9,1... | collective-permute-start | bytes 933896 | tf_op jit(solution)/shard_map/ppermute | solution.py:361
  74.0 7.6 %collective-permute-done.7.got_ref = bf16[304,512]{1,0:T(8,128)(2,1)S(1)} collective-permute-done((bf16[304,512]{1,0:T(8,128)(2,1)S(1)}, bf16[304,512]{1,0:T(8,128)(2,1)S(1)}, u32[]{:S(2)}, u32[]{:S(2)}) %collective-permute-start.7) | collective-permute-done | bytes 311328 | tf_op jit(solution)/shard_map/ppermute | solution.py:361
  81.6 1.5 shard_map.83
  83.1 9.3 %all-to-all-start.1 = ((bf16[32,88,128]{2,1,0:T(8,128)(2,1)}), bf16[32,88,128]{2,1,0:T(8,128)(2,1)}, u32[]{:S(2)}, u32[]{:S(2)}) async-start(bf16[32,88,128]{2,1,0:T(8,128)(2,1)} %bitcast.11), calls=%async_computation.1 | async-start | bytes 1441792 | tf_op jit(solution)/shard_map/all_to_all | solution.py:48
  92.4 7.8 %collective-permute-start.8 = (bf16[304,128]{1,0:T(8,128)(2,1)S(1)}, bf16[304,128]{1,0:T(8,128)(2,1)S(1)}, u32[]{:S(2)}, u32[]{:S(2)}) collective-permute-start(bf16[304,128]{1,0:T(8,128)(2,1)S(1)} %get-tuple-element.40), channel_id=1, source_target_pairs={{0,12},{4,0},{8,4},{12,8},{1,13},{5,1},{9,5},{13,9},{2,14},{6,2},{... | collective-permute-start | bytes 233480 | tf_op jit(solution)/shard_map/ppermute | solution.py:241
  100.2 1.9 %collective-permute-start.9 = (bf16[304,128]{1,0:T(8,128)(2,1)S(1)}, bf16[304,128]{1,0:T(8,128)(2,1)S(1)}, u32[]{:S(2)}, u32[]{:S(2)}) collective-permute-start(bf16[304,128]{1,0:T(8,128)(2,1)S(1)} %get-tuple-element.41), channel_id=1, source_target_pairs={{0,8},{4,12},{8,0},{12,4},{1,9},{5,13},{9,1},{13,5},{2,10},{6,14},... | collective-permute-start | bytes 233480 | tf_op jit(solution)/shard_map/ppermute | solution.py:241
  102.2 4.8 %collective-permute-start.10 = (bf16[304,128]{1,0:T(8,128)(2,1)S(1)}, bf16[304,128]{1,0:T(8,128)(2,1)S(1)}, u32[]{:S(2)}, u32[]{:S(2)}) collective-permute-start(bf16[304,128]{1,0:T(8,128)(2,1)S(1)} %get-tuple-element.42), channel_id=1, source_target_pairs={{0,4},{4,8},{8,12},{12,0},{1,5},{5,9},{9,13},{13,1},{2,6},{6,10},{... | collective-permute-start | bytes 233480 | tf_op jit(solution)/shard_map/ppermute | solution.py:241
  107.0 4.6 %collective-permute-done.9.refs_2_ = bf16[304,128]{1,0:T(8,128)(2,1)S(1)} collective-permute-done((bf16[304,128]{1,0:T(8,128)(2,1)S(1)}, bf16[304,128]{1,0:T(8,128)(2,1)S(1)}, u32[]{:S(2)}, u32[]{:S(2)}) %collective-permute-start.9) | collective-permute-done | bytes 77856 | tf_op jit(solution)/shard_map/ppermute | solution.py:241
  111.6 0.1 shard_map.84.refs_0_
  111.7 0.6 copy-done.3
  112.3 0.6 all-to-all-done.1.parts_ref
  113.0 1.9 %shard_map.85 = bf16[4,88,128]{2,1,0:T(8,128)(2,1)} custom-call(s32[12]{0:T(128)} %copy-done.8, bf16[32,88,128]{2,1,0:T(8,128)(2,1)} %all-to-all-done.1.parts_ref, bf16[288,128]{1,0:T(8,128)(2,1)} %copy-done.3), custom_call_target="tpu_custom_call" | custom-call | tf_op jit(solution)/shard_map/pallas_call | solution.py:377
  114.9 15.8 %all_to_all.33.parts_ref = bf16[4,88,128]{2,1,0:T(8,128)(2,1)S(1)} all-to-all(bf16[4,88,128]{2,1,0:T(8,128)(2,1)} %shard_map.85), channel_id=1, replica_groups=mesh['y'=8,'x'=4,'zh'=4,'zl'=2,'c'=2] {'zh'}, dimensions={0} | all-to-all | bytes 180224 | tf_op jit(solution)/shard_map/all_to_all | solution.py:48
  130.7 0.6 shard_map.86
  131.3 0.9 copy-done.1
  132.2 7.7 %all-to-all-start.3 = ((bf16[32,88,128]{2,1,0:T(8,128)(2,1)}), bf16[32,88,128]{2,1,0:T(8,128)(2,1)S(1)}, u32[]{:S(2)}, u32[]{:S(2)}) async-start(bf16[32,88,128]{2,1,0:T(8,128)(2,1)} %copy-done.1), calls=%async_computation.3 | async-start | bytes 1441792 | tf_op jit(solution)/shard_map/all_to_all | solution.py:48
  139.9 1.9 %collective-permute-start.13 = (bf16[288,128]{1,0:T(8,128)(2,1)S(1)}, bf16[288,128]{1,0:T(8,128)(2,1)S(1)}, u32[]{:S(2)}, u32[]{:S(2)}) collective-permute-start(bf16[288,128]{1,0:T(8,128)(2,1)S(1)} %copy-done.4), channel_id=1, source_target_pairs={{0,3},{1,2},{2,1},{3,0},{4,7},{5,6},{6,5},{7,4},{8,11},{9,10},{10,... | collective-permute-start | bytes 221192 | tf_op jit(solution)/shard_map/ppermute | solution.py:395
  141.9 4.3 %collective-permute-start.12 = (bf16[288,128]{1,0:T(8,128)(2,1)S(1)}, bf16[288,128]{1,0:T(8,128)(2,1)S(1)}, u32[]{:S(2)}, u32[]{:S(2)}) collective-permute-start(bf16[288,128]{1,0:T(8,128)(2,1)S(1)} %copy-done.4), channel_id=1, source_target_pairs={{0,2},{1,3},{2,0},{3,1},{4,6},{5,7},{6,4},{7,5},{8,10},{9,11},{10,... | collective-permute-start | bytes 221192 | tf_op jit(solution)/shard_map/ppermute | solution.py:395
  146.2 2.0 %collective-permute-start.11 = (bf16[288,128]{1,0:T(8,128)(2,1)S(1)}, bf16[288,128]{1,0:T(8,128)(2,1)S(1)}, u32[]{:S(2)}, u32[]{:S(2)}) collective-permute-start(bf16[288,128]{1,0:T(8,128)(2,1)S(1)} %copy-done.4), channel_id=1, source_target_pairs={{0,1},{1,0},{2,3},{3,2},{4,5},{5,4},{6,7},{7,6},{8,9},{9,8},{10,11... | collective-permute-start | bytes 221192 | tf_op jit(solution)/shard_map/ppermute | solution.py:395
  148.2 0.3 collective-permute-done.12.refs_2_
  148.5 0.8 collective-permute-done.11.refs_1_
  149.3 2.2 %shard_map.88 = bf16[128,1152]{1,0:T(8,128)(2,1)} custom-call(s32[12]{0:T(128)S(1)} %copy-done.9, bf16[1152,1152]{1,0:T(8,128)(2,1)S(1)} %copy-done, bf16[288,128]{1,0:T(8,128)(2,1)S(1)} %copy-done.4, bf16[288,128]{1,0:T(8,128)(2,1)S(1)} %collective-permute-done.11.refs_1_, bf16[288,128]{1,0:T(8,128)(2,1)S(1)} %collective-permute-done.12.refs_2_, ...), custom_call_target="tpu_custom_call" | custom-call | flops 339738624 | bytes 2949168 | tf_op jit(solution)/shard_map/pallas_call | solution.py:24
  151.6 6.4 %all-to-all-done.3 = bf16[32,88,128]{2,1,0:T(8,128)(2,1)S(1)} async-done(((bf16[32,88,128]{2,1,0:T(8,128)(2,1)}), bf16[32,88,128]{2,1,0:T(8,128)(2,1)S(1)}, u32[]{:S(2)}, u32[]{:S(2)}) %all-to-all-start.3) | async-done | bytes 720928 | tf_op jit(solution)/shard_map/all_to_all | solution.py:48
  157.9 1.0 shard_map.87
  (23 shorter events, 0.1 us)
Async XLA Ops:
  0.6 43.8 %copy-start.2 = (bf16[128,1152]{1,0:T(8,128)(2,1)S(1)}, bf16[128,1152]{1,0:T(8,128)(2,1)}, u32[]{:S(2)}) copy-start(bf16[128,1152]{1,0:T(8,128)(2,1)} %own_ref.1) | copy-start | bytes 884740
  0.6 0.9 copy-start.7
  1.6 42.8 %copy-start = (bf16[1152,1152]{1,0:T(8,128)(2,1)S(1)}, bf16[1152,1152]{1,0:T(8,128)(2,1)}, u32[]{:S(2)}) copy-start(bf16[1152,1152]{1,0:T(8,128)(2,1)} %weight_ref.1) | copy-start | bytes 7962628
  2.5 26.1 %all-to-all-start = ((bf16[8,32,1152]{2,1,0:T(8,128)(2,1)}), bf16[8,32,1152]{2,1,0:T(8,128)(2,1)S(1)}, u32[]{:S(2)}, u32[]{:S(2)}) async-start(bf16[8,32,1152]{2,1,0:T(8,128)(2,1)} %bitcast.9), calls=%async_computation | async-start | bytes 1179648 | tf_op jit(solution)/shard_map/all_to_all | solution.py:48
  9.8 28.8 %collective-permute-start.1 = (bf16[128,1152]{1,0:T(8,128)(2,1)}, bf16[128,1152]{1,0:T(8,128)(2,1)}, u32[]{:S(2)}, u32[]{:S(2)}) collective-permute-start(bf16[128,1152]{1,0:T(8,128)(2,1)} %own_ref.1), channel_id=1, source_target_pairs={{2,4},{3,6},{0,13},{1,15},{6,8},{7,10},{4,1},{5,3},{10,12},{11,14}... | collective-permute-start | bytes 884744 | tf_op jit(solution)/shard_map/ppermute | solution.py:288
  21.4 17.1 %collective-permute-start.2 = (bf16[64,1152]{1,0:T(8,128)(2,1)}, bf16[64,1152]{1,0:T(8,128)(2,1)}, u32[]{:S(2)}, u32[]{:S(2)}) collective-permute-start(bf16[64,1152]{1,0:T(8,128)(2,1)} %constant_dynamic-slice_fusion), channel_id=1, source_target_pairs={{2,8},{3,9},{0,10},{1,11},{6,12},{7,13},{4,14},{5,15},{10,0},{11,1... | collective-permute-start | bytes 442376 | tf_op jit(solution)/shard_map/ppermute | solution.py:287
  28.7 19.3 %collective-permute-start.5 = (bf16[256,1152]{1,0:T(8,128)(2,1)S(1)}, bf16[256,1152]{1,0:T(8,128)(2,1)}, u32[]{:S(2)}, u32[]{:S(2)}) collective-permute-start(bf16[256,1152]{1,0:T(8,128)(2,1)S(1)} %bitcast.16), channel_id=1, source_target_pairs={{0,16},{16,32},{32,48},{48,0},{1,17},{17,33},{33,49},{49,1},{2,18}... | collective-permute-start | bytes 1769480 | tf_op jit(solution)/shard_map/ppermute | solution.py:241
  32.1 19.5 %collective-permute-start.4 = (bf16[256,1152]{1,0:T(8,128)(2,1)S(1)}, bf16[256,1152]{1,0:T(8,128)(2,1)}, u32[]{:S(2)}, u32[]{:S(2)}) collective-permute-start(bf16[256,1152]{1,0:T(8,128)(2,1)S(1)} %bitcast.17), channel_id=1, source_target_pairs={{0,48},{16,0},{32,16},{48,32},{1,49},{17,1},{33,17},{49,33},{2,50}... | collective-permute-start | bytes 1769480 | tf_op jit(solution)/shard_map/ppermute | solution.py:241
  34.5 27.8 %collective-permute-start = (bf16[256,1152]{1,0:T(8,128)(2,1)S(1)}, bf16[256,1152]{1,0:T(8,128)(2,1)}, u32[]{:S(2)}, u32[]{:S(2)}) collective-permute-start(bf16[256,1152]{1,0:T(8,128)(2,1)S(1)} %bitcast.18), channel_id=1, source_target_pairs={{0,32},{16,48},{32,0},{48,16},{1,33},{17,49},{33,1},{49,17},{2,34}... | collective-permute-start | bytes 1769480 | tf_op jit(solution)/shard_map/ppermute | solution.py:241
  40.4 4.0 %collective-permute-start.3 = (bf16[192,1152]{1,0:T(8,128)(2,1)}, bf16[192,1152]{1,0:T(8,128)(2,1)}, u32[]{:S(2)}, u32[]{:S(2)}) collective-permute-start(bf16[192,1152]{1,0:T(8,128)(2,1)} %shard_map.77.fetched_ref), channel_id=1, source_target_pairs={{0,1},{1,0},{2,3},{3,2},{4,5},{5,4},{6,7},{7,6},{8,9},{9,8},{10,11... | collective-permute-start | bytes 1327112 | tf_op jit(solution)/shard_map/ppermute | solution.py:296
  43.7 25.1 %copy-start.8 = (s32[12]{0:T(128)}, s32[12]{0:T(128)S(1)}, u32[]{:S(2)}) copy-start(s32[12]{0:T(128)S(1)} %stack.48.at_ref) | copy-start | bytes 148
  48.0 3.6 %copy-start.5 = (f32[288,128]{1,0:T(8,128)}, f32[288,128]{1,0:T(8,128)S(1)}, u32[]{:S(2)}) copy-start(f32[288,128]{1,0:T(8,128)S(1)} %get-tuple-element.38.unit_ref) | copy-start | bytes 442372
  64.9 3.9 %collective-permute-start.6 = (bf16[592,512]{1,0:T(8,128)(2,1)S(1)}, bf16[592,512]{1,0:T(8,128)(2,1)S(1)}, u32[]{:S(2)}, u32[]{:S(2)}) collective-permute-start(bf16[592,512]{1,0:T(8,128)(2,1)S(1)} %get-tuple-element.31), channel_id=1, source_target_pairs={{0,1},{1,0},{2,3},{3,2},{4,5},{5,4},{6,7},{7,6},{8,9},{9,8},{10,11... | collective-permute-start | bytes 1818632 | tf_op jit(solution)/shard_map/ppermute | solution.py:352
  69.6 42.1 %copy-start.6 = (f32[288,128]{1,0:T(8,128)S(1)}, f32[288,128]{1,0:T(8,128)}, u32[]{:S(2)}) copy-start(f32[288,128]{1,0:T(8,128)} %copy-done.5) | copy-start | bytes 442372
  69.6 12.0 %collective-permute-start.7 = (bf16[304,512]{1,0:T(8,128)(2,1)S(1)}, bf16[304,512]{1,0:T(8,128)(2,1)S(1)}, u32[]{:S(2)}, u32[]{:S(2)}) collective-permute-start(bf16[304,512]{1,0:T(8,128)(2,1)S(1)} %get-tuple-element.33), channel_id=1, source_target_pairs={{0,2},{2,0},{1,3},{3,1},{4,6},{6,4},{5,7},{7,5},{8,10},{10,8},{9,1... | collective-permute-start | bytes 933896 | tf_op jit(solution)/shard_map/ppermute | solution.py:361
  81.6 49.1 %copy-start.9 = (s32[12]{0:T(128)S(1)}, s32[12]{0:T(128)}, u32[]{:S(2)}) copy-start(s32[12]{0:T(128)} %copy-done.8) | copy-start | bytes 148
  83.1 29.9 %all-to-all-start.1 = ((bf16[32,88,128]{2,1,0:T(8,128)(2,1)}), bf16[32,88,128]{2,1,0:T(8,128)(2,1)}, u32[]{:S(2)}, u32[]{:S(2)}) async-start(bf16[32,88,128]{2,1,0:T(8,128)(2,1)} %bitcast.11), calls=%async_computation.1 | async-start | bytes 1441792 | tf_op jit(solution)/shard_map/all_to_all | solution.py:48
  92.4 14.6 %collective-permute-start.8 = (bf16[304,128]{1,0:T(8,128)(2,1)S(1)}, bf16[304,128]{1,0:T(8,128)(2,1)S(1)}, u32[]{:S(2)}, u32[]{:S(2)}) collective-permute-start(bf16[304,128]{1,0:T(8,128)(2,1)S(1)} %get-tuple-element.40), channel_id=1, source_target_pairs={{0,12},{4,0},{8,4},{12,8},{1,13},{5,1},{9,5},{13,9},{2,14},{6,2},{... | collective-permute-start | bytes 233480 | tf_op jit(solution)/shard_map/ppermute | solution.py:241
  100.2 11.4 %collective-permute-start.9 = (bf16[304,128]{1,0:T(8,128)(2,1)S(1)}, bf16[304,128]{1,0:T(8,128)(2,1)S(1)}, u32[]{:S(2)}, u32[]{:S(2)}) collective-permute-start(bf16[304,128]{1,0:T(8,128)(2,1)S(1)} %get-tuple-element.41), channel_id=1, source_target_pairs={{0,8},{4,12},{8,0},{12,4},{1,9},{5,13},{9,1},{13,5},{2,10},{6,14},... | collective-permute-start | bytes 233480 | tf_op jit(solution)/shard_map/ppermute | solution.py:241
  102.2 9.5 %collective-permute-start.10 = (bf16[304,128]{1,0:T(8,128)(2,1)S(1)}, bf16[304,128]{1,0:T(8,128)(2,1)S(1)}, u32[]{:S(2)}, u32[]{:S(2)}) collective-permute-start(bf16[304,128]{1,0:T(8,128)(2,1)S(1)} %get-tuple-element.42), channel_id=1, source_target_pairs={{0,4},{4,8},{8,12},{12,0},{1,5},{5,9},{9,13},{13,1},{2,6},{6,10},{... | collective-permute-start | bytes 233480 | tf_op jit(solution)/shard_map/ppermute | solution.py:241
  111.7 0.6 copy-start.3
  113.0 26.9 %copy-start.4 = (bf16[288,128]{1,0:T(8,128)(2,1)S(1)}, bf16[288,128]{1,0:T(8,128)(2,1)}, u32[]{:S(2)}) copy-start(bf16[288,128]{1,0:T(8,128)(2,1)} %copy-done.3) | copy-start | bytes 221188
  131.3 0.9 copy-start.1
  132.2 25.7 %all-to-all-start.3 = ((bf16[32,88,128]{2,1,0:T(8,128)(2,1)}), bf16[32,88,128]{2,1,0:T(8,128)(2,1)S(1)}, u32[]{:S(2)}, u32[]{:S(2)}) async-start(bf16[32,88,128]{2,1,0:T(8,128)(2,1)} %copy-done.1), calls=%async_computation.3 | async-start | bytes 1441792 | tf_op jit(solution)/shard_map/all_to_all | solution.py:48
  139.9 8.3 %collective-permute-start.13 = (bf16[288,128]{1,0:T(8,128)(2,1)S(1)}, bf16[288,128]{1,0:T(8,128)(2,1)S(1)}, u32[]{:S(2)}, u32[]{:S(2)}) collective-permute-start(bf16[288,128]{1,0:T(8,128)(2,1)S(1)} %copy-done.4), channel_id=1, source_target_pairs={{0,3},{1,2},{2,1},{3,0},{4,7},{5,6},{6,5},{7,4},{8,11},{9,10},{10,... | collective-permute-start | bytes 221192 | tf_op jit(solution)/shard_map/ppermute | solution.py:395
  141.9 6.6 %collective-permute-start.12 = (bf16[288,128]{1,0:T(8,128)(2,1)S(1)}, bf16[288,128]{1,0:T(8,128)(2,1)S(1)}, u32[]{:S(2)}, u32[]{:S(2)}) collective-permute-start(bf16[288,128]{1,0:T(8,128)(2,1)S(1)} %copy-done.4), channel_id=1, source_target_pairs={{0,2},{1,3},{2,0},{3,1},{4,6},{5,7},{6,4},{7,5},{8,10},{9,11},{10,... | collective-permute-start | bytes 221192 | tf_op jit(solution)/shard_map/ppermute | solution.py:395
  146.2 3.2 %collective-permute-start.11 = (bf16[288,128]{1,0:T(8,128)(2,1)S(1)}, bf16[288,128]{1,0:T(8,128)(2,1)S(1)}, u32[]{:S(2)}, u32[]{:S(2)}) collective-permute-start(bf16[288,128]{1,0:T(8,128)(2,1)S(1)} %copy-done.4), channel_id=1, source_target_pairs={{0,1},{1,0},{2,3},{3,2},{4,5},{5,4},{6,7},{7,6},{8,9},{9,8},{10,11... | collective-permute-start | bytes 221192 | tf_op jit(solution)/shard_map/ppermute | solution.py:395

commit v14 on v9

--- a/solution.py
+++ b/solution.py
@@ -57,7 +57,12 @@
         out_ref[k * n : (k + 1) * n] = low
 
 
-def image_kernel(at_ref, wt_ref, own_ref, fetched_ref, swapped_ref, *refs):
+def join_kernel(a_ref, b_ref, out_ref):
+    out_ref[: a_ref.shape[0]] = a_ref[...]
+    out_ref[a_ref.shape[0] :] = b_ref[...]
+
+
+def image_kernel(at_ref, weight_ref, own_ref, fetched_ref, swapped_ref, *refs):
     unit_ref, low_ref, inv_ref, own_unit_ref, cols_ref, feats_ref = refs
     rows = own_ref.shape[0]
     part = rows // 2
@@ -67,7 +72,7 @@
         feats_ref[pl.ds(pl.multiple_of((1 + 2 * k) * rows, 16), rows), :] = ref[:rows]
         feats_ref[pl.ds(pl.multiple_of(2 * rows + k * part, 16), part), :] = ref[rows:]
     head = lax.dot_general(
-        wt_ref[...], feats_ref[...], (((1,), (1,)), ((), ())), preferred_element_type=F32
+        weight_ref[...], feats_ref[...], (((0,), (1,)), ((), ())), preferred_element_type=F32
     )
     inv = lax.rsqrt(jnp.sum(head * head, axis=0, keepdims=True) + EPS)
     unit = head * inv
@@ -279,7 +284,9 @@
     line = ("zh", "zl", "c")
     across = lax.ppermute(half_rows, line, cross)
     beside = lax.ppermute(img_feat, line, near)
-    fetched = jnp.concatenate([beside, across], axis=0)
+    fetched = call(
+        join_kernel, shape((beside.shape[0] + across.shape[0], width), BF16), beside, across
+    )
     own = to_all(copies, "y")
     far = shift_by(own, "x", 2)
     left = shift_by(own, "x", 1)
@@ -297,7 +304,7 @@
             shape((images, width), BF16),
         ],
         at,
-        head_weight.T,
+        head_weight,
         img_feat,
         fetched,
         swapped,
@@ -313,7 +320,7 @@
         left,
         low,
         smem=2,
-        flops=8 * width * images * own.shape[0],
+        flops=width,
     )
     keep, send = call(
         second_kernel,
@@ -327,7 +334,7 @@
         acc,
         loss_row,
         smem=2,
-        flops=8 * width * images * own.shape[0],
+        flops=width,
         scratch_shapes=[pltpu.VMEM((width, images), F32)],
     )
     got = lax.ppermute(send, "c", [(0, 1), (1, 0)])

time: 159 us -> 160 us (level)
  local copies, waits for them, and re-layouts: 9.56 us -> 4.11 us
  waiting for transfers between devices: 33.4 us -> 37.2 us
  Pallas kernels: 19.5 us -> 21.3 us
    all_to_all x3, waiting for transfers between devices: 3.37 us -> 9.68 us  [to_all(): return lax.all_to_all(copies, axes, 0, 0, tiled=True)]
    unnamed x16, local copies, waits for them, and re-layouts: 7.61 us -> 2.44 us
    ppermute x1, waiting for transfers between devices: 3.99 us -> 0.01 us  [local(): beside = lax.ppermute(img_feat, line, near)]
    ppermute x6, waiting for transfers between devices: 12.3 us -> 16.2 us  [shift_by(): return lax.ppermute(x, axis, [(k, (k + step) % n) for k in range(n)])]
    ppermute x3, waiting for transfers between devices: 4.11 us -> 1.08 us  [local(): lax.ppermute(back, ('zl', 'c'), [(k, k ^ d) for k in range(nrep)])]
    pallas_call x10 -> x11, Pallas kernels: 17.6 us -> 19.4 us  [call(): pl.pallas_call(body, out_shape=outs, in_specs=specs, out_specs=[VMEM] * l...]
  transfers between devices with their start and end apart: 17 -> 17, of which waited for: 8 -> 9; matrix products, arithmetic and copies ran while one was open for 3% -> 1% of each run, Pallas kernels for 6% -> 7%
where the time goes in v14:
time: 160 us; the launch traced here: 159 us
  starting transfers between devices  77.6 us (48%)
  waiting for transfers between devices  37.2 us (23%)
  Pallas kernels  21.3 us (13%)
  blocking collectives  16.5 us (10%)
  local copies, waits for them, and re-layouts  4.11 us (3%)
  between operations  2.28 us (1%)
    ppermute x6, starting transfers between devices, shift_by(): return lax.ppermute(x, axis, [(k, (k + step) % n) for k in range(n)])  25.3 us
    all_to_all x3, starting transfers between devices, to_all(): return lax.all_to_all(copies, axes, 0, 0, tiled=True)  22.2 us
    pallas_call x11, Pallas kernels, call(): pl.pallas_call(body, out_shape=outs, in_specs=specs, out_specs=[VMEM] * l...  19.4 us
    all_to_all x1, blocking collectives, to_all(): return lax.all_to_all(copies, axes, 0, 0, tiled=True)  16.5 us
    ppermute x6, waiting for transfers between devices, shift_by(): return lax.ppermute(x, axis, [(k, (k + step) % n) for k in range(n)])  16.2 us
    ppermute x1, starting transfers between devices, local(): beside = lax.ppermute(img_feat, line, near)  10.1 us
    all_to_all x3, waiting for transfers between devices, to_all(): return lax.all_to_all(copies, axes, 0, 0, tiled=True)  9.68 us
    ppermute x1, waiting for transfers between devices, local(): got2 = lax.ppermute(send2, 'zl', [(0, 1), (1, 0)])  7.64 us
  transfers between devices with their start and end apart: 17, of which 9 were waited for; matrix products, arithmetic and copies ran while one was open for 1% of the time, Pallas kernels for 7%

profile of v14, /device:TPU:2, one launch (start us, length us, event | category | flops | bytes accessed | tf_op | source)
XLA Modules:
  0.0 159.1 jit_solution(11604932998767105820)
XLA Ops:
  0.6 0.0 copy-start.2
  0.7 0.9 copy-done.7
  1.6 1.0 shard_map.76
  2.5 7.2 %all-to-all-start = ((bf16[8,32,1152]{2,1,0:T(8,128)(2,1)}), bf16[8,32,1152]{2,1,0:T(8,128)(2,1)S(1)}, u32[]{:S(2)}, u32[]{:S(2)}) async-start(bf16[8,32,1152]{2,1,0:T(8,128)(2,1)} %bitcast.9), calls=%async_computation | async-start | bytes 1179648 | tf_op jit(solution)/shard_map/all_to_all | solution.py:48
  9.8 10.1 %collective-permute-start.2 = (bf16[128,1152]{1,0:T(8,128)(2,1)}, bf16[128,1152]{1,0:T(8,128)(2,1)}, u32[]{:S(2)}, u32[]{:S(2)}) collective-permute-start(bf16[128,1152]{1,0:T(8,128)(2,1)} %own_ref.1), channel_id=1, source_target_pairs={{2,4},{3,6},{0,13},{1,15},{6,8},{7,10},{4,1},{5,3},{10,12},{11,14}... | collective-permute-start | bytes 884744 | tf_op jit(solution)/shard_map/ppermute | solution.py:286
  19.9 1.6 constant_dynamic-slice_fusion
  21.4 4.2 %collective-permute-start.3 = (bf16[64,1152]{1,0:T(8,128)(2,1)}, bf16[64,1152]{1,0:T(8,128)(2,1)}, u32[]{:S(2)}, u32[]{:S(2)}) collective-permute-start(bf16[64,1152]{1,0:T(8,128)(2,1)} %constant_dynamic-slice_fusion), channel_id=1, source_target_pairs={{2,8},{3,9},{0,10},{1,11},{6,12},{7,13},{4,14},{5,15},{10,0},{11,1... | collective-permute-start | bytes 442376 | tf_op jit(solution)/shard_map/ppermute | solution.py:285
  25.7 3.0 %all-to-all-done = bf16[8,32,1152]{2,1,0:T(8,128)(2,1)S(1)} async-done(((bf16[8,32,1152]{2,1,0:T(8,128)(2,1)}), bf16[8,32,1152]{2,1,0:T(8,128)(2,1)S(1)}, u32[]{:S(2)}, u32[]{:S(2)}) %all-to-all-start) | async-done | bytes 589856 | tf_op jit(solution)/shard_map/all_to_all | solution.py:48
  28.7 3.4 %collective-permute-start.5 = (bf16[256,1152]{1,0:T(8,128)(2,1)S(1)}, bf16[256,1152]{1,0:T(8,128)(2,1)}, u32[]{:S(2)}, u32[]{:S(2)}) collective-permute-start(bf16[256,1152]{1,0:T(8,128)(2,1)S(1)} %bitcast.16), channel_id=1, source_target_pairs={{0,16},{16,32},{32,48},{48,0},{1,17},{17,33},{33,49},{49,1},{2,18}... | collective-permute-start | bytes 1769480 | tf_op jit(solution)/shard_map/ppermute | solution.py:239
  32.1 3.0 %collective-permute-start.1 = (bf16[256,1152]{1,0:T(8,128)(2,1)S(1)}, bf16[256,1152]{1,0:T(8,128)(2,1)}, u32[]{:S(2)}, u32[]{:S(2)}) collective-permute-start(bf16[256,1152]{1,0:T(8,128)(2,1)S(1)} %bitcast.17), channel_id=1, source_target_pairs={{0,32},{16,48},{32,0},{48,16},{1,33},{17,49},{33,1},{49,17},{2,34}... | collective-permute-start | bytes 1769480 | tf_op jit(solution)/shard_map/ppermute | solution.py:239
  35.1 4.1 %collective-permute-start = (bf16[256,1152]{1,0:T(8,128)(2,1)S(1)}, bf16[256,1152]{1,0:T(8,128)(2,1)}, u32[]{:S(2)}, u32[]{:S(2)}) collective-permute-start(bf16[256,1152]{1,0:T(8,128)(2,1)S(1)} %bitcast.18), channel_id=1, source_target_pairs={{0,48},{16,0},{32,16},{48,32},{1,49},{17,1},{33,17},{49,33},{2,50}... | collective-permute-start | bytes 1769480 | tf_op jit(solution)/shard_map/ppermute | solution.py:239
  39.2 1.8 %shard_map.77.fetched_ref = bf16[192,1152]{1,0:T(8,128)(2,1)} custom-call(bf16[128,1152]{1,0:T(8,128)(2,1)} %collective-permute-done.2.a_ref, bf16[64,1152]{1,0:T(8,128)(2,1)} %collective-permute-done.3.b_ref), custom_call_target="tpu_custom_call" | custom-call | bytes 442368 | tf_op jit(solution)/shard_map/pallas_call | solution.py:24
  41.0 1.9 %collective-permute-start.4 = (bf16[192,1152]{1,0:T(8,128)(2,1)}, bf16[192,1152]{1,0:T(8,128)(2,1)}, u32[]{:S(2)}, u32[]{:S(2)}) collective-permute-start(bf16[192,1152]{1,0:T(8,128)(2,1)} %shard_map.77.fetched_ref), channel_id=1, source_target_pairs={{0,1},{1,0},{2,3},{3,2},{4,5},{5,4},{6,7},{7,6},{8,9},{9,8},{10,11... | collective-permute-start | bytes 1327112 | tf_op jit(solution)/shard_map/ppermute | solution.py:294
  44.2 0.1 stack.48.at_ref
  44.3 0.1 pad_maximum_fusion.par_ref
  44.4 0.6 collective-permute-done.4.swapped_ref
  45.0 3.5 %shard_map.78 = (f32[1152,512]{1,0:T(8,128)S(1)}, bf16[1152,512]{1,0:T(8,128)(2,1)S(1)}, f32[1,512]{1,0:T(1,128)S(1)}, f32[288,128]{1,0:T(8,128)S(1)}, f32[288,5...) custom-call(s32[12]{0:T(128)S(1)} %stack.48.at_ref, bf16[1152,1152]{1,0:T(8,128)(2,1)S(1)} %copy-done, ...), custom_call_target="tpu_custom_call" | custom-call | flops 2304 | bytes 3833904 | tf_op jit(solution)/shard_map/pallas_call | solution.py:24
  48.5 0.0 copy-start.5
  48.6 3.6 %shard_map.79 = (f32[1152,512]{1,0:T(8,128)S(1)}, f32[1,512]{1,0:T(1,128)S(1)}) custom-call(s32[12]{0:T(128)S(1)} %stack.48.at_ref, f32[2]{0:T(128)S(1)} %pad_maximum_fusion.par_ref, bf16[256,1152]{1,0:T(8,128)(2,1)S(1)} %bitcast.19, bf16[256,1152]{1,0:T(8,128)(2,1)} %collective-permute-done.5.left_ref, bf16[1152,512]{1,0:T(8,128)(2,1)S(1)} %get-tuple-element.22.low_ref), custom_call_target="tpu_custom_call" | custom-call | flops 1152 | bytes 2359352 | tf_op jit(solution)/shard_map/pallas_call | solution.py:24
  52.2 11.0 %collective-permute-done.right_ref = bf16[256,1152]{1,0:T(8,128)(2,1)} collective-permute-done((bf16[256,1152]{1,0:T(8,128)(2,1)S(1)}, bf16[256,1152]{1,0:T(8,128)(2,1)}, u32[]{:S(2)}, u32[]{:S(2)}) %collective-permute-start) | collective-permute-done | bytes 589856 | tf_op jit(solution)/shard_map/ppermute | solution.py:239
  63.2 3.5 %shard_map.80 = (f32[592,512]{1,0:T(8,128)S(1)}, bf16[592,512]{1,0:T(8,128)(2,1)S(1)}) custom-call(s32[12]{0:T(128)S(1)} %stack.48.at_ref, f32[2]{0:T(128)S(1)} %pad_maximum_fusion.par_ref, bf16[256,1152]{1,0:T(8,128)(2,1)} %collective-permute-done.right_ref, bf16[256,1152]{1,0:T(8,128)(2,1)} %collective-permute-done.1.far_ref, ...), custom_call_target="tpu_custom_call" | custom-call | flops 1152 | bytes 7079992 | tf_op jit(solution)/shard_map/pallas_call | solution.py:24
  66.7 1.9 %collective-permute-start.6 = (bf16[592,512]{1,0:T(8,128)(2,1)S(1)}, bf16[592,512]{1,0:T(8,128)(2,1)S(1)}, u32[]{:S(2)}, u32[]{:S(2)}) collective-permute-start(bf16[592,512]{1,0:T(8,128)(2,1)S(1)} %get-tuple-element.27), channel_id=1, source_target_pairs={{0,1},{1,0},{2,3},{3,2},{4,5},{5,4},{6,7},{7,6},{8,9},{9,8},{10,11... | collective-permute-start | bytes 1818632 | tf_op jit(solution)/shard_map/ppermute | solution.py:340
  68.6 2.0 %collective-permute-done.6.got_ref = bf16[592,512]{1,0:T(8,128)(2,1)S(1)} collective-permute-done((bf16[592,512]{1,0:T(8,128)(2,1)S(1)}, bf16[592,512]{1,0:T(8,128)(2,1)S(1)}, u32[]{:S(2)}, u32[]{:S(2)}) %collective-permute-start.6) | collective-permute-done | bytes 606240 | tf_op jit(solution)/shard_map/ppermute | solution.py:340
  70.6 0.7 shard_map.81
  71.4 4.4 %collective-permute-start.7 = (bf16[304,512]{1,0:T(8,128)(2,1)S(1)}, bf16[304,512]{1,0:T(8,128)(2,1)S(1)}, u32[]{:S(2)}, u32[]{:S(2)}) collective-permute-start(bf16[304,512]{1,0:T(8,128)(2,1)S(1)} %get-tuple-element.29), channel_id=1, source_target_pairs={{0,2},{2,0},{1,3},{3,1},{4,6},{6,4},{5,7},{7,5},{8,10},{10,8},{9,1... | collective-permute-start | bytes 933896 | tf_op jit(solution)/shard_map/ppermute | solution.py:349
  75.8 7.6 %collective-permute-done.7.got_ref = bf16[304,512]{1,0:T(8,128)(2,1)S(1)} collective-permute-done((bf16[304,512]{1,0:T(8,128)(2,1)S(1)}, bf16[304,512]{1,0:T(8,128)(2,1)S(1)}, u32[]{:S(2)}, u32[]{:S(2)}) %collective-permute-start.7) | collective-permute-done | bytes 311328 | tf_op jit(solution)/shard_map/ppermute | solution.py:349
  83.4 1.5 shard_map.82
  84.9 6.6 %all-to-all-start.1 = ((bf16[32,88,128]{2,1,0:T(8,128)(2,1)}), bf16[32,88,128]{2,1,0:T(8,128)(2,1)}, u32[]{:S(2)}, u32[]{:S(2)}) async-start(bf16[32,88,128]{2,1,0:T(8,128)(2,1)} %bitcast.11), calls=%async_computation.1 | async-start | bytes 1441792 | tf_op jit(solution)/shard_map/all_to_all | solution.py:48
  91.5 8.1 %collective-permute-start.8 = (bf16[304,128]{1,0:T(8,128)(2,1)S(1)}, bf16[304,128]{1,0:T(8,128)(2,1)S(1)}, u32[]{:S(2)}, u32[]{:S(2)}) collective-permute-start(bf16[304,128]{1,0:T(8,128)(2,1)S(1)} %get-tuple-element.36), channel_id=1, source_target_pairs={{0,12},{4,0},{8,4},{12,8},{1,13},{5,1},{9,5},{13,9},{2,14},{6,2},{... | collective-permute-start | bytes 233480 | tf_op jit(solution)/shard_map/ppermute | solution.py:239
  99.6 1.9 %collective-permute-start.9 = (bf16[304,128]{1,0:T(8,128)(2,1)S(1)}, bf16[304,128]{1,0:T(8,128)(2,1)S(1)}, u32[]{:S(2)}, u32[]{:S(2)}) collective-permute-start(bf16[304,128]{1,0:T(8,128)(2,1)S(1)} %get-tuple-element.37), channel_id=1, source_target_pairs={{0,8},{4,12},{8,0},{12,4},{1,9},{5,13},{9,1},{13,5},{2,10},{6,14},... | collective-permute-start | bytes 233480 | tf_op jit(solution)/shard_map/ppermute | solution.py:239
  101.6 4.8 %collective-permute-start.10 = (bf16[304,128]{1,0:T(8,128)(2,1)S(1)}, bf16[304,128]{1,0:T(8,128)(2,1)S(1)}, u32[]{:S(2)}, u32[]{:S(2)}) collective-permute-start(bf16[304,128]{1,0:T(8,128)(2,1)S(1)} %get-tuple-element.38), channel_id=1, source_target_pairs={{0,4},{4,8},{8,12},{12,0},{1,5},{5,9},{9,13},{13,1},{2,6},{6,10},{... | collective-permute-start | bytes 233480 | tf_op jit(solution)/shard_map/ppermute | solution.py:239
  106.4 5.2 %collective-permute-done.9.refs_2_ = bf16[304,128]{1,0:T(8,128)(2,1)S(1)} collective-permute-done((bf16[304,128]{1,0:T(8,128)(2,1)S(1)}, bf16[304,128]{1,0:T(8,128)(2,1)S(1)}, u32[]{:S(2)}, u32[]{:S(2)}) %collective-permute-start.9) | collective-permute-done | bytes 77856 | tf_op jit(solution)/shard_map/ppermute | solution.py:239
  111.6 0.1 shard_map.83.after_ref.refs_0_
  111.7 0.0 copy-start.3
  111.7 0.6 copy-done.3
  112.3 1.9 %shard_map.84 = f32[4,88,128]{2,1,0:T(8,128)} custom-call(bf16[32,88,128]{2,1,0:T(8,128)(2,1)} %all-to-all-done.1.parts_ref, bf16[288,128]{1,0:T(8,128)(2,1)} %copy-done.3), custom_call_target="tpu_custom_call" | custom-call | tf_op jit(solution)/shard_map/pallas_call | solution.py:365
  114.2 16.5 %all_to_all.33.parts_ref = f32[4,88,128]{2,1,0:T(8,128)S(1)} all-to-all(f32[4,88,128]{2,1,0:T(8,128)} %shard_map.84), channel_id=1, replica_groups=mesh['y'=8,'x'=4,'zh'=4,'zl'=2,'c'=2] {'zh'}, dimensions={0} | all-to-all | bytes 360448 | tf_op jit(solution)/shard_map/all_to_all | solution.py:48
  130.7 0.6 shard_map.85
  131.3 0.9 copy-done.1
  132.2 8.3 %all-to-all-start.3 = ((bf16[32,88,128]{2,1,0:T(8,128)(2,1)}), bf16[32,88,128]{2,1,0:T(8,128)(2,1)S(1)}, u32[]{:S(2)}, u32[]{:S(2)}) async-start(bf16[32,88,128]{2,1,0:T(8,128)(2,1)} %copy-done.1), calls=%async_computation.3 | async-start | bytes 1441792 | tf_op jit(solution)/shard_map/all_to_all | solution.py:48
  140.5 1.9 %collective-permute-start.13 = (bf16[288,128]{1,0:T(8,128)(2,1)S(1)}, bf16[288,128]{1,0:T(8,128)(2,1)S(1)}, u32[]{:S(2)}, u32[]{:S(2)}) collective-permute-start(bf16[288,128]{1,0:T(8,128)(2,1)S(1)} %copy-done.4), channel_id=1, source_target_pairs={{0,3},{1,2},{2,1},{3,0},{4,7},{5,6},{6,5},{7,4},{8,11},{9,10},{10,... | collective-permute-start | bytes 221192 | tf_op jit(solution)/shard_map/ppermute | solution.py:383
  142.4 3.6 %collective-permute-start.12 = (bf16[288,128]{1,0:T(8,128)(2,1)S(1)}, bf16[288,128]{1,0:T(8,128)(2,1)S(1)}, u32[]{:S(2)}, u32[]{:S(2)}) collective-permute-start(bf16[288,128]{1,0:T(8,128)(2,1)S(1)} %copy-done.4), channel_id=1, source_target_pairs={{0,2},{1,3},{2,0},{3,1},{4,6},{5,7},{6,4},{7,5},{8,10},{9,11},{10,... | collective-permute-start | bytes 221192 | tf_op jit(solution)/shard_map/ppermute | solution.py:383
  146.1 2.1 %collective-permute-start.11 = (bf16[288,128]{1,0:T(8,128)(2,1)S(1)}, bf16[288,128]{1,0:T(8,128)(2,1)S(1)}, u32[]{:S(2)}, u32[]{:S(2)}) collective-permute-start(bf16[288,128]{1,0:T(8,128)(2,1)S(1)} %copy-done.4), channel_id=1, source_target_pairs={{0,1},{1,0},{2,3},{3,2},{4,5},{5,4},{6,7},{7,6},{8,9},{9,8},{10,11... | collective-permute-start | bytes 221192 | tf_op jit(solution)/shard_map/ppermute | solution.py:383
  148.1 0.5 collective-permute-done.12.refs_2_
  148.7 0.5 collective-permute-done.11.refs_1_
  149.2 2.2 %shard_map.87 = bf16[128,1152]{1,0:T(8,128)(2,1)} custom-call(s32[12]{0:T(128)S(1)} %stack.48.at_ref, bf16[1152,1152]{1,0:T(8,128)(2,1)S(1)} %copy-done, bf16[288,128]{1,0:T(8,128)(2,1)S(1)} %copy-done.4, bf16[288,128]{1,0:T(8,128)(2,1)S(1)} %collective-permute-done.11.refs_1_, bf16[288,128]{1,0:T(8,128)(2,1)S(1)} %collective-permute-done.12.refs_2_, ...), custom_call_target="tpu_custom_call" | custom-call | flops 339738624 | bytes 2949168 | tf_op jit(solution)/shard_map/pallas_call | solution.py:24
  151.4 6.7 %all-to-all-done.3 = bf16[32,88,128]{2,1,0:T(8,128)(2,1)S(1)} async-done(((bf16[32,88,128]{2,1,0:T(8,128)(2,1)}), bf16[32,88,128]{2,1,0:T(8,128)(2,1)S(1)}, u32[]{:S(2)}, u32[]{:S(2)}) %all-to-all-start.3) | async-done | bytes 720928 | tf_op jit(solution)/shard_map/all_to_all | solution.py:48
  158.1 1.0 shard_map.86
  (18 shorter events, 0.0 us)
Async XLA Ops:
  0.6 44.4 %copy-start.2 = (bf16[128,1152]{1,0:T(8,128)(2,1)S(1)}, bf16[128,1152]{1,0:T(8,128)(2,1)}, u32[]{:S(2)}) copy-start(bf16[128,1152]{1,0:T(8,128)(2,1)} %own_ref.1) | copy-start | bytes 884740
  0.6 0.9 copy-start.7
  1.6 43.4 %copy-start = (bf16[1152,1152]{1,0:T(8,128)(2,1)S(1)}, bf16[1152,1152]{1,0:T(8,128)(2,1)}, u32[]{:S(2)}) copy-start(bf16[1152,1152]{1,0:T(8,128)(2,1)} %weight_ref.3) | copy-start | bytes 7962628
  2.5 26.1 %all-to-all-start = ((bf16[8,32,1152]{2,1,0:T(8,128)(2,1)}), bf16[8,32,1152]{2,1,0:T(8,128)(2,1)S(1)}, u32[]{:S(2)}, u32[]{:S(2)}) async-start(bf16[8,32,1152]{2,1,0:T(8,128)(2,1)} %bitcast.9), calls=%async_computation | async-start | bytes 1179648 | tf_op jit(solution)/shard_map/all_to_all | solution.py:48
  9.8 29.4 %collective-permute-start.2 = (bf16[128,1152]{1,0:T(8,128)(2,1)}, bf16[128,1152]{1,0:T(8,128)(2,1)}, u32[]{:S(2)}, u32[]{:S(2)}) collective-permute-start(bf16[128,1152]{1,0:T(8,128)(2,1)} %own_ref.1), channel_id=1, source_target_pairs={{2,4},{3,6},{0,13},{1,15},{6,8},{7,10},{4,1},{5,3},{10,12},{11,14}... | collective-permute-start | bytes 884744 | tf_op jit(solution)/shard_map/ppermute | solution.py:286
  21.4 17.7 %collective-permute-start.3 = (bf16[64,1152]{1,0:T(8,128)(2,1)}, bf16[64,1152]{1,0:T(8,128)(2,1)}, u32[]{:S(2)}, u32[]{:S(2)}) collective-permute-start(bf16[64,1152]{1,0:T(8,128)(2,1)} %constant_dynamic-slice_fusion), channel_id=1, source_target_pairs={{2,8},{3,9},{0,10},{1,11},{6,12},{7,13},{4,14},{5,15},{10,0},{11,1... | collective-permute-start | bytes 442376 | tf_op jit(solution)/shard_map/ppermute | solution.py:285
  28.7 19.9 %collective-permute-start.5 = (bf16[256,1152]{1,0:T(8,128)(2,1)S(1)}, bf16[256,1152]{1,0:T(8,128)(2,1)}, u32[]{:S(2)}, u32[]{:S(2)}) collective-permute-start(bf16[256,1152]{1,0:T(8,128)(2,1)S(1)} %bitcast.16), channel_id=1, source_target_pairs={{0,16},{16,32},{32,48},{48,0},{1,17},{17,33},{33,49},{49,1},{2,18}... | collective-permute-start | bytes 1769480 | tf_op jit(solution)/shard_map/ppermute | solution.py:239
  32.1 20.1 %collective-permute-start.1 = (bf16[256,1152]{1,0:T(8,128)(2,1)S(1)}, bf16[256,1152]{1,0:T(8,128)(2,1)}, u32[]{:S(2)}, u32[]{:S(2)}) collective-permute-start(bf16[256,1152]{1,0:T(8,128)(2,1)S(1)} %bitcast.17), channel_id=1, source_target_pairs={{0,32},{16,48},{32,0},{48,16},{1,33},{17,49},{33,1},{49,17},{2,34}... | collective-permute-start | bytes 1769480 | tf_op jit(solution)/shard_map/ppermute | solution.py:239
  35.1 28.1 %collective-permute-start = (bf16[256,1152]{1,0:T(8,128)(2,1)S(1)}, bf16[256,1152]{1,0:T(8,128)(2,1)}, u32[]{:S(2)}, u32[]{:S(2)}) collective-permute-start(bf16[256,1152]{1,0:T(8,128)(2,1)S(1)} %bitcast.18), channel_id=1, source_target_pairs={{0,48},{16,0},{32,16},{48,32},{1,49},{17,1},{33,17},{49,33},{2,50}... | collective-permute-start | bytes 1769480 | tf_op jit(solution)/shard_map/ppermute | solution.py:239
  41.0 4.0 %collective-permute-start.4 = (bf16[192,1152]{1,0:T(8,128)(2,1)}, bf16[192,1152]{1,0:T(8,128)(2,1)}, u32[]{:S(2)}, u32[]{:S(2)}) collective-permute-start(bf16[192,1152]{1,0:T(8,128)(2,1)} %shard_map.77.fetched_ref), channel_id=1, source_target_pairs={{0,1},{1,0},{2,3},{3,2},{4,5},{5,4},{6,7},{7,6},{8,9},{9,8},{10,11... | collective-permute-start | bytes 1327112 | tf_op jit(solution)/shard_map/ppermute | solution.py:294
  48.5 18.2 %copy-start.5 = (f32[288,128]{1,0:T(8,128)}, f32[288,128]{1,0:T(8,128)S(1)}, u32[]{:S(2)}) copy-start(f32[288,128]{1,0:T(8,128)S(1)} %get-tuple-element.34.unit_ref) | copy-start | bytes 442372
  66.7 3.9 %collective-permute-start.6 = (bf16[592,512]{1,0:T(8,128)(2,1)S(1)}, bf16[592,512]{1,0:T(8,128)(2,1)S(1)}, u32[]{:S(2)}, u32[]{:S(2)}) collective-permute-start(bf16[592,512]{1,0:T(8,128)(2,1)S(1)} %get-tuple-element.27), channel_id=1, source_target_pairs={{0,1},{1,0},{2,3},{3,2},{4,5},{5,4},{6,7},{7,6},{8,9},{9,8},{10,11... | collective-permute-start | bytes 1818632 | tf_op jit(solution)/shard_map/ppermute | solution.py:340
  71.4 40.2 %copy-start.6 = (f32[288,128]{1,0:T(8,128)S(1)}, f32[288,128]{1,0:T(8,128)}, u32[]{:S(2)}) copy-start(f32[288,128]{1,0:T(8,128)} %copy-done.5) | copy-start | bytes 442372
  71.4 12.1 %collective-permute-start.7 = (bf16[304,512]{1,0:T(8,128)(2,1)S(1)}, bf16[304,512]{1,0:T(8,128)(2,1)S(1)}, u32[]{:S(2)}, u32[]{:S(2)}) collective-permute-start(bf16[304,512]{1,0:T(8,128)(2,1)S(1)} %get-tuple-element.29), channel_id=1, source_target_pairs={{0,2},{2,0},{1,3},{3,1},{4,6},{6,4},{5,7},{7,5},{8,10},{10,8},{9,1... | collective-permute-start | bytes 933896 | tf_op jit(solution)/shard_map/ppermute | solution.py:349
  84.9 27.4 %all-to-all-start.1 = ((bf16[32,88,128]{2,1,0:T(8,128)(2,1)}), bf16[32,88,128]{2,1,0:T(8,128)(2,1)}, u32[]{:S(2)}, u32[]{:S(2)}) async-start(bf16[32,88,128]{2,1,0:T(8,128)(2,1)} %bitcast.11), calls=%async_computation.1 | async-start | bytes 1441792 | tf_op jit(solution)/shard_map/all_to_all | solution.py:48
  91.5 14.8 %collective-permute-start.8 = (bf16[304,128]{1,0:T(8,128)(2,1)S(1)}, bf16[304,128]{1,0:T(8,128)(2,1)S(1)}, u32[]{:S(2)}, u32[]{:S(2)}) collective-permute-start(bf16[304,128]{1,0:T(8,128)(2,1)S(1)} %get-tuple-element.36), channel_id=1, source_target_pairs={{0,12},{4,0},{8,4},{12,8},{1,13},{5,1},{9,5},{13,9},{2,14},{6,2},{... | collective-permute-start | bytes 233480 | tf_op jit(solution)/shard_map/ppermute | solution.py:239
  99.6 11.9 %collective-permute-start.9 = (bf16[304,128]{1,0:T(8,128)(2,1)S(1)}, bf16[304,128]{1,0:T(8,128)(2,1)S(1)}, u32[]{:S(2)}, u32[]{:S(2)}) collective-permute-start(bf16[304,128]{1,0:T(8,128)(2,1)S(1)} %get-tuple-element.37), channel_id=1, source_target_pairs={{0,8},{4,12},{8,0},{12,4},{1,9},{5,13},{9,1},{13,5},{2,10},{6,14},... | collective-permute-start | bytes 233480 | tf_op jit(solution)/shard_map/ppermute | solution.py:239
  101.6 10.0 %collective-permute-start.10 = (bf16[304,128]{1,0:T(8,128)(2,1)S(1)}, bf16[304,128]{1,0:T(8,128)(2,1)S(1)}, u32[]{:S(2)}, u32[]{:S(2)}) collective-permute-start(bf16[304,128]{1,0:T(8,128)(2,1)S(1)} %get-tuple-element.38), channel_id=1, source_target_pairs={{0,4},{4,8},{8,12},{12,0},{1,5},{5,9},{9,13},{13,1},{2,6},{6,10},{... | collective-permute-start | bytes 233480 | tf_op jit(solution)/shard_map/ppermute | solution.py:239
  111.7 0.6 copy-start.3
  112.3 28.2 %copy-start.4 = (bf16[288,128]{1,0:T(8,128)(2,1)S(1)}, bf16[288,128]{1,0:T(8,128)(2,1)}, u32[]{:S(2)}) copy-start(bf16[288,128]{1,0:T(8,128)(2,1)} %copy-done.3) | copy-start | bytes 221188
  131.3 0.9 copy-start.1
  132.2 25.9 %all-to-all-start.3 = ((bf16[32,88,128]{2,1,0:T(8,128)(2,1)}), bf16[32,88,128]{2,1,0:T(8,128)(2,1)S(1)}, u32[]{:S(2)}, u32[]{:S(2)}) async-start(bf16[32,88,128]{2,1,0:T(8,128)(2,1)} %copy-done.1), calls=%async_computation.3 | async-start | bytes 1441792 | tf_op jit(solution)/shard_map/all_to_all | solution.py:48
  140.5 7.6 %collective-permute-start.13 = (bf16[288,128]{1,0:T(8,128)(2,1)S(1)}, bf16[288,128]{1,0:T(8,128)(2,1)S(1)}, u32[]{:S(2)}, u32[]{:S(2)}) collective-permute-start(bf16[288,128]{1,0:T(8,128)(2,1)S(1)} %copy-done.4), channel_id=1, source_target_pairs={{0,3},{1,2},{2,1},{3,0},{4,7},{5,6},{6,5},{7,4},{8,11},{9,10},{10,... | collective-permute-start | bytes 221192 | tf_op jit(solution)/shard_map/ppermute | solution.py:383
  142.4 6.2 %collective-permute-start.12 = (bf16[288,128]{1,0:T(8,128)(2,1)S(1)}, bf16[288,128]{1,0:T(8,128)(2,1)S(1)}, u32[]{:S(2)}, u32[]{:S(2)}) collective-permute-start(bf16[288,128]{1,0:T(8,128)(2,1)S(1)} %copy-done.4), channel_id=1, source_target_pairs={{0,2},{1,3},{2,0},{3,1},{4,6},{5,7},{6,4},{7,5},{8,10},{9,11},{10,... | collective-permute-start | bytes 221192 | tf_op jit(solution)/shard_map/ppermute | solution.py:383
  146.1 3.2 %collective-permute-start.11 = (bf16[288,128]{1,0:T(8,128)(2,1)S(1)}, bf16[288,128]{1,0:T(8,128)(2,1)S(1)}, u32[]{:S(2)}, u32[]{:S(2)}) collective-permute-start(bf16[288,128]{1,0:T(8,128)(2,1)S(1)} %copy-done.4), channel_id=1, source_target_pairs={{0,1},{1,0},{2,3},{3,2},{4,5},{5,4},{6,7},{7,6},{8,9},{9,8},{10,11... | collective-permute-start | bytes 221192 | tf_op jit(solution)/shard_map/ppermute | solution.py:383

commit v15 on v12

--- a/solution.py
+++ b/solution.py
@@ -67,7 +67,7 @@
         feats_ref[pl.ds(pl.multiple_of((1 + 2 * k) * rows, 16), rows), :] = ref[:rows]
         feats_ref[pl.ds(pl.multiple_of(2 * rows + k * part, 16), part), :] = ref[rows:]
     head = lax.dot_general(
-        wt_ref[...], feats_ref[...], (((0,), (1,)), ((), ())), preferred_element_type=F32
+        wt_ref[...], feats_ref[...], (((1,), (1,)), ((), ())), preferred_element_type=F32
     )
     inv = lax.rsqrt(jnp.sum(head * head, axis=0, keepdims=True) + EPS)
     unit = head * inv
@@ -294,7 +294,7 @@
             shape((images, width), BF16),
         ],
         at,
-        head_weight,
+        head_weight.T,
         img_feat,
         fetched,
         swapped,

time: 160 us -> 158 us (0.988)
  the two profiles are of different devices: /device:TPU:2 before, /device:TPU:64 now
where the time goes in v15:
time: 158 us; the launch traced here: 157 us
  starting transfers between devices  73.5 us (47%)
  waiting for transfers between devices  36.3 us (23%)
  Pallas kernels  19.5 us (12%)
  blocking collectives  15.4 us (10%)
  local copies, waits for them, and re-layouts  9.56 us (6%)
  between operations  2.28 us (1%)
    ppermute x6, starting transfers between devices, shift_by(): return lax.ppermute(x, axis, [(k, (k + step) % n) for k in range(n)])  26.5 us
    all_to_all x3, starting transfers between devices, to_all(): return lax.all_to_all(copies, axes, 0, 0, tiled=True)  22.7 us
    pallas_call x10, Pallas kernels, call(): pl.pallas_call(body, out_shape=outs, in_specs=specs, out_specs=[VMEM] * l...  17.6 us
    all_to_all x1, blocking collectives, to_all(): return lax.all_to_all(copies, axes, 0, 0, tiled=True)  15.4 us
    ppermute x6, waiting for transfers between devices, shift_by(): return lax.ppermute(x, axis, [(k, (k + step) % n) for k in range(n)])  9.37 us
    ppermute x1, waiting for transfers between devices, local(): got2 = lax.ppermute(send2, 'zl', [(0, 1), (1, 0)])  9.37 us
    all_to_all x3, waiting for transfers between devices, to_all(): return lax.all_to_all(copies, axes, 0, 0, tiled=True)  8.66 us
    unnamed x20, local copies, waits for them, and re-layouts  7.62 us
  transfers between devices with their start and end apart: 17, of which 10 were waited for; matrix products, arithmetic and copies ran while one was open for 3% of the time, Pallas kernels for 6%

profile of v15, /device:TPU:64, one launch (start us, length us, event | category | flops | bytes accessed | tf_op | source)
XLA Modules:
  0.0 156.6 jit_solution(6867610110320612937)
XLA Ops:
  0.7 1.0 copy-done.6
  1.7 1.0 shard_map.76
  2.6 7.1 %all-to-all-start = ((bf16[8,32,1152]{2,1,0:T(8,128)(2,1)}), bf16[8,32,1152]{2,1,0:T(8,128)(2,1)}, u32[]{:S(2)}, u32[]{:S(2)}) async-start(bf16[8,32,1152]{2,1,0:T(8,128)(2,1)} %bitcast.9), calls=%async_computation | async-start | bytes 1179648 | tf_op jit(solution)/shard_map/all_to_all | solution.py:48
  9.7 4.3 %collective-permute-start.2 = (bf16[128,1152]{1,0:T(8,128)(2,1)}, bf16[128,1152]{1,0:T(8,128)(2,1)S(1)}, u32[]{:S(2)}, u32[]{:S(2)}) collective-permute-start(bf16[128,1152]{1,0:T(8,128)(2,1)} %own_ref.1), channel_id=1, source_target_pairs={{2,4},{3,6},{0,13},{1,15},{6,8},{7,10},{4,1},{5,3},{10,12},{11,14}... | collective-permute-start | bytes 884744 | tf_op jit(solution)/shard_map/ppermute | solution.py:278
  14.0 0.9 constant_dynamic-slice_fusion
  14.9 6.7 %collective-permute-start.3 = (bf16[64,1152]{1,0:T(8,128)(2,1)S(1)}, bf16[64,1152]{1,0:T(8,128)(2,1)}, u32[]{:S(2)}, u32[]{:S(2)}) collective-permute-start(bf16[64,1152]{1,0:T(8,128)(2,1)S(1)} %constant_dynamic-slice_fusion), channel_id=1, source_target_pairs={{2,8},{3,9},{0,10},{1,11},{6,12},{7,13},{4,14},{5,15},{10,0},{11,1... | collective-permute-start | bytes 442376 | tf_op jit(solution)/shard_map/ppermute | solution.py:277
  21.7 3.8 %collective-permute-done.2 = bf16[128,1152]{1,0:T(8,128)(2,1)S(1)} collective-permute-done((bf16[128,1152]{1,0:T(8,128)(2,1)}, bf16[128,1152]{1,0:T(8,128)(2,1)S(1)}, u32[]{:S(2)}, u32[]{:S(2)}) %collective-permute-start.2) | collective-permute-done | bytes 294944 | tf_op jit(solution)/shard_map/ppermute | solution.py:278
  25.6 3.2 %all-to-all-done = bf16[8,32,1152]{2,1,0:T(8,128)(2,1)} async-done(((bf16[8,32,1152]{2,1,0:T(8,128)(2,1)}), bf16[8,32,1152]{2,1,0:T(8,128)(2,1)}, u32[]{:S(2)}, u32[]{:S(2)}) %all-to-all-start) | async-done | bytes 589856 | tf_op jit(solution)/shard_map/all_to_all | solution.py:48
  28.7 3.4 %collective-permute-start.5 = (bf16[256,1152]{1,0:T(8,128)(2,1)}, bf16[256,1152]{1,0:T(8,128)(2,1)}, u32[]{:S(2)}, u32[]{:S(2)}) collective-permute-start(bf16[256,1152]{1,0:T(8,128)(2,1)} %bitcast.10.own_ref), channel_id=1, source_target_pairs={{0,16},{16,32},{32,48},{48,0},{1,17},{17,33},{33,49},{49,1},{2,18}... | collective-permute-start | bytes 1769480 | tf_op jit(solution)/shard_map/ppermute | solution.py:231
  32.1 3.7 %collective-permute-start = (bf16[256,1152]{1,0:T(8,128)(2,1)}, bf16[256,1152]{1,0:T(8,128)(2,1)}, u32[]{:S(2)}, u32[]{:S(2)}) collective-permute-start(bf16[256,1152]{1,0:T(8,128)(2,1)} %bitcast.10.own_ref), channel_id=1, source_target_pairs={{0,48},{16,0},{32,16},{48,32},{1,49},{17,1},{33,17},{49,33},{2,50}... | collective-permute-start | bytes 1769480 | tf_op jit(solution)/shard_map/ppermute | solution.py:231
  35.8 3.7 %collective-permute-start.1 = (bf16[256,1152]{1,0:T(8,128)(2,1)}, bf16[256,1152]{1,0:T(8,128)(2,1)}, u32[]{:S(2)}, u32[]{:S(2)}) collective-permute-start(bf16[256,1152]{1,0:T(8,128)(2,1)} %bitcast.10.own_ref), channel_id=1, source_target_pairs={{0,32},{16,48},{32,0},{48,16},{1,33},{17,49},{33,1},{49,17},{2,34}... | collective-permute-start | bytes 1769480 | tf_op jit(solution)/shard_map/ppermute | solution.py:231
  39.5 0.9 constant_dynamic-update-slice_fusion.fetched_ref
  40.5 1.9 %collective-permute-start.4 = (bf16[192,1152]{1,0:T(8,128)(2,1)S(1)}, bf16[192,1152]{1,0:T(8,128)(2,1)}, u32[]{:S(2)}, u32[]{:S(2)}) collective-permute-start(bf16[192,1152]{1,0:T(8,128)(2,1)S(1)} %constant_dynamic-update-slice_fusion.fetched_ref), channel_id=1, source_target_pairs={{0,1},{1,0},{2,3},{3,2},{4,5},{5,4},{6,7},{7,6},{8,9},{9,8},{10,11... | collective-permute-start | bytes 1327112 | tf_op jit(solution)/shard_map/ppermute | solution.py:284
  42.4 3.3 %copy.8 = bf16[1152,1152]{0,1:T(8,128)(2,1)} copy(bf16[1152,1152]{1,0:T(8,128)(2,1)S(1)} %copy-done) | data formatting | bytes 5308416 | tf_op args[1]
  47.1 0.1 stack.48.at_ref
  47.2 0.1 pad_maximum_fusion.par_ref
  47.2 1.7 %copy-done.1 = bf16[1152,1152]{0,1:T(8,128)(2,1)S(1)} copy-done((bf16[1152,1152]{0,1:T(8,128)(2,1)S(1)}, bf16[1152,1152]{0,1:T(8,128)(2,1)}, u32[]{:S(2)}) %copy-start.1) | copy-done | bytes 2654232
  49.0 3.4 %shard_map.77 = (f32[1152,512]{1,0:T(8,128)S(1)}, bf16[1152,512]{1,0:T(8,128)(2,1)S(1)}, f32[1,512]{1,0:T(1,128)S(1)}, f32[288,128]{1,0:T(8,128)S(1)}, f32[288,5...) custom-call(s32[12]{0:T(128)S(1)} %stack.48.at_ref, bf16[1152,1152]{1,0:T(8,128)(2,1)S(1)} %bitcast.16, ...), custom_call_target="tpu_custom_call" | custom-call | flops 2304 | bytes 3833904 | tf_op jit(solution)/shard_map/pallas_call | solution.py:24
  52.4 3.7 %shard_map.78 = (f32[1152,512]{1,0:T(8,128)S(1)}, f32[1,512]{1,0:T(1,128)S(1)}) custom-call(s32[12]{0:T(128)S(1)} %stack.48.at_ref, f32[2]{0:T(128)S(1)} %pad_maximum_fusion.par_ref, bf16[256,1152]{1,0:T(8,128)(2,1)} %bitcast.10.own_ref, bf16[256,1152]{1,0:T(8,128)(2,1)} %collective-permute-done.5.left_ref, bf16[1152,512]{1,0:T(8,128)(2,1)S(1)} %get-tuple-element.22.low_ref), custom_call_target="tpu_custom_call" | custom-call | flops 1207959552 | bytes 2359352 | tf_op jit(solution)/shard_map/pallas_call | solution.py:24
  56.2 5.1 %collective-permute-done.right_ref = bf16[256,1152]{1,0:T(8,128)(2,1)} collective-permute-done((bf16[256,1152]{1,0:T(8,128)(2,1)}, bf16[256,1152]{1,0:T(8,128)(2,1)}, u32[]{:S(2)}, u32[]{:S(2)}) %collective-permute-start) | collective-permute-done | bytes 589856 | tf_op jit(solution)/shard_map/ppermute | solution.py:231
  61.2 3.5 %shard_map.79 = (f32[592,512]{1,0:T(8,128)S(1)}, bf16[592,512]{1,0:T(8,128)(2,1)S(1)}) custom-call(s32[12]{0:T(128)S(1)} %stack.48.at_ref, f32[2]{0:T(128)S(1)} %pad_maximum_fusion.par_ref, bf16[256,1152]{1,0:T(8,128)(2,1)} %collective-permute-done.right_ref, bf16[256,1152]{1,0:T(8,128)(2,1)} %collective-permute-done.1.far_ref, ...), custom_call_target="tpu_custom_call" | custom-call | flops 1207959552 | bytes 7079992 | tf_op jit(solution)/shard_map/pallas_call | solution.py:24
  64.8 1.9 %collective-permute-start.6 = (bf16[592,512]{1,0:T(8,128)(2,1)S(1)}, bf16[592,512]{1,0:T(8,128)(2,1)S(1)}, u32[]{:S(2)}, u32[]{:S(2)}) collective-permute-start(bf16[592,512]{1,0:T(8,128)(2,1)S(1)} %get-tuple-element.27), channel_id=1, source_target_pairs={{0,1},{1,0},{2,3},{3,2},{4,5},{5,4},{6,7},{7,6},{8,9},{9,8},{10,11... | collective-permute-start | bytes 1818632 | tf_op jit(solution)/shard_map/ppermute | solution.py:330
  66.7 2.0 %collective-permute-done.6.got_ref = bf16[592,512]{1,0:T(8,128)(2,1)S(1)} collective-permute-done((bf16[592,512]{1,0:T(8,128)(2,1)S(1)}, bf16[592,512]{1,0:T(8,128)(2,1)S(1)}, u32[]{:S(2)}, u32[]{:S(2)}) %collective-permute-start.6) | collective-permute-done | bytes 606240 | tf_op jit(solution)/shard_map/ppermute | solution.py:330
  68.7 0.7 shard_map.80
  69.4 1.9 %collective-permute-start.7 = (bf16[304,512]{1,0:T(8,128)(2,1)S(1)}, bf16[304,512]{1,0:T(8,128)(2,1)S(1)}, u32[]{:S(2)}, u32[]{:S(2)}) collective-permute-start(bf16[304,512]{1,0:T(8,128)(2,1)S(1)} %get-tuple-element.29), channel_id=1, source_target_pairs={{0,2},{2,0},{1,3},{3,1},{4,6},{6,4},{5,7},{7,5},{8,10},{10,8},{9,1... | collective-permute-start | bytes 933896 | tf_op jit(solution)/shard_map/ppermute | solution.py:339
  71.4 9.4 %collective-permute-done.7.got_ref = bf16[304,512]{1,0:T(8,128)(2,1)S(1)} collective-permute-done((bf16[304,512]{1,0:T(8,128)(2,1)S(1)}, bf16[304,512]{1,0:T(8,128)(2,1)S(1)}, u32[]{:S(2)}, u32[]{:S(2)}) %collective-permute-start.7) | collective-permute-done | bytes 311328 | tf_op jit(solution)/shard_map/ppermute | solution.py:339
  80.7 1.5 shard_map.81
  82.2 7.7 %all-to-all-start.1 = ((bf16[32,88,128]{2,1,0:T(8,128)(2,1)}), bf16[32,88,128]{2,1,0:T(8,128)(2,1)}, u32[]{:S(2)}, u32[]{:S(2)}) async-start(bf16[32,88,128]{2,1,0:T(8,128)(2,1)} %bitcast.12), calls=%async_computation.1 | async-start | bytes 1441792 | tf_op jit(solution)/shard_map/all_to_all | solution.py:48
  89.9 7.0 %collective-permute-start.10 = (bf16[304,128]{1,0:T(8,128)(2,1)S(1)}, bf16[304,128]{1,0:T(8,128)(2,1)S(1)}, u32[]{:S(2)}, u32[]{:S(2)}) collective-permute-start(bf16[304,128]{1,0:T(8,128)(2,1)S(1)} %get-tuple-element.38), channel_id=1, source_target_pairs={{0,4},{4,8},{8,12},{12,0},{1,5},{5,9},{9,13},{13,1},{2,6},{6,10},{... | collective-permute-start | bytes 233480 | tf_op jit(solution)/shard_map/ppermute | solution.py:231
  96.9 2.7 %collective-permute-start.8 = (bf16[304,128]{1,0:T(8,128)(2,1)S(1)}, bf16[304,128]{1,0:T(8,128)(2,1)S(1)}, u32[]{:S(2)}, u32[]{:S(2)}) collective-permute-start(bf16[304,128]{1,0:T(8,128)(2,1)S(1)} %get-tuple-element.36), channel_id=1, source_target_pairs={{0,12},{4,0},{8,4},{12,8},{1,13},{5,1},{9,5},{13,9},{2,14},{6,2},{... | collective-permute-start | bytes 233480 | tf_op jit(solution)/shard_map/ppermute | solution.py:231
  99.6 6.0 %collective-permute-start.9 = (bf16[304,128]{1,0:T(8,128)(2,1)S(1)}, bf16[304,128]{1,0:T(8,128)(2,1)S(1)}, u32[]{:S(2)}, u32[]{:S(2)}) collective-permute-start(bf16[304,128]{1,0:T(8,128)(2,1)S(1)} %get-tuple-element.37), channel_id=1, source_target_pairs={{0,8},{4,12},{8,0},{12,4},{1,9},{5,13},{9,1},{13,5},{2,10},{6,14},... | collective-permute-start | bytes 233480 | tf_op jit(solution)/shard_map/ppermute | solution.py:231
  105.7 4.3 %collective-permute-done.9.refs_2_ = bf16[304,128]{1,0:T(8,128)(2,1)S(1)} collective-permute-done((bf16[304,128]{1,0:T(8,128)(2,1)S(1)}, bf16[304,128]{1,0:T(8,128)(2,1)S(1)}, u32[]{:S(2)}, u32[]{:S(2)}) %collective-permute-start.9) | collective-permute-done | bytes 77856 | tf_op jit(solution)/shard_map/ppermute | solution.py:231
  110.0 0.1 shard_map.82.refs_0_
  110.0 0.6 copy-done.4
  110.7 0.7 all-to-all-done.1.parts_ref
  111.3 1.9 %shard_map.83 = bf16[4,88,128]{2,1,0:T(8,128)(2,1)} custom-call(s32[12]{0:T(128)} %copy-done.7, bf16[32,88,128]{2,1,0:T(8,128)(2,1)} %all-to-all-done.1.parts_ref, bf16[288,128]{1,0:T(8,128)(2,1)} %copy-done.4), custom_call_target="tpu_custom_call" | custom-call | tf_op jit(solution)/shard_map/pallas_call | solution.py:355
  113.2 15.4 %all_to_all.33.parts_ref = bf16[4,88,128]{2,1,0:T(8,128)(2,1)S(1)} all-to-all(bf16[4,88,128]{2,1,0:T(8,128)(2,1)} %shard_map.83), channel_id=1, replica_groups=mesh['y'=8,'x'=4,'zh'=4,'zl'=2,'c'=2] {'zh'}, dimensions={0} | all-to-all | bytes 180224 | tf_op jit(solution)/shard_map/all_to_all | solution.py:48
  128.6 0.6 shard_map.84
  129.2 0.9 copy-done.2
  130.1 7.9 %all-to-all-start.3 = ((bf16[32,88,128]{2,1,0:T(8,128)(2,1)}), bf16[32,88,128]{2,1,0:T(8,128)(2,1)S(1)}, u32[]{:S(2)}, u32[]{:S(2)}) async-start(bf16[32,88,128]{2,1,0:T(8,128)(2,1)} %copy-done.2), calls=%async_computation.3 | async-start | bytes 1441792 | tf_op jit(solution)/shard_map/all_to_all | solution.py:48
  138.0 1.9 %collective-permute-start.11 = (bf16[288,128]{1,0:T(8,128)(2,1)S(1)}, bf16[288,128]{1,0:T(8,128)(2,1)S(1)}, u32[]{:S(2)}, u32[]{:S(2)}) collective-permute-start(bf16[288,128]{1,0:T(8,128)(2,1)S(1)} %copy-done.5), channel_id=1, source_target_pairs={{0,1},{1,0},{2,3},{3,2},{4,5},{5,4},{6,7},{7,6},{8,9},{9,8},{10,11... | collective-permute-start | bytes 221192 | tf_op jit(solution)/shard_map/ppermute | solution.py:373
  139.9 2.6 %collective-permute-start.12 = (bf16[288,128]{1,0:T(8,128)(2,1)S(1)}, bf16[288,128]{1,0:T(8,128)(2,1)S(1)}, u32[]{:S(2)}, u32[]{:S(2)}) collective-permute-start(bf16[288,128]{1,0:T(8,128)(2,1)S(1)} %copy-done.5), channel_id=1, source_target_pairs={{0,2},{1,3},{2,0},{3,1},{4,6},{5,7},{6,4},{7,5},{8,10},{9,11},{10,... | collective-permute-start | bytes 221192 | tf_op jit(solution)/shard_map/ppermute | solution.py:373
  142.5 3.1 %collective-permute-start.13 = (bf16[288,128]{1,0:T(8,128)(2,1)S(1)}, bf16[288,128]{1,0:T(8,128)(2,1)S(1)}, u32[]{:S(2)}, u32[]{:S(2)}) collective-permute-start(bf16[288,128]{1,0:T(8,128)(2,1)S(1)} %copy-done.5), channel_id=1, source_target_pairs={{0,3},{1,2},{2,1},{3,0},{4,7},{5,6},{6,5},{7,4},{8,11},{9,10},{10,... | collective-permute-start | bytes 221192 | tf_op jit(solution)/shard_map/ppermute | solution.py:373
  145.6 0.9 collective-permute-done.12.refs_2_
  146.5 2.2 %collective-permute-done.13.refs_3_ = bf16[288,128]{1,0:T(8,128)(2,1)S(1)} collective-permute-done((bf16[288,128]{1,0:T(8,128)(2,1)S(1)}, bf16[288,128]{1,0:T(8,128)(2,1)S(1)}, u32[]{:S(2)}, u32[]{:S(2)}) %collective-permute-start.13) | collective-permute-done | bytes 73760 | tf_op jit(solution)/shard_map/ppermute | solution.py:373
  148.6 2.2 %shard_map.86 = bf16[128,1152]{1,0:T(8,128)(2,1)} custom-call(s32[12]{0:T(128)S(1)} %copy-done.8, bf16[1152,1152]{1,0:T(8,128)(2,1)S(1)} %copy-done, bf16[288,128]{1,0:T(8,128)(2,1)S(1)} %copy-done.5, bf16[288,128]{1,0:T(8,128)(2,1)S(1)} %collective-permute-done.11.refs_1_, bf16[288,128]{1,0:T(8,128)(2,1)S(1)} %collective-permute-done.12.refs_2_, ...), custom_call_target="tpu_custom_call" | custom-call | flops 339738624 | bytes 2949168 | tf_op jit(solution)/shard_map/pallas_call | solution.py:24
  150.9 4.8 %all-to-all-done.3 = bf16[32,88,128]{2,1,0:T(8,128)(2,1)S(1)} async-done(((bf16[32,88,128]{2,1,0:T(8,128)(2,1)}), bf16[32,88,128]{2,1,0:T(8,128)(2,1)S(1)}, u32[]{:S(2)}, u32[]{:S(2)}) %all-to-all-start.3) | async-done | bytes 720928 | tf_op jit(solution)/shard_map/all_to_all | solution.py:48
  155.7 1.0 shard_map.85
  (22 shorter events, 0.1 us)
Async XLA Ops:
  0.6 41.8 %copy-start = (bf16[1152,1152]{1,0:T(8,128)(2,1)S(1)}, bf16[1152,1152]{1,0:T(8,128)(2,1)}, u32[]{:S(2)}) copy-start(bf16[1152,1152]{1,0:T(8,128)(2,1)} %weight_ref.1) | copy-start | bytes 7962628
  0.6 1.0 copy-start.6
  2.6 26.1 %all-to-all-start = ((bf16[8,32,1152]{2,1,0:T(8,128)(2,1)}), bf16[8,32,1152]{2,1,0:T(8,128)(2,1)}, u32[]{:S(2)}, u32[]{:S(2)}) async-start(bf16[8,32,1152]{2,1,0:T(8,128)(2,1)} %bitcast.9), calls=%async_computation | async-start | bytes 1179648 | tf_op jit(solution)/shard_map/all_to_all | solution.py:48
  9.7 15.8 %collective-permute-start.2 = (bf16[128,1152]{1,0:T(8,128)(2,1)}, bf16[128,1152]{1,0:T(8,128)(2,1)S(1)}, u32[]{:S(2)}, u32[]{:S(2)}) collective-permute-start(bf16[128,1152]{1,0:T(8,128)(2,1)} %own_ref.1), channel_id=1, source_target_pairs={{2,4},{3,6},{0,13},{1,15},{6,8},{7,10},{4,1},{5,3},{10,12},{11,14}... | collective-permute-start | bytes 884744 | tf_op jit(solution)/shard_map/ppermute | solution.py:278
  14.9 24.6 %collective-permute-start.3 = (bf16[64,1152]{1,0:T(8,128)(2,1)S(1)}, bf16[64,1152]{1,0:T(8,128)(2,1)}, u32[]{:S(2)}, u32[]{:S(2)}) collective-permute-start(bf16[64,1152]{1,0:T(8,128)(2,1)S(1)} %constant_dynamic-slice_fusion), channel_id=1, source_target_pairs={{2,8},{3,9},{0,10},{1,11},{6,12},{7,13},{4,14},{5,15},{10,0},{11,1... | collective-permute-start | bytes 442376 | tf_op jit(solution)/shard_map/ppermute | solution.py:277
  28.7 23.7 %collective-permute-start.5 = (bf16[256,1152]{1,0:T(8,128)(2,1)}, bf16[256,1152]{1,0:T(8,128)(2,1)}, u32[]{:S(2)}, u32[]{:S(2)}) collective-permute-start(bf16[256,1152]{1,0:T(8,128)(2,1)} %bitcast.10.own_ref), channel_id=1, source_target_pairs={{0,16},{16,32},{32,48},{48,0},{1,17},{17,33},{33,49},{49,1},{2,18}... | collective-permute-start | bytes 1769480 | tf_op jit(solution)/shard_map/ppermute | solution.py:231
  32.1 29.1 %collective-permute-start = (bf16[256,1152]{1,0:T(8,128)(2,1)}, bf16[256,1152]{1,0:T(8,128)(2,1)}, u32[]{:S(2)}, u32[]{:S(2)}) collective-permute-start(bf16[256,1152]{1,0:T(8,128)(2,1)} %bitcast.10.own_ref), channel_id=1, source_target_pairs={{0,48},{16,0},{32,16},{48,32},{1,49},{17,1},{33,17},{49,33},{2,50}... | collective-permute-start | bytes 1769480 | tf_op jit(solution)/shard_map/ppermute | solution.py:231
  35.8 25.5 %collective-permute-start.1 = (bf16[256,1152]{1,0:T(8,128)(2,1)}, bf16[256,1152]{1,0:T(8,128)(2,1)}, u32[]{:S(2)}, u32[]{:S(2)}) collective-permute-start(bf16[256,1152]{1,0:T(8,128)(2,1)} %bitcast.10.own_ref), channel_id=1, source_target_pairs={{0,32},{16,48},{32,0},{48,16},{1,33},{17,49},{33,1},{49,17},{2,34}... | collective-permute-start | bytes 1769480 | tf_op jit(solution)/shard_map/ppermute | solution.py:231
  40.5 6.8 %collective-permute-start.4 = (bf16[192,1152]{1,0:T(8,128)(2,1)S(1)}, bf16[192,1152]{1,0:T(8,128)(2,1)}, u32[]{:S(2)}, u32[]{:S(2)}) collective-permute-start(bf16[192,1152]{1,0:T(8,128)(2,1)S(1)} %constant_dynamic-update-slice_fusion.fetched_ref), channel_id=1, source_target_pairs={{0,1},{1,0},{2,3},{3,2},{4,5},{5,4},{6,7},{7,6},{8,9},{9,8},{10,11... | collective-permute-start | bytes 1327112 | tf_op jit(solution)/shard_map/ppermute | solution.py:284
  42.4 4.8 %copy-start.3 = (bf16[128,1152]{1,0:T(8,128)(2,1)S(1)}, bf16[128,1152]{1,0:T(8,128)(2,1)}, u32[]{:S(2)}) copy-start(bf16[128,1152]{1,0:T(8,128)(2,1)} %own_ref.1) | copy-start | bytes 884740
  47.1 21.6 %copy-start.7 = (s32[12]{0:T(128)}, s32[12]{0:T(128)S(1)}, u32[]{:S(2)}) copy-start(s32[12]{0:T(128)S(1)} %stack.48.at_ref) | copy-start | bytes 148
  47.2 1.8 %copy-start.1 = (bf16[1152,1152]{0,1:T(8,128)(2,1)S(1)}, bf16[1152,1152]{0,1:T(8,128)(2,1)}, u32[]{:S(2)}) copy-start(bf16[1152,1152]{0,1:T(8,128)(2,1)} %copy.8) | copy-start | bytes 7962628
  64.8 3.9 %collective-permute-start.6 = (bf16[592,512]{1,0:T(8,128)(2,1)S(1)}, bf16[592,512]{1,0:T(8,128)(2,1)S(1)}, u32[]{:S(2)}, u32[]{:S(2)}) collective-permute-start(bf16[592,512]{1,0:T(8,128)(2,1)S(1)} %get-tuple-element.27), channel_id=1, source_target_pairs={{0,1},{1,0},{2,3},{3,2},{4,5},{5,4},{6,7},{7,6},{8,9},{9,8},{10,11... | collective-permute-start | bytes 1818632 | tf_op jit(solution)/shard_map/ppermute | solution.py:330
  69.4 11.3 %collective-permute-start.7 = (bf16[304,512]{1,0:T(8,128)(2,1)S(1)}, bf16[304,512]{1,0:T(8,128)(2,1)S(1)}, u32[]{:S(2)}, u32[]{:S(2)}) collective-permute-start(bf16[304,512]{1,0:T(8,128)(2,1)S(1)} %get-tuple-element.29), channel_id=1, source_target_pairs={{0,2},{2,0},{1,3},{3,1},{4,6},{6,4},{5,7},{7,5},{8,10},{10,8},{9,1... | collective-permute-start | bytes 933896 | tf_op jit(solution)/shard_map/ppermute | solution.py:339
  80.7 47.9 %copy-start.8 = (s32[12]{0:T(128)S(1)}, s32[12]{0:T(128)}, u32[]{:S(2)}) copy-start(s32[12]{0:T(128)} %copy-done.7) | copy-start | bytes 148
  82.2 29.1 %all-to-all-start.1 = ((bf16[32,88,128]{2,1,0:T(8,128)(2,1)}), bf16[32,88,128]{2,1,0:T(8,128)(2,1)}, u32[]{:S(2)}, u32[]{:S(2)}) async-start(bf16[32,88,128]{2,1,0:T(8,128)(2,1)} %bitcast.12), calls=%async_computation.1 | async-start | bytes 1441792 | tf_op jit(solution)/shard_map/all_to_all | solution.py:48
  89.9 15.7 %collective-permute-start.10 = (bf16[304,128]{1,0:T(8,128)(2,1)S(1)}, bf16[304,128]{1,0:T(8,128)(2,1)S(1)}, u32[]{:S(2)}, u32[]{:S(2)}) collective-permute-start(bf16[304,128]{1,0:T(8,128)(2,1)S(1)} %get-tuple-element.38), channel_id=1, source_target_pairs={{0,4},{4,8},{8,12},{12,0},{1,5},{5,9},{9,13},{13,1},{2,6},{6,10},{... | collective-permute-start | bytes 233480 | tf_op jit(solution)/shard_map/ppermute | solution.py:231
  96.9 8.7 %collective-permute-start.8 = (bf16[304,128]{1,0:T(8,128)(2,1)S(1)}, bf16[304,128]{1,0:T(8,128)(2,1)S(1)}, u32[]{:S(2)}, u32[]{:S(2)}) collective-permute-start(bf16[304,128]{1,0:T(8,128)(2,1)S(1)} %get-tuple-element.36), channel_id=1, source_target_pairs={{0,12},{4,0},{8,4},{12,8},{1,13},{5,1},{9,5},{13,9},{2,14},{6,2},{... | collective-permute-start | bytes 233480 | tf_op jit(solution)/shard_map/ppermute | solution.py:231
  99.6 10.3 %collective-permute-start.9 = (bf16[304,128]{1,0:T(8,128)(2,1)S(1)}, bf16[304,128]{1,0:T(8,128)(2,1)S(1)}, u32[]{:S(2)}, u32[]{:S(2)}) collective-permute-start(bf16[304,128]{1,0:T(8,128)(2,1)S(1)} %get-tuple-element.37), channel_id=1, source_target_pairs={{0,8},{4,12},{8,0},{12,4},{1,9},{5,13},{9,1},{13,5},{2,10},{6,14},... | collective-permute-start | bytes 233480 | tf_op jit(solution)/shard_map/ppermute | solution.py:231
  110.0 0.6 copy-start.4
  111.3 26.7 %copy-start.5 = (bf16[288,128]{1,0:T(8,128)(2,1)S(1)}, bf16[288,128]{1,0:T(8,128)(2,1)}, u32[]{:S(2)}) copy-start(bf16[288,128]{1,0:T(8,128)(2,1)} %copy-done.4) | copy-start | bytes 221188
  129.2 0.9 copy-start.2
  130.1 25.6 %all-to-all-start.3 = ((bf16[32,88,128]{2,1,0:T(8,128)(2,1)}), bf16[32,88,128]{2,1,0:T(8,128)(2,1)S(1)}, u32[]{:S(2)}, u32[]{:S(2)}) async-start(bf16[32,88,128]{2,1,0:T(8,128)(2,1)} %copy-done.2), calls=%async_computation.3 | async-start | bytes 1441792 | tf_op jit(solution)/shard_map/all_to_all | solution.py:48
  138.0 7.6 %collective-permute-start.11 = (bf16[288,128]{1,0:T(8,128)(2,1)S(1)}, bf16[288,128]{1,0:T(8,128)(2,1)S(1)}, u32[]{:S(2)}, u32[]{:S(2)}) collective-permute-start(bf16[288,128]{1,0:T(8,128)(2,1)S(1)} %copy-done.5), channel_id=1, source_target_pairs={{0,1},{1,0},{2,3},{3,2},{4,5},{5,4},{6,7},{7,6},{8,9},{9,8},{10,11... | collective-permute-start | bytes 221192 | tf_op jit(solution)/shard_map/ppermute | solution.py:373
  139.9 6.6 %collective-permute-start.12 = (bf16[288,128]{1,0:T(8,128)(2,1)S(1)}, bf16[288,128]{1,0:T(8,128)(2,1)S(1)}, u32[]{:S(2)}, u32[]{:S(2)}) collective-permute-start(bf16[288,128]{1,0:T(8,128)(2,1)S(1)} %copy-done.5), channel_id=1, source_target_pairs={{0,2},{1,3},{2,0},{3,1},{4,6},{5,7},{6,4},{7,5},{8,10},{9,11},{10,... | collective-permute-start | bytes 221192 | tf_op jit(solution)/shard_map/ppermute | solution.py:373
  142.5 6.1 %collective-permute-start.13 = (bf16[288,128]{1,0:T(8,128)(2,1)S(1)}, bf16[288,128]{1,0:T(8,128)(2,1)S(1)}, u32[]{:S(2)}, u32[]{:S(2)}) collective-permute-start(bf16[288,128]{1,0:T(8,128)(2,1)S(1)} %copy-done.5), channel_id=1, source_target_pairs={{0,3},{1,2},{2,1},{3,0},{4,7},{5,6},{6,5},{7,4},{8,11},{9,10},{10,... | collective-permute-start | bytes 221192 | tf_op jit(solution)/shard_map/ppermute | solution.py:373
